TPU v7x, 32 devices: a whole 2x2x4 slice. The times are simulated.
32 devices in a mesh: dp: 16 (over z, y, x), pair: 2 (over core).
Axes of the slice: x: 2, y: 2, z: 4, core: 2. Of those that a mesh axis runs over, the one named last changes fastest.
Arguments:
- tokens: bfloat16 [4096, 2, 1024], P(('dp', 'pair')), may hold values from -6 to 6
- norm_attn: bfloat16 [2, 1024], P(None, ('dp', 'pair')), may hold values from 0.099609375 to 1.8984375
- w_qkv: bfloat16 [2, 1024, 3072], P(None, ('dp', 'pair')), may hold values from -0.1875 to 0.1875
- w_out: bfloat16 [2, 1024, 1024], P(None, ('dp', 'pair')), may hold values from -0.375 to 0.375
- norm_ff: bfloat16 [2, 1024], P(None, ('dp', 'pair')), may hold values from 0.099609375 to 1.8984375
- w_gate_up: bfloat16 [2, 1024, 8192], P(None, ('dp', 'pair')), may hold values from -0.1875 to 0.1875
- w_down: bfloat16 [2, 4096, 1024], P(None, ('dp', 'pair')), may hold values from -0.125 to 0.125
- cotangent: bfloat16 [4096, 2, 1024], P(('dp', 'pair')), may hold values from -6 to 6
- valid_frames: int32 [32], P(('dp', 'pair')), may hold values from 32 to 128, as said below
- item_lengths: int32 [4], replicated, may hold values from 512 to 1536, as said below
Outputs:
- output: bfloat16 [4096, 2, 1024], P(('dp', 'pair'))
- grad_tokens: float32 [4096, 2, 1024], P(('dp', 'pair'))
- grad_norm_attn: float32 [2, 1024], P(None, ('dp', 'pair'))
- grad_w_qkv: float32 [2, 1024, 3072], P(None, ('dp', 'pair'))
- grad_w_out: float32 [2, 1024, 1024], P(None, ('dp', 'pair'))
- grad_norm_ff: float32 [2, 1024], P(None, ('dp', 'pair'))
- grad_w_gate_up: float32 [2, 1024, 8192], P(None, ('dp', 'pair'))
- grad_w_down: float32 [2, 4096, 1024], P(None, ('dp', 'pair'))
Inputs may be any that keep to these rules, and one draw needn't show every extreme that they name: `valid_frames`: entry j counts the slots, from the first, of device j's 128 frame slots that hold data; some device is full in every draw. `item_lengths`: the items tile all 4096 slots in order, padding slots included, so the lengths sum to 4096; some item has exactly 1536 slots.
All inputs are finite; a program needn't handle non-finite values.
Results may differ from a plain program's by a relative error of at most 0.0095.
Values may be sent and summed in bfloat16 or wider, within the bound.
A program may use at most 448 MiB of HBM per device.

v0:
```python
import math

import jax
import jax.numpy as jnp
from jax import lax
from jax.sharding import PartitionSpec as P

HEAD_DIM = 64


def per_pos(activations, weight):
    return jnp.einsum("fgk,gke->fge", activations, weight, preferred_element_type=jnp.float32)


def per_pos_back(gradients, weight):
    return jnp.einsum("fge,gke->fgk", gradients, weight, preferred_element_type=jnp.float32)


def pos_grad(activations, gradients):
    return jnp.einsum("fgk,fge->kge", activations, gradients, preferred_element_type=jnp.float32)


def gain_grad(normed_rows, gradients):
    return jnp.transpose(jnp.sum(normed_rows * gradients, axis=0))


def back_layout(share):
    return jnp.swapaxes(share, 0, 1)


def normed(values):
    inverse = lax.rsqrt(jnp.mean(values * values, axis=-1, keepdims=True) + 1e-05)
    return (values * inverse, inverse)


def norm_back(normed_rows, inverse, gradients):
    return inverse * (
        gradients - normed_rows * jnp.mean(gradients * normed_rows, axis=-1, keepdims=True)
    )


def gather_ff_fwd(norm_ff, w_gate_up, w_down, start, group):
    return (
        lax.all_gather(norm_ff[start : start + group], ("dp", "pair"), axis=1, tiled=True),
        lax.all_gather(w_gate_up[start : start + group], ("dp", "pair"), axis=1, tiled=True),
        lax.all_gather(w_down[start : start + group], ("dp", "pair"), axis=1, tiled=True),
    )


def gather_ff_back(norm_ff, w_gate_up, w_down, start, group):
    return (
        lax.all_gather(norm_ff[start : start + group], ("dp", "pair"), axis=1, tiled=True),
        lax.all_gather(w_gate_up[start : start + group], ("dp", "pair"), axis=1, tiled=True),
        lax.all_gather(w_down[start : start + group], ("dp", "pair"), axis=1, tiled=True),
    )


def local(
    tokens,
    norm_attn,
    w_qkv,
    w_out,
    norm_ff,
    w_gate_up,
    w_down,
    cotangent,
    valid_frames,
    item_lengths,
):
    frame_count, positions, model_width = tokens.shape
    head_count = model_width // HEAD_DIM
    ff_units = w_gate_up.shape[2] // 2
    score_scale = 1.0 / math.sqrt(HEAD_DIM)
    causal = jnp.arange(positions)[:, None] >= jnp.arange(positions)[None, :]
    head_shape = (frame_count, positions, head_count, HEAD_DIM)
    group = 1
    gains_attn, qkv_full, out_full = (
        lax.all_gather(norm_attn, ("dp", "pair"), axis=1, tiled=True),
        lax.all_gather(w_qkv, ("dp", "pair"), axis=1, tiled=True),
        lax.all_gather(w_out, ("dp", "pair"), axis=1, tiled=True),
    )
    resid_in = tokens.astype(jnp.float32)
    normed_one, inverse_one = normed(resid_in)
    attn_in = (normed_one * gains_attn.astype(jnp.float32)[None]).astype(jnp.bfloat16)
    qkv_rows = per_pos(attn_in, qkv_full).astype(jnp.bfloat16)
    queries = qkv_rows[..., :model_width].reshape(head_shape)
    key_heads = qkv_rows[..., model_width : 2 * model_width].reshape(head_shape)
    value_heads = qkv_rows[..., 2 * model_width :].reshape(head_shape)
    scores = (
        jnp.einsum("fphd,fqhd->fhpq", queries, key_heads, preferred_element_type=jnp.float32)
        * score_scale
    )
    scores = jnp.where(causal, scores, -1e30)
    row_max = jnp.max(scores, axis=-1, keepdims=True)
    attn_probs = jnp.exp(scores - row_max)
    attn_probs = attn_probs / jnp.sum(attn_probs, axis=-1, keepdims=True)
    probs_low = attn_probs.astype(jnp.bfloat16)
    context = jnp.einsum(
        "fhpq,fqhd->fphd", probs_low, value_heads, preferred_element_type=jnp.float32
    )
    context = context.astype(jnp.bfloat16).reshape(frame_count, positions, model_width)
    resid_mid = resid_in + per_pos(context, out_full)
    kept_parts = []
    out_parts = []
    for start in range(0, positions, group):
        gains_ff, gate_up_full, down_full = gather_ff_fwd(norm_ff, w_gate_up, w_down, start, group)
        mid_part = resid_mid[:, start : start + group]
        normed_two, inverse_two = normed(mid_part)
        ff_in = (normed_two * gains_ff.astype(jnp.float32)[None]).astype(jnp.bfloat16)
        gate_up = per_pos(ff_in, gate_up_full)
        gate_part = gate_up[..., :ff_units]
        up_part = gate_up[..., ff_units:]
        sigmoid_gate = jax.nn.sigmoid(gate_part)
        silu_gate = gate_part * sigmoid_gate
        hidden = (silu_gate * up_part).astype(jnp.bfloat16)
        out_parts.append(mid_part + per_pos(hidden, down_full))
        kept_parts.append(
            (normed_two, inverse_two, ff_in, gate_part, up_part, sigmoid_gate, silu_gate, hidden)
        )
    output = jnp.concatenate(out_parts, axis=1).astype(jnp.bfloat16)
    device_index = lax.axis_index(("dp", "pair"))
    local_ids = jnp.arange(frame_count, dtype=jnp.int32)
    frame_ids = device_index * frame_count + local_ids
    item_ends = jnp.cumsum(item_lengths)
    item_starts = item_ends - item_lengths
    in_item = (frame_ids[:, None] >= item_starts[None, :]) & (
        frame_ids[:, None] < item_ends[None, :]
    )
    item_share = 8 * frame_count / item_lengths.astype(jnp.float32)
    frame_weight = jnp.sum(jnp.where(in_item, item_share[None, :], 0.0), axis=1)
    frame_weight = jnp.where(local_ids < valid_frames[0], frame_weight, 0.0)
    grad_out = cotangent.astype(jnp.float32) * frame_weight[:, None, None]
    mid_grads = []
    share_norm_ff_parts = []
    share_gate_up_parts = []
    share_down_parts = []
    for index, start in enumerate(range(0, positions, group)):
        normed_two, inverse_two, ff_in, gate_part, up_part, sigmoid_gate, silu_gate, hidden = (
            kept_parts[index]
        )
        gains_ff, gate_up_full, down_full = gather_ff_back(norm_ff, w_gate_up, w_down, start, group)
        grad_part = grad_out[:, start : start + group]
        grad_low = grad_part.astype(jnp.bfloat16)
        grad_down = pos_grad(hidden, grad_low)
        d_hidden = per_pos_back(grad_low, down_full)
        d_gate = d_hidden * up_part * sigmoid_gate * (1.0 + gate_part * (1.0 - sigmoid_gate))
        d_up = d_hidden * silu_gate
        d_gate_up = jnp.concatenate([d_gate, d_up], axis=-1).astype(jnp.bfloat16)
        grad_gate_up = pos_grad(ff_in, d_gate_up)
        d_ff_in = per_pos_back(d_gate_up, gate_up_full)
        grad_norm_ff = gain_grad(normed_two, d_ff_in)
        mid_grads.append(
            grad_part
            + norm_back(normed_two, inverse_two, d_ff_in * gains_ff.astype(jnp.float32)[None])
        )
        share_a, share_b, share_c = (
            lax.psum_scatter(grad_norm_ff, ("dp", "pair"), scatter_dimension=0, tiled=True),
            lax.psum_scatter(grad_gate_up, ("dp", "pair"), scatter_dimension=0, tiled=True),
            lax.psum_scatter(grad_down, ("dp", "pair"), scatter_dimension=0, tiled=True),
        )
        share_norm_ff_parts.append(jnp.transpose(share_a))
        share_gate_up_parts.append(back_layout(share_b))
        share_down_parts.append(back_layout(share_c))
    d_mid = jnp.concatenate(mid_grads, axis=1)
    gains_attn, qkv_full, out_full = (
        lax.all_gather(norm_attn, ("dp", "pair"), axis=1, tiled=True),
        lax.all_gather(w_qkv, ("dp", "pair"), axis=1, tiled=True),
        lax.all_gather(w_out, ("dp", "pair"), axis=1, tiled=True),
    )
    d_mid_low = d_mid.astype(jnp.bfloat16)
    grad_out_proj = pos_grad(context, d_mid_low)
    d_context = per_pos_back(d_mid_low, out_full).astype(jnp.bfloat16).reshape(head_shape)
    d_probs = jnp.einsum(
        "fphd,fqhd->fhpq", d_context, value_heads, preferred_element_type=jnp.float32
    )
    d_values = jnp.einsum(
        "fhpq,fphd->fqhd", probs_low, d_context, preferred_element_type=jnp.float32
    )
    d_scores = attn_probs * (d_probs - jnp.sum(attn_probs * d_probs, axis=-1, keepdims=True))
    d_scores = d_scores.astype(jnp.bfloat16)
    d_queries = (
        jnp.einsum("fhpq,fqhd->fphd", d_scores, key_heads, preferred_element_type=jnp.float32)
        * score_scale
    )
    d_keys = (
        jnp.einsum("fhpq,fphd->fqhd", d_scores, queries, preferred_element_type=jnp.float32)
        * score_scale
    )
    row_shape = (frame_count, positions, model_width)
    d_qkv = jnp.concatenate(
        [d_queries.reshape(row_shape), d_keys.reshape(row_shape), d_values.reshape(row_shape)],
        axis=-1,
    ).astype(jnp.bfloat16)
    grad_qkv = pos_grad(attn_in, d_qkv)
    d_attn_in = per_pos_back(d_qkv, qkv_full)
    grad_norm_attn = gain_grad(normed_one, d_attn_in)
    grad_tokens = d_mid + norm_back(
        normed_one, inverse_one, d_attn_in * gains_attn.astype(jnp.float32)[None]
    )
    share_norm_attn, share_qkv, share_out = (
        lax.psum_scatter(grad_norm_attn, ("dp", "pair"), scatter_dimension=0, tiled=True),
        lax.psum_scatter(grad_qkv, ("dp", "pair"), scatter_dimension=0, tiled=True),
        lax.psum_scatter(grad_out_proj, ("dp", "pair"), scatter_dimension=0, tiled=True),
    )
    share_norm_attn = jnp.transpose(share_norm_attn)
    share_qkv = back_layout(share_qkv)
    share_out = back_layout(share_out)
    share_norm_ff = jnp.concatenate(share_norm_ff_parts, axis=0)
    share_gate_up = jnp.concatenate(share_gate_up_parts, axis=0)
    share_down = jnp.concatenate(share_down_parts, axis=0)
    return (
        output,
        grad_tokens,
        share_norm_attn,
        share_qkv,
        share_out,
        share_norm_ff,
        share_gate_up,
        share_down,
    )


def solution(mesh):
    in_specs = (
        P(("dp", "pair"), None, None),
        P(None, ("dp", "pair")),
        P(None, ("dp", "pair"), None),
        P(None, ("dp", "pair"), None),
        P(None, ("dp", "pair")),
        P(None, ("dp", "pair"), None),
        P(None, ("dp", "pair"), None),
        P(("dp", "pair"), None, None),
        P(("dp", "pair")),
        P(),
    )
    out_specs = (
        P(("dp", "pair"), None, None),
        P(("dp", "pair"), None, None),
        P(None, ("dp", "pair")),
        P(None, ("dp", "pair"), None),
        P(None, ("dp", "pair"), None),
        P(None, ("dp", "pair")),
        P(None, ("dp", "pair"), None),
        P(None, ("dp", "pair"), None),
    )
    return jax.shard_map(local, mesh=mesh, in_specs=in_specs, out_specs=out_specs, check_vma=False)
```

profile of v0, /device:TPU:0, one launch (start us, length us, event | category | flops | bytes accessed | tf_op | source)
XLA Modules:
  0.0 2993.3 jit_solution(14894287163715438821)
XLA Ops:
  13.2 43.3 %all-gather = bf16[32,32,2]{1,2,0:T(2,128)(2,1)S(1)} all-gather(bf16[1,32,2]{1,2,0:T(2,128)(2,1)S(1)} %bitcast.263), channel_id=1, replica_groups=mesh['dp'=16,'pair'=2] {'dp','pair'}, dimensions={0}, use_global_device_ids=true | all-gather | bytes 4224 | tf_op jit(solution)/shard_map/all_gather | solution.py:78
  57.0 39.9 %all-reduce.6 = (bf16[1024]{0:T(1024)(128)(2,1)S(1)}, bf16[1024]{0:T(1024)(128)(2,1)S(1)}) all-reduce(bf16[1024]{0:T(1024)(128)(2,1)S(1)} %dynamic-update-slice.1, bf16[1024]{0:T(1024)(128)(2,1)S(1)} %dynamic-update-slice), channel_id=1, replica_groups=mesh['dp'=16,'pair'=2] {'dp','pair'}, use_global_device_ids=true, to_apply=%add.1 | all-reduce | flops 2048 | bytes 8192
  98.3 11.5 all-gather.8.cloned.1.call-done
  125.1 9.6 fusion.110
  145.2 27.8 all-gather.10.cloned.1.call-done
  176.2 113.6 %all-gather.16.cloned.1.call-done = bf16[1,1024,8192]{2,1,0:T(8,128)(2,1)} async-done(((bf16[1,32,8192]{2,1,0:T(8,128)(2,1)}), bf16[1,1024,8192]{2,1,0:T(8,128)(2,1)}) %all-gather.16.cloned.1.call-update) | async-done | bytes 16777232 | tf_op jit(solution)/shard_map/all_gather | solution.py:45
  289.9 10.2 fusion.12
  300.1 68.2 %all-gather.18.cloned.1.call-done = bf16[1,4096,1024]{2,1,0:T(8,128)(2,1)} async-done(((bf16[1,128,1024]{2,1,0:T(8,128)(2,1)}), bf16[1,4096,1024]{2,1,0:T(8,128)(2,1)}) %all-gather.18.cloned.1.call-update) | async-done | bytes 8388624 | tf_op jit(solution)/shard_map/all_gather | solution.py:46
  368.2 9.5 fusion.77
  377.7 107.3 %all-gather.12.cloned.1.call-done = bf16[1,1024,8192]{2,1,0:T(8,128)(2,1)} async-done(((bf16[1,32,8192]{2,1,0:T(8,128)(2,1)}), bf16[1,1024,8192]{2,1,0:T(8,128)(2,1)}) %all-gather.12.cloned.1.call-update) | async-done | bytes 16777232 | tf_op jit(solution)/shard_map/all_gather | solution.py:45
  485.0 10.2 fusion.9
  495.2 68.5 %all-gather.14.cloned.1.call-done = bf16[1,4096,1024]{2,1,0:T(8,128)(2,1)} async-done(((bf16[1,128,1024]{2,1,0:T(8,128)(2,1)}), bf16[1,4096,1024]{2,1,0:T(8,128)(2,1)}) %all-gather.14.cloned.1.call-update) | async-done | bytes 8388624 | tf_op jit(solution)/shard_map/all_gather | solution.py:46
  563.7 9.5 fusion.76
  573.2 12.5 fusion.50
  585.7 13.1 multiply_reduce_fusion.2
  648.2 10.4 fusion.70
  665.5 13.4 copy.179
  678.9 11.7 convolution_bitcast_fusion.2
  690.6 37.5 %copy.176 = f32[1024,2,3072]{2,1,0:T(2,128)} copy(f32[1024,2,3072]{0,2,1:T(8,128)} %convolution_bitcast_fusion.2) | data formatting | bytes 50331648 | tf_op jit(solution)/shard_map/fgk,fge->kge/transpose | solution.py:20
  728.2 14.9 convolution_bitcast_fusion
  743.0 68.5 %copy.181 = f32[1024,1,8192]{2,1,0:T(1,128)} copy(f32[1024,1,8192]{0,2,1:T(8,128)} %convolution_bitcast_fusion) | data formatting | bytes 67108864 | tf_op jit(solution)/shard_map/fgk,fge->kge/transpose | solution.py:20
  811.7 15.1 convolution_bitcast_fusion.1
  826.7 68.6 %copy.180 = f32[1024,1,8192]{2,1,0:T(1,128)} copy(f32[1024,1,8192]{0,2,1:T(8,128)} %convolution_bitcast_fusion.1) | data formatting | bytes 67108864 | tf_op jit(solution)/shard_map/fgk,fge->kge/transpose | solution.py:20
  895.4 9.3 convolution_bitcast_fusion.3
  904.8 9.4 convolution_bitcast_fusion.4
  930.7 91.7 %reduce-scatter.16.cloned.1.call-done = f32[32,2]{1,0:T(8,128)} async-done(((f32[1024,2]{1,0:T(8,128)}), f32[32,2]{1,0:T(8,128)}) %reduce-scatter.16.cloned.1.call-update) | async-done | bytes 272
  1023.7 179.6 %all-reduce.14.cloned.1.call-done = f32[1024,2,1024]{2,1,0:T(2,128)} async-done(((f32[1024,2,1024]{2,1,0:T(2,128)}), f32[1024,2,1024]{2,1,0:T(2,128)}) %all-reduce.14.cloned.1.call-update) | async-done | bytes 8388624
  1205.1 395.9 %all-reduce.12.cloned.1.call-done = f32[1024,2,3072]{2,1,0:T(2,128)} async-done(((f32[1024,2,3072]{2,1,0:T(2,128)}), f32[1024,2,3072]{2,1,0:T(2,128)}) %all-reduce.12.cloned.1.call-update) | async-done | bytes 25165840
  1603.3 503.7 %all-reduce.18.cloned.1.call-done = f32[1024,1,8192]{2,1,0:T(1,128)} async-done(((f32[1024,1,8192]{2,1,0:T(1,128)}), f32[1024,1,8192]{2,1,0:T(1,128)}) %all-reduce.18.cloned.1.call-update) | async-done | bytes 33554448
  2108.9 503.4 %all-reduce.16.cloned.1.call-done = f32[1024,1,8192]{2,1,0:T(1,128)} async-done(((f32[1024,1,8192]{2,1,0:T(1,128)}), f32[1024,1,8192]{2,1,0:T(1,128)}) %all-reduce.16.cloned.1.call-update) | async-done | bytes 33554448
  2615.7 181.3 %reduce-scatter.14.cloned.1.call-done = f32[128,1,1024]{0,2,1:T(8,128)} async-done(((f32[4096,1,1024]{0,2,1:T(8,128)}), f32[128,1,1024]{0,2,1:T(8,128)}) %reduce-scatter.14.cloned.1.call-update) | async-done | bytes 524304 | tf_op jit(solution)/shard_map/reduce_scatter | solution.py:159
  2797.1 186.6 %reduce-scatter.12.cloned.1.call-done = f32[128,1,1024]{0,2,1:T(8,128)} async-done(((f32[4096,1,1024]{0,2,1:T(8,128)}), f32[128,1,1024]{0,2,1:T(8,128)}) %reduce-scatter.12.cloned.1.call-update) | async-done | bytes 524304 | tf_op jit(solution)/shard_map/reduce_scatter | solution.py:159
  (158 shorter events, 122.1 us)
Async XLA Ops:
  7.2 3.9 copy-start.19
  7.2 102.6 %all-gather.8.cloned.1.call-start = ((), (), s32[]{:S(2)}) async-start(), calls=%async_computation.5 | async-start | bytes 12976128 | tf_op jit(solution)/shard_map/all_gather | solution.py:79
  7.9 165.1 %all-gather.10.cloned.1.call-start = ((), (), s32[]{:S(2)}) async-start(), calls=%async_computation.6 | async-start | bytes 4325376 | tf_op jit(solution)/shard_map/all_gather | solution.py:80
  8.7 4.5 copy-start.22
  8.7 47.9 %copy-start.21 = (bf16[2,32]{1,0:T(2,128)(2,1)S(1)}, bf16[2,32]{1,0:T(2,128)(2,1)}, u32[]{:S(2)}) copy-start(bf16[2,32]{1,0:T(2,128)(2,1)} %param.14) | copy-start | bytes 388
  8.7 88.9 %copy-start.23 = (s32[4]{0:T(128)S(1)}, s32[4]{0:T(128)}, u32[]{:S(2)}) copy-start(s32[4]{0:T(128)} %param.19) | copy-start | bytes 52
  8.7 89.2 %copy-start = (bf16[128,2,1024]{2,1,0:T(2,128)(2,1)S(1)}, bf16[128,2,1024]{2,1,0:T(2,128)(2,1)}, u32[]{:S(2)}) copy-start(bf16[128,2,1024]{2,1,0:T(2,128)(2,1)} %param.10) | copy-start | bytes 1572868
  8.7 281.2 %all-gather.16.cloned.1.call-start = ((), (), s32[]{:S(2)}) async-start(), calls=%async_computation.9 | async-start | bytes 17301504 | tf_op jit(solution)/shard_map/all_gather | solution.py:45
  11.0 87.1 %copy-start.20 = (bf16[128,2,1024]{2,1,0:T(2,128)(2,1)S(1)}, bf16[128,2,1024]{2,1,0:T(2,128)(2,1)}, u32[]{:S(2)}) copy-start(bf16[128,2,1024]{2,1,0:T(2,128)(2,1)} %param.17) | copy-start | bytes 1572868
  11.1 357.2 %all-gather.18.cloned.1.call-start = ((), (), s32[]{:S(2)}) async-start(), calls=%async_computation.10 | async-start | bytes 8650752 | tf_op jit(solution)/shard_map/all_gather | solution.py:46
  12.0 473.0 %all-gather.12.cloned.1.call-start = ((), (), s32[]{:S(2)}) async-start(), calls=%async_computation.7 | async-start | bytes 17301504 | tf_op jit(solution)/shard_map/all_gather | solution.py:45
  12.6 551.2 %all-gather.14.cloned.1.call-start = ((), (), s32[]{:S(2)}) async-start(), calls=%async_computation.8 | async-start | bytes 8650752 | tf_op jit(solution)/shard_map/all_gather | solution.py:46
  13.1 915.4 %reduce-scatter.20.cloned.1.call-start = ((), (), s32[]{:S(2)}) async-start(), calls=%async_computation.15 | async-start | bytes 540672
  134.7 2.8 copy-start.8
  134.7 4.1 copy-start.16
  145.1 30.9 %copy-start.5 = (bf16[128,2,16,64]{0,3,2,1:T(8,128)(2,1)}, bf16[128,2,16,64]{0,3,2,1:T(8,128)(2,1)S(1)}, u32[]{:S(2)}) copy-start(bf16[128,2,16,64]{0,3,2,1:T(8,128)(2,1)S(1)} %copy.159) | copy-start | bytes 1572868
  585.7 13.1 copy-start.12
  609.4 5.4 copy-start.11
  609.4 5.4 copy-start.17
  609.4 5.4 copy-start.18
  614.8 3.5 copy-start.2
  614.8 3.5 copy-start.9
  620.5 3.7 copy-start.14
  625.3 304.0 %reduce-scatter.18.cloned.1.call-start = ((), (), s32[]{:S(2)}) async-start(), calls=%async_computation.14 | async-start | bytes 540672
  648.2 374.2 %reduce-scatter.16.cloned.1.call-start = ((), (), s32[]{:S(2)}) async-start(), calls=%async_computation.13 | async-start | bytes 540672
  659.7 543.6 %all-reduce.14.cloned.1.call-start = ((), (), s32[]{:S(2)}) async-start(), calls=%async_computation.17 | async-start | bytes 16777216
  678.9 922.1 %all-reduce.12.cloned.1.call-start = ((), (), s32[]{:S(2)}) async-start(), calls=%async_computation.16 | async-start | bytes 50331648
  728.1 1378.9 %all-reduce.18.cloned.1.call-start = ((), (), s32[]{:S(2)}) async-start(), calls=%async_computation.19 | async-start | bytes 67108864
  811.6 1800.7 %all-reduce.16.cloned.1.call-start = ((), (), s32[]{:S(2)}) async-start(), calls=%async_computation.18 | async-start | bytes 67108864
  895.4 1901.7 %reduce-scatter.14.cloned.1.call-start = ((), (), s32[]{:S(2)}) async-start(), calls=%async_computation.12 | async-start | bytes 17301504 | tf_op jit(solution)/shard_map/reduce_scatter | solution.py:159
  904.8 2078.9 %reduce-scatter.12.cloned.1.call-start = ((), (), s32[]{:S(2)}) async-start(), calls=%async_computation.11 | async-start | bytes 17301504 | tf_op jit(solution)/shard_map/reduce_scatter | solution.py:159
  915.5 4.8 copy-start.7
  (7 other events, 10.9 us)
Sparse Core Ops, SparseCore 0:
  10.8 98.8 all-gather.7
  112.7 60.2 all-gather.9
  176.4 113.4 all-gather.15
  292.6 75.6 all-gather.17
  371.5 113.4 all-gather.11
  488.3 75.3 all-gather.13
  625.4 132.4 reduce-scatter.19
  760.3 129.9 reduce-scatter.17
  892.5 129.8 reduce-scatter.15
  1028.9 174.4 all-reduce.13
  1210.9 390.0 all-reduce.11
  1608.4 498.6 all-reduce.17
  2113.4 498.8 all-reduce.15
  2614.5 182.4 reduce-scatter.13
  2799.3 184.3 reduce-scatter.11
where the time goes:
time: 3010 us; the launch traced here: 2990 us
  waiting for transfers between devices  2440 us (81%)
  local copies, waits for them, and re-layouts  248 us (8%)
  matrix products  193 us (6%)
  blocking collectives  83.1 us (3%)
    unnamed x22, waiting for transfers between devices  1680 us
    reduce_scatter x2, waiting for transfers between devices, local(): lax.psum_scatter(grad_down, ('dp', 'pair'), scatter_dimension=0, tiled=True)  368 us
    all_gather x2, waiting for transfers between devices, gather_ff_fwd(): lax.all_gather(w_gate_up[start:start + group], ('dp', 'pair'), axis=1, ti...  221 us
    transpose x4, local copies, waits for them, and re-layouts, pos_grad(): jnp.einsum('fgk,fge->kge', activations, gradients, preferred_element_type...  188 us
    all_gather x2, waiting for transfers between devices, gather_ff_fwd(): lax.all_gather(w_down[start:start + group], ('dp', 'pair'), axis=1, tiled...  137 us
    dot_general x6, matrix products, pos_grad(): jnp.einsum('fgk,fge->kge', activations, gradients, preferred_element_type...  66.1 us
  transfers between devices with their start and end apart: 15, of which 13 were waited for; matrix products, arithmetic and copies ran while one was open for 13% of the time, Pallas kernels for 0%

commit v1 on v0

--- a/solution.py
+++ b/solution.py
@@ -1,8 +1,11 @@
+import functools
 import math
 
 import jax
 import jax.numpy as jnp
 from jax import lax
+from jax.experimental import pallas as pl
+from jax.experimental.pallas import tpu as pltpu
 from jax.sharding import PartitionSpec as P
 
 HEAD_DIM = 64
@@ -220,6 +223,1082 @@
     )
 
 
+MESH_ID = pl.DeviceIdType.MESH
+BF16 = jnp.bfloat16
+F32 = jnp.float32
+
+
+def here():
+    dp = lax.axis_index("dp")
+    core = lax.axis_index("pair")
+    return lax.div(dp, 4), lax.rem(lax.div(dp, 2), 2), lax.rem(dp, 2), core
+
+
+def flip(value, bit):
+    return 1 - value if bit else value
+
+
+def push(src, dst, send_sem, recv_sem, to):
+    return pltpu.make_async_remote_copy(
+        src_ref=src,
+        dst_ref=dst,
+        send_sem=send_sem,
+        recv_sem=recv_sem,
+        device_id=to,
+        device_id_type=MESH_ID,
+    )
+
+
+def arrived(dst, recv_sem, to):
+    push(dst, dst, recv_sem, recv_sem, to).wait_recv()
+
+
+def greet_all(z, y, x, core):
+    barrier = pltpu.get_barrier_semaphore()
+    me = 2 * (z * 4 + y * 2 + x) + core
+
+    def one(step, carry):
+        other = lax.rem(me + step, 32)
+        pl.semaphore_signal(
+            barrier, inc=1, device_id=(lax.div(other, 2), lax.rem(other, 2)), device_id_type=MESH_ID
+        )
+        return carry
+
+    lax.fori_loop(1, 32, one, 0)
+    pl.semaphore_wait(barrier, 31)
+
+
+def greet(peers):
+    barrier = pltpu.get_barrier_semaphore()
+    for to in peers:
+        pl.semaphore_signal(barrier, inc=1, device_id=to, device_id_type=MESH_ID)
+    pl.semaphore_wait(barrier, len(peers))
+
+
+def maybe(condition, do):
+    if condition is None:
+        do()
+    else:
+        pl.when(condition)(do)
+
+
+OFFSETS = [
+    (dz, dy, dx) for dz in (0, -1, 1, -2, 2, -3, 3) for dy in (0, 1) for dx in (0, 1)
+]
+ORDERS = ("zxy", "zyx", "xyz", "yxz")
+
+
+def hops(offset):
+    return abs(offset[0]) + offset[1] + offset[2]
+
+
+def arrival_axis(order, offset):
+    part = dict(z=offset[0], y=offset[1], x=offset[2])
+    last = None
+    for axis in order:
+        if part[axis] != 0:
+            last = axis
+    return last
+
+
+def onward(order, offset):
+    directions = []
+    last = arrival_axis(order, offset)
+    start = 0
+    if last is not None:
+        start = order.index(last) + 1
+        if last == "z":
+            directions.append("u" if offset[0] < 0 else "d")
+    for axis in order[start:]:
+        directions.extend(["u", "d"] if axis == "z" else [axis])
+    return directions
+
+
+def came_from(order, offset):
+    last = arrival_axis(order, offset)
+    if last == "z":
+        return "d" if offset[0] < 0 else "u"
+    return last
+
+
+def offset_exists(offset, z):
+    if offset[0] < 0:
+        return z >= -offset[0]
+    if offset[0] > 0:
+        return z <= 3 - offset[0]
+    return None
+
+
+def direction_exists(direction, z):
+    return {"u": z < 3, "d": z > 0}.get(direction)
+
+
+DIRECTIONS = ("x", "y", "u", "d", "s")
+
+
+def neighbour(direction, z, y, x, core):
+    if direction == "x":
+        return (z * 4 + y * 2 + 1 - x, core)
+    if direction == "y":
+        return (z * 4 + (1 - y) * 2 + x, core)
+    if direction == "u":
+        return (z * 4 + 4 + y * 2 + x, core)
+    if direction == "d":
+        return (z * 4 - 4 + y * 2 + x, core)
+    return (z * 4 + y * 2 + x, 1 - core)
+
+
+def chip_of(offset, z, y, x):
+    return (z + offset[0]) * 4 + flip(y, offset[1]) * 2 + flip(x, offset[2])
+
+
+def gather_attn_kernel(
+    gains_ref,
+    qkv_ref,
+    out_ref,
+    gains_full,
+    qkv_full,
+    out_full,
+    plane_sem,
+    sibling_sem,
+    send_sem,
+    local_sem,
+    gains_send,
+    gains_recv,
+):
+    z, y, x, core = here()
+    me = 2 * (z * 4 + y * 2 + x) + core
+    greet_all(z, y, x, core)
+    pieces = [
+        (qkv_ref, qkv_full, 0, "zxy"),
+        (qkv_ref, qkv_full, 1, "zyx"),
+        (out_ref, out_full, 0, "xyz"),
+        (out_ref, out_full, 1, "yxz"),
+    ]
+
+    def rows(piece, device):
+        source, full, index, _ = pieces[piece]
+        height = source.shape[1]
+        return full.at[index, pl.ds(pl.multiple_of(device * height, height), height), :]
+
+    pending = []
+
+    def send(piece, offset, direction):
+        source, full, index, _ = pieces[piece]
+        chip = chip_of(offset, z, y, x)
+        block = rows(piece, 2 * chip + core)
+        src = source.at[index] if hops(offset) == 0 else block
+        recv = sibling_sem if direction == "s" else plane_sem
+        return push(
+            src,
+            block,
+            send_sem.at[piece, chip, DIRECTIONS.index(direction)],
+            recv.at[piece, chip],
+            neighbour(direction, z, y, x, core),
+        )
+
+    def handle(piece, offset, finish):
+        order = pieces[piece][3]
+
+        def go():
+            chip = chip_of(offset, z, y, x)
+            if hops(offset) > 0 and not finish:
+                arrived(
+                    rows(piece, 2 * chip + core),
+                    plane_sem.at[piece, chip],
+                    neighbour("s", z, y, x, core),
+                )
+            for direction in onward(order, offset) + ["s"]:
+                copy = send(piece, offset, direction)
+                maybe(
+                    direction_exists(direction, z), copy.wait_send if finish else copy.start
+                )
+
+        maybe(offset_exists(offset, z), go)
+
+    events = sorted(
+        ((hops(offset), rank, piece, offset) for piece in range(4) for rank, offset in enumerate(OFFSETS)),
+        key=lambda event: event[:3],
+    )
+    for _, _, piece, offset in events:
+        if hops(offset) == 0:
+            handle(piece, offset, False)
+
+    def gains_copy(step):
+        other = lax.rem(me + step, 32)
+        return push(
+            gains_ref,
+            gains_full.at[me],
+            gains_send.at[step],
+            gains_recv.at[me],
+            (lax.div(other, 2), lax.rem(other, 2)),
+        )
+
+    def gains_start(step, carry):
+        gains_copy(step).start()
+        return carry
+
+    lax.fori_loop(1, 32, gains_start, 0)
+    own = [
+        pltpu.make_async_copy(source.at[index], rows(piece, me), local_sem.at[piece])
+        for piece, (source, full, index, _) in enumerate(pieces)
+    ]
+    own.append(pltpu.make_async_copy(gains_ref, gains_full.at[me], local_sem.at[4]))
+    for copy in own:
+        copy.start()
+    for _, _, piece, offset in events:
+        if hops(offset) > 0:
+            handle(piece, offset, False)
+    for _, _, piece, offset in events:
+        handle(piece, offset, True)
+
+    def sibling_wait(chip, carry):
+        for piece in range(4):
+            arrived(
+                rows(piece, 2 * chip + 1 - core),
+                sibling_sem.at[piece, chip],
+                neighbour("s", z, y, x, core),
+            )
+        return carry
+
+    lax.fori_loop(0, 16, sibling_wait, 0)
+
+    def gains_wait(step, carry):
+        other = lax.rem(me + step, 32)
+        gains_copy(step).wait_send()
+        arrived(gains_full.at[other], gains_recv.at[other], neighbour("s", z, y, x, core))
+        return carry
+
+    lax.fori_loop(1, 32, gains_wait, 0)
+    for copy in own:
+        copy.wait()
+
+
+def gather_attn(gains, w_qkv, w_out):
+    sets, height, qkv_width = w_qkv.shape
+    out_width = w_out.shape[2]
+    dma = pltpu.SemaphoreType.DMA
+    return pl.pallas_call(
+        gather_attn_kernel,
+        out_shape=(
+            jax.ShapeDtypeStruct((32,) + gains.shape, BF16),
+            jax.ShapeDtypeStruct((sets, 32 * height, qkv_width), BF16),
+            jax.ShapeDtypeStruct((sets, 32 * height, out_width), BF16),
+        ),
+        in_specs=[pl.BlockSpec(memory_space=pl.ANY)] * 3,
+        out_specs=(pl.BlockSpec(memory_space=pl.ANY),) * 3,
+        scratch_shapes=[
+            dma((4, 16)),
+            dma((4, 16)),
+            dma((4, 16, 5)),
+            dma((5,)),
+            dma((32,)),
+            dma((32,)),
+        ],
+        compiler_params=pltpu.CompilerParams(collective_id=0, has_side_effects=True),
+        name="gather_attn",
+    )(gains, w_qkv, w_out)
+
+
+RANK_STEPS = sorted(
+    ((dl, dx, dc) for dl in (0, 1) for dx in (0, 1) for dc in (0, 1)), key=lambda step: (sum(step), step)
+)
+
+
+def group_place(z, y, x, core):
+    zh, zl = lax.div(z, 2), lax.rem(z, 2)
+
+    def member(step):
+        return ((2 * zh + flip(zl, step[0])) * 4 + y * 2 + flip(x, step[1]), flip(core, step[2]))
+
+    def rank(step):
+        return 4 * flip(zl, step[0]) + 2 * flip(x, step[1]) + flip(core, step[2])
+
+    def device(step, dzh=0, dy=0):
+        return 16 * flip(zh, dzh) + 4 * flip(y, dy) + 8 * flip(zl, step[0]) + 2 * flip(x, step[1]) + flip(core, step[2])
+
+    far = ((2 * (1 - zh) + zl) * 4 + y * 2 + x, core)
+    across = (z * 4 + (1 - y) * 2 + x, core)
+    return zh, zl, member, rank, device, far, across
+
+
+def gather_ff_kernel(
+    gate_up_ref,
+    down_ref,
+    rows_ref,
+    grads_ref,
+    gate_up_full,
+    down_full,
+    rows_full,
+    grads_full,
+    rank_send,
+    rank_recv,
+    far_send,
+    far_recv,
+    across_send,
+    across_recv,
+    act_send,
+    act_recv,
+    local_sem,
+):
+    z, y, x, core = here()
+    zh, zl, member, rank, device, far, across = group_place(z, y, x, core)
+    own_step = (0, 0, 0)
+    others = RANK_STEPS[1:]
+    greet([member(step) for step in others] + [far, across])
+    height = gate_up_ref.shape[2]
+    down_height = down_ref.shape[1]
+    act_height = rows_ref.shape[1]
+    sends = []
+
+    def start(copy):
+        copy.start()
+        sends.append(copy)
+
+    def weight_rows(number):
+        return gate_up_full.at[:, pl.ds(pl.multiple_of(number * height, height), height), :]
+
+    def down_rows(dzh, dy):
+        number = 2 * flip(zh, dzh) + flip(y, dy)
+        return down_full.at[:, pl.ds(pl.multiple_of(number * down_height, down_height), down_height), :]
+
+    def act_rows(full, step):
+        return full.at[:, pl.ds(pl.multiple_of(rank(step) * act_height, act_height), act_height), :]
+
+    acts = [(rows_ref, rows_full), (grads_ref, grads_full)]
+
+    def send_act(which, step, source, hop):
+        to = member(tuple(1 if axis == hop else 0 for axis in range(3)))
+        landed = tuple(bit ^ (1 if axis == hop else 0) for axis, bit in enumerate(step))
+        start(
+            push(
+                source,
+                act_rows(acts[which][1], step),
+                act_send.at[which, 4 * step[0] + 2 * step[1] + step[2], hop],
+                act_recv.at[which, 4 * landed[0] + 2 * landed[1] + landed[2]],
+                to,
+            )
+        )
+
+    def wait_act(which, step):
+        arrived(
+            act_rows(acts[which][1], step),
+            act_recv.at[which, 4 * step[0] + 2 * step[1] + step[2]],
+            across,
+        )
+
+    mine = gate_up_ref.at[rank(own_step)]
+    for slot, step in enumerate(RANK_STEPS):
+        if step != own_step:
+            start(
+                push(
+                    gate_up_ref.at[rank(step)],
+                    weight_rows(device(own_step)),
+                    rank_send.at[slot],
+                    rank_recv.at[slot],
+                    member(step),
+                )
+            )
+    start(push(mine, weight_rows(device(own_step)), far_send.at[0], far_recv.at[0], far))
+    start(push(mine, weight_rows(device(own_step)), across_send.at[0, 0], across_recv.at[0, 0], across))
+    start(push(down_ref, down_rows(0, 0), far_send.at[8], far_recv.at[8], far))
+    start(push(down_ref, down_rows(0, 0), across_send.at[0, 8], across_recv.at[0, 8], across))
+    for which in (0, 1):
+        for hop in (0, 1, 2):
+            send_act(which, own_step, acts[which][0], hop)
+    local = [
+        pltpu.make_async_copy(mine, weight_rows(device(own_step)), local_sem.at[0]),
+        pltpu.make_async_copy(down_ref, down_rows(0, 0), local_sem.at[1]),
+        pltpu.make_async_copy(rows_ref, act_rows(rows_full, own_step), local_sem.at[2]),
+        pltpu.make_async_copy(grads_ref, act_rows(grads_full, own_step), local_sem.at[3]),
+    ]
+    for copy in local:
+        copy.start()
+    for slot, step in enumerate(RANK_STEPS):
+        if step == own_step:
+            continue
+        block = weight_rows(device(step))
+        arrived(block, rank_recv.at[slot], member(step))
+        start(push(block, block, far_send.at[slot], far_recv.at[slot], far))
+        start(push(block, block, across_send.at[0, slot], across_recv.at[0, slot], across))
+    for slot, step in enumerate(RANK_STEPS):
+        block = weight_rows(device(step, 1, 0))
+        arrived(block, far_recv.at[slot], far)
+        start(push(block, block, across_send.at[1, slot], across_recv.at[1, slot], across))
+    block = down_rows(1, 0)
+    arrived(block, far_recv.at[8], far)
+    start(push(block, block, across_send.at[1, 8], across_recv.at[1, 8], across))
+    for which in (0, 1):
+        step = (1, 0, 0)
+        wait_act(which, step)
+        block = act_rows(acts[which][1], step)
+        send_act(which, step, block, 1)
+        send_act(which, step, block, 2)
+    for which in (0, 1):
+        for step in ((0, 1, 0), (1, 1, 0)):
+            wait_act(which, step)
+            send_act(which, step, act_rows(acts[which][1], step), 2)
+    for which in (0, 1):
+        for step in ((0, 0, 1), (1, 0, 1), (0, 1, 1), (1, 1, 1)):
+            wait_act(which, step)
+    for dzh in (0, 1):
+        for slot, step in enumerate(RANK_STEPS):
+            arrived(weight_rows(device(step, dzh, 1)), across_recv.at[dzh, slot], across)
+        arrived(down_rows(dzh, 1), across_recv.at[dzh, 8], across)
+    for copy in sends:
+        copy.wait_send()
+    for copy in local:
+        copy.wait()
+
+
+def gather_ff(gate_up_parts, w_down, rows, grads):
+    ranks, sets, height, width = gate_up_parts.shape
+    dma = pltpu.SemaphoreType.DMA
+    return pl.pallas_call(
+        gather_ff_kernel,
+        out_shape=(
+            jax.ShapeDtypeStruct((sets, 32 * height, width), BF16),
+            jax.ShapeDtypeStruct((sets, 4 * w_down.shape[1], w_down.shape[2]), BF16),
+            jax.ShapeDtypeStruct((sets, ranks * rows.shape[1], rows.shape[2]), BF16),
+            jax.ShapeDtypeStruct((sets, ranks * grads.shape[1], grads.shape[2]), BF16),
+        ),
+        in_specs=[pl.BlockSpec(memory_space=pl.ANY)] * 4,
+        out_specs=(pl.BlockSpec(memory_space=pl.ANY),) * 4,
+        scratch_shapes=[
+            dma((8,)),
+            dma((8,)),
+            dma((9,)),
+            dma((9,)),
+            dma((2, 9)),
+            dma((2, 9)),
+            dma((2, 8, 3)),
+            dma((2, 8)),
+            dma((4,)),
+        ],
+        compiler_params=pltpu.CompilerParams(collective_id=1, has_side_effects=True),
+        name="gather_ff",
+    )(gate_up_parts, w_down, rows, grads)
+
+
+def add_into(target, sources, rows=16, columns=1024):
+    height, width = target.shape
+    across = width // columns
+
+    def one(step, carry):
+        top = pl.multiple_of(lax.div(step, across) * rows, rows)
+        left = pl.multiple_of(lax.rem(step, across) * columns, columns)
+        spot = (pl.ds(top, rows), pl.ds(left, columns))
+        total = sources[0][spot].astype(F32)
+        for source in sources[1:]:
+            total = total + source[spot].astype(F32)
+        target[spot] = total.astype(target.dtype)
+        return carry
+
+    lax.fori_loop(0, (height // rows) * across, one, 0)
+
+
+def scatter_ff_kernel(
+    out_ref,
+    back_ref,
+    gate_up_ref,
+    down_ref,
+    out_sum,
+    back_sum,
+    gate_up_sum,
+    down_sum,
+    core_buf,
+    x_buf,
+    z_buf,
+    across_gate,
+    across_down,
+    far_gate,
+    far_down,
+    rank_buf,
+    core_send,
+    core_recv,
+    x_send,
+    x_recv,
+    z_send,
+    z_recv,
+    across_send,
+    across_recv,
+    far_send,
+    far_recv,
+    rank_send,
+    rank_recv,
+):
+    z, y, x, core = here()
+    zh, zl, member, rank, device, far, across = group_place(z, y, x, core)
+    own_step = (0, 0, 0)
+    others = RANK_STEPS[1:]
+    greet([member(step) for step in others] + [far, across])
+    sets = out_ref.shape[0]
+    act_height = out_sum.shape[1]
+    height = gate_up_sum.shape[2]
+    down_height = down_sum.shape[1]
+    sends = []
+
+    def start(copy):
+        copy.start()
+        sends.append(copy)
+
+    def run_rows(dzh, dy, low):
+        number = 16 * flip(zh, dzh) + 4 * flip(y, dy) + 8 * low
+        return pl.ds(pl.multiple_of(number * height, 4 * height), 4 * height)
+
+    def down_rows(dzh, dy):
+        number = 2 * flip(zh, dzh) + flip(y, dy)
+        return pl.ds(pl.multiple_of(number * down_height, down_height), down_height)
+
+    def act_rows(step):
+        return pl.ds(pl.multiple_of(rank(step) * act_height, act_height), act_height)
+
+    for turn, dzh in enumerate((1, 0)):
+        for s in range(sets):
+            for low in (0, 1):
+                start(
+                    push(
+                        gate_up_ref.at[s, run_rows(dzh, 1, low)],
+                        across_gate.at[turn, s, low],
+                        across_send.at[turn, s, low],
+                        across_recv.at[turn, s, low],
+                        across,
+                    )
+                )
+            start(
+                push(
+                    down_ref.at[s, down_rows(dzh, 1)],
+                    across_down.at[turn, s],
+                    across_send.at[turn, s, 2],
+                    across_recv.at[turn, s, 2],
+                    across,
+                )
+            )
+    acts = [back_ref, out_ref]
+    act_sums = [back_sum, out_sum]
+    sibling = member((0, 0, 1))
+    plan = [(1, 1), (0, 1), (1, 0), (0, 0)]
+    for which in (0, 1):
+        for dl, dx in plan:
+            start(
+                push(
+                    acts[which].at[:, act_rows((dl, dx, 1))],
+                    core_buf.at[which, dl, dx],
+                    core_send.at[which, dl, dx],
+                    core_recv.at[which, dl, dx],
+                    sibling,
+                )
+            )
+
+    def core_add(which, dl, dx):
+        block = core_buf.at[which, dl, dx]
+        arrived(block, core_recv.at[which, dl, dx], sibling)
+        for s in range(sets):
+            add_into(block.at[s], [block.at[s], acts[which].at[s, act_rows((dl, dx, 0))]])
+
+    for which in (0, 1):
+        for dl in (1, 0):
+            core_add(which, dl, 1)
+            start(
+                push(
+                    core_buf.at[which, dl, 1],
+                    x_buf.at[which, dl],
+                    x_send.at[which, dl],
+                    x_recv.at[which, dl],
+                    member((0, 1, 0)),
+                )
+            )
+    for s in range(sets):
+        for low in (0, 1):
+            block = across_gate.at[0, s, low]
+            arrived(block, across_recv.at[0, s, low], across)
+            add_into(block, [block, gate_up_ref.at[s, run_rows(1, 0, low)]])
+            start(push(block, far_gate.at[s, low], far_send.at[s, low], far_recv.at[s, low], far))
+        block = across_down.at[0, s]
+        arrived(block, across_recv.at[0, s, 2], across)
+        add_into(block, [block, down_ref.at[s, down_rows(1, 0)]])
+        start(push(block, far_down.at[s], far_send.at[s, 2], far_recv.at[s, 2], far))
+    for which in (0, 1):
+        core_add(which, 1, 0)
+        arrived(x_buf.at[which, 1], x_recv.at[which, 1], member((0, 1, 0)))
+        for s in range(sets):
+            block = x_buf.at[which, 1, s]
+            add_into(block, [block, core_buf.at[which, 1, 0, s]])
+        start(
+            push(
+                x_buf.at[which, 1],
+                z_buf.at[which],
+                z_send.at[which],
+                z_recv.at[which],
+                member((1, 0, 0)),
+            )
+        )
+    for which in (0, 1):
+        core_add(which, 0, 0)
+        arrived(x_buf.at[which, 0], x_recv.at[which, 0], member((0, 1, 0)))
+        arrived(z_buf.at[which], z_recv.at[which], member((1, 0, 0)))
+        for s in range(sets):
+            add_into(
+                act_sums[which].at[s],
+                [core_buf.at[which, 0, 0, s], x_buf.at[which, 0, s], z_buf.at[which, s]],
+            )
+    for s in range(sets):
+        for low in (0, 1):
+            block = across_gate.at[1, s, low]
+            arrived(block, across_recv.at[1, s, low], across)
+            arrived(far_gate.at[s, low], far_recv.at[s, low], far)
+            add_into(block, [block, far_gate.at[s, low], gate_up_ref.at[s, run_rows(0, 0, low)]])
+        arrived(across_down.at[1, s], across_recv.at[1, s, 2], across)
+        arrived(far_down.at[s], far_recv.at[s, 2], far)
+        add_into(
+            down_sum.at[s],
+            [across_down.at[1, s], far_down.at[s], down_ref.at[s, down_rows(0, 0)]],
+        )
+
+    def share(step, s):
+        number = 2 * flip(x, step[1]) + flip(core, step[2])
+        return across_gate.at[1, s, flip(zl, step[0]), pl.ds(pl.multiple_of(number * height, height), height)]
+
+    for slot, step in enumerate(RANK_STEPS):
+        if step != own_step:
+            for s in range(sets):
+                start(
+                    push(
+                        share(step, s),
+                        rank_buf.at[slot, s],
+                        rank_send.at[slot, s],
+                        rank_recv.at[slot, s],
+                        member(step),
+                    )
+                )
+    for slot, step in enumerate(RANK_STEPS):
+        for s in range(sets):
+            if step == own_step:
+                add_into(gate_up_sum.at[rank(step), s], [share(step, s)])
+            else:
+                arrived(rank_buf.at[slot, s], rank_recv.at[slot, s], member(step))
+                add_into(gate_up_sum.at[rank(step), s], [rank_buf.at[slot, s]])
+    for copy in sends:
+        copy.wait_send()
+
+
+def scatter_ff(out_part, back_part, gate_up_grad, down_grad):
+    sets, rows, model = out_part.shape
+    width = gate_up_grad.shape[2]
+    act_height = rows // 8
+    height = gate_up_grad.shape[1] // 32
+    down_height = down_grad.shape[1] // 4
+    dma = pltpu.SemaphoreType.DMA
+    vmem = pl.BlockSpec(memory_space=pltpu.VMEM)
+    return pl.pallas_call(
+        scatter_ff_kernel,
+        out_shape=(
+            jax.ShapeDtypeStruct((sets, act_height, model), F32),
+            jax.ShapeDtypeStruct((sets, act_height, model), F32),
+            jax.ShapeDtypeStruct((8, sets, height, width), F32),
+            jax.ShapeDtypeStruct((sets, down_height, model), F32),
+        ),
+        in_specs=[vmem] * 4,
+        out_specs=(vmem,) * 4,
+        scratch_shapes=[
+            pltpu.VMEM((2, 2, 2, sets, act_height, model), BF16),
+            pltpu.VMEM((2, 2, sets, act_height, model), BF16),
+            pltpu.VMEM((2, sets, act_height, model), BF16),
+            pltpu.VMEM((2, sets, 2, 4 * height, width), BF16),
+            pltpu.VMEM((2, sets, down_height, model), BF16),
+            pltpu.VMEM((sets, 2, 4 * height, width), BF16),
+            pltpu.VMEM((sets, down_height, model), BF16),
+            pltpu.VMEM((8, sets, height, width), BF16),
+            dma((2, 2, 2)),
+            dma((2, 2, 2)),
+            dma((2, 2)),
+            dma((2, 2)),
+            dma((2,)),
+            dma((2,)),
+            dma((2, sets, 3)),
+            dma((2, sets, 3)),
+            dma((sets, 3)),
+            dma((sets, 3)),
+            dma((8, sets)),
+            dma((8, sets)),
+        ],
+        compiler_params=pltpu.CompilerParams(
+            collective_id=2, has_side_effects=True, vmem_limit_bytes=60 * 2**20
+        ),
+        name="scatter_ff",
+    )(out_part, back_part, gate_up_grad, down_grad)
+
+
+def slot_index(order, direction, offset, z, y, x):
+    axis = {"u": "z", "d": "z"}.get(direction, direction)
+    index, count = 0, 1
+    values = dict(z=z + offset[0], y=flip(y, offset[1]), x=flip(x, offset[2]))
+    sizes = dict(z=4, y=2, x=2)
+    for earlier in order[: order.index(axis)]:
+        index = index * sizes[earlier] + values[earlier]
+        count *= sizes[earlier]
+    if axis == "z":
+        index = index * 4 + values["z"]
+        count *= 4
+    return index, count
+
+
+def slot_base(order):
+    base, total = {}, 0
+    for direction in ("x", "y", "u", "d"):
+        base[direction] = total
+        total += slot_index(order, direction, (0, 0, 0), 0, 0, 0)[1]
+    return base, total
+
+
+def scatter_attn_kernel(
+    gains_ref,
+    qkv_ref,
+    out_ref,
+    gains_sum,
+    qkv_sum,
+    out_sum,
+    core_qkv,
+    core_out,
+    slots_0,
+    slots_1,
+    slots_2,
+    slots_3,
+    gains_buf,
+    core_send,
+    core_recv,
+    tree_send,
+    tree_recv,
+    gains_send,
+    gains_recv,
+):
+    z, y, x, core = here()
+    me = 2 * (z * 4 + y * 2 + x) + core
+    greet_all(z, y, x, core)
+    height = qkv_sum.shape[1]
+    pieces = [
+        (qkv_ref, qkv_sum, core_qkv, 0, "zxy", slots_0),
+        (qkv_ref, qkv_sum, core_qkv, 1, "zyx", slots_1),
+        (out_ref, out_sum, core_out, 0, "xyz", slots_2),
+        (out_ref, out_sum, core_out, 1, "yxz", slots_3),
+    ]
+    sibling = neighbour("s", z, y, x, core)
+    events = sorted(
+        ((-hops(offset), rank, piece, offset) for piece in range(4) for rank, offset in enumerate(OFFSETS)),
+        key=lambda event: event[:3],
+    )
+
+    def own_rows(piece, chip, of_core):
+        source, _, _, index, _, _ = pieces[piece]
+        return source.at[index, pl.ds(pl.multiple_of((2 * chip + of_core) * height, height), height), :]
+
+    def core_copy(piece, offset):
+        chip = chip_of(offset, z, y, x)
+        _, _, buf, index, _, _ = pieces[piece]
+        return push(
+            own_rows(piece, chip, 1 - core),
+            buf.at[index, chip],
+            core_send.at[piece, chip],
+            core_recv.at[piece, chip],
+            sibling,
+        )
+
+    def tree_copy(piece, offset):
+        _, _, buf, index, order, slots = pieces[piece]
+        chip = chip_of(offset, z, y, x)
+        toward = came_from(order, offset)
+        seen = {"x": "x", "y": "y", "u": "d", "d": "u"}[toward]
+        base, _ = slot_base(order)
+        index_there, _ = slot_index(order, seen, offset, z, y, x)
+        place = base[seen] + index_there
+        return push(
+            buf.at[index, chip],
+            slots.at[place],
+            tree_send.at[piece, chip],
+            tree_recv.at[piece, place],
+            neighbour(toward, z, y, x, core),
+        )
+
+    def gains_copy(step):
+        other = lax.rem(me + step, 32)
+        return push(
+            gains_ref.at[other],
+            gains_buf.at[me],
+            gains_send.at[step],
+            gains_recv.at[me],
+            (lax.div(other, 2), lax.rem(other, 2)),
+        )
+
+    for _, _, piece, offset in events:
+        maybe(offset_exists(offset, z), core_copy(piece, offset).start)
+
+    def gains_start(step, carry):
+        gains_copy(step).start()
+        return carry
+
+    lax.fori_loop(1, 32, gains_start, 0)
+
+    def handle(piece, offset):
+        _, result, buf, index, order, slots = pieces[piece]
+        base, _ = slot_base(order)
+
+        def go():
+            chip = chip_of(offset, z, y, x)
+            block = buf.at[index, chip]
+            arrived(block, core_recv.at[piece, chip], sibling)
+            sure, unsure = [], []
+            for direction in onward(order, offset):
+                local, _ = slot_index(order, direction, offset, z, y, x)
+                place = base[direction] + local
+                (sure if direction in "xy" else unsure).append((direction, place))
+            terms = [block, own_rows(piece, chip, core)]
+            for direction, place in sure:
+                arrived(slots.at[place], tree_recv.at[piece, place], sibling)
+                terms.append(slots.at[place])
+            last = hops(offset) == 0
+            target = result.at[index] if last else block
+            add_into(target, terms)
+            for direction, place in unsure:
+
+                def more(place=place):
+                    arrived(slots.at[place], tree_recv.at[piece, place], sibling)
+                    add_into(target, [target, slots.at[place]])
+
+                maybe(direction_exists(direction, z), more)
+            if not last:
+                tree_copy(piece, offset).start()
+
+        maybe(offset_exists(offset, z), go)
+
+    for _, _, piece, offset in events:
+        handle(piece, offset)
+
+    gains_sum[...] = gains_ref[me]
+
+    def gains_wait(step, carry):
+        other = lax.rem(me + step, 32)
+        gains_copy(step).wait_send()
+        arrived(gains_buf.at[other], gains_recv.at[other], sibling)
+        gains_sum[...] += gains_buf[other]
+        return carry
+
+    lax.fori_loop(1, 32, gains_wait, 0)
+    for _, _, piece, offset in events:
+
+        def finish(piece=piece, offset=offset):
+            core_copy(piece, offset).wait_send()
+            if hops(offset) > 0:
+                tree_copy(piece, offset).wait_send()
+
+        maybe(offset_exists(offset, z), finish)
+
+
+def scatter_attn(gain_parts, qkv_grad, out_grad):
+    sets, rows, qkv_width = qkv_grad.shape
+    out_width = out_grad.shape[2]
+    height = rows // 32
+    dma = pltpu.SemaphoreType.DMA
+    vmem = pl.BlockSpec(memory_space=pltpu.VMEM)
+    places = [slot_base(order)[1] for order in ORDERS]
+    return pl.pallas_call(
+        scatter_attn_kernel,
+        out_shape=(
+            jax.ShapeDtypeStruct(gain_parts.shape[1:], F32),
+            jax.ShapeDtypeStruct((sets, height, qkv_width), F32),
+            jax.ShapeDtypeStruct((sets, height, out_width), F32),
+        ),
+        in_specs=[vmem] * 3,
+        out_specs=(vmem,) * 3,
+        scratch_shapes=[
+            pltpu.VMEM((sets, 16, height, qkv_width), BF16),
+            pltpu.VMEM((sets, 16, height, out_width), BF16),
+            pltpu.VMEM((places[0], height, qkv_width), BF16),
+            pltpu.VMEM((places[1], height, qkv_width), BF16),
+            pltpu.VMEM((places[2], height, out_width), BF16),
+            pltpu.VMEM((places[3], height, out_width), BF16),
+            pltpu.VMEM((32,) + gain_parts.shape[1:], F32),
+            dma((4, 16)),
+            dma((4, 16)),
+            dma((4, 16)),
+            dma((4, max(places))),
+            dma((32,)),
+            dma((32,)),
+        ],
+        compiler_params=pltpu.CompilerParams(
+            collective_id=3, has_side_effects=True, vmem_limit_bytes=60 * 2**20
+        ),
+        name="scatter_attn",
+    )(gain_parts, qkv_grad, out_grad)
+
+
+def by_set(activations, weight):
+    return jnp.einsum("sfk,ske->sfe", activations, weight, preferred_element_type=F32)
+
+
+def by_set_back(gradients, weight):
+    return jnp.einsum("sfe,ske->sfk", gradients, weight, preferred_element_type=F32)
+
+
+def set_grad(activations, gradients):
+    return jnp.einsum("sfk,sfe->ske", activations, gradients, preferred_element_type=F32)
+
+
+def head_sums(product, spread):
+    high = product.astype(BF16)
+    low = (product - high.astype(F32)).astype(BF16)
+    sums = jnp.dot(high, spread, preferred_element_type=F32)
+    return sums + jnp.dot(low, spread, preferred_element_type=F32)
+
+
+def over_heads(values, spread):
+    return lax.dot_general(
+        values, spread, (((1,), (1,)), ((), ())), preferred_element_type=F32
+    )
+
+
+def local_fast(
+    tokens,
+    norm_attn,
+    w_qkv,
+    w_out,
+    norm_ff,
+    w_gate_up,
+    w_down,
+    cotangent,
+    valid_frames,
+    item_lengths,
+):
+    frame_count, positions, model = tokens.shape
+    head_count = model // HEAD_DIM
+    ff_units = w_gate_up.shape[2] // 2
+    score_scale = 1.0 / math.sqrt(HEAD_DIM)
+    own_gain = norm_attn.shape[1]
+    gains = jnp.zeros((16, 128), BF16)
+    gains = gains.at[0:positions, :own_gain].set(norm_attn)
+    gains = gains.at[positions : 2 * positions, :own_gain].set(norm_ff)
+    gains_full, qkv_full, out_full = gather_attn(gains, w_qkv, w_out)
+    gains_rows = jnp.swapaxes(gains_full[:, : 2 * positions, :own_gain], 0, 1)
+    gains_rows = gains_rows.reshape(2 * positions, model).astype(F32)
+    gain_one = gains_rows[:positions, None, :]
+    gain_two = gains_rows[positions:, None, :]
+
+    spread = (
+        jnp.arange(model)[:, None] // HEAD_DIM == jnp.arange(128)[None, :]
+    ).astype(BF16)
+
+    device_index = lax.axis_index(("dp", "pair"))
+    local_ids = jnp.arange(frame_count, dtype=jnp.int32)
+    frame_ids = device_index * frame_count + local_ids
+    item_ends = jnp.cumsum(item_lengths)
+    item_starts = item_ends - item_lengths
+    in_item = (frame_ids[:, None] >= item_starts[None, :]) & (
+        frame_ids[:, None] < item_ends[None, :]
+    )
+    item_share = 8 * frame_count / item_lengths.astype(F32)
+    frame_weight = jnp.sum(jnp.where(in_item, item_share[None, :], 0.0), axis=1)
+    frame_weight = jnp.where(local_ids < valid_frames[0], frame_weight, 0.0)
+    grad_out = jnp.swapaxes(cotangent, 0, 1).astype(F32) * frame_weight[None, :, None]
+    grad_low = grad_out.astype(BF16)
+
+    resid_in = jnp.swapaxes(tokens, 0, 1).astype(F32)
+    normed_one, inverse_one = normed(resid_in)
+    attn_in = (normed_one * gain_one).astype(BF16)
+    qkv = by_set(attn_in, qkv_full).astype(BF16)
+    queries = [qkv[p, :, :model].astype(F32) for p in range(positions)]
+    keys = [qkv[p, :, model : 2 * model].astype(F32) for p in range(positions)]
+    values = [qkv[p, :, 2 * model :].astype(F32) for p in range(positions)]
+    probs = []
+    contexts = []
+    for p in range(positions):
+        scores = [head_sums(queries[p] * keys[q], spread) * score_scale for q in range(p + 1)]
+        top = functools.reduce(jnp.maximum, scores)
+        powers = [jnp.exp(score - top) for score in scores]
+        total = functools.reduce(jnp.add, powers)
+        probs.append([power / total for power in powers])
+        context = sum(
+            over_heads(prob.astype(BF16), spread) * values[q] for q, prob in enumerate(probs[p])
+        )
+        contexts.append(context.astype(BF16))
+    context = jnp.stack(contexts)
+    resid_mid = resid_in + by_set(context, out_full)
+    normed_two, inverse_two = normed(resid_mid)
+    ff_in = (normed_two * gain_two).astype(BF16)
+
+    unit = w_down.shape[1]
+    parts = w_gate_up.reshape(positions, -1, 2, 2, 2, 2, 2, 2, unit)
+    parts = parts.transpose(4, 6, 7, 0, 1, 2, 3, 5, 8)
+    parts = parts.reshape(8, positions, w_gate_up.shape[1], 8 * unit)
+    gate_up_full, down_full, ff_rows, grad_rows = gather_ff(parts, w_down, ff_in, grad_low)
+    split = 4 * unit
+    gate_up = by_set(ff_rows, gate_up_full)
+    gate, up = gate_up[..., :split], gate_up[..., split:]
+    sigmoid_gate = jax.nn.sigmoid(gate)
+    silu_gate = gate * sigmoid_gate
+    hidden = (silu_gate * up).astype(BF16)
+    out_part = by_set(hidden, down_full).astype(BF16)
+    d_hidden = by_set_back(grad_rows, down_full)
+    d_gate = d_hidden * up * sigmoid_gate * (1.0 + gate * (1.0 - sigmoid_gate))
+    d_up = d_hidden * silu_gate
+    d_gate_up = jnp.concatenate([d_gate, d_up], axis=-1).astype(BF16)
+    down_grad = set_grad(hidden, grad_rows).astype(BF16)
+    gate_up_grad = set_grad(ff_rows, d_gate_up).astype(BF16)
+    back_part = by_set_back(d_gate_up, gate_up_full).astype(BF16)
+    out_sum, d_ff_in, gate_up_sum, down_sum = scatter_ff(
+        out_part, back_part, gate_up_grad, down_grad
+    )
+    output = jnp.swapaxes((resid_mid + out_sum).astype(BF16), 0, 1)
+    share_gate_up = gate_up_sum.reshape(2, 2, 2, positions, -1, 2, 2, 2, unit)
+    share_gate_up = share_gate_up.transpose(3, 4, 5, 6, 0, 7, 1, 2, 8)
+    share_gate_up = share_gate_up.reshape(w_gate_up.shape)
+
+    grad_norm_ff = jnp.sum(normed_two * d_ff_in, axis=1)
+    d_mid = grad_out + norm_back(normed_two, inverse_two, d_ff_in * gain_two)
+    d_mid_low = d_mid.astype(BF16)
+    out_grad = set_grad(context, d_mid_low).astype(BF16)
+    d_context = by_set_back(d_mid_low, out_full).astype(BF16).astype(F32)
+    d_queries = []
+    d_keys = [0.0] * positions
+    d_values = [0.0] * positions
+    for p in range(positions):
+        d_probs = [head_sums(d_context[p] * values[q], spread) for q in range(p + 1)]
+        mean = functools.reduce(jnp.add, [prob * d for prob, d in zip(probs[p], d_probs)])
+        d_query = 0.0
+        for q in range(p + 1):
+            d_score = (probs[p][q] * (d_probs[q] - mean)).astype(BF16)
+            d_score = over_heads(d_score, spread)
+            d_values[q] += over_heads(probs[p][q].astype(BF16), spread) * d_context[p]
+            d_query += d_score * keys[q]
+            d_keys[q] += d_score * queries[p]
+        d_queries.append(d_query)
+    d_qkv = jnp.stack(
+        [
+            jnp.concatenate(
+                [d_queries[p] * score_scale, d_keys[p] * score_scale, d_values[p]], axis=-1
+            )
+            for p in range(positions)
+        ]
+    ).astype(BF16)
+    qkv_grad = set_grad(attn_in, d_qkv).astype(BF16)
+    d_attn_in = by_set_back(d_qkv, qkv_full)
+    grad_norm_attn = jnp.sum(normed_one * d_attn_in, axis=1)
+    grad_tokens = d_mid + norm_back(normed_one, inverse_one, d_attn_in * gain_one)
+    grad_tokens = jnp.swapaxes(grad_tokens, 0, 1)
+    gain_grads = jnp.concatenate([grad_norm_attn, grad_norm_ff], axis=0)
+    gain_grads = jnp.swapaxes(gain_grads.reshape(2 * positions, 32, own_gain), 0, 1)
+    gain_parts = jnp.zeros((32, 8, 128), F32).at[:, : 2 * positions, :own_gain].set(gain_grads)
+    gains_sum, share_qkv, share_out = scatter_attn(gain_parts, qkv_grad, out_grad)
+    return (
+        output,
+        grad_tokens,
+        gains_sum[:positions, :own_gain],
+        share_qkv,
+        share_out,
+        gains_sum[positions : 2 * positions, :own_gain],
+        share_gate_up,
+        down_sum,
+    )
+
+
 def solution(mesh):
     in_specs = (
         P(("dp", "pair"), None, None),
@@ -243,4 +1322,5 @@
         P(None, ("dp", "pair"), None),
         P(None, ("dp", "pair"), None),
     )
-    return jax.shard_map(local, mesh=mesh, in_specs=in_specs, out_specs=out_specs, check_vma=False)
+    body = local_fast if mesh.shape["dp"] == 16 and mesh.shape["pair"] == 2 else local
+    return jax.shard_map(body, mesh=mesh, in_specs=in_specs, out_specs=out_specs, check_vma=False)

time: 3010 us -> 512 us (0.17)
  waiting for transfers between devices: 2440 us -> 0 us
  Pallas kernels: 0 us -> 374 us
  local copies, waits for them, and re-layouts: 248 us -> 29.7 us
  matrix products: 193 us -> 87.3 us
  blocking collectives: 83.1 us -> 0 us
    unnamed x22 -> x0, waiting for transfers between devices: 1680 us -> none
    all_gather x6 -> x0, waiting for transfers between devices: 397 us -> none  [the longest x2 221 us: gather_ff_fwd(): lax.all_gather(w_gate_up[start:start + group], ('dp', 'pair'), axis=1, ti...]
    pallas_call x0 -> x4, Pallas kernels: none -> 374 us  [the longest x1 115 us: scatter_ff(): pl.pallas_call(scatter_ff_kernel, out_shape=(jax.ShapeDtypeStruct((sets,...]
    reduce_scatter x2 -> x0, waiting for transfers between devices: 368 us -> none  [local(): lax.psum_scatter(grad_down, ('dp', 'pair'), scatter_dimension=0, tiled=True)]
    transpose x11 -> x1, local copies, waits for them, and re-layouts: 198 us -> 4.55 us  [local_fast(): share_gate_up = share_gate_up.transpose(3, 4, 5, 6, 0, 7, 1, 2, 8)]
    dot_general x23 -> x29, matrix products: 184 us -> 87.3 us  [the longest x4 26.7 us: by_set_back(): jnp.einsum('sfe,ske->sfk', gradients, weight, preferred_element_type=F32)]
    all_gather x1 -> x0, blocking collectives: 43.3 us -> none  [local(): lax.all_gather(norm_attn, ('dp', 'pair'), axis=1, tiled=True)]
    unnamed x1 -> x0, blocking collectives: 39.9 us -> none
  transfers between devices with their start and end apart: 15 -> 0, of which waited for: 13 -> 0; matrix products, arithmetic and copies ran while one was open for 13% -> 0% of each run, Pallas kernels for 0% -> 0%
where the time goes in v1:
time: 512 us; the launch traced here: 507 us
  Pallas kernels  374 us (73%)
  matrix products  87.3 us (17%)
  local copies, waits for them, and re-layouts  29.7 us (6%)
  other arithmetic  14.7 us (3%)
    pallas_call x1, Pallas kernels, scatter_ff(): pl.pallas_call(scatter_ff_kernel, out_shape=(jax.ShapeDtypeStruct((sets,...  115 us
    pallas_call x1, Pallas kernels, gather_ff(): pl.pallas_call(gather_ff_kernel, out_shape=(jax.ShapeDtypeStruct((sets, 3...  98.9 us
    pallas_call x1, Pallas kernels, gather_attn(): pl.pallas_call(gather_attn_kernel, out_shape=(jax.ShapeDtypeStruct((32,)...  83 us
    pallas_call x1, Pallas kernels, scatter_attn(): pl.pallas_call(scatter_attn_kernel, out_shape=(jax.ShapeDtypeStruct(gain_...  76.4 us
    dot_general x4, matrix products, by_set_back(): jnp.einsum('sfe,ske->sfk', gradients, weight, preferred_element_type=F32)  26.7 us
    dot_general x4, matrix products, by_set(): jnp.einsum('sfk,ske->sfe', activations, weight, preferred_element_type=F32)  25.1 us
    dot_general x4, matrix products, set_grad(): jnp.einsum('sfk,sfe->ske', activations, gradients, preferred_element_type...  25 us

profile of v1, /device:TPU:0, one launch (start us, length us, event | category | flops | bytes accessed | tf_op | source)
XLA Modules:
  0.0 507.2 jit_solution(11496036638077390769)
XLA Ops:
  3.5 1.2 fusion.23
  5.5 1.5 scatter.11.gains_ref
  7.0 2.0 bitcast_convert_fusion.grads_ref
  9.0 1.8 reshape.242
  11.7 1.5 reshape.243.gate_up_ref
  13.3 83.0 %gather_attn.1 = (bf16[32,16,128]{2,1,0:T(8,128)(2,1)}, bf16[2,1024,3072]{2,1,0:T(8,128)(2,1)}, bf16[2,1024,1024]{2,1,0:T(8,128)(2,1)}) custom-call(bf16[16,128]{1,0:T(8,128)(2,1)} %copy-done.16, bf16[2,32,3072]{2,1,0:T(8,128)(2,1)} %qkv_ref.1, bf16[2,32,1024]{2,1,0:T(8,128)(2,1)} %out_ref.1), custom_call_target="tpu_custom_call" | custom-call | tf_op jit(solution)/shard_map/gather_attn/pallas_call | solution.py:481
  97.4 6.5 %convolution_convert_fusion.1 = bf16[2,128,3072]{2,1,0:T(8,128)(2,1)S(1)} fusion(bf16[2,1024,3072]{2,1,0:T(8,128)(2,1)} %get-tuple-element.59, f32[2,1024]{1,0:T(2,128)S(1)} %slice.125, f32[2,128]{1,0:T(2,128)S(1)} %add_rsqrt_fusion.1, bf16[128,2,1024]{2,1,0:T(2,128)(2,1)S(1)} %copy-done), kind=kOutput, calls=%fused_computation.7 | convolution fusion | flops 1612447744 | bytes 14689280 | tf_op jit(solution)/shard_map/sfk,ske->sfe/dot_general | solution.py:1135
  110.2 98.9 %gather_ff.1 = (bf16[2,1024,1024]{2,1,0:T(8,128)(2,1)}, bf16[2,512,1024]{2,1,0:T(8,128)(2,1)}, bf16[2,1024,1024]{2,1,0:T(8,128)(2,1)}, bf16[2,1024,1024]{2,1,0:T(8,128)(2,1)}) custom-call(bf16[8,2,32,1024]{3,2,1,0:T(8,128)(2,1)} %reshape.243.gate_up_ref, bf16[2,128,1024]{2,1,0:T(8,128)(2,1)} %down_ref.1, ...), custom_call_target="tpu_custom_call" | custom-call | tf_op jit(solution)/shard_map/gather_ff/pallas_call | solution.py:657
  209.1 11.5 %fusion.111 = f32[2,1024,1024]{1,2,0:T(8,128)} fusion(bf16[2,1024,1024]{2,1,0:T(8,128)(2,1)} %get-tuple-element.61, bf16[2,1024,1024]{2,1,0:T(8,128)(2,1)} %get-tuple-element.62), kind=kOutput, calls=%fused_computation.188 | convolution fusion | flops 4294967296 | bytes 16777216 | tf_op jit(solution)/shard_map/sfk,ske->sfe/dot_general | solution.py:1135
  220.7 7.6 %multiply_convert_fusion.1 = (bf16[2,1024,512]{1,2,0:T(8,128)(2,1)}, bf16[2,1024,512]{1,2,0:T(8,128)(2,1)}, bf16[2,1024,512]{1,2,0:T(8,128)(2,1)S(1)}) fusion(f32[2,1024,1024]{1,2,0:T(8,128)} %fusion.111, bf16[2,1024,1024]{2,1,0:T(8,128)(2,1)S(1)} %copy-done.20, bf16[2,512,1024]{2,1,0:T(8,128)(2,1)S(1)} %copy-done.21), kind=kOutput, calls=%fused_computation.3 | convolution fusion | flops 2163212288 | bytes 20971520 | tf_op jit(solution)/shard_map/sfe,ske->sfk/dot_general | solution.py:1139
  228.3 3.7 convolution_convert_fusion.4.down_ref
  231.9 10.7 %fusion.4.gate_up_ref = bf16[2,1024,1024]{2,1,0:T(8,128)(2,1)} fusion(bf16[2,1024,1024]{2,1,0:T(8,128)(2,1)} %get-tuple-element.61, bf16[2,1024,512]{1,2,0:T(8,128)(2,1)} %get-tuple-element.101, bf16[2,1024,512]{1,2,0:T(8,128)(2,1)} %get-tuple-element.100), kind=kOutput, calls=%fused_computation.11 | convolution fusion | flops 4305453056 | bytes 12582912 | tf_op jit(solution)/shard_map/sfk,sfe->ske/dot_general | solution.py:1143
  242.6 10.1 %fusion.3.back_ref = bf16[2,1024,1024]{2,1,0:T(8,128)(2,1)} fusion(bf16[2,1024,1024]{2,1,0:T(8,128)(2,1)S(1)} %copy-done.19, bf16[2,1024,512]{1,2,0:T(8,128)(2,1)} %get-tuple-element.101, bf16[2,1024,512]{1,2,0:T(8,128)(2,1)} %get-tuple-element.100), kind=kOutput, calls=%fused_computation.10 | convolution fusion | flops 4305453056 | bytes 12582912 | tf_op jit(solution)/shard_map/sfe,ske->sfk/dot_general | solution.py:1139
  252.7 6.0 %convolution_convert_fusion.3.out_ref = bf16[2,1024,1024]{2,1,0:T(8,128)(2,1)} fusion(bf16[2,1024,512]{1,2,0:T(8,128)(2,1)} %copy-done.22, bf16[2,512,1024]{2,1,0:T(8,128)(2,1)S(1)} %copy-done.21), kind=kOutput, calls=%fused_computation.13 | convolution fusion | flops 2149580800 | bytes 8388608 | tf_op jit(solution)/shard_map/sfk,ske->sfe/dot_general | solution.py:1135
  258.7 115.2 %scatter_ff.1 = (f32[2,128,1024]{2,1,0:T(8,128)}, f32[2,128,1024]{2,1,0:T(8,128)}, f32[8,2,32,1024]{3,2,1,0:T(8,128)}, f32[2,128,1024]{2,1,0:T(8,128)}) custom-call(bf16[2,1024,1024]{2,1,0:T(8,128)(2,1)} %convolution_convert_fusion.3.out_ref, bf16[2,1024,1024]{2,1,0:T(8,128)(2,1)} %fusion.3.back_ref, bf16[2,1024,1024]{2,1,0:T(8,128)(2,1)} %fusion.4.gate_up_ref, ...), custom_call_target="tpu_custom_call" | custom-call | tf_op jit(solution)/shard_map/scatter_ff/pallas_call | solution.py:893
  374.0 2.3 multiply_reduce_fusion
  376.3 2.0 bitcast_add_fusion
  378.3 1.5 fusion.5
  380.9 1.3 copy.61
  386.3 3.2 fusion.34
  389.5 1.5 maximum_bitcast_fusion
  391.0 7.5 %fusion.22 = (f32[2,1024]{1,0:T(2,128)S(1)}, f32[2,128]{1,0:T(2,128)S(1)}, f32[2,128,1024]{2,1,0:T(8,128)S(1)}) fusion(f32[2,128]{1,0:T(2,128)S(1)} %add_rsqrt_fusion.1, bf16[128,2,1024]{2,1,0:T(2,128)(2,1)S(1)} %copy-done, f32[2,1024]{1,0:T(2,128)S(1)} %slice.125, bf16[2,1024,3072]{2,1,0:T(8,128)(2,1)} %get-tuple-element.59, ...), kind=kOutput, calls=%fused_computation.45 | convolution fusion | flops 1613231872 | bytes 15747072 | tf_op jit(solution)/shard_map/sfe,ske->sfk/dot_general | solution.py:1139
  398.8 1.8 copy.62
  401.4 4.1 reshape.247
  405.5 4.5 copy.60
  410.1 3.9 reshape.248
  414.0 4.2 convolution_convert_fusion.2.out_ref
  418.2 6.5 %convolution_convert_fusion.qkv_ref = bf16[2,1024,3072]{2,1,0:T(8,128)(2,1)} fusion(bf16[1,128,3072]{2,1,0:T(8,128)(2,1)S(1)} %get-tuple-element.121, bf16[1,128,3072]{2,1,0:T(8,128)(2,1)S(1)} %get-tuple-element.120, f32[2,1024]{1,0:T(2,128)S(1)} %slice.125, f32[2,128]{1,0:T(2,128)S(1)} %add_rsqrt_fusion.1, bf16[128,2,1024]{2,1,0:T(2,128)(2,1)S(1)} %copy-done), kind=kOutput, calls=%fused_computation | convolution fusion | flops 1618739200 | bytes 14689280 | tf_op jit(solution)/shard_map/sfk,sfe->ske/dot_general | solution.py:1143
  424.6 76.4 %scatter_attn.1 = (f32[8,128]{1,0:T(8,128)}, f32[2,32,3072]{2,1,0:T(8,128)}, f32[2,32,1024]{2,1,0:T(8,128)}) custom-call(f32[32,8,128]{2,1,0:T(8,128)} %scatter.14.gains_ref, bf16[2,1024,3072]{2,1,0:T(8,128)(2,1)} %convolution_convert_fusion.qkv_ref, bf16[2,1024,1024]{2,1,0:T(8,128)(2,1)} %convolution_convert_fusion.2.out_ref), custom_call_target="tpu_custom_call" | custom-call | tf_op jit(solution)/shard_map/scatter_attn/pallas_call | solution.py:1103
  501.0 1.3 fusion.110
  502.3 2.1 copy.94
  504.4 1.7 copy.95
  (91 shorter events, 18.2 us)
Async XLA Ops:
  3.5 92.8 %copy-start.17 = (f32[128]{0:T(128)}, f32[128]{0:T(128)S(1)}, u32[]{:S(2)}) copy-start(f32[128]{0:T(128)S(1)} %compare_select_fusion) | copy-start | bytes 1540
  4.8 92.6 %copy-start = (bf16[128,2,1024]{2,1,0:T(2,128)(2,1)S(1)}, bf16[128,2,1024]{2,1,0:T(2,128)(2,1)}, u32[]{:S(2)}) copy-start(bf16[128,2,1024]{2,1,0:T(2,128)(2,1)} %param.16) | copy-start | bytes 1572868
  7.0 6.2 %copy-start.16 = (bf16[16,128]{1,0:T(8,128)(2,1)}, bf16[16,128]{1,0:T(8,128)(2,1)S(1)}, u32[]{:S(2)}) copy-start(bf16[16,128]{1,0:T(8,128)(2,1)S(1)} %scatter.11.gains_ref) | copy-start | bytes 12292
  97.3 276.6 %copy-start.12 = (f32[2,1024]{1,0:T(2,128)}, f32[2,1024]{1,0:T(2,128)S(1)}, u32[]{:S(2)}) copy-start(f32[2,1024]{1,0:T(2,128)S(1)} %slice.133) | copy-start | bytes 24580
  104.0 3.7 copy-start.3
  104.7 3.5 copy-start.1
  106.2 1.4 copy-start.13
  106.6 1.1 copy-start.7
  107.4 0.8 copy-start.5
  107.7 1.6 copy-start.9
  109.3 264.7 %copy-start.15 = (f32[2,128]{1,0:T(2,128)}, f32[2,128]{1,0:T(2,128)S(1)}, u32[]{:S(2)}) copy-start(f32[2,128]{1,0:T(2,128)S(1)} %add_rsqrt_fusion) | copy-start | bytes 3076
  209.1 11.6 %copy-start.20 = (bf16[2,1024,1024]{2,1,0:T(8,128)(2,1)S(1)}, bf16[2,1024,1024]{2,1,0:T(8,128)(2,1)}, u32[]{:S(2)}) copy-start(bf16[2,1024,1024]{2,1,0:T(8,128)(2,1)} %get-tuple-element.64) | copy-start | bytes 12582916
  209.1 11.5 %copy-start.21 = (bf16[2,512,1024]{2,1,0:T(8,128)(2,1)S(1)}, bf16[2,512,1024]{2,1,0:T(8,128)(2,1)}, u32[]{:S(2)}) copy-start(bf16[2,512,1024]{2,1,0:T(8,128)(2,1)} %get-tuple-element.63) | copy-start | bytes 6291460
  228.3 3.7 copy-start.22
  231.9 10.7 %copy-start.19 = (bf16[2,1024,1024]{2,1,0:T(8,128)(2,1)S(1)}, bf16[2,1024,1024]{2,1,0:T(8,128)(2,1)}, u32[]{:S(2)}) copy-start(bf16[2,1024,1024]{2,1,0:T(8,128)(2,1)} %get-tuple-element.62) | copy-start | bytes 12582916
  258.7 117.6 %copy-start.10 = (bf16[128,2,1024]{2,1,0:T(2,128)(2,1)S(1)}, bf16[128,2,1024]{2,1,0:T(2,128)(2,1)}, u32[]{:S(2)}) copy-start(bf16[128,2,1024]{2,1,0:T(2,128)(2,1)} %param.23) | copy-start | bytes 1572868
  258.7 117.6 %copy-start.18 = (f32[128]{0:T(128)S(1)}, f32[128]{0:T(128)}, u32[]{:S(2)}) copy-start(f32[128]{0:T(128)} %copy-done.17) | copy-start | bytes 1540
  373.9 4.4 copy-start.2
  378.3 1.6 copy-start.6
  378.3 1.6 copy-start.8
  378.3 3.9 copy-start.4
  391.0 7.5 %copy-start.14 = (f32[2,1024]{1,0:T(2,128)S(1)}, f32[2,1024]{1,0:T(2,128)}, u32[]{:S(2)}) copy-start(f32[2,1024]{1,0:T(2,128)} %get-tuple-element.96) | copy-start | bytes 24580
  424.6 81.4 %copy-start.11 = (f32[2,128,1024]{2,1,0:T(8,128)S(1)}, f32[2,128,1024]{2,1,0:T(8,128)}, u32[]{:S(2)}) copy-start(f32[2,128,1024]{2,1,0:T(8,128)} %get-tuple-element.137) | copy-start | bytes 3145732

commit v2 on v1

--- a/solution.py
+++ b/solution.py
@@ -352,154 +352,6 @@
     return (z + offset[0]) * 4 + flip(y, offset[1]) * 2 + flip(x, offset[2])
 
 
-def gather_attn_kernel(
-    gains_ref,
-    qkv_ref,
-    out_ref,
-    gains_full,
-    qkv_full,
-    out_full,
-    plane_sem,
-    sibling_sem,
-    send_sem,
-    local_sem,
-    gains_send,
-    gains_recv,
-):
-    z, y, x, core = here()
-    me = 2 * (z * 4 + y * 2 + x) + core
-    greet_all(z, y, x, core)
-    pieces = [
-        (qkv_ref, qkv_full, 0, "zxy"),
-        (qkv_ref, qkv_full, 1, "zyx"),
-        (out_ref, out_full, 0, "xyz"),
-        (out_ref, out_full, 1, "yxz"),
-    ]
-
-    def rows(piece, device):
-        source, full, index, _ = pieces[piece]
-        height = source.shape[1]
-        return full.at[index, pl.ds(pl.multiple_of(device * height, height), height), :]
-
-    pending = []
-
-    def send(piece, offset, direction):
-        source, full, index, _ = pieces[piece]
-        chip = chip_of(offset, z, y, x)
-        block = rows(piece, 2 * chip + core)
-        src = source.at[index] if hops(offset) == 0 else block
-        recv = sibling_sem if direction == "s" else plane_sem
-        return push(
-            src,
-            block,
-            send_sem.at[piece, chip, DIRECTIONS.index(direction)],
-            recv.at[piece, chip],
-            neighbour(direction, z, y, x, core),
-        )
-
-    def handle(piece, offset, finish):
-        order = pieces[piece][3]
-
-        def go():
-            chip = chip_of(offset, z, y, x)
-            if hops(offset) > 0 and not finish:
-                arrived(
-                    rows(piece, 2 * chip + core),
-                    plane_sem.at[piece, chip],
-                    neighbour("s", z, y, x, core),
-                )
-            for direction in onward(order, offset) + ["s"]:
-                copy = send(piece, offset, direction)
-                maybe(
-                    direction_exists(direction, z), copy.wait_send if finish else copy.start
-                )
-
-        maybe(offset_exists(offset, z), go)
-
-    events = sorted(
-        ((hops(offset), rank, piece, offset) for piece in range(4) for rank, offset in enumerate(OFFSETS)),
-        key=lambda event: event[:3],
-    )
-    for _, _, piece, offset in events:
-        if hops(offset) == 0:
-            handle(piece, offset, False)
-
-    def gains_copy(step):
-        other = lax.rem(me + step, 32)
-        return push(
-            gains_ref,
-            gains_full.at[me],
-            gains_send.at[step],
-            gains_recv.at[me],
-            (lax.div(other, 2), lax.rem(other, 2)),
-        )
-
-    def gains_start(step, carry):
-        gains_copy(step).start()
-        return carry
-
-    lax.fori_loop(1, 32, gains_start, 0)
-    own = [
-        pltpu.make_async_copy(source.at[index], rows(piece, me), local_sem.at[piece])
-        for piece, (source, full, index, _) in enumerate(pieces)
-    ]
-    own.append(pltpu.make_async_copy(gains_ref, gains_full.at[me], local_sem.at[4]))
-    for copy in own:
-        copy.start()
-    for _, _, piece, offset in events:
-        if hops(offset) > 0:
-            handle(piece, offset, False)
-    for _, _, piece, offset in events:
-        handle(piece, offset, True)
-
-    def sibling_wait(chip, carry):
-        for piece in range(4):
-            arrived(
-                rows(piece, 2 * chip + 1 - core),
-                sibling_sem.at[piece, chip],
-                neighbour("s", z, y, x, core),
-            )
-        return carry
-
-    lax.fori_loop(0, 16, sibling_wait, 0)
-
-    def gains_wait(step, carry):
-        other = lax.rem(me + step, 32)
-        gains_copy(step).wait_send()
-        arrived(gains_full.at[other], gains_recv.at[other], neighbour("s", z, y, x, core))
-        return carry
-
-    lax.fori_loop(1, 32, gains_wait, 0)
-    for copy in own:
-        copy.wait()
-
-
-def gather_attn(gains, w_qkv, w_out):
-    sets, height, qkv_width = w_qkv.shape
-    out_width = w_out.shape[2]
-    dma = pltpu.SemaphoreType.DMA
-    return pl.pallas_call(
-        gather_attn_kernel,
-        out_shape=(
-            jax.ShapeDtypeStruct((32,) + gains.shape, BF16),
-            jax.ShapeDtypeStruct((sets, 32 * height, qkv_width), BF16),
-            jax.ShapeDtypeStruct((sets, 32 * height, out_width), BF16),
-        ),
-        in_specs=[pl.BlockSpec(memory_space=pl.ANY)] * 3,
-        out_specs=(pl.BlockSpec(memory_space=pl.ANY),) * 3,
-        scratch_shapes=[
-            dma((4, 16)),
-            dma((4, 16)),
-            dma((4, 16, 5)),
-            dma((5,)),
-            dma((32,)),
-            dma((32,)),
-        ],
-        compiler_params=pltpu.CompilerParams(collective_id=0, has_side_effects=True),
-        name="gather_attn",
-    )(gains, w_qkv, w_out)
-
-
 RANK_STEPS = sorted(
     ((dl, dx, dc) for dl in (0, 1) for dx in (0, 1) for dc in (0, 1)), key=lambda step: (sum(step), step)
 )
@@ -520,164 +372,6 @@
     far = ((2 * (1 - zh) + zl) * 4 + y * 2 + x, core)
     across = (z * 4 + (1 - y) * 2 + x, core)
     return zh, zl, member, rank, device, far, across
-
-
-def gather_ff_kernel(
-    gate_up_ref,
-    down_ref,
-    rows_ref,
-    grads_ref,
-    gate_up_full,
-    down_full,
-    rows_full,
-    grads_full,
-    rank_send,
-    rank_recv,
-    far_send,
-    far_recv,
-    across_send,
-    across_recv,
-    act_send,
-    act_recv,
-    local_sem,
-):
-    z, y, x, core = here()
-    zh, zl, member, rank, device, far, across = group_place(z, y, x, core)
-    own_step = (0, 0, 0)
-    others = RANK_STEPS[1:]
-    greet([member(step) for step in others] + [far, across])
-    height = gate_up_ref.shape[2]
-    down_height = down_ref.shape[1]
-    act_height = rows_ref.shape[1]
-    sends = []
-
-    def start(copy):
-        copy.start()
-        sends.append(copy)
-
-    def weight_rows(number):
-        return gate_up_full.at[:, pl.ds(pl.multiple_of(number * height, height), height), :]
-
-    def down_rows(dzh, dy):
-        number = 2 * flip(zh, dzh) + flip(y, dy)
-        return down_full.at[:, pl.ds(pl.multiple_of(number * down_height, down_height), down_height), :]
-
-    def act_rows(full, step):
-        return full.at[:, pl.ds(pl.multiple_of(rank(step) * act_height, act_height), act_height), :]
-
-    acts = [(rows_ref, rows_full), (grads_ref, grads_full)]
-
-    def send_act(which, step, source, hop):
-        to = member(tuple(1 if axis == hop else 0 for axis in range(3)))
-        landed = tuple(bit ^ (1 if axis == hop else 0) for axis, bit in enumerate(step))
-        start(
-            push(
-                source,
-                act_rows(acts[which][1], step),
-                act_send.at[which, 4 * step[0] + 2 * step[1] + step[2], hop],
-                act_recv.at[which, 4 * landed[0] + 2 * landed[1] + landed[2]],
-                to,
-            )
-        )
-
-    def wait_act(which, step):
-        arrived(
-            act_rows(acts[which][1], step),
-            act_recv.at[which, 4 * step[0] + 2 * step[1] + step[2]],
-            across,
-        )
-
-    mine = gate_up_ref.at[rank(own_step)]
-    for slot, step in enumerate(RANK_STEPS):
-        if step != own_step:
-            start(
-                push(
-                    gate_up_ref.at[rank(step)],
-                    weight_rows(device(own_step)),
-                    rank_send.at[slot],
-                    rank_recv.at[slot],
-                    member(step),
-                )
-            )
-    start(push(mine, weight_rows(device(own_step)), far_send.at[0], far_recv.at[0], far))
-    start(push(mine, weight_rows(device(own_step)), across_send.at[0, 0], across_recv.at[0, 0], across))
-    start(push(down_ref, down_rows(0, 0), far_send.at[8], far_recv.at[8], far))
-    start(push(down_ref, down_rows(0, 0), across_send.at[0, 8], across_recv.at[0, 8], across))
-    for which in (0, 1):
-        for hop in (0, 1, 2):
-            send_act(which, own_step, acts[which][0], hop)
-    local = [
-        pltpu.make_async_copy(mine, weight_rows(device(own_step)), local_sem.at[0]),
-        pltpu.make_async_copy(down_ref, down_rows(0, 0), local_sem.at[1]),
-        pltpu.make_async_copy(rows_ref, act_rows(rows_full, own_step), local_sem.at[2]),
-        pltpu.make_async_copy(grads_ref, act_rows(grads_full, own_step), local_sem.at[3]),
-    ]
-    for copy in local:
-        copy.start()
-    for slot, step in enumerate(RANK_STEPS):
-        if step == own_step:
-            continue
-        block = weight_rows(device(step))
-        arrived(block, rank_recv.at[slot], member(step))
-        start(push(block, block, far_send.at[slot], far_recv.at[slot], far))
-        start(push(block, block, across_send.at[0, slot], across_recv.at[0, slot], across))
-    for slot, step in enumerate(RANK_STEPS):
-        block = weight_rows(device(step, 1, 0))
-        arrived(block, far_recv.at[slot], far)
-        start(push(block, block, across_send.at[1, slot], across_recv.at[1, slot], across))
-    block = down_rows(1, 0)
-    arrived(block, far_recv.at[8], far)
-    start(push(block, block, across_send.at[1, 8], across_recv.at[1, 8], across))
-    for which in (0, 1):
-        step = (1, 0, 0)
-        wait_act(which, step)
-        block = act_rows(acts[which][1], step)
-        send_act(which, step, block, 1)
-        send_act(which, step, block, 2)
-    for which in (0, 1):
-        for step in ((0, 1, 0), (1, 1, 0)):
-            wait_act(which, step)
-            send_act(which, step, act_rows(acts[which][1], step), 2)
-    for which in (0, 1):
-        for step in ((0, 0, 1), (1, 0, 1), (0, 1, 1), (1, 1, 1)):
-            wait_act(which, step)
-    for dzh in (0, 1):
-        for slot, step in enumerate(RANK_STEPS):
-            arrived(weight_rows(device(step, dzh, 1)), across_recv.at[dzh, slot], across)
-        arrived(down_rows(dzh, 1), across_recv.at[dzh, 8], across)
-    for copy in sends:
-        copy.wait_send()
-    for copy in local:
-        copy.wait()
-
-
-def gather_ff(gate_up_parts, w_down, rows, grads):
-    ranks, sets, height, width = gate_up_parts.shape
-    dma = pltpu.SemaphoreType.DMA
-    return pl.pallas_call(
-        gather_ff_kernel,
-        out_shape=(
-            jax.ShapeDtypeStruct((sets, 32 * height, width), BF16),
-            jax.ShapeDtypeStruct((sets, 4 * w_down.shape[1], w_down.shape[2]), BF16),
-            jax.ShapeDtypeStruct((sets, ranks * rows.shape[1], rows.shape[2]), BF16),
-            jax.ShapeDtypeStruct((sets, ranks * grads.shape[1], grads.shape[2]), BF16),
-        ),
-        in_specs=[pl.BlockSpec(memory_space=pl.ANY)] * 4,
-        out_specs=(pl.BlockSpec(memory_space=pl.ANY),) * 4,
-        scratch_shapes=[
-            dma((8,)),
-            dma((8,)),
-            dma((9,)),
-            dma((9,)),
-            dma((2, 9)),
-            dma((2, 9)),
-            dma((2, 8, 3)),
-            dma((2, 8)),
-            dma((4,)),
-        ],
-        compiler_params=pltpu.CompilerParams(collective_id=1, has_side_effects=True),
-        name="gather_ff",
-    )(gate_up_parts, w_down, rows, grads)
 
 
 def add_into(target, sources, rows=16, columns=1024):
@@ -1131,6 +825,448 @@
     )(gain_parts, qkv_grad, out_grad)
 
 
+def row_loop(height, chunk, body):
+    def one(step, carry):
+        body(pl.ds(pl.multiple_of(step * chunk, chunk), chunk))
+        return carry
+
+    lax.fori_loop(0, height // chunk, one, 0)
+
+
+def tile_loop(width, tile, body):
+    def one(step, carry):
+        body(pl.ds(pl.multiple_of(step * tile, tile), tile))
+        return carry
+
+    lax.fori_loop(0, width // tile, one, 0)
+
+
+def make_spread(spread):
+    height, width = spread.shape
+    head = lax.broadcasted_iota(jnp.int32, (height, width), 0) // HEAD_DIM
+    spread[...] = jnp.where(
+        head == lax.broadcasted_iota(jnp.int32, (height, width), 1), 1.0, 0.0
+    ).astype(BF16)
+
+
+def pairs_of(positions):
+    return [(p, q) for p in range(positions) for q in range(p + 1)]
+
+
+def split_product(product):
+    high = product.astype(BF16)
+    return high, (product - high.astype(F32)).astype(BF16)
+
+
+def sums_over_heads(halves, spread, index, height):
+    return jnp.dot(
+        halves[2 * index], spread[...], preferred_element_type=F32
+    ) + jnp.dot(halves[2 * index + 1], spread[...], preferred_element_type=F32)
+
+
+def to_heads(values, spread):
+    return lax.dot_general(
+        values, spread[...], (((1,), (1,)), ((), ())), preferred_element_type=F32
+    ).astype(BF16)
+
+
+def attention_probs(qkv, halves, spread, model):
+    positions, height, _ = qkv.shape
+    scale = 1.0 / math.sqrt(HEAD_DIM)
+    pairs = pairs_of(positions)
+
+    def products(rows):
+        for index, (p, q) in enumerate(pairs):
+            product = qkv[p, rows, :model].astype(F32) * qkv[q, rows, model : 2 * model].astype(F32)
+            halves[2 * index, rows, :], halves[2 * index + 1, rows, :] = split_product(product)
+
+    row_loop(height, 16, products)
+    scores = [sums_over_heads(halves, spread, index, height) * scale for index in range(len(pairs))]
+    probs = []
+    for p in range(positions):
+        own = [scores[index] for index, pair in enumerate(pairs) if pair[0] == p]
+        top = functools.reduce(jnp.maximum, own)
+        powers = [jnp.exp(score - top) for score in own]
+        total = functools.reduce(jnp.add, powers)
+        probs.extend([power / total for power in powers])
+    return probs
+
+
+def forward_kernel(
+    gains_ref,
+    tokens_ref,
+    qkv_ref,
+    out_ref,
+    gate_up_ref,
+    down_ref,
+    grads_ref,
+    gain_rows,
+    qkv_rows,
+    context,
+    resid_mid,
+    qkv_full,
+    out_full,
+    gate_up_full,
+    down_full,
+    rows_full,
+    grads_full,
+    qkv_buf,
+    out_buf,
+    gains_all,
+    attn_in,
+    ff_in,
+    halves,
+    spread,
+    plane_sem,
+    sibling_sem,
+    send_sem,
+    gains_send,
+    gains_recv,
+    rank_send,
+    rank_recv,
+    far_send,
+    far_recv,
+    across_send,
+    across_recv,
+    act_send,
+    act_recv,
+    local_sem,
+    keep_sem,
+):
+    z, y, x, core = here()
+    me = 2 * (z * 4 + y * 2 + x) + core
+    zh, zl, member, rank, device, far, across = group_place(z, y, x, core)
+    own_step = (0, 0, 0)
+    positions, act_height, model = tokens_ref.shape
+    height = gate_up_ref.shape[2]
+    down_height = down_ref.shape[1]
+    sibling = neighbour("s", z, y, x, core)
+    greet_all(z, y, x, core)
+    pieces = [
+        (qkv_ref, qkv_buf, 0, "zxy"),
+        (qkv_ref, qkv_buf, 1, "zyx"),
+        (out_ref, out_buf, 0, "xyz"),
+        (out_ref, out_buf, 1, "yxz"),
+    ]
+
+    def piece_rows(piece, number):
+        _, full, index, _ = pieces[piece]
+        return full.at[index, pl.ds(pl.multiple_of(number * height, height), height), :]
+
+    def tree_send(piece, offset, direction):
+        source, _, index, _ = pieces[piece]
+        chip = chip_of(offset, z, y, x)
+        block = piece_rows(piece, 2 * chip + core)
+        recv = sibling_sem if direction == "s" else plane_sem
+        return push(
+            source.at[index] if hops(offset) == 0 else block,
+            block,
+            send_sem.at[piece, chip, DIRECTIONS.index(direction)],
+            recv.at[piece, chip],
+            neighbour(direction, z, y, x, core),
+        )
+
+    def tree_step(piece, offset, finish=False):
+        order = pieces[piece][3]
+
+        def go():
+            chip = chip_of(offset, z, y, x)
+            if hops(offset) > 0 and not finish:
+                arrived(piece_rows(piece, 2 * chip + core), plane_sem.at[piece, chip], sibling)
+            for direction in onward(order, offset) + ["s"]:
+                copy = tree_send(piece, offset, direction)
+                maybe(direction_exists(direction, z), copy.wait_send if finish else copy.start)
+
+        maybe(offset_exists(offset, z), go)
+
+    events = sorted(
+        ((hops(offset), place, piece, offset) for piece in range(4) for place, offset in enumerate(OFFSETS)),
+        key=lambda event: event[:3],
+    )
+
+    def tree_steps(distance):
+        for hop, _, piece, offset in events:
+            if hop == distance:
+                tree_step(piece, offset)
+
+    def gains_copy(step):
+        other = lax.rem(me + step, 32)
+        return push(
+            gains_ref,
+            gains_all.at[me],
+            gains_send.at[step],
+            gains_recv.at[me],
+            (lax.div(other, 2), lax.rem(other, 2)),
+        )
+
+    def gains_start(step, carry):
+        gains_copy(step).start()
+        return carry
+
+    def gains_wait(step, carry):
+        other = lax.rem(me + step, 32)
+        gains_copy(step).wait_send()
+        arrived(gains_all.at[other], gains_recv.at[other], sibling)
+        return carry
+
+    sends = []
+
+    def start(copy):
+        copy.start()
+        sends.append(copy)
+
+    def weight_rows(number):
+        return gate_up_full.at[:, pl.ds(pl.multiple_of(number * height, height), height), :]
+
+    def down_rows(dzh, dy):
+        number = 2 * flip(zh, dzh) + flip(y, dy)
+        return down_full.at[:, pl.ds(pl.multiple_of(number * down_height, down_height), down_height), :]
+
+    def act_rows(which, step):
+        full = (rows_full, grads_full)[which]
+        return full.at[:, pl.ds(pl.multiple_of(rank(step) * act_height, act_height), act_height), :]
+
+    def send_act(which, step, source, hop):
+        landed = tuple(bit ^ (1 if axis == hop else 0) for axis, bit in enumerate(step))
+        start(
+            push(
+                source,
+                act_rows(which, step),
+                act_send.at[which, 4 * step[0] + 2 * step[1] + step[2], hop],
+                act_recv.at[which, 4 * landed[0] + 2 * landed[1] + landed[2]],
+                member(tuple(1 if axis == hop else 0 for axis in range(3))),
+            )
+        )
+
+    def wait_act(which, step):
+        arrived(
+            act_rows(which, step), act_recv.at[which, 4 * step[0] + 2 * step[1] + step[2]], sibling
+        )
+
+    def act_own(which, source):
+        for hop in (0, 1, 2):
+            send_act(which, own_step, source, hop)
+
+    def act_from_z(which):
+        step = (1, 0, 0)
+        wait_act(which, step)
+        send_act(which, step, act_rows(which, step), 1)
+        send_act(which, step, act_rows(which, step), 2)
+
+    def act_from_x(which):
+        for step in ((0, 1, 0), (1, 1, 0)):
+            wait_act(which, step)
+            send_act(which, step, act_rows(which, step), 2)
+
+    def act_from_core(which):
+        for step in ((0, 0, 1), (1, 0, 1), (0, 1, 1), (1, 1, 1)):
+            wait_act(which, step)
+
+    mine = gate_up_ref.at[rank(own_step)]
+
+    def ff_own():
+        for slot, step in enumerate(RANK_STEPS):
+            if step != own_step:
+                start(
+                    push(
+                        gate_up_ref.at[rank(step)],
+                        weight_rows(device(own_step)),
+                        rank_send.at[slot],
+                        rank_recv.at[slot],
+                        member(step),
+                    )
+                )
+        start(push(mine, weight_rows(device(own_step)), far_send.at[0], far_recv.at[0], far))
+        start(push(down_ref, down_rows(0, 0), far_send.at[8], far_recv.at[8], far))
+        start(push(mine, weight_rows(device(own_step)), across_send.at[0, 0], across_recv.at[0, 0], across))
+        start(push(down_ref, down_rows(0, 0), across_send.at[0, 8], across_recv.at[0, 8], across))
+
+    def ff_from_rank(slots):
+        for slot in slots:
+            step = RANK_STEPS[slot]
+            block = weight_rows(device(step))
+            arrived(block, rank_recv.at[slot], sibling)
+            start(push(block, block, far_send.at[slot], far_recv.at[slot], far))
+            start(push(block, block, across_send.at[0, slot], across_recv.at[0, slot], across))
+
+    def ff_from_far(slots):
+        for slot in slots:
+            block = down_rows(1, 0) if slot == 8 else weight_rows(device(RANK_STEPS[slot], 1, 0))
+            arrived(block, far_recv.at[slot], sibling)
+            start(push(block, block, across_send.at[1, slot], across_recv.at[1, slot], across))
+
+    tree_steps(0)
+    lax.fori_loop(1, 32, gains_start, 0)
+    ff_own()
+    act_own(1, grads_ref)
+    local = [
+        pltpu.make_async_copy(source.at[index], piece_rows(piece, me), local_sem.at[piece])
+        for piece, (source, _, index, _) in enumerate(pieces)
+    ]
+    local.append(pltpu.make_async_copy(gains_ref, gains_all.at[me], local_sem.at[4]))
+    local.append(pltpu.make_async_copy(mine, weight_rows(device(own_step)), local_sem.at[5]))
+    local.append(pltpu.make_async_copy(down_ref, down_rows(0, 0), local_sem.at[6]))
+    local.append(pltpu.make_async_copy(grads_ref, act_rows(1, own_step), local_sem.at[7]))
+    for copy in local:
+        copy.start()
+    make_spread(spread)
+    tree_steps(1)
+    ff_from_rank((1, 2, 3, 4))
+    lax.fori_loop(1, 32, gains_wait, 0)
+    local[4].wait()
+    for block in range(8):
+        total = gains_all[4 * block].astype(F32)
+        for part in range(1, 4):
+            total = total + gains_all[4 * block + part].astype(F32)
+        gain_rows[:, 128 * block : 128 * block + 128] = total
+
+    def first_norm(rows):
+        for p in range(positions):
+            values = tokens_ref[p, rows, :].astype(F32)
+            r, _ = normed(values)
+            attn_in[p, rows, :] = (r * gain_rows[p : p + 1, :]).astype(BF16)
+
+    row_loop(act_height, 16, first_norm)
+    tree_steps(2)
+    ff_from_rank((5, 6, 7))
+    act_from_z(1)
+    tree_steps(3)
+    ff_from_far((0, 8, 1, 2))
+    tree_steps(4)
+    ff_from_far((3, 4, 5))
+    act_from_x(1)
+    tree_steps(5)
+    ff_from_far((6, 7))
+
+    def sibling_wait(chip, carry):
+        for piece in range(4):
+            arrived(piece_rows(piece, 2 * chip + 1 - core), sibling_sem.at[piece, chip], sibling)
+        return carry
+
+    lax.fori_loop(0, 16, sibling_wait, 0)
+    for piece in range(4):
+        local[piece].wait()
+    keep = [
+        pltpu.make_async_copy(qkv_buf, qkv_full, keep_sem.at[0]),
+        pltpu.make_async_copy(out_buf, out_full, keep_sem.at[1]),
+    ]
+    for copy in keep:
+        copy.start()
+
+    for p in range(positions):
+
+        def project(columns, p=p):
+            qkv_rows[p, :, columns] = jnp.dot(
+                attn_in[p], qkv_buf[p, :, columns], preferred_element_type=F32
+            ).astype(BF16)
+
+        tile_loop(3 * model, 512, project)
+    pairs = pairs_of(positions)
+    probs = attention_probs(qkv_rows, halves, spread, model)
+    for index in range(len(pairs)):
+        halves[2 * index] = to_heads(probs[index].astype(BF16), spread)
+
+    def mix(rows):
+        for p in range(positions):
+            total = None
+            for index, (own, q) in enumerate(pairs):
+                if own == p:
+                    term = halves[2 * index, rows, :].astype(F32) * qkv_rows[
+                        q, rows, 2 * model :
+                    ].astype(F32)
+                    total = term if total is None else total + term
+            context[p, rows, :] = total.astype(BF16)
+
+    row_loop(act_height, 16, mix)
+    for p in range(positions):
+
+        def attend(columns, p=p):
+            resid_mid[p, :, columns] = tokens_ref[p, :, columns].astype(F32) + jnp.dot(
+                context[p], out_buf[p, :, columns], preferred_element_type=F32
+            )
+
+        tile_loop(model, 512, attend)
+
+    def second_norm(rows):
+        for p in range(positions):
+            r, _ = normed(resid_mid[p, rows, :])
+            ff_in[p, rows, :] = (r * gain_rows[positions + p : positions + p + 1, :]).astype(BF16)
+
+    row_loop(act_height, 16, second_norm)
+    act_own(0, ff_in)
+    own_rows = pltpu.make_async_copy(ff_in, act_rows(0, own_step), local_sem.at[8])
+    own_rows.start()
+    act_from_z(0)
+    act_from_x(0)
+    act_from_core(1)
+    for dzh in (0, 1):
+        for slot, step in enumerate(RANK_STEPS):
+            arrived(weight_rows(device(step, dzh, 1)), across_recv.at[dzh, slot], sibling)
+        arrived(down_rows(dzh, 1), across_recv.at[dzh, 8], sibling)
+    for _, _, piece, offset in events:
+        tree_step(piece, offset, finish=True)
+    act_from_core(0)
+    for copy in sends:
+        copy.wait_send()
+    for copy in local[5:] + keep + [own_rows]:
+        copy.wait()
+
+
+def forward_gather(gains, tokens, w_qkv, w_out, gate_up_parts, w_down, grads):
+    positions, act_height, model = tokens.shape
+    _, height, qkv_width = w_qkv.shape
+    ranks, _, _, width = gate_up_parts.shape
+    dma = pltpu.SemaphoreType.DMA
+    vmem = pl.BlockSpec(memory_space=pltpu.VMEM)
+    anywhere = pl.BlockSpec(memory_space=pl.ANY)
+    pair_count = len(pairs_of(positions))
+    return pl.pallas_call(
+        forward_kernel,
+        out_shape=(
+            jax.ShapeDtypeStruct((16, model), F32),
+            jax.ShapeDtypeStruct((positions, act_height, 3 * model), BF16),
+            jax.ShapeDtypeStruct((positions, act_height, model), BF16),
+            jax.ShapeDtypeStruct((positions, act_height, model), F32),
+            jax.ShapeDtypeStruct((positions, model, qkv_width), BF16),
+            jax.ShapeDtypeStruct((positions, model, model), BF16),
+            jax.ShapeDtypeStruct((positions, model, width), BF16),
+            jax.ShapeDtypeStruct((positions, 4 * w_down.shape[1], model), BF16),
+            jax.ShapeDtypeStruct((positions, ranks * act_height, model), BF16),
+            jax.ShapeDtypeStruct((positions, ranks * act_height, model), BF16),
+        ),
+        in_specs=[anywhere, vmem] + [anywhere] * 5,
+        out_specs=(vmem,) * 4 + (anywhere,) * 6,
+        scratch_shapes=[
+            pltpu.VMEM((positions, model, qkv_width), BF16),
+            pltpu.VMEM((positions, model, model), BF16),
+            pltpu.VMEM((32, 16, 128), BF16),
+            pltpu.VMEM((positions, act_height, model), BF16),
+            pltpu.VMEM((positions, act_height, model), BF16),
+            pltpu.VMEM((2 * pair_count, act_height, model), BF16),
+            pltpu.VMEM((model, 128), BF16),
+            dma((4, 16)),
+            dma((4, 16)),
+            dma((4, 16, 5)),
+            dma((32,)),
+            dma((32,)),
+            dma((8,)),
+            dma((8,)),
+            dma((9,)),
+            dma((9,)),
+            dma((2, 9)),
+            dma((2, 9)),
+            dma((2, 8, 3)),
+            dma((2, 8)),
+            dma((9,)),
+            dma((2,)),
+        ],
+        compiler_params=pltpu.CompilerParams(
+            collective_id=4, has_side_effects=True, vmem_limit_bytes=56 * 2**20
+        ),
+        name="forward_gather",
+    )(gains, tokens, w_qkv, w_out, gate_up_parts, w_down, grads)
+
+
 def by_set(activations, weight):
     return jnp.einsum("sfk,ske->sfe", activations, weight, preferred_element_type=F32)
 
@@ -1173,15 +1309,6 @@
     ff_units = w_gate_up.shape[2] // 2
     score_scale = 1.0 / math.sqrt(HEAD_DIM)
     own_gain = norm_attn.shape[1]
-    gains = jnp.zeros((16, 128), BF16)
-    gains = gains.at[0:positions, :own_gain].set(norm_attn)
-    gains = gains.at[positions : 2 * positions, :own_gain].set(norm_ff)
-    gains_full, qkv_full, out_full = gather_attn(gains, w_qkv, w_out)
-    gains_rows = jnp.swapaxes(gains_full[:, : 2 * positions, :own_gain], 0, 1)
-    gains_rows = gains_rows.reshape(2 * positions, model).astype(F32)
-    gain_one = gains_rows[:positions, None, :]
-    gain_two = gains_rows[positions:, None, :]
-
     spread = (
         jnp.arange(model)[:, None] // HEAD_DIM == jnp.arange(128)[None, :]
     ).astype(BF16)
@@ -1200,35 +1327,44 @@
     grad_out = jnp.swapaxes(cotangent, 0, 1).astype(F32) * frame_weight[None, :, None]
     grad_low = grad_out.astype(BF16)
 
-    resid_in = jnp.swapaxes(tokens, 0, 1).astype(F32)
-    normed_one, inverse_one = normed(resid_in)
+    unit_gains = jnp.concatenate([norm_attn, norm_ff], axis=0)
+    lanes = jnp.arange(128, dtype=jnp.int32) // own_gain
+    gains = jnp.where(lanes == lax.rem(device_index, 128 // own_gain), jnp.tile(unit_gains, (1, 128 // own_gain)), 0)
+    gains = jnp.pad(gains, ((0, 16 - 2 * positions), (0, 0)))
+
+    unit = w_down.shape[1]
+    parts = w_gate_up.reshape(positions, -1, 2, 2, 2, 2, 2, 2, unit)
+    parts = parts.transpose(4, 6, 7, 0, 1, 2, 3, 5, 8)
+    parts = parts.reshape(8, positions, w_gate_up.shape[1], 8 * unit)
+    tokens_low = jnp.swapaxes(tokens, 0, 1)
+    (
+        gains_rows,
+        qkv,
+        context,
+        resid_mid,
+        qkv_full,
+        out_full,
+        gate_up_full,
+        down_full,
+        ff_rows,
+        grad_rows,
+    ) = forward_gather(gains, tokens_low, w_qkv, w_out, parts, w_down, grad_low)
+    gain_one = gains_rows[:positions, None, :]
+    gain_two = gains_rows[positions : 2 * positions, None, :]
+    normed_one, inverse_one = normed(tokens_low.astype(F32))
     attn_in = (normed_one * gain_one).astype(BF16)
-    qkv = by_set(attn_in, qkv_full).astype(BF16)
+    normed_two, inverse_two = normed(resid_mid)
     queries = [qkv[p, :, :model].astype(F32) for p in range(positions)]
     keys = [qkv[p, :, model : 2 * model].astype(F32) for p in range(positions)]
     values = [qkv[p, :, 2 * model :].astype(F32) for p in range(positions)]
     probs = []
-    contexts = []
     for p in range(positions):
         scores = [head_sums(queries[p] * keys[q], spread) * score_scale for q in range(p + 1)]
         top = functools.reduce(jnp.maximum, scores)
         powers = [jnp.exp(score - top) for score in scores]
         total = functools.reduce(jnp.add, powers)
         probs.append([power / total for power in powers])
-        context = sum(
-            over_heads(prob.astype(BF16), spread) * values[q] for q, prob in enumerate(probs[p])
-        )
-        contexts.append(context.astype(BF16))
-    context = jnp.stack(contexts)
-    resid_mid = resid_in + by_set(context, out_full)
-    normed_two, inverse_two = normed(resid_mid)
-    ff_in = (normed_two * gain_two).astype(BF16)
-
-    unit = w_down.shape[1]
-    parts = w_gate_up.reshape(positions, -1, 2, 2, 2, 2, 2, 2, unit)
-    parts = parts.transpose(4, 6, 7, 0, 1, 2, 3, 5, 8)
-    parts = parts.reshape(8, positions, w_gate_up.shape[1], 8 * unit)
-    gate_up_full, down_full, ff_rows, grad_rows = gather_ff(parts, w_down, ff_in, grad_low)
+
     split = 4 * unit
     gate_up = by_set(ff_rows, gate_up_full)
     gate, up = gate_up[..., :split], gate_up[..., split:]

time: 512 us -> 484 us (0.945)
  matrix products: 87.3 us -> 72.6 us
  local copies, waits for them, and re-layouts: 29.7 us -> 24.5 us
    dot_general x4 -> x2, matrix products: 25.1 us -> 12.1 us  [by_set(): jnp.einsum('sfk,ske->sfe', activations, weight, preferred_element_type=F32)]
    pallas_call x2 -> x1, Pallas kernels: 182 us -> 176 us  [forward_gather(): pl.pallas_call(forward_kernel, out_shape=(jax.ShapeDtypeStruct((16, model...]
where the time goes in v2:
time: 484 us; the launch traced here: 480 us
  Pallas kernels  370 us (76%)
  matrix products  72.6 us (15%)
  local copies, waits for them, and re-layouts  24.5 us (5%)
  other arithmetic  11.1 us (2%)
    pallas_call x1, Pallas kernels, forward_gather(): pl.pallas_call(forward_kernel, out_shape=(jax.ShapeDtypeStruct((16, model...  176 us
    pallas_call x1, Pallas kernels, scatter_ff(): pl.pallas_call(scatter_ff_kernel, out_shape=(jax.ShapeDtypeStruct((sets,...  117 us
    pallas_call x1, Pallas kernels, scatter_attn(): pl.pallas_call(scatter_attn_kernel, out_shape=(jax.ShapeDtypeStruct(gain_...  76.6 us
    dot_general x4, matrix products, by_set_back(): jnp.einsum('sfe,ske->sfk', gradients, weight, preferred_element_type=F32)  24.7 us
    dot_general x4, matrix products, set_grad(): jnp.einsum('sfk,sfe->ske', activations, gradients, preferred_element_type...  22.7 us
    dot_general x2, matrix products, by_set(): jnp.einsum('sfk,ske->sfe', activations, weight, preferred_element_type=F32)  12.1 us

profile of v2, /device:TPU:0, one launch (start us, length us, event | category | flops | bytes accessed | tf_op | source)
XLA Modules:
  0.0 479.9 jit_solution(9820496126747146818)
XLA Ops:
  5.0 2.0 bitcast_convert_fusion.grads_ref
  7.0 1.8 reshape.182
  9.7 1.5 reshape.183.gate_up_ref
  12.2 176.3 %forward_gather.1 = (f32[16,1024]{1,0:T(8,128)}, bf16[2,128,3072]{2,1,0:T(8,128)(2,1)}, bf16[2,128,1024]{2,1,0:T(8,128)(2,1)}, f32[2,128,1024]{2,1,0:T(8,128)}, ...) custom-call(bf16[16,128]{1,0:T(8,128)(2,1)} %pad.9.gains_ref, ...), custom_call_target="tpu_custom_call" | custom-call | tf_op jit(solution)/shard_map/forward_gather/pallas_call | solution.py:1223
  188.5 7.8 %fusion.134 = f32[2,1024,1024]{1,2,0:T(8,128)S(1)} fusion(bf16[2,1024,1024]{2,1,0:T(8,128)(2,1)} %get-tuple-element.38, bf16[2,1024,1024]{2,1,0:T(8,128)(2,1)} %get-tuple-element.39), kind=kOutput, calls=%fused_computation.206 | convolution fusion | flops 4294967296 | bytes 16777216 | tf_op jit(solution)/shard_map/sfk,ske->sfe/dot_general | solution.py:1271
  196.3 5.4 %multiply_convert_fusion.1 = (bf16[2,1024,512]{1,2,0:T(8,128)(2,1)}, bf16[2,1024,512]{1,2,0:T(8,128)(2,1)}, bf16[2,1024,512]{1,2,0:T(8,128)(2,1)S(1)}) fusion(f32[2,1024,1024]{1,2,0:T(8,128)S(1)} %fusion.134, bf16[2,1024,1024]{2,1,0:T(8,128)(2,1)S(1)} %copy-done.12, bf16[2,512,1024]{2,1,0:T(8,128)(2,1)S(1)} %copy-done.13), kind=kOutput, calls=%fused_computation.3 | convolution fusion | flops 2163212288 | bytes 20971520 | tf_op jit(solution)/shard_map/sfe,ske->sfk/dot_general | solution.py:1275
  201.8 3.7 convolution_convert_fusion.3.down_ref
  205.4 9.4 %fusion.4.gate_up_ref = bf16[2,1024,1024]{2,1,0:T(8,128)(2,1)} fusion(bf16[2,1024,1024]{2,1,0:T(8,128)(2,1)S(1)} %copy-done.11, bf16[2,1024,512]{1,2,0:T(8,128)(2,1)} %get-tuple-element.83, bf16[2,1024,512]{1,2,0:T(8,128)(2,1)} %get-tuple-element.82), kind=kOutput, calls=%fused_computation.10 | convolution fusion | flops 4305453056 | bytes 12582912 | tf_op jit(solution)/shard_map/sfk,sfe->ske/dot_general | solution.py:1279
  214.8 9.9 %fusion.3.back_ref = bf16[2,1024,1024]{2,1,0:T(8,128)(2,1)} fusion(bf16[2,1024,1024]{2,1,0:T(8,128)(2,1)S(1)} %copy-done.10, bf16[2,1024,512]{1,2,0:T(8,128)(2,1)} %get-tuple-element.83, bf16[2,1024,512]{1,2,0:T(8,128)(2,1)} %get-tuple-element.82), kind=kOutput, calls=%fused_computation.9 | convolution fusion | flops 4305453056 | bytes 12582912 | tf_op jit(solution)/shard_map/sfe,ske->sfk/dot_general | solution.py:1275
  224.7 4.4 convolution_convert_fusion.2.out_ref
  229.1 116.9 %scatter_ff.1 = (f32[2,128,1024]{2,1,0:T(8,128)}, f32[2,128,1024]{2,1,0:T(8,128)}, f32[8,2,32,1024]{3,2,1,0:T(8,128)}, f32[2,128,1024]{2,1,0:T(8,128)}) custom-call(bf16[2,1024,1024]{2,1,0:T(8,128)(2,1)} %convolution_convert_fusion.2.out_ref, bf16[2,1024,1024]{2,1,0:T(8,128)(2,1)} %fusion.3.back_ref, bf16[2,1024,1024]{2,1,0:T(8,128)(2,1)} %fusion.4.gate_up_ref, ...), custom_call_target="tpu_custom_call" | custom-call | tf_op jit(solution)/shard_map/scatter_ff/pallas_call | solution.py:587
  347.0 2.2 multiply_reduce_fusion
  349.2 2.0 bitcast_add_fusion
  351.2 3.2 convolution_convert_fusion.1.out_ref
  355.9 1.5 fusion.9
  357.9 1.0 fusion.48
  360.3 1.2 fusion.41
  361.5 1.2 fusion.42
  363.1 1.0 fusion.18
  364.1 3.4 fusion.35
  367.8 1.2 fusion.11
  369.1 1.3 maximum_bitcast_fusion
  370.6 6.4 %convolution_convert_fusion.qkv_ref = bf16[2,1024,3072]{2,1,0:T(8,128)(2,1)} fusion(bf16[1,128,3072]{2,1,0:T(8,128)(2,1)S(1)} %get-tuple-element.97, bf16[1,128,3072]{2,1,0:T(8,128)(2,1)S(1)} %get-tuple-element.96, f32[2,1024]{1,0:T(2,128)S(1)} %get-tuple-element.91, f32[2,128]{1,0:T(2,128)S(1)} %add_rsqrt_fusion, bf16[128,2,1024]{2,1,0:T(2,128)(2,1)S(1)} %copy-done.1), kind=kOutput, calls=%fused_computation | convolution fusion | flops 1618739200 | bytes 14689280 | tf_op jit(solution)/shard_map/sfk,sfe->ske/dot_general | solution.py:1279
  377.0 7.9 %fusion.24 = (f32[2,1024]{1,0:T(2,128)S(1)}, f32[2,128]{1,0:T(2,128)S(1)}, f32[2,128,1024]{2,1,0:T(8,128)S(1)}) fusion(f32[2,128]{1,0:T(2,128)S(1)} %add_rsqrt_fusion, bf16[128,2,1024]{2,1,0:T(2,128)(2,1)S(1)} %copy-done.1, f32[2,1024]{1,0:T(2,128)S(1)} %get-tuple-element.91, bf16[2,1024,3072]{2,1,0:T(8,128)(2,1)} %get-tuple-element.47, ...), kind=kOutput, calls=%fused_computation.46 | convolution fusion | flops 1613231872 | bytes 15747072 | tf_op jit(solution)/shard_map/sfe,ske->sfk/dot_general | solution.py:1275
  385.8 76.6 %scatter_attn.1 = (f32[8,128]{1,0:T(8,128)}, f32[2,32,3072]{2,1,0:T(8,128)}, f32[2,32,1024]{2,1,0:T(8,128)}) custom-call(f32[32,8,128]{2,1,0:T(8,128)} %scatter.4.gains_ref, bf16[2,1024,3072]{2,1,0:T(8,128)(2,1)} %convolution_convert_fusion.qkv_ref, bf16[2,1024,1024]{2,1,0:T(8,128)(2,1)} %convolution_convert_fusion.1.out_ref), custom_call_target="tpu_custom_call" | custom-call | tf_op jit(solution)/shard_map/scatter_attn/pallas_call | solution.py:797
  462.3 1.3 fusion.133
  464.0 1.8 copy.58
  465.8 3.0 reshape.187
  468.8 2.9 copy.56
  471.8 4.0 reshape.188
  475.8 1.3 copy.57
  478.7 1.0 copy.91
  (74 shorter events, 13.5 us)
Async XLA Ops:
  0.6 10.6 %copy-start.1 = (bf16[128,2,1024]{2,1,0:T(2,128)(2,1)S(1)}, bf16[128,2,1024]{2,1,0:T(2,128)(2,1)}, u32[]{:S(2)}) copy-start(bf16[128,2,1024]{2,1,0:T(2,128)(2,1)} %param.12) | copy-start | bytes 1572868
  188.5 7.8 %copy-start.12 = (bf16[2,1024,1024]{2,1,0:T(8,128)(2,1)S(1)}, bf16[2,1024,1024]{2,1,0:T(8,128)(2,1)}, u32[]{:S(2)}) copy-start(bf16[2,1024,1024]{2,1,0:T(8,128)(2,1)} %get-tuple-element.41) | copy-start | bytes 12582916
  188.5 7.8 %copy-start.13 = (bf16[2,512,1024]{2,1,0:T(8,128)(2,1)S(1)}, bf16[2,512,1024]{2,1,0:T(8,128)(2,1)}, u32[]{:S(2)}) copy-start(bf16[2,512,1024]{2,1,0:T(8,128)(2,1)} %get-tuple-element.40) | copy-start | bytes 6291460
  201.8 3.7 copy-start.15
  201.8 3.7 copy-start.11
  205.4 9.4 %copy-start.10 = (bf16[2,1024,1024]{2,1,0:T(8,128)(2,1)S(1)}, bf16[2,1024,1024]{2,1,0:T(8,128)(2,1)}, u32[]{:S(2)}) copy-start(bf16[2,1024,1024]{2,1,0:T(8,128)(2,1)} %get-tuple-element.39) | copy-start | bytes 12582916
  214.8 9.9 %copy-start.14 = (bf16[2,512,1024]{2,1,0:T(8,128)(2,1)S(1)}, bf16[2,512,1024]{2,1,0:T(8,128)(2,1)}, u32[]{:S(2)}) copy-start(bf16[2,512,1024]{2,1,0:T(8,128)(2,1)} %get-tuple-element.40) | copy-start | bytes 6291460
  214.8 9.9 %copy-start.16 = (bf16[2,1024,512]{1,2,0:T(8,128)(2,1)S(1)}, bf16[2,1024,512]{1,2,0:T(8,128)(2,1)}, u32[]{:S(2)}) copy-start(bf16[2,1024,512]{1,2,0:T(8,128)(2,1)} %copy-done.15) | copy-start | bytes 6291460
  229.1 116.9 %copy-start = (f32[2,128,1024]{2,1,0:T(8,128)S(1)}, f32[2,128,1024]{2,1,0:T(8,128)}, u32[]{:S(2)}) copy-start(f32[2,128,1024]{2,1,0:T(8,128)} %get-tuple-element.37) | copy-start | bytes 3145732
  229.1 120.1 %copy-start.3 = (bf16[128,2,1024]{2,1,0:T(2,128)(2,1)S(1)}, bf16[128,2,1024]{2,1,0:T(2,128)(2,1)}, u32[]{:S(2)}) copy-start(bf16[128,2,1024]{2,1,0:T(2,128)(2,1)} %param.19) | copy-start | bytes 1572868
  346.0 5.2 %copy-start.6 = (bf16[2,128,1024]{2,1,0:T(8,128)(2,1)S(1)}, bf16[2,128,1024]{2,1,0:T(8,128)(2,1)}, u32[]{:S(2)}) copy-start(bf16[2,128,1024]{2,1,0:T(8,128)(2,1)} %get-tuple-element.48) | copy-start | bytes 1572868
  351.2 3.3 copy-start.7
  351.2 4.7 copy-start.2
  377.0 7.9 %copy-start.9 = (f32[2,1024]{1,0:T(2,128)S(1)}, f32[2,1024]{1,0:T(2,128)}, u32[]{:S(2)}) copy-start(f32[2,1024]{1,0:T(2,128)} %get-tuple-element.78) | copy-start | bytes 24580
  471.8 5.4 %copy-start.5 = (f32[2,32,3072]{2,1,0:T(8,128)S(1)}, f32[2,32,3072]{2,1,0:T(8,128)}, u32[]{:S(2)}) copy-start(f32[2,32,3072]{2,1,0:T(8,128)} %get-tuple-element.109) | copy-start | bytes 2359300
  471.8 6.3 %copy-start.8 = (f32[2,32,1024]{2,1,0:T(8,128)S(1)}, f32[2,32,1024]{2,1,0:T(8,128)}, u32[]{:S(2)}) copy-start(f32[2,32,1024]{2,1,0:T(8,128)} %get-tuple-element.110) | copy-start | bytes 786436
  471.8 7.0 %copy-start.4 = (f32[2,128,1024]{2,1,0:T(8,128)S(1)}, f32[2,128,1024]{2,1,0:T(8,128)}, u32[]{:S(2)}) copy-start(f32[2,128,1024]{2,1,0:T(8,128)} %get-tuple-element.113) | copy-start | bytes 3145732

commit v3 on v2

--- a/solution.py
+++ b/solution.py
@@ -389,440 +389,6 @@
         return carry
 
     lax.fori_loop(0, (height // rows) * across, one, 0)
-
-
-def scatter_ff_kernel(
-    out_ref,
-    back_ref,
-    gate_up_ref,
-    down_ref,
-    out_sum,
-    back_sum,
-    gate_up_sum,
-    down_sum,
-    core_buf,
-    x_buf,
-    z_buf,
-    across_gate,
-    across_down,
-    far_gate,
-    far_down,
-    rank_buf,
-    core_send,
-    core_recv,
-    x_send,
-    x_recv,
-    z_send,
-    z_recv,
-    across_send,
-    across_recv,
-    far_send,
-    far_recv,
-    rank_send,
-    rank_recv,
-):
-    z, y, x, core = here()
-    zh, zl, member, rank, device, far, across = group_place(z, y, x, core)
-    own_step = (0, 0, 0)
-    others = RANK_STEPS[1:]
-    greet([member(step) for step in others] + [far, across])
-    sets = out_ref.shape[0]
-    act_height = out_sum.shape[1]
-    height = gate_up_sum.shape[2]
-    down_height = down_sum.shape[1]
-    sends = []
-
-    def start(copy):
-        copy.start()
-        sends.append(copy)
-
-    def run_rows(dzh, dy, low):
-        number = 16 * flip(zh, dzh) + 4 * flip(y, dy) + 8 * low
-        return pl.ds(pl.multiple_of(number * height, 4 * height), 4 * height)
-
-    def down_rows(dzh, dy):
-        number = 2 * flip(zh, dzh) + flip(y, dy)
-        return pl.ds(pl.multiple_of(number * down_height, down_height), down_height)
-
-    def act_rows(step):
-        return pl.ds(pl.multiple_of(rank(step) * act_height, act_height), act_height)
-
-    for turn, dzh in enumerate((1, 0)):
-        for s in range(sets):
-            for low in (0, 1):
-                start(
-                    push(
-                        gate_up_ref.at[s, run_rows(dzh, 1, low)],
-                        across_gate.at[turn, s, low],
-                        across_send.at[turn, s, low],
-                        across_recv.at[turn, s, low],
-                        across,
-                    )
-                )
-            start(
-                push(
-                    down_ref.at[s, down_rows(dzh, 1)],
-                    across_down.at[turn, s],
-                    across_send.at[turn, s, 2],
-                    across_recv.at[turn, s, 2],
-                    across,
-                )
-            )
-    acts = [back_ref, out_ref]
-    act_sums = [back_sum, out_sum]
-    sibling = member((0, 0, 1))
-    plan = [(1, 1), (0, 1), (1, 0), (0, 0)]
-    for which in (0, 1):
-        for dl, dx in plan:
-            start(
-                push(
-                    acts[which].at[:, act_rows((dl, dx, 1))],
-                    core_buf.at[which, dl, dx],
-                    core_send.at[which, dl, dx],
-                    core_recv.at[which, dl, dx],
-                    sibling,
-                )
-            )
-
-    def core_add(which, dl, dx):
-        block = core_buf.at[which, dl, dx]
-        arrived(block, core_recv.at[which, dl, dx], sibling)
-        for s in range(sets):
-            add_into(block.at[s], [block.at[s], acts[which].at[s, act_rows((dl, dx, 0))]])
-
-    for which in (0, 1):
-        for dl in (1, 0):
-            core_add(which, dl, 1)
-            start(
-                push(
-                    core_buf.at[which, dl, 1],
-                    x_buf.at[which, dl],
-                    x_send.at[which, dl],
-                    x_recv.at[which, dl],
-                    member((0, 1, 0)),
-                )
-            )
-    for s in range(sets):
-        for low in (0, 1):
-            block = across_gate.at[0, s, low]
-            arrived(block, across_recv.at[0, s, low], across)
-            add_into(block, [block, gate_up_ref.at[s, run_rows(1, 0, low)]])
-            start(push(block, far_gate.at[s, low], far_send.at[s, low], far_recv.at[s, low], far))
-        block = across_down.at[0, s]
-        arrived(block, across_recv.at[0, s, 2], across)
-        add_into(block, [block, down_ref.at[s, down_rows(1, 0)]])
-        start(push(block, far_down.at[s], far_send.at[s, 2], far_recv.at[s, 2], far))
-    for which in (0, 1):
-        core_add(which, 1, 0)
-        arrived(x_buf.at[which, 1], x_recv.at[which, 1], member((0, 1, 0)))
-        for s in range(sets):
-            block = x_buf.at[which, 1, s]
-            add_into(block, [block, core_buf.at[which, 1, 0, s]])
-        start(
-            push(
-                x_buf.at[which, 1],
-                z_buf.at[which],
-                z_send.at[which],
-                z_recv.at[which],
-                member((1, 0, 0)),
-            )
-        )
-    for which in (0, 1):
-        core_add(which, 0, 0)
-        arrived(x_buf.at[which, 0], x_recv.at[which, 0], member((0, 1, 0)))
-        arrived(z_buf.at[which], z_recv.at[which], member((1, 0, 0)))
-        for s in range(sets):
-            add_into(
-                act_sums[which].at[s],
-                [core_buf.at[which, 0, 0, s], x_buf.at[which, 0, s], z_buf.at[which, s]],
-            )
-    for s in range(sets):
-        for low in (0, 1):
-            block = across_gate.at[1, s, low]
-            arrived(block, across_recv.at[1, s, low], across)
-            arrived(far_gate.at[s, low], far_recv.at[s, low], far)
-            add_into(block, [block, far_gate.at[s, low], gate_up_ref.at[s, run_rows(0, 0, low)]])
-        arrived(across_down.at[1, s], across_recv.at[1, s, 2], across)
-        arrived(far_down.at[s], far_recv.at[s, 2], far)
-        add_into(
-            down_sum.at[s],
-            [across_down.at[1, s], far_down.at[s], down_ref.at[s, down_rows(0, 0)]],
-        )
-
-    def share(step, s):
-        number = 2 * flip(x, step[1]) + flip(core, step[2])
-        return across_gate.at[1, s, flip(zl, step[0]), pl.ds(pl.multiple_of(number * height, height), height)]
-
-    for slot, step in enumerate(RANK_STEPS):
-        if step != own_step:
-            for s in range(sets):
-                start(
-                    push(
-                        share(step, s),
-                        rank_buf.at[slot, s],
-                        rank_send.at[slot, s],
-                        rank_recv.at[slot, s],
-                        member(step),
-                    )
-                )
-    for slot, step in enumerate(RANK_STEPS):
-        for s in range(sets):
-            if step == own_step:
-                add_into(gate_up_sum.at[rank(step), s], [share(step, s)])
-            else:
-                arrived(rank_buf.at[slot, s], rank_recv.at[slot, s], member(step))
-                add_into(gate_up_sum.at[rank(step), s], [rank_buf.at[slot, s]])
-    for copy in sends:
-        copy.wait_send()
-
-
-def scatter_ff(out_part, back_part, gate_up_grad, down_grad):
-    sets, rows, model = out_part.shape
-    width = gate_up_grad.shape[2]
-    act_height = rows // 8
-    height = gate_up_grad.shape[1] // 32
-    down_height = down_grad.shape[1] // 4
-    dma = pltpu.SemaphoreType.DMA
-    vmem = pl.BlockSpec(memory_space=pltpu.VMEM)
-    return pl.pallas_call(
-        scatter_ff_kernel,
-        out_shape=(
-            jax.ShapeDtypeStruct((sets, act_height, model), F32),
-            jax.ShapeDtypeStruct((sets, act_height, model), F32),
-            jax.ShapeDtypeStruct((8, sets, height, width), F32),
-            jax.ShapeDtypeStruct((sets, down_height, model), F32),
-        ),
-        in_specs=[vmem] * 4,
-        out_specs=(vmem,) * 4,
-        scratch_shapes=[
-            pltpu.VMEM((2, 2, 2, sets, act_height, model), BF16),
-            pltpu.VMEM((2, 2, sets, act_height, model), BF16),
-            pltpu.VMEM((2, sets, act_height, model), BF16),
-            pltpu.VMEM((2, sets, 2, 4 * height, width), BF16),
-            pltpu.VMEM((2, sets, down_height, model), BF16),
-            pltpu.VMEM((sets, 2, 4 * height, width), BF16),
-            pltpu.VMEM((sets, down_height, model), BF16),
-            pltpu.VMEM((8, sets, height, width), BF16),
-            dma((2, 2, 2)),
-            dma((2, 2, 2)),
-            dma((2, 2)),
-            dma((2, 2)),
-            dma((2,)),
-            dma((2,)),
-            dma((2, sets, 3)),
-            dma((2, sets, 3)),
-            dma((sets, 3)),
-            dma((sets, 3)),
-            dma((8, sets)),
-            dma((8, sets)),
-        ],
-        compiler_params=pltpu.CompilerParams(
-            collective_id=2, has_side_effects=True, vmem_limit_bytes=60 * 2**20
-        ),
-        name="scatter_ff",
-    )(out_part, back_part, gate_up_grad, down_grad)
-
-
-def slot_index(order, direction, offset, z, y, x):
-    axis = {"u": "z", "d": "z"}.get(direction, direction)
-    index, count = 0, 1
-    values = dict(z=z + offset[0], y=flip(y, offset[1]), x=flip(x, offset[2]))
-    sizes = dict(z=4, y=2, x=2)
-    for earlier in order[: order.index(axis)]:
-        index = index * sizes[earlier] + values[earlier]
-        count *= sizes[earlier]
-    if axis == "z":
-        index = index * 4 + values["z"]
-        count *= 4
-    return index, count
-
-
-def slot_base(order):
-    base, total = {}, 0
-    for direction in ("x", "y", "u", "d"):
-        base[direction] = total
-        total += slot_index(order, direction, (0, 0, 0), 0, 0, 0)[1]
-    return base, total
-
-
-def scatter_attn_kernel(
-    gains_ref,
-    qkv_ref,
-    out_ref,
-    gains_sum,
-    qkv_sum,
-    out_sum,
-    core_qkv,
-    core_out,
-    slots_0,
-    slots_1,
-    slots_2,
-    slots_3,
-    gains_buf,
-    core_send,
-    core_recv,
-    tree_send,
-    tree_recv,
-    gains_send,
-    gains_recv,
-):
-    z, y, x, core = here()
-    me = 2 * (z * 4 + y * 2 + x) + core
-    greet_all(z, y, x, core)
-    height = qkv_sum.shape[1]
-    pieces = [
-        (qkv_ref, qkv_sum, core_qkv, 0, "zxy", slots_0),
-        (qkv_ref, qkv_sum, core_qkv, 1, "zyx", slots_1),
-        (out_ref, out_sum, core_out, 0, "xyz", slots_2),
-        (out_ref, out_sum, core_out, 1, "yxz", slots_3),
-    ]
-    sibling = neighbour("s", z, y, x, core)
-    events = sorted(
-        ((-hops(offset), rank, piece, offset) for piece in range(4) for rank, offset in enumerate(OFFSETS)),
-        key=lambda event: event[:3],
-    )
-
-    def own_rows(piece, chip, of_core):
-        source, _, _, index, _, _ = pieces[piece]
-        return source.at[index, pl.ds(pl.multiple_of((2 * chip + of_core) * height, height), height), :]
-
-    def core_copy(piece, offset):
-        chip = chip_of(offset, z, y, x)
-        _, _, buf, index, _, _ = pieces[piece]
-        return push(
-            own_rows(piece, chip, 1 - core),
-            buf.at[index, chip],
-            core_send.at[piece, chip],
-            core_recv.at[piece, chip],
-            sibling,
-        )
-
-    def tree_copy(piece, offset):
-        _, _, buf, index, order, slots = pieces[piece]
-        chip = chip_of(offset, z, y, x)
-        toward = came_from(order, offset)
-        seen = {"x": "x", "y": "y", "u": "d", "d": "u"}[toward]
-        base, _ = slot_base(order)
-        index_there, _ = slot_index(order, seen, offset, z, y, x)
-        place = base[seen] + index_there
-        return push(
-            buf.at[index, chip],
-            slots.at[place],
-            tree_send.at[piece, chip],
-            tree_recv.at[piece, place],
-            neighbour(toward, z, y, x, core),
-        )
-
-    def gains_copy(step):
-        other = lax.rem(me + step, 32)
-        return push(
-            gains_ref.at[other],
-            gains_buf.at[me],
-            gains_send.at[step],
-            gains_recv.at[me],
-            (lax.div(other, 2), lax.rem(other, 2)),
-        )
-
-    for _, _, piece, offset in events:
-        maybe(offset_exists(offset, z), core_copy(piece, offset).start)
-
-    def gains_start(step, carry):
-        gains_copy(step).start()
-        return carry
-
-    lax.fori_loop(1, 32, gains_start, 0)
-
-    def handle(piece, offset):
-        _, result, buf, index, order, slots = pieces[piece]
-        base, _ = slot_base(order)
-
-        def go():
-            chip = chip_of(offset, z, y, x)
-            block = buf.at[index, chip]
-            arrived(block, core_recv.at[piece, chip], sibling)
-            sure, unsure = [], []
-            for direction in onward(order, offset):
-                local, _ = slot_index(order, direction, offset, z, y, x)
-                place = base[direction] + local
-                (sure if direction in "xy" else unsure).append((direction, place))
-            terms = [block, own_rows(piece, chip, core)]
-            for direction, place in sure:
-                arrived(slots.at[place], tree_recv.at[piece, place], sibling)
-                terms.append(slots.at[place])
-            last = hops(offset) == 0
-            target = result.at[index] if last else block
-            add_into(target, terms)
-            for direction, place in unsure:
-
-                def more(place=place):
-                    arrived(slots.at[place], tree_recv.at[piece, place], sibling)
-                    add_into(target, [target, slots.at[place]])
-
-                maybe(direction_exists(direction, z), more)
-            if not last:
-                tree_copy(piece, offset).start()
-
-        maybe(offset_exists(offset, z), go)
-
-    for _, _, piece, offset in events:
-        handle(piece, offset)
-
-    gains_sum[...] = gains_ref[me]
-
-    def gains_wait(step, carry):
-        other = lax.rem(me + step, 32)
-        gains_copy(step).wait_send()
-        arrived(gains_buf.at[other], gains_recv.at[other], sibling)
-        gains_sum[...] += gains_buf[other]
-        return carry
-
-    lax.fori_loop(1, 32, gains_wait, 0)
-    for _, _, piece, offset in events:
-
-        def finish(piece=piece, offset=offset):
-            core_copy(piece, offset).wait_send()
-            if hops(offset) > 0:
-                tree_copy(piece, offset).wait_send()
-
-        maybe(offset_exists(offset, z), finish)
-
-
-def scatter_attn(gain_parts, qkv_grad, out_grad):
-    sets, rows, qkv_width = qkv_grad.shape
-    out_width = out_grad.shape[2]
-    height = rows // 32
-    dma = pltpu.SemaphoreType.DMA
-    vmem = pl.BlockSpec(memory_space=pltpu.VMEM)
-    places = [slot_base(order)[1] for order in ORDERS]
-    return pl.pallas_call(
-        scatter_attn_kernel,
-        out_shape=(
-            jax.ShapeDtypeStruct(gain_parts.shape[1:], F32),
-            jax.ShapeDtypeStruct((sets, height, qkv_width), F32),
-            jax.ShapeDtypeStruct((sets, height, out_width), F32),
-        ),
-        in_specs=[vmem] * 3,
-        out_specs=(vmem,) * 3,
-        scratch_shapes=[
-            pltpu.VMEM((sets, 16, height, qkv_width), BF16),
-            pltpu.VMEM((sets, 16, height, out_width), BF16),
-            pltpu.VMEM((places[0], height, qkv_width), BF16),
-            pltpu.VMEM((places[1], height, qkv_width), BF16),
-            pltpu.VMEM((places[2], height, out_width), BF16),
-            pltpu.VMEM((places[3], height, out_width), BF16),
-            pltpu.VMEM((32,) + gain_parts.shape[1:], F32),
-            dma((4, 16)),
-            dma((4, 16)),
-            dma((4, 16)),
-            dma((4, max(places))),
-            dma((32,)),
-            dma((32,)),
-        ],
-        compiler_params=pltpu.CompilerParams(
-            collective_id=3, has_side_effects=True, vmem_limit_bytes=60 * 2**20
-        ),
-        name="scatter_attn",
-    )(gain_parts, qkv_grad, out_grad)
 
 
 def row_loop(height, chunk, body):
@@ -1267,6 +833,752 @@
     )(gains, tokens, w_qkv, w_out, gate_up_parts, w_down, grads)
 
 
+def slot_index(order, direction, offset, z, y, x):
+    axis = {"u": "z", "d": "z"}.get(direction, direction)
+    index, count = 0, 1
+    values = dict(z=z + offset[0], y=flip(y, offset[1]), x=flip(x, offset[2]))
+    sizes = dict(z=4, y=2, x=2)
+    for earlier in order[: order.index(axis)]:
+        index = index * sizes[earlier] + values[earlier]
+        count *= sizes[earlier]
+    if axis == "z":
+        index = index * 5 + (4 if direction == "d" and offset[0] == 0 else values["z"])
+        count *= 5
+    return index, count
+
+
+def slot_base(order):
+    base, total = {}, 0
+    for axis, direction in (("x", "x"), ("y", "y"), ("z", "u")):
+        base[axis] = total
+        total += slot_index(order, direction, (0, 0, 0), 0, 0, 0)[1]
+    base["u"] = base["d"] = base["z"]
+    return base, total
+
+
+def backward_kernel(
+    tokens_ref,
+    cot_ref,
+    gain_rows,
+    qkv_rows,
+    context,
+    resid_mid,
+    qkv_full,
+    out_full,
+    out_ref,
+    back_ref,
+    gate_up_ref,
+    down_ref,
+    output,
+    grad_tokens,
+    gains_sum,
+    qkv_sum,
+    attn_out_sum,
+    gate_up_sum,
+    down_sum,
+    act_own,
+    core_buf,
+    x_buf,
+    z_buf,
+    gate_own,
+    down_own,
+    across_gate,
+    across_down,
+    far_gate,
+    far_down,
+    qkv_grad,
+    out_grad,
+    slots_0,
+    slots_1,
+    slots_2,
+    slots_3,
+    qkv_tiles,
+    out_tiles,
+    turned,
+    attn_turned,
+    context_turned,
+    d_qkv,
+    d_mid_low,
+    d_mid,
+    d_context,
+    d_rows,
+    halves,
+    probs_buf,
+    spread,
+    gain_acc,
+    gains_part,
+    gains_buf,
+    core_send,
+    core_recv,
+    x_send,
+    x_recv,
+    z_send,
+    z_recv,
+    across_send,
+    across_recv,
+    far_send,
+    far_recv,
+    rank_send,
+    rank_recv,
+    swap_send,
+    swap_recv,
+    tree_send,
+    tree_recv,
+    gains_send,
+    gains_recv,
+    own_sem,
+    part_sem,
+    tile_sem,
+):
+    z, y, x, core = here()
+    me = 2 * (z * 4 + y * 2 + x) + core
+    zh, zl, member, rank, device, far, across = group_place(z, y, x, core)
+    own_step = (0, 0, 0)
+    positions, act_height, model = tokens_ref.shape
+    sets = positions
+    height = qkv_sum.shape[1]
+    down_height = down_sum.shape[1]
+    half = 16 * height
+    sibling = member((0, 0, 1))
+    scale = 1.0 / math.sqrt(HEAD_DIM)
+    pairs = pairs_of(positions)
+    greet_all(z, y, x, core)
+    sends = []
+
+    def start(copy):
+        copy.start()
+        sends.append(copy)
+
+    def run_rows(dzh, dy, low):
+        number = 16 * flip(zh, dzh) + 4 * flip(y, dy) + 8 * low
+        return pl.ds(pl.multiple_of(number * height, 4 * height), 4 * height)
+
+    def down_rows(dzh, dy):
+        number = 2 * flip(zh, dzh) + flip(y, dy)
+        return pl.ds(pl.multiple_of(number * down_height, down_height), down_height)
+
+    def ff_across(turn):
+        dzh = 1 - turn
+        for s in range(sets):
+            for low in (0, 1):
+                start(
+                    push(
+                        gate_up_ref.at[s, run_rows(dzh, 1, low)],
+                        across_gate.at[turn, s, low],
+                        across_send.at[turn, s, low],
+                        across_recv.at[turn, s, low],
+                        across,
+                    )
+                )
+            start(
+                push(
+                    down_ref.at[s, down_rows(dzh, 1)],
+                    across_down.at[turn, s],
+                    across_send.at[turn, s, 2],
+                    across_recv.at[turn, s, 2],
+                    across,
+                )
+            )
+
+    part_copies = []
+    for turn in (0, 1):
+        for s in range(sets):
+            for low in (0, 1):
+                part_copies.append(
+                    pltpu.make_async_copy(
+                        gate_up_ref.at[s, run_rows(1 - turn, 0, low)],
+                        gate_own.at[turn, s, low],
+                        part_sem.at[turn, s, low],
+                    )
+                )
+            part_copies.append(
+                pltpu.make_async_copy(
+                    down_ref.at[s, down_rows(1 - turn, 0)], down_own.at[turn, s], part_sem.at[turn, s, 2]
+                )
+            )
+
+    def ff_first():
+        for s in range(sets):
+            for low in (0, 1):
+                block = across_gate.at[0, s, low]
+                arrived(block, across_recv.at[0, s, low], across)
+                add_into(block, [block, gate_own.at[0, s, low]])
+                start(push(block, far_gate.at[s, low], far_send.at[s, low], far_recv.at[s, low], far))
+            block = across_down.at[0, s]
+            arrived(block, across_recv.at[0, s, 2], across)
+            add_into(block, [block, down_own.at[0, s]])
+            start(push(block, far_down.at[s], far_send.at[s, 2], far_recv.at[s, 2], far))
+
+    def share(step, s):
+        number = 2 * flip(x, step[1]) + flip(core, step[2])
+        return across_gate.at[
+            1, s, flip(zl, step[0]), pl.ds(pl.multiple_of(number * height, height), height)
+        ]
+
+    def ff_second():
+        for s in range(sets):
+            for low in (0, 1):
+                block = across_gate.at[1, s, low]
+                arrived(block, across_recv.at[1, s, low], across)
+                arrived(far_gate.at[s, low], far_recv.at[s, low], far)
+                add_into(block, [block, far_gate.at[s, low], gate_own.at[1, s, low]])
+            for slot, step in enumerate(RANK_STEPS):
+                if step != own_step:
+                    start(
+                        push(
+                            share(step, s),
+                            gate_up_sum.at[rank(own_step), s],
+                            rank_send.at[slot, s],
+                            rank_recv.at[slot, s],
+                            member(step),
+                        )
+                    )
+            add_into(gate_up_sum.at[rank(own_step), s], [share(own_step, s)])
+            arrived(across_down.at[1, s], across_recv.at[1, s, 2], across)
+            arrived(far_down.at[s], far_recv.at[s, 2], far)
+            add_into(down_sum.at[s], [across_down.at[1, s], far_down.at[s], down_own.at[1, s]])
+
+    def ff_last():
+        for slot, step in enumerate(RANK_STEPS):
+            for s in range(sets):
+                if step != own_step:
+                    arrived(gate_up_sum.at[rank(step), s], rank_recv.at[slot, s], member(step))
+
+    acts = [back_ref, out_ref]
+
+    def act_rows(step):
+        return pl.ds(pl.multiple_of(rank(step) * act_height, act_height), act_height)
+
+    def act_core_sends(which):
+        for dl, dx in ((1, 1), (0, 1), (1, 0), (0, 0)):
+            start(
+                push(
+                    acts[which].at[:, act_rows((dl, dx, 1))],
+                    core_buf.at[which, dl, dx],
+                    core_send.at[which, dl, dx],
+                    core_recv.at[which, dl, dx],
+                    sibling,
+                )
+            )
+
+    def act_load(which):
+        return [
+            pltpu.make_async_copy(
+                acts[which].at[:, act_rows((dl, dx, 0))], act_own.at[dl, dx], own_sem.at[which, dl, dx]
+            )
+            for dl in (0, 1)
+            for dx in (0, 1)
+        ]
+
+    def core_add(which, dl, dx):
+        block = core_buf.at[which, dl, dx]
+        arrived(block, core_recv.at[which, dl, dx], sibling)
+        for s in range(sets):
+            add_into(block.at[s], [block.at[s], act_own.at[dl, dx, s]])
+
+    def act_first(which):
+        for dl in (1, 0):
+            core_add(which, dl, 1)
+            start(
+                push(
+                    core_buf.at[which, dl, 1],
+                    x_buf.at[which, dl],
+                    x_send.at[which, dl],
+                    x_recv.at[which, dl],
+                    member((0, 1, 0)),
+                )
+            )
+        core_add(which, 1, 0)
+        core_add(which, 0, 0)
+
+    def act_second(which):
+        arrived(x_buf.at[which, 1], x_recv.at[which, 1], member((0, 1, 0)))
+        for s in range(sets):
+            block = x_buf.at[which, 1, s]
+            add_into(block, [block, core_buf.at[which, 1, 0, s]])
+        start(
+            push(
+                x_buf.at[which, 1], z_buf.at[which], z_send.at[which], z_recv.at[which], member((1, 0, 0))
+            )
+        )
+
+    def act_third(which):
+        arrived(x_buf.at[which, 0], x_recv.at[which, 0], member((0, 1, 0)))
+        arrived(z_buf.at[which], z_recv.at[which], member((1, 0, 0)))
+
+    pieces = [
+        (qkv_grad, qkv_sum, 0, "zxy", slots_0),
+        (qkv_grad, qkv_sum, 1, "zyx", slots_1),
+        (out_grad, attn_out_sum, 0, "xyz", slots_2),
+        (out_grad, attn_out_sum, 1, "yxz", slots_3),
+    ]
+    events = sorted(
+        ((-hops(offset), place, piece, offset) for piece in range(4) for place, offset in enumerate(OFFSETS)),
+        key=lambda event: event[:3],
+    )
+
+    def tree_block(piece, offset):
+        source, _, index, _, _ = pieces[piece]
+        chip = chip_of(offset, z, y, x)
+        return source.at[index, pl.ds(pl.multiple_of(chip * height, height), height), :]
+
+    def tree_copy(piece, offset):
+        _, _, _, order, slots = pieces[piece]
+        toward = came_from(order, offset)
+        base, _ = slot_base(order)
+        seen = {"x": "x", "y": "y", "u": "d", "d": "u"}[toward]
+        nearer = offset
+        if toward == "u":
+            nearer = (offset[0] - 1, offset[1], offset[2])
+        if toward == "d":
+            nearer = (offset[0] + 1, offset[1], offset[2])
+        there = {"u": z + 1, "d": z - 1}.get(toward, z)
+        index_there, _ = slot_index(
+            order, seen, nearer, there, y if toward != "y" else 1 - y, x if toward != "x" else 1 - x
+        )
+        if toward in "xy":
+            index_there, _ = slot_index(order, seen, offset, z, y, x)
+        place = base[seen] + index_there
+        return push(
+            tree_block(piece, offset),
+            slots.at[place],
+            tree_send.at[piece, chip_of(offset, z, y, x)],
+            tree_recv.at[piece, place],
+            neighbour(toward, z, y, x, core),
+        )
+
+    def tree_step(piece, offset):
+        _, result, index, order, slots = pieces[piece]
+        base, _ = slot_base(order)
+
+        def go():
+            block = tree_block(piece, offset)
+            sure, unsure = [], []
+            for direction in onward(order, offset):
+                local, _ = slot_index(order, direction, offset, z, y, x)
+                place = base[direction] + local
+                (sure if direction in "xy" else unsure).append((direction, place))
+            terms = [block]
+            for _, place in sure:
+                arrived(slots.at[place], tree_recv.at[piece, place], sibling)
+                terms.append(slots.at[place])
+            last = hops(offset) == 0
+            target = result.at[index] if last else block
+            if last or len(terms) > 1:
+                add_into(target, terms)
+            for direction, place in unsure:
+
+                def more(place=place):
+                    arrived(slots.at[place], tree_recv.at[piece, place], sibling)
+                    add_into(target, [target, slots.at[place]])
+
+                maybe(direction_exists(direction, z), more)
+            if not last:
+                tree_copy(piece, offset).start()
+
+        maybe(offset_exists(offset, z), go)
+
+    def tree_steps(which, distances):
+        for hop, _, piece, offset in events:
+            if piece in which and -hop in distances:
+                tree_step(piece, offset)
+
+    def gains_copy(step):
+        other = lax.rem(me + step, 32)
+        return push(
+            gains_part.at[lax.div(other, 4)],
+            gains_buf.at[me],
+            gains_send.at[step],
+            gains_recv.at[me],
+            (lax.div(other, 2), lax.rem(other, 2)),
+        )
+
+    def gains_start(step, carry):
+        gains_copy(step).start()
+        return carry
+
+    def gains_wait(step, carry):
+        other = lax.rem(me + step, 32)
+        gains_copy(step).wait_send()
+        arrived(gains_buf.at[other], gains_recv.at[other], sibling)
+        gains_sum[...] += gains_buf[other]
+        return carry
+
+    def swap_copy(index, source, target):
+        return push(source, target, swap_send.at[index], swap_recv.at[index], sibling)
+
+    def turn(source, target, slot):
+        def one(block, p):
+            flat = source(p, block)
+            turned[slot, p, pl.ds(2 * block, 2)] = flat.T.astype(BF16).reshape(2, 2, height, act_height)
+
+        for p in range(positions):
+            for block in range(model // 128):
+                one(block, p)
+            target[p, :, :, :act_height] = turned[slot, p, :, core]
+
+    qkv_tile = qkv_tiles.shape[1]
+    tile_count = model // qkv_tile
+
+    def qkv_load(number):
+        p, tile = divmod(number, tile_count)
+        return pltpu.make_async_copy(
+            qkv_full.at[p, pl.ds(tile * qkv_tile, qkv_tile)],
+            qkv_tiles.at[number % 2],
+            tile_sem.at[number % 2],
+        )
+
+    out_loads = [
+        pltpu.make_async_copy(out_full.at[p], out_tiles.at[p], tile_sem.at[2 + p]) for p in range(positions)
+    ]
+
+    act_core_sends(0)
+    ff_across(0)
+    ff_across(1)
+    load_back = act_load(0)
+    for copy in load_back + out_loads + part_copies:
+        copy.start()
+    act_core_sends(1)
+    qkv_load(0).start()
+    qkv_load(1).start()
+    make_spread(spread)
+    gain_acc[...] = jnp.zeros_like(gain_acc)
+    for copy in load_back:
+        copy.wait()
+    act_first(0)
+    load_out = act_load(1)
+    for copy in load_out:
+        copy.start()
+
+    def context_block(p, block):
+        return context[p, :, 128 * block : 128 * block + 128].astype(F32)
+
+    def attn_norm(rows):
+        for p in range(positions):
+            r, _ = normed(tokens_ref[p, rows, :].astype(F32))
+            d_rows[p, rows, :] = r * gain_rows[p : p + 1, :]
+
+    row_loop(act_height, 16, attn_norm)
+    turn(context_block, context_turned, 0)
+    turn(
+        lambda p, block: d_rows[p, :, 128 * block : 128 * block + 128], attn_turned, 1
+    )
+    swaps = []
+    for p in range(positions):
+        swaps.append(
+            swap_copy(
+                4 * p,
+                turned.at[0, p, :, 1 - core],
+                context_turned.at[p, :, :, pl.ds(act_height, act_height)],
+            )
+        )
+        swaps.append(
+            swap_copy(
+                4 * p + 1,
+                turned.at[1, p, :, 1 - core],
+                attn_turned.at[p, :, :, pl.ds(act_height, act_height)],
+            )
+        )
+        swaps[-1].start()
+        swaps[-2].start()
+    act_second(0)
+    for copy in part_copies:
+        copy.wait()
+    ff_first()
+    probs = attention_probs(qkv_rows, halves, spread, model)
+    for index in range(len(pairs)):
+        probs_buf[index] = probs[index]
+    act_third(0)
+
+    def mid_back(rows):
+        for p in range(positions):
+            d_ff_in = (
+                core_buf[0, 0, 0, p, rows, :].astype(F32)
+                + x_buf[0, 0, p, rows, :].astype(F32)
+                + z_buf[0, p, rows, :].astype(F32)
+            )
+            r, inverse = normed(resid_mid[p, rows, :])
+            gain_acc[positions + p] += r * d_ff_in
+            total = cot_ref[p, rows, :] + norm_back(
+                r, inverse, d_ff_in * gain_rows[positions + p : positions + p + 1, :]
+            )
+            d_mid[p, rows, :] = total
+            d_mid_low[p, rows, :] = total.astype(BF16)
+
+    row_loop(act_height, 16, mid_back)
+    for p in range(positions):
+        swaps.append(
+            swap_copy(
+                4 * p + 2,
+                d_mid_low.at[p, pl.ds(0, act_height)],
+                d_mid_low.at[p, pl.ds(act_height, act_height)],
+            )
+        )
+        swaps[-1].start()
+    for copy in out_loads:
+        copy.wait()
+    for p in range(positions):
+
+        def context_back(columns, p=p):
+            d_context[p, :, columns] = lax.dot_general(
+                d_mid_low[p, :act_height, :],
+                out_tiles[p, columns, :],
+                (((1,), (1,)), ((), ())),
+                preferred_element_type=F32,
+            ).astype(BF16)
+
+        tile_loop(model, 256, context_back)
+
+    def context_products(rows):
+        for index, (p, q) in enumerate(pairs):
+            product = d_context[p, rows, :].astype(F32) * qkv_rows[q, rows, 2 * model :].astype(F32)
+            halves[2 * index, rows, :], halves[2 * index + 1, rows, :] = split_product(product)
+
+    row_loop(act_height, 16, context_products)
+    d_probs = [sums_over_heads(halves, spread, index, act_height) for index in range(len(pairs))]
+    for p in range(positions):
+        own = [index for index, pair in enumerate(pairs) if pair[0] == p]
+        mean = functools.reduce(jnp.add, [probs_buf[index] * d_probs[index] for index in own])
+        for index in own:
+            d_score = (probs_buf[index] * (d_probs[index] - mean)).astype(BF16)
+            halves[2 * index] = to_heads(d_score, spread)
+            halves[2 * index + 1] = to_heads(probs_buf[index].astype(BF16), spread)
+
+    def qkv_back(rows):
+        d_keys = [None] * positions
+        d_values = [None] * positions
+
+        def plus(total, term):
+            return term if total is None else total + term
+
+        for p in range(positions):
+            d_query = None
+            d_own = d_context[p, rows, :].astype(F32)
+            query = qkv_rows[p, rows, :model].astype(F32)
+            for index, (own, q) in enumerate(pairs):
+                if own == p:
+                    d_score = halves[2 * index, rows, :].astype(F32)
+                    key = qkv_rows[q, rows, model : 2 * model].astype(F32)
+                    d_query = plus(d_query, d_score * key)
+                    d_keys[q] = plus(d_keys[q], d_score * query)
+                    d_values[q] = plus(d_values[q], halves[2 * index + 1, rows, :].astype(F32) * d_own)
+            d_qkv[p, rows, :model] = (d_query * scale).astype(BF16)
+        for p in range(positions):
+            d_qkv[p, rows, model : 2 * model] = (d_keys[p] * scale).astype(BF16)
+            d_qkv[p, rows, 2 * model :] = d_values[p].astype(BF16)
+
+    row_loop(act_height, 16, qkv_back)
+    for p in range(positions):
+        swaps.append(
+            swap_copy(
+                4 * p + 3,
+                d_qkv.at[p, pl.ds(0, act_height)],
+                d_qkv.at[p, pl.ds(act_height, act_height)],
+            )
+        )
+        swaps[-1].start()
+
+    def swap_wait(index, target):
+        arrived(target, swap_recv.at[index], sibling)
+
+    for p in range(positions):
+        swap_wait(4 * p, context_turned.at[p, :, :, pl.ds(act_height, act_height)])
+        swap_wait(4 * p + 2, d_mid_low.at[p, pl.ds(act_height, act_height)])
+
+        def out_weights(columns, p=p):
+            out_grad[p, :, columns] = jnp.dot(
+                context_turned[p].reshape(half, 2 * act_height),
+                d_mid_low[p, :, columns],
+                preferred_element_type=F32,
+            ).astype(BF16)
+
+        tile_loop(model, 256, out_weights)
+    tree_steps((2, 3), (5,))
+    for copy in load_out:
+        copy.wait()
+    act_first(1)
+    for p in range(positions):
+        swap_wait(4 * p + 1, attn_turned.at[p, :, :, pl.ds(act_height, act_height)])
+        swap_wait(4 * p + 3, d_qkv.at[p, pl.ds(act_height, act_height)])
+
+        def qkv_weights(columns, p=p):
+            qkv_grad[p, :, columns] = jnp.dot(
+                attn_turned[p].reshape(half, 2 * act_height),
+                d_qkv[p, :, columns],
+                preferred_element_type=F32,
+            ).astype(BF16)
+
+        tile_loop(3 * model, 256, qkv_weights)
+        tree_steps((p,), (5,))
+    tree_steps((0, 1, 2, 3), (4,))
+    act_second(1)
+    ff_second()
+    for number in range(positions * tile_count):
+        p, tile = divmod(number, tile_count)
+        qkv_load(number).wait()
+        d_rows[p, :, tile * qkv_tile : (tile + 1) * qkv_tile] = lax.dot_general(
+            d_qkv[p, :act_height, :],
+            qkv_tiles[number % 2],
+            (((1,), (1,)), ((), ())),
+            preferred_element_type=F32,
+        )
+        if number + 2 < positions * tile_count:
+            qkv_load(number + 2).start()
+    tree_steps((0, 1, 2, 3), (3,))
+
+    def attn_back(rows):
+        for p in range(positions):
+            r, inverse = normed(tokens_ref[p, rows, :].astype(F32))
+            d_attn_in = d_rows[p, rows, :]
+            gain_acc[p] += r * d_attn_in
+            grad_tokens[p, rows, :] = d_mid[p, rows, :] + norm_back(
+                r, inverse, d_attn_in * gain_rows[p : p + 1, :]
+            )
+
+    row_loop(act_height, 16, attn_back)
+    gains_part[...] = jnp.zeros_like(gains_part)
+    for index in range(2 * positions):
+        sums = jnp.sum(gain_acc[index], axis=0, keepdims=True)
+        for block in range(8):
+            gains_part[block, index : index + 1, :] = sums[:, 128 * block : 128 * block + 128]
+    lax.fori_loop(1, 32, gains_start, 0)
+    tree_steps((0, 1, 2, 3), (2,))
+    act_third(1)
+
+    def finish_output(rows):
+        for p in range(positions):
+            total = (
+                core_buf[1, 0, 0, p, rows, :].astype(F32)
+                + x_buf[1, 0, p, rows, :].astype(F32)
+                + z_buf[1, p, rows, :].astype(F32)
+            )
+            output[p, rows, :] = (resid_mid[p, rows, :] + total).astype(BF16)
+
+    row_loop(act_height, 16, finish_output)
+    tree_steps((0, 1, 2, 3), (1,))
+    tree_steps((0, 1, 2, 3), (0,))
+    ff_last()
+    gains_sum[...] = gains_part[lax.div(me, 4)]
+    lax.fori_loop(1, 32, gains_wait, 0)
+    for _, _, piece, offset in events:
+        if hops(offset) > 0:
+            maybe(offset_exists(offset, z), tree_copy(piece, offset).wait_send)
+    for copy in sends + swaps:
+        copy.wait_send()
+
+
+def backward_scatter(
+    tokens,
+    grads,
+    gain_rows,
+    qkv_rows,
+    context,
+    resid_mid,
+    qkv_full,
+    out_full,
+    out_part,
+    back_part,
+    gate_up_grad,
+    down_grad,
+):
+    sets, act_height, model = tokens.shape
+    width = gate_up_grad.shape[2]
+    height = model // 32
+    down_height = down_grad.shape[1] // 4
+    dma = pltpu.SemaphoreType.DMA
+    vmem = pl.BlockSpec(memory_space=pltpu.VMEM)
+    anywhere = pl.BlockSpec(memory_space=pl.ANY)
+    places = [slot_base(order)[1] for order in ORDERS]
+    pair_count = len(pairs_of(sets))
+    act = (sets, act_height, model)
+    return pl.pallas_call(
+        backward_kernel,
+        out_shape=(
+            jax.ShapeDtypeStruct(act, BF16),
+            jax.ShapeDtypeStruct(act, F32),
+            jax.ShapeDtypeStruct((8, 128), F32),
+            jax.ShapeDtypeStruct((sets, height, 3 * model), F32),
+            jax.ShapeDtypeStruct((sets, height, model), F32),
+            jax.ShapeDtypeStruct((8, sets, height, width), BF16),
+            jax.ShapeDtypeStruct((sets, down_height, model), F32),
+        ),
+        in_specs=[vmem] * 6 + [anywhere] * 6,
+        out_specs=(vmem,) * 7,
+        scratch_shapes=[
+            pltpu.VMEM((2, 2) + act, BF16),
+            pltpu.VMEM((2, 2, 2) + act, BF16),
+            pltpu.VMEM((2, 2) + act, BF16),
+            pltpu.VMEM((2,) + act, BF16),
+            pltpu.VMEM((2, sets, 2, 4 * height, width), BF16),
+            pltpu.VMEM((2, sets, down_height, model), BF16),
+            pltpu.VMEM((2, sets, 2, 4 * height, width), BF16),
+            pltpu.VMEM((2, sets, down_height, model), BF16),
+            pltpu.VMEM((sets, 2, 4 * height, width), BF16),
+            pltpu.VMEM((sets, down_height, model), BF16),
+            pltpu.VMEM((sets, 16 * height, 3 * model), BF16),
+            pltpu.VMEM((sets, 16 * height, model), BF16),
+            pltpu.VMEM((places[0], height, 3 * model), BF16),
+            pltpu.VMEM((places[1], height, 3 * model), BF16),
+            pltpu.VMEM((places[2], height, model), BF16),
+            pltpu.VMEM((places[3], height, model), BF16),
+            pltpu.VMEM((2, 128, 3 * model), BF16),
+            pltpu.VMEM((sets, model, model), BF16),
+            pltpu.VMEM((2, sets, 16, 2, height, act_height), BF16),
+            pltpu.VMEM((sets, 16, height, 2 * act_height), BF16),
+            pltpu.VMEM((sets, 16, height, 2 * act_height), BF16),
+            pltpu.VMEM((sets, 2 * act_height, 3 * model), BF16),
+            pltpu.VMEM((sets, 2 * act_height, model), BF16),
+            pltpu.VMEM(act, F32),
+            pltpu.VMEM(act, BF16),
+            pltpu.VMEM(act, F32),
+            pltpu.VMEM((2 * pair_count, act_height, model), BF16),
+            pltpu.VMEM((pair_count, act_height, 128), F32),
+            pltpu.VMEM((model, 128), BF16),
+            pltpu.VMEM((2 * sets, 16, model), F32),
+            pltpu.VMEM((8, 8, 128), F32),
+            pltpu.VMEM((32, 8, 128), F32),
+            dma((2, 2, 2)),
+            dma((2, 2, 2)),
+            dma((2, 2)),
+            dma((2, 2)),
+            dma((2,)),
+            dma((2,)),
+            dma((2, sets, 3)),
+            dma((2, sets, 3)),
+            dma((sets, 3)),
+            dma((sets, 3)),
+            dma((8, sets)),
+            dma((8, sets)),
+            dma((4 * sets,)),
+            dma((4 * sets,)),
+            dma((4, 16)),
+            dma((4, max(places))),
+            dma((32,)),
+            dma((32,)),
+            dma((2, 2, 2)),
+            dma((2, sets, 3)),
+            dma((2 + sets,)),
+        ],
+        compiler_params=pltpu.CompilerParams(
+            collective_id=5, has_side_effects=True, vmem_limit_bytes=63 * 2**20
+        ),
+        name="backward_scatter",
+    )(
+        tokens,
+        grads,
+        gain_rows,
+        qkv_rows,
+        context,
+        resid_mid,
+        qkv_full,
+        out_full,
+        out_part,
+        back_part,
+        gate_up_grad,
+        down_grad,
+    )
+
+
 def by_set(activations, weight):
     return jnp.einsum("sfk,ske->sfe", activations, weight, preferred_element_type=F32)
 
@@ -1277,19 +1589,6 @@
 
 def set_grad(activations, gradients):
     return jnp.einsum("sfk,sfe->ske", activations, gradients, preferred_element_type=F32)
-
-
-def head_sums(product, spread):
-    high = product.astype(BF16)
-    low = (product - high.astype(F32)).astype(BF16)
-    sums = jnp.dot(high, spread, preferred_element_type=F32)
-    return sums + jnp.dot(low, spread, preferred_element_type=F32)
-
-
-def over_heads(values, spread):
-    return lax.dot_general(
-        values, spread, (((1,), (1,)), ((), ())), preferred_element_type=F32
-    )
 
 
 def local_fast(
@@ -1305,14 +1604,7 @@
     item_lengths,
 ):
     frame_count, positions, model = tokens.shape
-    head_count = model // HEAD_DIM
-    ff_units = w_gate_up.shape[2] // 2
-    score_scale = 1.0 / math.sqrt(HEAD_DIM)
     own_gain = norm_attn.shape[1]
-    spread = (
-        jnp.arange(model)[:, None] // HEAD_DIM == jnp.arange(128)[None, :]
-    ).astype(BF16)
-
     device_index = lax.axis_index(("dp", "pair"))
     local_ids = jnp.arange(frame_count, dtype=jnp.int32)
     frame_ids = device_index * frame_count + local_ids
@@ -1349,22 +1641,6 @@
         ff_rows,
         grad_rows,
     ) = forward_gather(gains, tokens_low, w_qkv, w_out, parts, w_down, grad_low)
-    gain_one = gains_rows[:positions, None, :]
-    gain_two = gains_rows[positions : 2 * positions, None, :]
-    normed_one, inverse_one = normed(tokens_low.astype(F32))
-    attn_in = (normed_one * gain_one).astype(BF16)
-    normed_two, inverse_two = normed(resid_mid)
-    queries = [qkv[p, :, :model].astype(F32) for p in range(positions)]
-    keys = [qkv[p, :, model : 2 * model].astype(F32) for p in range(positions)]
-    values = [qkv[p, :, 2 * model :].astype(F32) for p in range(positions)]
-    probs = []
-    for p in range(positions):
-        scores = [head_sums(queries[p] * keys[q], spread) * score_scale for q in range(p + 1)]
-        top = functools.reduce(jnp.maximum, scores)
-        powers = [jnp.exp(score - top) for score in scores]
-        total = functools.reduce(jnp.add, powers)
-        probs.append([power / total for power in powers])
-
     split = 4 * unit
     gate_up = by_set(ff_rows, gate_up_full)
     gate, up = gate_up[..., :split], gate_up[..., split:]
@@ -1379,57 +1655,34 @@
     down_grad = set_grad(hidden, grad_rows).astype(BF16)
     gate_up_grad = set_grad(ff_rows, d_gate_up).astype(BF16)
     back_part = by_set_back(d_gate_up, gate_up_full).astype(BF16)
-    out_sum, d_ff_in, gate_up_sum, down_sum = scatter_ff(
-        out_part, back_part, gate_up_grad, down_grad
-    )
-    output = jnp.swapaxes((resid_mid + out_sum).astype(BF16), 0, 1)
+    output, grad_tokens, gains_sum, share_qkv, share_out, gate_up_sum, down_sum = backward_scatter(
+        tokens_low,
+        grad_out,
+        gains_rows,
+        qkv,
+        context,
+        resid_mid,
+        qkv_full,
+        out_full,
+        out_part,
+        back_part,
+        gate_up_grad,
+        down_grad,
+    )
+    output = jnp.swapaxes(output, 0, 1)
+    grad_tokens = jnp.swapaxes(grad_tokens, 0, 1)
     share_gate_up = gate_up_sum.reshape(2, 2, 2, positions, -1, 2, 2, 2, unit)
     share_gate_up = share_gate_up.transpose(3, 4, 5, 6, 0, 7, 1, 2, 8)
-    share_gate_up = share_gate_up.reshape(w_gate_up.shape)
-
-    grad_norm_ff = jnp.sum(normed_two * d_ff_in, axis=1)
-    d_mid = grad_out + norm_back(normed_two, inverse_two, d_ff_in * gain_two)
-    d_mid_low = d_mid.astype(BF16)
-    out_grad = set_grad(context, d_mid_low).astype(BF16)
-    d_context = by_set_back(d_mid_low, out_full).astype(BF16).astype(F32)
-    d_queries = []
-    d_keys = [0.0] * positions
-    d_values = [0.0] * positions
-    for p in range(positions):
-        d_probs = [head_sums(d_context[p] * values[q], spread) for q in range(p + 1)]
-        mean = functools.reduce(jnp.add, [prob * d for prob, d in zip(probs[p], d_probs)])
-        d_query = 0.0
-        for q in range(p + 1):
-            d_score = (probs[p][q] * (d_probs[q] - mean)).astype(BF16)
-            d_score = over_heads(d_score, spread)
-            d_values[q] += over_heads(probs[p][q].astype(BF16), spread) * d_context[p]
-            d_query += d_score * keys[q]
-            d_keys[q] += d_score * queries[p]
-        d_queries.append(d_query)
-    d_qkv = jnp.stack(
-        [
-            jnp.concatenate(
-                [d_queries[p] * score_scale, d_keys[p] * score_scale, d_values[p]], axis=-1
-            )
-            for p in range(positions)
-        ]
-    ).astype(BF16)
-    qkv_grad = set_grad(attn_in, d_qkv).astype(BF16)
-    d_attn_in = by_set_back(d_qkv, qkv_full)
-    grad_norm_attn = jnp.sum(normed_one * d_attn_in, axis=1)
-    grad_tokens = d_mid + norm_back(normed_one, inverse_one, d_attn_in * gain_one)
-    grad_tokens = jnp.swapaxes(grad_tokens, 0, 1)
-    gain_grads = jnp.concatenate([grad_norm_attn, grad_norm_ff], axis=0)
-    gain_grads = jnp.swapaxes(gain_grads.reshape(2 * positions, 32, own_gain), 0, 1)
-    gain_parts = jnp.zeros((32, 8, 128), F32).at[:, : 2 * positions, :own_gain].set(gain_grads)
-    gains_sum, share_qkv, share_out = scatter_attn(gain_parts, qkv_grad, out_grad)
+    share_gate_up = share_gate_up.reshape(w_gate_up.shape).astype(F32)
+    shift = lax.rem(device_index, 128 // own_gain) * own_gain
+    gain_grads = lax.dynamic_slice(gains_sum, (0, shift), (2 * positions, own_gain))
     return (
         output,
         grad_tokens,
-        gains_sum[:positions, :own_gain],
+        gain_grads[:positions],
         share_qkv,
         share_out,
-        gains_sum[positions : 2 * positions, :own_gain],
+        gain_grads[positions:],
         share_gate_up,
         down_sum,
     )

time: 484 us -> 418 us (0.86)
  matrix products: 72.6 us -> 40.5 us
  Pallas kernels: 370 us -> 340 us
  other arithmetic: 11.1 us -> 4.27 us
    pallas_call x2 -> x1, Pallas kernels: 193 us -> 164 us  [backward_scatter(): pl.pallas_call(backward_kernel, out_shape=(jax.ShapeDtypeStruct(act, BF16...]
    dot_general x17 -> x0, matrix products: 13 us -> none  [the longest x6 7.71 us: over_heads(): lax.dot_general(values, spread, (((1,), (1,)), ((), ())), preferred_eleme...]
    convert_element_type x0 -> x3, local copies, waits for them, and re-layouts: none -> 10.1 us  [local_fast(): share_gate_up = share_gate_up.reshape(w_gate_up.shape).astype(F32)]
    dot_general x4 -> x2, matrix products: 22.7 us -> 13 us  [set_grad(): jnp.einsum('sfk,sfe->ske', activations, gradients, preferred_element_type...]
    dot_general x4 -> x2, matrix products: 24.7 us -> 15.3 us  [by_set_back(): jnp.einsum('sfe,ske->sfk', gradients, weight, preferred_element_type=F32)]
    reshape x4 -> x0, local copies, waits for them, and re-layouts: 7.19 us -> none  [the longest x1 4.03 us: local_fast(): share_gate_up = share_gate_up.reshape(w_gate_up.shape)]
    unnamed x40 -> x28, local copies, waits for them, and re-layouts: 6.64 us -> 9.93 us
where the time goes in v3:
time: 418 us; the launch traced here: 413 us
  Pallas kernels  340 us (81%)
  matrix products  40.5 us (10%)
  local copies, waits for them, and re-layouts  26.2 us (6%)
  other arithmetic  4.27 us (1%)
    pallas_call x1, Pallas kernels, forward_gather(): pl.pallas_call(forward_kernel, out_shape=(jax.ShapeDtypeStruct((16, model...  176 us
    pallas_call x1, Pallas kernels, backward_scatter(): pl.pallas_call(backward_kernel, out_shape=(jax.ShapeDtypeStruct(act, BF16...  164 us
    dot_general x2, matrix products, by_set_back(): jnp.einsum('sfe,ske->sfk', gradients, weight, preferred_element_type=F32)  15.3 us
    dot_general x2, matrix products, set_grad(): jnp.einsum('sfk,sfe->ske', activations, gradients, preferred_element_type...  13 us
    dot_general x2, matrix products, by_set(): jnp.einsum('sfk,ske->sfe', activations, weight, preferred_element_type=F32)  12.2 us
    convert_element_type x3, local copies, waits for them, and re-layouts, local_fast(): share_gate_up = share_gate_up.reshape(w_gate_up.shape).astype(F32)  10.1 us
    unnamed x28, local copies, waits for them, and re-layouts  9.93 us

profile of v3, /device:TPU:0, one launch (start us, length us, event | category | flops | bytes accessed | tf_op | source)
XLA Modules:
  0.0 413.2 jit_solution(2308698304423586009)
XLA Ops:
  1.4 0.8 reduce-window.8
  2.2 0.7 bitcast_subtract_fusion
  2.9 0.7 convert_divide_fusion
  3.5 0.1 select_reduce_fusion
  3.6 0.7 pad_maximum_fusion.7
  4.3 0.1 tile.10
  4.4 0.6 pad.4.gains_ref
  5.0 2.0 copy.51
  7.0 1.8 reshape.70
  8.8 0.9 copy.50
  9.7 1.5 reshape.71.gate_up_ref
  11.2 1.3 fusion.8
  12.5 176.3 %forward_gather.1 = (f32[16,1024]{1,0:T(8,128)}, bf16[2,128,3072]{2,1,0:T(8,128)(2,1)}, bf16[2,128,1024]{2,1,0:T(8,128)(2,1)}, f32[2,128,1024]{2,1,0:T(8,128)}, ...) custom-call(bf16[16,128]{1,0:T(8,128)(2,1)} %pad.4.gains_ref, ...), custom_call_target="tpu_custom_call" | custom-call | tf_op jit(solution)/shard_map/forward_gather/pallas_call | solution.py:789
  188.9 7.8 %fusion.10 = f32[2,1024,1024]{1,2,0:T(8,128)S(1)} fusion(bf16[2,1024,1024]{2,1,0:T(8,128)(2,1)} %get-tuple-element.31, bf16[2,1024,1024]{2,1,0:T(8,128)(2,1)} %get-tuple-element.32), kind=kOutput, calls=%fused_computation.32 | convolution fusion | flops 4294967296 | bytes 16777216 | tf_op jit(solution)/shard_map/sfk,ske->sfe/dot_general | solution.py:1583
  196.7 0.0 copy-done.6
  196.7 0.0 copy-done.7
  196.7 5.5 %multiply_convert_fusion.1 = (bf16[2,1024,512]{1,2,0:T(8,128)(2,1)}, bf16[2,1024,512]{1,2,0:T(8,128)(2,1)}, bf16[2,1024,512]{1,2,0:T(8,128)(2,1)S(1)}) fusion(f32[2,1024,1024]{1,2,0:T(8,128)S(1)} %fusion.10, bf16[2,1024,1024]{2,1,0:T(8,128)(2,1)S(1)} %copy-done.6, bf16[2,512,1024]{2,1,0:T(8,128)(2,1)S(1)} %copy-done.7), kind=kOutput, calls=%fused_computation.2 | convolution fusion | flops 2163212288 | bytes 20971520 | tf_op jit(solution)/shard_map/sfe,ske->sfk/dot_general | solution.py:1587
  202.1 3.7 convolution_convert_fusion.1.down_ref
  205.8 9.3 %fusion.4.gate_up_ref = bf16[2,1024,1024]{2,1,0:T(8,128)(2,1)} fusion(bf16[2,1024,1024]{2,1,0:T(8,128)(2,1)S(1)} %copy-done.5, bf16[2,1024,512]{1,2,0:T(8,128)(2,1)} %get-tuple-element.59, bf16[2,1024,512]{1,2,0:T(8,128)(2,1)} %get-tuple-element.58), kind=kOutput, calls=%fused_computation.9 | convolution fusion | flops 4305453056 | bytes 12582912 | tf_op jit(solution)/shard_map/sfk,sfe->ske/dot_general | solution.py:1591
  215.1 9.9 %fusion.3.back_ref = bf16[2,1024,1024]{2,1,0:T(8,128)(2,1)} fusion(bf16[2,1024,1024]{2,1,0:T(8,128)(2,1)S(1)} %copy-done.4, bf16[2,1024,512]{1,2,0:T(8,128)(2,1)} %get-tuple-element.59, bf16[2,1024,512]{1,2,0:T(8,128)(2,1)} %get-tuple-element.58), kind=kOutput, calls=%fused_computation.8 | convolution fusion | flops 4305453056 | bytes 12582912 | tf_op jit(solution)/shard_map/sfe,ske->sfk/dot_general | solution.py:1587
  225.0 4.4 %convolution_convert_fusion.out_ref = bf16[2,1024,1024]{2,1,0:T(8,128)(2,1)} fusion(bf16[2,1024,512]{1,2,0:T(8,128)(2,1)S(1)} %copy-done.10, bf16[2,512,1024]{2,1,0:T(8,128)(2,1)S(1)} %copy-done.8), kind=kOutput, calls=%fused_computation.10 | convolution fusion | flops 2149580800 | bytes 8388608 | tf_op jit(solution)/shard_map/sfk,ske->sfe/dot_general | solution.py:1583
  229.4 164.2 %backward_scatter.1 = (bf16[2,128,1024]{2,1,0:T(8,128)(2,1)}, f32[2,128,1024]{2,1,0:T(8,128)}, f32[8,128]{1,0:T(8,128)}, f32[2,32,3072]{2,1,0:T(8,128)}, f32[2,3...) custom-call(bf16[2,128,1024]{2,1,0:T(8,128)(2,1)} %bitcast.32, ...), custom_call_target="tpu_custom_call" | custom-call | tf_op jit(solution)/shard_map/backward_scatter/pallas_call | solution.py:1494
  393.6 2.4 copy.38
  396.0 3.0 copy.39
  399.0 0.7 constant_dynamic-slice_fusion
  399.7 0.6 fusion.9
  400.3 3.2 reshape.73
  403.4 3.0 copy.37
  406.4 4.0 reshape.72
  410.4 0.9 copy.56
  411.3 0.7 copy.57
  412.0 1.0 copy.58
  (25 shorter events, 0.1 us)
Async XLA Ops:
  0.6 10.6 %copy-start.2 = (bf16[128,2,1024]{2,1,0:T(2,128)(2,1)S(1)}, bf16[128,2,1024]{2,1,0:T(2,128)(2,1)}, u32[]{:S(2)}) copy-start(bf16[128,2,1024]{2,1,0:T(2,128)(2,1)} %param.17) | copy-start | bytes 1572868
  188.9 7.8 %copy-start.6 = (bf16[2,1024,1024]{2,1,0:T(8,128)(2,1)S(1)}, bf16[2,1024,1024]{2,1,0:T(8,128)(2,1)}, u32[]{:S(2)}) copy-start(bf16[2,1024,1024]{2,1,0:T(8,128)(2,1)} %get-tuple-element.34) | copy-start | bytes 12582916
  188.9 7.8 %copy-start.7 = (bf16[2,512,1024]{2,1,0:T(8,128)(2,1)S(1)}, bf16[2,512,1024]{2,1,0:T(8,128)(2,1)}, u32[]{:S(2)}) copy-start(bf16[2,512,1024]{2,1,0:T(8,128)(2,1)} %get-tuple-element.33) | copy-start | bytes 6291460
  202.1 3.7 copy-start.9
  202.1 3.7 copy-start.5
  205.8 9.3 %copy-start.4 = (bf16[2,1024,1024]{2,1,0:T(8,128)(2,1)S(1)}, bf16[2,1024,1024]{2,1,0:T(8,128)(2,1)}, u32[]{:S(2)}) copy-start(bf16[2,1024,1024]{2,1,0:T(8,128)(2,1)} %get-tuple-element.32) | copy-start | bytes 12582916
  215.1 9.9 %copy-start.8 = (bf16[2,512,1024]{2,1,0:T(8,128)(2,1)S(1)}, bf16[2,512,1024]{2,1,0:T(8,128)(2,1)}, u32[]{:S(2)}) copy-start(bf16[2,512,1024]{2,1,0:T(8,128)(2,1)} %get-tuple-element.33) | copy-start | bytes 6291460
  215.1 9.9 %copy-start.10 = (bf16[2,1024,512]{1,2,0:T(8,128)(2,1)S(1)}, bf16[2,1024,512]{1,2,0:T(8,128)(2,1)}, u32[]{:S(2)}) copy-start(bf16[2,1024,512]{1,2,0:T(8,128)(2,1)} %copy-done.9) | copy-start | bytes 6291460
  403.4 7.0 %copy-start.1 = (f32[2,32,3072]{2,1,0:T(8,128)S(1)}, f32[2,32,3072]{2,1,0:T(8,128)}, u32[]{:S(2)}) copy-start(f32[2,32,3072]{2,1,0:T(8,128)} %get-tuple-element.76) | copy-start | bytes 2359300
  403.4 7.8 %copy-start.3 = (f32[2,32,1024]{2,1,0:T(8,128)S(1)}, f32[2,32,1024]{2,1,0:T(8,128)}, u32[]{:S(2)}) copy-start(f32[2,32,1024]{2,1,0:T(8,128)} %get-tuple-element.77) | copy-start | bytes 786436
  406.4 5.6 %copy-start = (f32[2,128,1024]{2,1,0:T(8,128)S(1)}, f32[2,128,1024]{2,1,0:T(8,128)}, u32[]{:S(2)}) copy-start(f32[2,128,1024]{2,1,0:T(8,128)} %get-tuple-element.80) | copy-start | bytes 3145732

commit v4 on v3

--- a/solution.py
+++ b/solution.py
@@ -407,6 +407,18 @@
     lax.fori_loop(0, width // tile, one, 0)
 
 
+def dot(left, right):
+    return jnp.dot(left, right, preferred_element_type=F32)
+
+
+def dot_back(left, right):
+    return lax.dot_general(left, right, (((1,), (1,)), ((), ())), preferred_element_type=F32)
+
+
+def dot_grad(left, right):
+    return lax.dot_general(left, right, (((0,), (0,)), ((), ())), preferred_element_type=F32)
+
+
 def make_spread(spread):
     height, width = spread.shape
     head = lax.broadcasted_iota(jnp.int32, (height, width), 0) // HEAD_DIM
@@ -424,38 +436,31 @@
     return high, (product - high.astype(F32)).astype(BF16)
 
 
-def sums_over_heads(halves, spread, index, height):
-    return jnp.dot(
-        halves[2 * index], spread[...], preferred_element_type=F32
-    ) + jnp.dot(halves[2 * index + 1], spread[...], preferred_element_type=F32)
+def sums_over_heads(halves, spread, index):
+    return dot(halves[2 * index], spread[...]) + dot(halves[2 * index + 1], spread[...])
 
 
 def to_heads(values, spread):
-    return lax.dot_general(
-        values, spread[...], (((1,), (1,)), ((), ())), preferred_element_type=F32
-    ).astype(BF16)
-
-
-def attention_probs(qkv, halves, spread, model):
-    positions, height, _ = qkv.shape
+    return dot_back(values, spread[...]).astype(BF16)
+
+
+def attention_probs(qkv, halves, spread, model, position):
+    height = qkv.shape[1]
     scale = 1.0 / math.sqrt(HEAD_DIM)
-    pairs = pairs_of(positions)
 
     def products(rows):
-        for index, (p, q) in enumerate(pairs):
-            product = qkv[p, rows, :model].astype(F32) * qkv[q, rows, model : 2 * model].astype(F32)
-            halves[2 * index, rows, :], halves[2 * index + 1, rows, :] = split_product(product)
+        for q in range(position + 1):
+            product = qkv[position, rows, :model].astype(F32) * qkv[
+                q, rows, model : 2 * model
+            ].astype(F32)
+            halves[2 * q, rows, :], halves[2 * q + 1, rows, :] = split_product(product)
 
     row_loop(height, 16, products)
-    scores = [sums_over_heads(halves, spread, index, height) * scale for index in range(len(pairs))]
-    probs = []
-    for p in range(positions):
-        own = [scores[index] for index, pair in enumerate(pairs) if pair[0] == p]
-        top = functools.reduce(jnp.maximum, own)
-        powers = [jnp.exp(score - top) for score in own]
-        total = functools.reduce(jnp.add, powers)
-        probs.extend([power / total for power in powers])
-    return probs
+    scores = [sums_over_heads(halves, spread, q) * scale for q in range(position + 1)]
+    top = functools.reduce(jnp.maximum, scores)
+    powers = [jnp.exp(score - top) for score in scores]
+    total = functools.reduce(jnp.add, powers)
+    return [power / total for power in powers]
 
 
 def forward_kernel(
@@ -472,15 +477,24 @@
     resid_mid,
     qkv_full,
     out_full,
-    gate_up_full,
-    down_full,
-    rows_full,
-    grads_full,
+    ff_out,
+    ff_back,
+    gate_up_grad,
+    down_grad,
     qkv_buf,
     out_buf,
+    gate_up_buf,
+    down_buf,
+    rows_buf,
+    grads_buf,
+    hidden,
+    d_gate_up,
+    out_stage,
+    back_stage,
+    gate_up_stage,
+    down_stage,
     gains_all,
     attn_in,
-    ff_in,
     halves,
     spread,
     plane_sem,
@@ -498,6 +512,7 @@
     act_recv,
     local_sem,
     keep_sem,
+    stage_sem,
 ):
     z, y, x, core = here()
     me = 2 * (z * 4 + y * 2 + x) + core
@@ -506,26 +521,27 @@
     positions, act_height, model = tokens_ref.shape
     height = gate_up_ref.shape[2]
     down_height = down_ref.shape[1]
+    split = 4 * down_height
     sibling = neighbour("s", z, y, x, core)
     greet_all(z, y, x, core)
-    pieces = [
-        (qkv_ref, qkv_buf, 0, "zxy"),
-        (qkv_ref, qkv_buf, 1, "zyx"),
-        (out_ref, out_buf, 0, "xyz"),
-        (out_ref, out_buf, 1, "yxz"),
-    ]
+    part = qkv_ref.shape[2] // 2
+    pieces = []
+    for s in range(positions):
+        pieces.append((qkv_ref, qkv_buf, s, pl.ds(0, part), "zxy"))
+        pieces.append((qkv_ref, qkv_buf, s, pl.ds(part, part), "zyx"))
+        pieces.append((out_ref, out_buf, s, pl.ds(0, model), ("xyz", "yxz")[s % 2]))
 
     def piece_rows(piece, number):
-        _, full, index, _ = pieces[piece]
-        return full.at[index, pl.ds(pl.multiple_of(number * height, height), height), :]
+        _, full, index, columns, _ = pieces[piece]
+        return full.at[index, pl.ds(pl.multiple_of(number * height, height), height), columns]
 
     def tree_send(piece, offset, direction):
-        source, _, index, _ = pieces[piece]
+        source, _, index, columns, _ = pieces[piece]
         chip = chip_of(offset, z, y, x)
         block = piece_rows(piece, 2 * chip + core)
         recv = sibling_sem if direction == "s" else plane_sem
         return push(
-            source.at[index] if hops(offset) == 0 else block,
+            source.at[index, :, columns] if hops(offset) == 0 else block,
             block,
             send_sem.at[piece, chip, DIRECTIONS.index(direction)],
             recv.at[piece, chip],
@@ -533,7 +549,7 @@
         )
 
     def tree_step(piece, offset, finish=False):
-        order = pieces[piece][3]
+        order = pieces[piece][4]
 
         def go():
             chip = chip_of(offset, z, y, x)
@@ -546,14 +562,37 @@
         maybe(offset_exists(offset, z), go)
 
     events = sorted(
-        ((hops(offset), place, piece, offset) for piece in range(4) for place, offset in enumerate(OFFSETS)),
+        (
+            (hops(offset), place, piece, offset)
+            for piece in range(len(pieces))
+            for place, offset in enumerate(OFFSETS)
+        ),
         key=lambda event: event[:3],
     )
 
-    def tree_steps(distance):
+    def tree_steps(s, distance):
         for hop, _, piece, offset in events:
-            if hop == distance:
+            if hop == distance and pieces[piece][2] == s:
                 tree_step(piece, offset)
+
+    def tree_end(s):
+        mine = [piece for piece in range(len(pieces)) if pieces[piece][2] == s]
+
+        def sibling_wait(chip, carry):
+            for piece in mine:
+                arrived(piece_rows(piece, 2 * chip + 1 - core), sibling_sem.at[piece, chip], sibling)
+            return carry
+
+        lax.fori_loop(0, 16, sibling_wait, 0)
+        for piece in mine:
+            tree_own[piece].wait()
+
+    tree_own = [
+        pltpu.make_async_copy(
+            source.at[index, :, columns], piece_rows(piece, me), local_sem.at[piece]
+        )
+        for piece, (source, _, index, columns, _) in enumerate(pieces)
+    ]
 
     def gains_copy(step):
         other = lax.rem(me + step, 32)
@@ -581,211 +620,315 @@
         copy.start()
         sends.append(copy)
 
-    def weight_rows(number):
-        return gate_up_full.at[:, pl.ds(pl.multiple_of(number * height, height), height), :]
-
-    def down_rows(dzh, dy):
+    def weight_rows(s, number):
+        return gate_up_buf.at[s, pl.ds(pl.multiple_of(number * height, height), height), :]
+
+    def down_rows(s, dzh, dy):
         number = 2 * flip(zh, dzh) + flip(y, dy)
-        return down_full.at[:, pl.ds(pl.multiple_of(number * down_height, down_height), down_height), :]
-
-    def act_rows(which, step):
-        full = (rows_full, grads_full)[which]
-        return full.at[:, pl.ds(pl.multiple_of(rank(step) * act_height, act_height), act_height), :]
-
-    def send_act(which, step, source, hop):
+        return down_buf.at[s, pl.ds(pl.multiple_of(number * down_height, down_height), down_height), :]
+
+    def act_rows(which, s, step):
+        full = (rows_buf, grads_buf)[which]
+        return full.at[s, pl.ds(pl.multiple_of(rank(step) * act_height, act_height), act_height), :]
+
+    def send_act(which, s, step, source, hop):
         landed = tuple(bit ^ (1 if axis == hop else 0) for axis, bit in enumerate(step))
         start(
             push(
                 source,
-                act_rows(which, step),
-                act_send.at[which, 4 * step[0] + 2 * step[1] + step[2], hop],
-                act_recv.at[which, 4 * landed[0] + 2 * landed[1] + landed[2]],
+                act_rows(which, s, step),
+                act_send.at[which, s, 4 * step[0] + 2 * step[1] + step[2], hop],
+                act_recv.at[which, s, 4 * landed[0] + 2 * landed[1] + landed[2]],
                 member(tuple(1 if axis == hop else 0 for axis in range(3))),
             )
         )
 
-    def wait_act(which, step):
+    def wait_act(which, s, step):
         arrived(
-            act_rows(which, step), act_recv.at[which, 4 * step[0] + 2 * step[1] + step[2]], sibling
-        )
-
-    def act_own(which, source):
+            act_rows(which, s, step),
+            act_recv.at[which, s, 4 * step[0] + 2 * step[1] + step[2]],
+            sibling,
+        )
+
+    def act_own(which, s):
+        source = act_rows(0, s, own_step) if which == 0 else grads_ref.at[s]
         for hop in (0, 1, 2):
-            send_act(which, own_step, source, hop)
-
-    def act_from_z(which):
+            send_act(which, s, own_step, source, hop)
+
+    def act_from_z(which, s):
         step = (1, 0, 0)
-        wait_act(which, step)
-        send_act(which, step, act_rows(which, step), 1)
-        send_act(which, step, act_rows(which, step), 2)
-
-    def act_from_x(which):
-        for step in ((0, 1, 0), (1, 1, 0)):
-            wait_act(which, step)
-            send_act(which, step, act_rows(which, step), 2)
-
-    def act_from_core(which):
-        for step in ((0, 0, 1), (1, 0, 1), (0, 1, 1), (1, 1, 1)):
-            wait_act(which, step)
-
-    mine = gate_up_ref.at[rank(own_step)]
-
-    def ff_own():
+        wait_act(which, s, step)
+        send_act(which, s, step, act_rows(which, s, step), 1)
+        send_act(which, s, step, act_rows(which, s, step), 2)
+
+    def act_from_x(which, s, steps=((0, 1, 0), (1, 1, 0))):
+        for step in steps:
+            wait_act(which, s, step)
+            send_act(which, s, step, act_rows(which, s, step), 2)
+
+    def act_from_core(which, s, steps=((0, 0, 1), (1, 0, 1), (0, 1, 1), (1, 1, 1))):
+        for step in steps:
+            wait_act(which, s, step)
+
+    def mine(s):
+        return gate_up_ref.at[rank(own_step), s]
+
+    def ff_to_ranks(s):
         for slot, step in enumerate(RANK_STEPS):
             if step != own_step:
                 start(
                     push(
-                        gate_up_ref.at[rank(step)],
-                        weight_rows(device(own_step)),
-                        rank_send.at[slot],
-                        rank_recv.at[slot],
+                        gate_up_ref.at[rank(step), s],
+                        weight_rows(s, device(own_step)),
+                        rank_send.at[s, slot],
+                        rank_recv.at[s, slot],
                         member(step),
                     )
                 )
-        start(push(mine, weight_rows(device(own_step)), far_send.at[0], far_recv.at[0], far))
-        start(push(down_ref, down_rows(0, 0), far_send.at[8], far_recv.at[8], far))
-        start(push(mine, weight_rows(device(own_step)), across_send.at[0, 0], across_recv.at[0, 0], across))
-        start(push(down_ref, down_rows(0, 0), across_send.at[0, 8], across_recv.at[0, 8], across))
-
-    def ff_from_rank(slots):
+
+    def ff_own_far(s):
+        start(push(mine(s), weight_rows(s, device(own_step)), far_send.at[s, 0], far_recv.at[s, 0], far))
+        start(push(down_ref.at[s], down_rows(s, 0, 0), far_send.at[s, 8], far_recv.at[s, 8], far))
+
+    def ff_own_across(s):
+        for slot, source, target in (
+            (0, mine(s), weight_rows(s, device(own_step))),
+            (8, down_ref.at[s], down_rows(s, 0, 0)),
+        ):
+            start(push(source, target, across_send.at[s, 0, slot], across_recv.at[s, 0, slot], across))
+
+    def ff_from_rank(s, slots):
         for slot in slots:
-            step = RANK_STEPS[slot]
-            block = weight_rows(device(step))
-            arrived(block, rank_recv.at[slot], sibling)
-            start(push(block, block, far_send.at[slot], far_recv.at[slot], far))
-            start(push(block, block, across_send.at[0, slot], across_recv.at[0, slot], across))
-
-    def ff_from_far(slots):
+            block = weight_rows(s, device(RANK_STEPS[slot]))
+            arrived(block, rank_recv.at[s, slot], sibling)
+            start(push(block, block, far_send.at[s, slot], far_recv.at[s, slot], far))
+            start(push(block, block, across_send.at[s, 0, slot], across_recv.at[s, 0, slot], across))
+
+    def ff_from_far(s, slots):
         for slot in slots:
-            block = down_rows(1, 0) if slot == 8 else weight_rows(device(RANK_STEPS[slot], 1, 0))
-            arrived(block, far_recv.at[slot], sibling)
-            start(push(block, block, across_send.at[1, slot], across_recv.at[1, slot], across))
-
-    tree_steps(0)
+            block = down_rows(s, 1, 0) if slot == 8 else weight_rows(s, device(RANK_STEPS[slot], 1, 0))
+            arrived(block, far_recv.at[s, slot], sibling)
+            start(push(block, block, across_send.at[s, 1, slot], across_recv.at[s, 1, slot], across))
+
+    def ff_end(s):
+        for dzh in (0, 1):
+            for slot, step in enumerate(RANK_STEPS):
+                arrived(weight_rows(s, device(step, dzh, 1)), across_recv.at[s, dzh, slot], sibling)
+            arrived(down_rows(s, dzh, 1), across_recv.at[s, dzh, 8], sibling)
+
+    ff_local = []
+    for s in range(positions):
+        ff_local.append(
+            [
+                pltpu.make_async_copy(mine(s), weight_rows(s, device(own_step)), local_sem.at[7 + 3 * s]),
+                pltpu.make_async_copy(down_ref.at[s], down_rows(s, 0, 0), local_sem.at[8 + 3 * s]),
+                pltpu.make_async_copy(grads_ref.at[s], act_rows(1, s, own_step), local_sem.at[9 + 3 * s]),
+            ]
+        )
+    gains_local = pltpu.make_async_copy(gains_ref, gains_all.at[me], local_sem.at[6])
+
+    def take_gains():
+        lax.fori_loop(1, 32, gains_wait, 0)
+        gains_local.wait()
+        for block in range(8):
+            total = gains_all[4 * block].astype(F32)
+            for extra in range(1, 4):
+                total = total + gains_all[4 * block + extra].astype(F32)
+            gain_rows[:, 128 * block : 128 * block + 128] = total
+
+        def first_norm(rows):
+            for p in range(positions):
+                r, _ = normed(tokens_ref[p, rows, :].astype(F32))
+                attn_in[p, rows, :] = (r * gain_rows[p : p + 1, :]).astype(BF16)
+
+        row_loop(act_height, 16, first_norm)
+
+    keep = []
+
+    def attention(p):
+        for source, target, slot in (
+            (qkv_buf.at[p], qkv_full.at[p], 2 * p),
+            (out_buf.at[p], out_full.at[p], 2 * p + 1),
+        ):
+            keep.append(pltpu.make_async_copy(source, target, keep_sem.at[slot]))
+            keep[-1].start()
+
+        def project(columns):
+            qkv_rows[p, :, columns] = dot(attn_in[p], qkv_buf[p, :, columns]).astype(BF16)
+
+        tile_loop(3 * model, 512, project)
+        probs = attention_probs(qkv_rows, halves, spread, model, p)
+        for q in range(p + 1):
+            halves[2 * q] = to_heads(probs[q].astype(BF16), spread)
+
+        def mix(rows):
+            total = None
+            for q in range(p + 1):
+                term = halves[2 * q, rows, :].astype(F32) * qkv_rows[q, rows, 2 * model :].astype(F32)
+                total = term if total is None else total + term
+            context[p, rows, :] = total.astype(BF16)
+
+        row_loop(act_height, 16, mix)
+
+        def attend(columns):
+            resid_mid[p, :, columns] = tokens_ref[p, :, columns].astype(F32) + dot(
+                context[p], out_buf[p, :, columns]
+            )
+
+        tile_loop(model, 512, attend)
+
+        def second_norm(step, carry):
+            rows = pl.ds(pl.multiple_of(step * 16, 16), 16)
+            r, _ = normed(resid_mid[p, rows, :])
+            top = rank(own_step) * act_height + step * 16
+            rows_buf[p, pl.ds(pl.multiple_of(top, 16), 16), :] = (
+                r * gain_rows[positions + p : positions + p + 1, :]
+            ).astype(BF16)
+            return carry
+
+        lax.fori_loop(0, act_height // 16, second_norm, 0)
+
+    def ff_block(s, number):
+        rows = pl.ds(pl.multiple_of(number * 2 * act_height, 2 * act_height), 2 * act_height)
+        normed_rows = rows_buf[s, rows, :]
+        grads = grads_buf[s, rows, :]
+        for tile in range(split // 256):
+            left, right = pl.ds(tile * 256, 256), pl.ds(split + tile * 256, 256)
+            gate = dot(normed_rows, gate_up_buf[s, :, left])
+            up = dot(normed_rows, gate_up_buf[s, :, right])
+            d_hidden = dot_back(grads, down_buf[s, left, :])
+            sigmoid_gate = jax.nn.sigmoid(gate)
+            silu_gate = gate * sigmoid_gate
+            hidden[rows, left] = (silu_gate * up).astype(BF16)
+            d_gate_up[rows, left] = (
+                d_hidden * up * sigmoid_gate * (1.0 + gate * (1.0 - sigmoid_gate))
+            ).astype(BF16)
+            d_gate_up[rows, right] = (d_hidden * silu_gate).astype(BF16)
+        for tile in range(model // 512):
+            columns = pl.ds(tile * 512, 512)
+            out_stage[rows, columns] = dot(hidden[rows, :], down_buf[s, :, columns]).astype(BF16)
+            back_stage[rows, columns] = dot_back(
+                d_gate_up[rows, :], gate_up_buf[s, columns, :]
+            ).astype(BF16)
+
+    def ff_blocks(s):
+        def one(number, carry):
+            ff_block(s, number)
+            return carry
+
+        lax.fori_loop(0, 4, one, 0)
+
+    stages = []
+
+    def stage_out(s, first):
+        chosen = (
+            [(out_stage, ff_out, 0), (back_stage, ff_back, 1)]
+            if first
+            else [(gate_up_stage, gate_up_grad, 2), (down_stage, down_grad, 3)]
+        )
+        for source, target, slot in chosen:
+            stages.append(pltpu.make_async_copy(source, target.at[s], stage_sem.at[s, slot]))
+            stages[-1].start()
+
+    def ff_grads(s):
+        stage_out(s, True)
+
+        def gate_up_tile(columns):
+            gate_up_stage[:, columns] = dot_grad(rows_buf[s], d_gate_up[:, columns]).astype(BF16)
+
+        def down_tile(columns):
+            down_stage[:, columns] = dot_grad(hidden[...], grads_buf[s, :, columns]).astype(BF16)
+
+        tile_loop(2 * split, 256, gate_up_tile)
+        tile_loop(model, 256, down_tile)
+        stage_out(s, False)
+
+    def stages_end():
+        while stages:
+            stages.pop(0).wait()
+
+    tree_steps(0, 0)
     lax.fori_loop(1, 32, gains_start, 0)
-    ff_own()
-    act_own(1, grads_ref)
-    local = [
-        pltpu.make_async_copy(source.at[index], piece_rows(piece, me), local_sem.at[piece])
-        for piece, (source, _, index, _) in enumerate(pieces)
-    ]
-    local.append(pltpu.make_async_copy(gains_ref, gains_all.at[me], local_sem.at[4]))
-    local.append(pltpu.make_async_copy(mine, weight_rows(device(own_step)), local_sem.at[5]))
-    local.append(pltpu.make_async_copy(down_ref, down_rows(0, 0), local_sem.at[6]))
-    local.append(pltpu.make_async_copy(grads_ref, act_rows(1, own_step), local_sem.at[7]))
-    for copy in local:
+    ff_to_ranks(0)
+    ff_own_far(0)
+    ff_own_across(0)
+    act_own(1, 0)
+    for copy in tree_own + ff_local[0] + ff_local[1] + [gains_local]:
         copy.start()
     make_spread(spread)
-    tree_steps(1)
-    ff_from_rank((1, 2, 3, 4))
-    lax.fori_loop(1, 32, gains_wait, 0)
-    local[4].wait()
-    for block in range(8):
-        total = gains_all[4 * block].astype(F32)
-        for part in range(1, 4):
-            total = total + gains_all[4 * block + part].astype(F32)
-        gain_rows[:, 128 * block : 128 * block + 128] = total
-
-    def first_norm(rows):
-        for p in range(positions):
-            values = tokens_ref[p, rows, :].astype(F32)
-            r, _ = normed(values)
-            attn_in[p, rows, :] = (r * gain_rows[p : p + 1, :]).astype(BF16)
-
-    row_loop(act_height, 16, first_norm)
-    tree_steps(2)
-    ff_from_rank((5, 6, 7))
-    act_from_z(1)
-    tree_steps(3)
-    ff_from_far((0, 8, 1, 2))
-    tree_steps(4)
-    ff_from_far((3, 4, 5))
-    act_from_x(1)
-    tree_steps(5)
-    ff_from_far((6, 7))
-
-    def sibling_wait(chip, carry):
-        for piece in range(4):
-            arrived(piece_rows(piece, 2 * chip + 1 - core), sibling_sem.at[piece, chip], sibling)
-        return carry
-
-    lax.fori_loop(0, 16, sibling_wait, 0)
-    for piece in range(4):
-        local[piece].wait()
-    keep = [
-        pltpu.make_async_copy(qkv_buf, qkv_full, keep_sem.at[0]),
-        pltpu.make_async_copy(out_buf, out_full, keep_sem.at[1]),
-    ]
-    for copy in keep:
-        copy.start()
-
-    for p in range(positions):
-
-        def project(columns, p=p):
-            qkv_rows[p, :, columns] = jnp.dot(
-                attn_in[p], qkv_buf[p, :, columns], preferred_element_type=F32
-            ).astype(BF16)
-
-        tile_loop(3 * model, 512, project)
-    pairs = pairs_of(positions)
-    probs = attention_probs(qkv_rows, halves, spread, model)
-    for index in range(len(pairs)):
-        halves[2 * index] = to_heads(probs[index].astype(BF16), spread)
-
-    def mix(rows):
-        for p in range(positions):
-            total = None
-            for index, (own, q) in enumerate(pairs):
-                if own == p:
-                    term = halves[2 * index, rows, :].astype(F32) * qkv_rows[
-                        q, rows, 2 * model :
-                    ].astype(F32)
-                    total = term if total is None else total + term
-            context[p, rows, :] = total.astype(BF16)
-
-    row_loop(act_height, 16, mix)
-    for p in range(positions):
-
-        def attend(columns, p=p):
-            resid_mid[p, :, columns] = tokens_ref[p, :, columns].astype(F32) + jnp.dot(
-                context[p], out_buf[p, :, columns], preferred_element_type=F32
-            )
-
-        tile_loop(model, 512, attend)
-
-    def second_norm(rows):
-        for p in range(positions):
-            r, _ = normed(resid_mid[p, rows, :])
-            ff_in[p, rows, :] = (r * gain_rows[positions + p : positions + p + 1, :]).astype(BF16)
-
-    row_loop(act_height, 16, second_norm)
-    act_own(0, ff_in)
-    own_rows = pltpu.make_async_copy(ff_in, act_rows(0, own_step), local_sem.at[8])
-    own_rows.start()
-    act_from_z(0)
-    act_from_x(0)
-    act_from_core(1)
-    for dzh in (0, 1):
-        for slot, step in enumerate(RANK_STEPS):
-            arrived(weight_rows(device(step, dzh, 1)), across_recv.at[dzh, slot], sibling)
-        arrived(down_rows(dzh, 1), across_recv.at[dzh, 8], sibling)
+    tree_steps(0, 1)
+    ff_from_rank(0, (1, 2, 3, 4))
+    take_gains()
+    tree_steps(0, 2)
+    ff_from_rank(0, (5, 6, 7))
+    act_from_z(1, 0)
+    tree_steps(1, 0)
+    tree_steps(0, 3)
+    ff_from_far(0, (0, 8, 1, 2))
+    tree_steps(0, 4)
+    tree_steps(0, 5)
+    tree_steps(1, 1)
+    ff_to_ranks(1)
+    tree_end(0)
+    attention(0)
+    act_own(0, 0)
+    ff_from_far(0, (3, 4, 5, 6, 7))
+    act_from_x(1, 0)
+    tree_steps(1, 2)
+    act_from_z(0, 0)
+    ff_own_far(1)
+    ff_own_across(1)
+    act_own(1, 1)
+    tree_steps(1, 3)
+    act_from_x(0, 0)
+    ff_from_rank(1, (1, 2, 3, 4))
+    tree_steps(1, 4)
+    ff_from_rank(1, (5, 6, 7))
+    tree_steps(1, 5)
+    act_from_z(1, 1)
+    tree_end(1)
+    attention(1)
+    act_own(0, 1)
+    ff_from_far(1, (0, 8, 1, 2, 3))
+    act_from_core(1, 0)
+    act_from_core(0, 0)
+    for copy in ff_local[0]:
+        copy.wait()
+    ff_end(0)
+    ff_blocks(0)
+    act_from_z(0, 1)
+    ff_from_far(1, (4, 5, 6, 7))
+    act_from_x(1, 1)
+    act_from_x(0, 1, ((0, 1, 0),))
+    ff_grads(0)
+    act_from_x(0, 1, ((1, 1, 0),))
+    for copy in ff_local[1]:
+        copy.wait()
+    act_from_core(1, 1)
+    ff_end(1)
+    stages_end()
+    for step in ((0, 0, 1), (1, 0, 1), (0, 1, 1), (1, 1, 1)):
+        act_from_core(0, 1, (step,))
+        ff_block(1, 2 * flip(zl, step[0]) + flip(x, step[1]))
+    ff_grads(1)
     for _, _, piece, offset in events:
         tree_step(piece, offset, finish=True)
-    act_from_core(0)
     for copy in sends:
         copy.wait_send()
-    for copy in local[5:] + keep + [own_rows]:
+    for copy in keep:
         copy.wait()
+    stages_end()
 
 
 def forward_gather(gains, tokens, w_qkv, w_out, gate_up_parts, w_down, grads):
     positions, act_height, model = tokens.shape
     _, height, qkv_width = w_qkv.shape
     ranks, _, _, width = gate_up_parts.shape
+    split = 4 * w_down.shape[1]
+    group_rows = ranks * act_height
     dma = pltpu.SemaphoreType.DMA
     vmem = pl.BlockSpec(memory_space=pltpu.VMEM)
     anywhere = pl.BlockSpec(memory_space=pl.ANY)
-    pair_count = len(pairs_of(positions))
     return pl.pallas_call(
         forward_kernel,
         out_shape=(
@@ -795,39 +938,49 @@
             jax.ShapeDtypeStruct((positions, act_height, model), F32),
             jax.ShapeDtypeStruct((positions, model, qkv_width), BF16),
             jax.ShapeDtypeStruct((positions, model, model), BF16),
+            jax.ShapeDtypeStruct((positions, group_rows, model), BF16),
+            jax.ShapeDtypeStruct((positions, group_rows, model), BF16),
             jax.ShapeDtypeStruct((positions, model, width), BF16),
-            jax.ShapeDtypeStruct((positions, 4 * w_down.shape[1], model), BF16),
-            jax.ShapeDtypeStruct((positions, ranks * act_height, model), BF16),
-            jax.ShapeDtypeStruct((positions, ranks * act_height, model), BF16),
+            jax.ShapeDtypeStruct((positions, split, model), BF16),
         ),
         in_specs=[anywhere, vmem] + [anywhere] * 5,
         out_specs=(vmem,) * 4 + (anywhere,) * 6,
         scratch_shapes=[
             pltpu.VMEM((positions, model, qkv_width), BF16),
             pltpu.VMEM((positions, model, model), BF16),
+            pltpu.VMEM((positions, model, width), BF16),
+            pltpu.VMEM((positions, split, model), BF16),
+            pltpu.VMEM((positions, group_rows, model), BF16),
+            pltpu.VMEM((positions, group_rows, model), BF16),
+            pltpu.VMEM((group_rows, split), BF16),
+            pltpu.VMEM((group_rows, width), BF16),
+            pltpu.VMEM((group_rows, model), BF16),
+            pltpu.VMEM((group_rows, model), BF16),
+            pltpu.VMEM((model, width), BF16),
+            pltpu.VMEM((split, model), BF16),
             pltpu.VMEM((32, 16, 128), BF16),
             pltpu.VMEM((positions, act_height, model), BF16),
-            pltpu.VMEM((positions, act_height, model), BF16),
-            pltpu.VMEM((2 * pair_count, act_height, model), BF16),
+            pltpu.VMEM((2 * positions, act_height, model), BF16),
             pltpu.VMEM((model, 128), BF16),
-            dma((4, 16)),
-            dma((4, 16)),
-            dma((4, 16, 5)),
+            dma((6, 16)),
+            dma((6, 16)),
+            dma((6, 16, 5)),
             dma((32,)),
             dma((32,)),
-            dma((8,)),
-            dma((8,)),
-            dma((9,)),
-            dma((9,)),
+            dma((2, 8)),
+            dma((2, 8)),
             dma((2, 9)),
             dma((2, 9)),
-            dma((2, 8, 3)),
-            dma((2, 8)),
-            dma((9,)),
-            dma((2,)),
+            dma((2, 2, 9)),
+            dma((2, 2, 9)),
+            dma((2, 2, 8, 3)),
+            dma((2, 2, 8)),
+            dma((13,)),
+            dma((4,)),
+            dma((2, 4)),
         ],
         compiler_params=pltpu.CompilerParams(
-            collective_id=4, has_side_effects=True, vmem_limit_bytes=56 * 2**20
+            collective_id=4, has_side_effects=True, vmem_limit_bytes=62 * 2**20
         ),
         name="forward_gather",
     )(gains, tokens, w_qkv, w_out, gate_up_parts, w_down, grads)
@@ -1285,9 +1438,10 @@
     for copy in part_copies:
         copy.wait()
     ff_first()
-    probs = attention_probs(qkv_rows, halves, spread, model)
-    for index in range(len(pairs)):
-        probs_buf[index] = probs[index]
+    for p in range(positions):
+        probs = attention_probs(qkv_rows, halves, spread, model, p)
+        for q in range(p + 1):
+            probs_buf[pairs.index((p, q))] = probs[q]
     act_third(0)
 
     def mid_back(rows):
@@ -1335,7 +1489,7 @@
             halves[2 * index, rows, :], halves[2 * index + 1, rows, :] = split_product(product)
 
     row_loop(act_height, 16, context_products)
-    d_probs = [sums_over_heads(halves, spread, index, act_height) for index in range(len(pairs))]
+    d_probs = [sums_over_heads(halves, spread, index) for index in range(len(pairs))]
     for p in range(positions):
         own = [index for index, pair in enumerate(pairs) if pair[0] == p]
         mean = functools.reduce(jnp.add, [probs_buf[index] * d_probs[index] for index in own])
@@ -1579,18 +1733,6 @@
     )
 
 
-def by_set(activations, weight):
-    return jnp.einsum("sfk,ske->sfe", activations, weight, preferred_element_type=F32)
-
-
-def by_set_back(gradients, weight):
-    return jnp.einsum("sfe,ske->sfk", gradients, weight, preferred_element_type=F32)
-
-
-def set_grad(activations, gradients):
-    return jnp.einsum("sfk,sfe->ske", activations, gradients, preferred_element_type=F32)
-
-
 def local_fast(
     tokens,
     norm_attn,
@@ -1636,25 +1778,11 @@
         resid_mid,
         qkv_full,
         out_full,
-        gate_up_full,
-        down_full,
-        ff_rows,
-        grad_rows,
+        out_part,
+        back_part,
+        gate_up_grad,
+        down_grad,
     ) = forward_gather(gains, tokens_low, w_qkv, w_out, parts, w_down, grad_low)
-    split = 4 * unit
-    gate_up = by_set(ff_rows, gate_up_full)
-    gate, up = gate_up[..., :split], gate_up[..., split:]
-    sigmoid_gate = jax.nn.sigmoid(gate)
-    silu_gate = gate * sigmoid_gate
-    hidden = (silu_gate * up).astype(BF16)
-    out_part = by_set(hidden, down_full).astype(BF16)
-    d_hidden = by_set_back(grad_rows, down_full)
-    d_gate = d_hidden * up * sigmoid_gate * (1.0 + gate * (1.0 - sigmoid_gate))
-    d_up = d_hidden * silu_gate
-    d_gate_up = jnp.concatenate([d_gate, d_up], axis=-1).astype(BF16)
-    down_grad = set_grad(hidden, grad_rows).astype(BF16)
-    gate_up_grad = set_grad(ff_rows, d_gate_up).astype(BF16)
-    back_part = by_set_back(d_gate_up, gate_up_full).astype(BF16)
     output, grad_tokens, gains_sum, share_qkv, share_out, gate_up_sum, down_sum = backward_scatter(
         tokens_low,
         grad_out,

time: 418 us -> 379 us (0.907)
  matrix products: 40.5 us -> 0 us
  Pallas kernels: 340 us -> 346 us
    dot_general x6 -> x0, matrix products: 40.5 us -> none  [the longest x2 15.3 us: by_set_back(): jnp.einsum('sfe,ske->sfk', gradients, weight, preferred_element_type=F32)]
    pallas_call x1, Pallas kernels: 176 us -> 181 us  [forward_gather(): pl.pallas_call(forward_kernel, out_shape=(jax.ShapeDtypeStruct((16, model...]
    unnamed x28 -> x14, local copies, waits for them, and re-layouts: 9.93 us -> 9.9 us
where the time goes in v4:
time: 379 us; the launch traced here: 378 us
  Pallas kernels  346 us (91%)
  local copies, waits for them, and re-layouts  26.2 us (7%)
  other arithmetic  4.27 us (1%)
    pallas_call x1, Pallas kernels, forward_gather(): pl.pallas_call(forward_kernel, out_shape=(jax.ShapeDtypeStruct((16, model...  181 us
    pallas_call x1, Pallas kernels, backward_scatter(): pl.pallas_call(backward_kernel, out_shape=(jax.ShapeDtypeStruct(act, BF16...  165 us
    convert_element_type x3, local copies, waits for them, and re-layouts, local_fast(): share_gate_up = share_gate_up.reshape(w_gate_up.shape).astype(F32)  10.1 us
    unnamed x14, local copies, waits for them, and re-layouts  9.9 us

profile of v4, /device:TPU:0, one launch (start us, length us, event | category | flops | bytes accessed | tf_op | source)
XLA Modules:
  0.0 378.1 jit_solution(1547992324310426896)
XLA Ops:
  0.6 0.0 copy-start.2
  1.4 0.8 reduce-window.8
  2.2 0.7 bitcast_subtract_fusion
  2.9 0.7 convert_divide_fusion
  3.5 0.1 select_reduce_fusion
  3.6 0.7 pad_maximum_fusion
  4.3 0.1 tile.10
  4.4 0.6 pad.4.gains_ref
  5.0 2.0 copy.36
  7.0 1.8 reshape.70
  8.8 0.9 copy.35
  9.7 1.5 reshape.71.gate_up_ref
  11.2 0.0 copy-done.2
  11.2 1.3 fusion.1
  12.5 181.5 %forward_gather.1 = (f32[16,1024]{1,0:T(8,128)}, bf16[2,128,3072]{2,1,0:T(8,128)(2,1)}, bf16[2,128,1024]{2,1,0:T(8,128)(2,1)}, f32[2,128,1024]{2,1,0:T(8,128)}, ...) custom-call(bf16[16,128]{1,0:T(8,128)(2,1)} %pad.4.gains_ref, ...), custom_call_target="tpu_custom_call" | custom-call | tf_op jit(solution)/shard_map/forward_gather/pallas_call | solution.py:932
  194.0 164.6 %backward_scatter.1 = (bf16[2,128,1024]{2,1,0:T(8,128)(2,1)}, f32[2,128,1024]{2,1,0:T(8,128)}, f32[8,128]{1,0:T(8,128)}, f32[2,32,3072]{2,1,0:T(8,128)}, f32[2,3...) custom-call(bf16[2,128,1024]{2,1,0:T(8,128)(2,1)} %bitcast.22, ...), custom_call_target="tpu_custom_call" | custom-call | tf_op jit(solution)/shard_map/backward_scatter/pallas_call | solution.py:1648
  358.7 2.4 copy.28
  361.1 3.0 copy.29
  364.1 0.8 constant_dynamic-slice_fusion
  364.8 0.6 fusion.2
  365.4 3.2 reshape.73
  368.6 0.0 copy-start.1
  368.6 0.0 copy-start.3
  368.6 3.0 copy.27
  371.5 0.0 copy-start
  371.5 4.0 %reshape.72 = f32[2,32,8192]{2,1,0:T(8,128)} reshape(f32[2,32,2,2,2,2,2,2,128]{8,7,6,5,4,3,2,1,0:T(2,128)} %copy.27) | data formatting | bytes 4194304 | tf_op jit(solution)/shard_map/convert_element_type | solution.py:1804
  375.5 0.0 copy-done.1
  375.5 0.9 copy.41
  376.4 0.0 copy-done.3
  376.4 0.7 copy.42
  377.1 0.0 copy-done
  377.1 1.0 copy.43
  (5 shorter events, 0.0 us)
Async XLA Ops:
  0.6 10.6 %copy-start.2 = (bf16[128,2,1024]{2,1,0:T(2,128)(2,1)S(1)}, bf16[128,2,1024]{2,1,0:T(2,128)(2,1)}, u32[]{:S(2)}) copy-start(bf16[128,2,1024]{2,1,0:T(2,128)(2,1)} %param.17) | copy-start | bytes 1572868
  368.6 7.0 %copy-start.1 = (f32[2,32,3072]{2,1,0:T(8,128)S(1)}, f32[2,32,3072]{2,1,0:T(8,128)}, u32[]{:S(2)}) copy-start(f32[2,32,3072]{2,1,0:T(8,128)} %get-tuple-element.73) | copy-start | bytes 2359300
  368.6 7.8 %copy-start.3 = (f32[2,32,1024]{2,1,0:T(8,128)S(1)}, f32[2,32,1024]{2,1,0:T(8,128)}, u32[]{:S(2)}) copy-start(f32[2,32,1024]{2,1,0:T(8,128)} %get-tuple-element.74) | copy-start | bytes 786436
  371.5 5.6 %copy-start = (f32[2,128,1024]{2,1,0:T(8,128)S(1)}, f32[2,128,1024]{2,1,0:T(8,128)}, u32[]{:S(2)}) copy-start(f32[2,128,1024]{2,1,0:T(8,128)} %get-tuple-element.77) | copy-start | bytes 3145732

commit v5 on v4

--- a/solution.py
+++ b/solution.py
@@ -463,15 +463,89 @@
     return [power / total for power in powers]
 
 
+FORWARD_STEPS = [
+    ("tree", 3, 0, 0, 0), ("tree", 5, 0, 0, 0), ("tree", 0, 0, 0, 0), ("tree", 2, 0, 0, 0),
+    ("tree", 5, 1, 0, 0), ("parts",), ("to_rank", 0, 7), ("tree", 0, -1, 0, 0), ("tree", 0, 0, 0, 1),
+    ("to_rank", 0, 3), ("tree", 2, 0, 0, 1), ("tree", 1, 0, 0, 0), ("tree", 0, -2, 0, 0), ("cot",),
+    ("rank_far", 0, 3), ("tree", 0, 0, 1, 0), ("tree", 4, 0, 0, 0), ("to_rank", 1, 4), ("tree", 1, -1, 0, 0),
+    ("to_rank", 0, 2), ("to_rank", 1, 2), ("tree", 2, 0, 1, 1), ("tree", 0, 1, 0, 0), ("tree", 2, 0, 1, 0),
+    ("own_across", 0, 0), ("tree", 1, 1, 0, 0), ("tree", 2, -1, 0, 0), ("tree", 0, -1, 0, 1),
+    ("tree", 0, -3, 0, 0), ("to_rank", 0, 1), ("tree", 0, -2, 0, 1), ("tree", 1, 0, 1, 0),
+    ("tree", 2, 1, 0, 1), ("tree", 0, 2, 0, 0), ("grads", 0), ("to_rank", 0, 6), ("rank_far", 0, 1),
+    ("own_across", 1, 8), ("tree", 2, -2, 0, 0), ("own_across", 0, 8), ("tree", 2, -1, 1, 0),
+    ("to_rank", 0, 5), ("rank_far", 0, 2), ("tree", 3, 0, 0, 1), ("own_far", 0, 8), ("tree", 1, -1, 1, 0),
+    ("tree", 2, -1, 1, 1), ("far_across", 0, 2), ("rank_far", 0, 6), ("tree", 3, 0, 1, 1), ("gains",),
+    ("tree", 2, 1, 0, 0), ("tree", 1, 2, 0, 0), ("rank_across", 0, 3), ("tree", 1, -2, 0, 0),
+    ("tree", 0, 3, 0, 0), ("tree", 2, 1, 1, 1), ("tree", 5, 0, 0, 1), ("tree", 2, 2, 0, 0), ("to_rank", 0, 4),
+    ("tree", 1, 2, 1, 0), ("tree", 3, -1, 0, 0), ("tree", 4, 1, 0, 0), ("tree", 0, -1, 1, 1),
+    ("tree", 0, 2, 0, 1), ("rank_far", 0, 7), ("rank_far", 0, 4), ("far_across", 0, 3), ("tree", 2, 2, 1, 1),
+    ("tree", 1, 3, 0, 0), ("tree", 1, 1, 1, 0), ("rank_across", 0, 1), ("to_rank", 1, 6),
+    ("tree", 2, -3, 0, 0), ("tree", 0, -3, 0, 1), ("tree", 0, 0, 1, 1), ("tree", 1, 2, 0, 1),
+    ("tree", 2, 1, 1, 0), ("tree", 2, -1, 0, 1), ("tree", 1, 0, 1, 1), ("tree", 2, -2, 1, 0),
+    ("tree", 2, 3, 1, 1), ("far_across", 0, 6), ("own_far", 0, 0), ("tree", 1, -2, 0, 1),
+    ("tree", 0, 2, 1, 1), ("tree", 4, 2, 0, 0), ("tree", 1, 3, 0, 1), ("tree", 3, 1, 0, 0),
+    ("tree", 2, -2, 1, 1), ("rank_far", 0, 5), ("tree", 0, -2, 1, 1), ("tree", 0, 1, 1, 0),
+    ("tree", 5, 0, 1, 0), ("far_across", 0, 1), ("tree", 1, -2, 1, 0), ("tree", 1, 2, 1, 1),
+    ("tree", 2, 2, 1, 0), ("tree", 1, -3, 0, 0), ("to_rank", 1, 5), ("tree", 0, -1, 1, 0),
+    ("tree", 3, -2, 0, 0), ("tree", 1, 3, 1, 0), ("act_z", 1, 0), ("tree", 0, 1, 0, 1), ("tree", 3, 1, 0, 1),
+    ("tree", 2, 2, 0, 1), ("tree", 0, 3, 1, 0), ("tree", 4, -1, 0, 0), ("tree", 2, -2, 0, 1),
+    ("tree", 2, -3, 1, 1), ("tree", 0, -3, 1, 1), ("far_across", 0, 7), ("tree", 0, -3, 1, 0),
+    ("tree", 0, 2, 1, 0), ("tree", 3, 1, 1, 0), ("tree", 2, -3, 1, 0), ("tree", 1, -1, 0, 1),
+    ("tree", 1, -3, 1, 0), ("rank_across", 0, 7), ("far_across", 0, 0), ("tree", 1, 3, 1, 1),
+    ("tree", 3, 2, 0, 0), ("tree", 2, 3, 0, 0), ("rank_across", 0, 6), ("tree", 5, 1, 1, 0),
+    ("tree", 0, 3, 0, 1), ("tree", 1, -3, 0, 1), ("tree", 3, -2, 0, 1), ("act_c", 1, 0, 0, 0),
+    ("tree", 4, 0, 1, 0), ("tree", 5, 0, 1, 1), ("tree", 4, -2, 0, 0), ("far_across", 0, 4), ("grads", 1),
+    ("tree", 2, -3, 0, 1), ("tree", 5, -1, 1, 0), ("tree", 1, -3, 1, 1), ("act_c", 1, 0, 1, 0),
+    ("far_across", 0, 8), ("tree", 5, 1, 0, 1), ("far_across", 0, 5), ("tree", 1, -1, 1, 1),
+    ("tree", 1, 0, 0, 1), ("rank_across", 0, 5), ("tree", 5, -1, 0, 0), ("tree", 3, -3, 0, 0),
+    ("to_rank", 1, 1), ("act_x", 1, 0, 1), ("tree", 1, 1, 0, 1), ("tree", 5, 2, 1, 0), ("own_far", 1, 8),
+    ("act_x", 1, 0, 0), ("tree", 5, -1, 0, 1), ("tree", 4, -3, 0, 0), ("tree", 0, 1, 1, 1),
+    ("tree", 1, 1, 1, 1), ("tree", 2, 3, 0, 1), ("tree", 3, 1, 1, 1), ("tree", 3, -1, 0, 1),
+    ("tree", 4, -1, 1, 0), ("tree", 3, -3, 0, 1), ("tree", 3, 2, 0, 1), ("own_across", 1, 0),
+    ("tree", 1, -2, 1, 1), ("to_rank", 1, 3), ("tree", 3, 0, 1, 0), ("tree", 0, 3, 1, 1),
+    ("tree", 0, -2, 1, 0), ("tree", 3, 2, 1, 0), ("tree", 2, 3, 1, 0), ("tree", 3, 3, 0, 0), ("tree_end", 0),
+    ("tree", 4, -1, 1, 1), ("to_rank", 1, 7), ("attention", 0), ("tree", 4, 3, 0, 0), ("act_x", 0, 0, 0),
+    ("tree", 4, 3, 1, 0), ("tree", 3, -3, 1, 0), ("tree", 4, 3, 0, 1), ("tree", 4, -2, 1, 0),
+    ("tree", 3, 3, 0, 1), ("tree", 5, -1, 1, 1), ("rank_far", 1, 7), ("rank_across", 0, 2),
+    ("tree", 4, 2, 1, 0), ("tree", 5, 1, 1, 1), ("tree", 5, 3, 1, 0), ("tree", 4, -3, 0, 1),
+    ("rank_across", 0, 4), ("tree", 4, -3, 1, 0), ("own_far", 1, 0), ("rank_far", 1, 2), ("tree", 4, 3, 1, 1),
+    ("rank_across", 1, 7), ("far_across", 1, 8), ("tree", 4, 1, 1, 0), ("act_z", 1, 1), ("tree", 5, -2, 0, 1),
+    ("tree", 4, -3, 1, 1), ("tree", 3, 2, 1, 1), ("tree", 5, -2, 0, 0), ("act_z", 0, 0), ("tree", 4, 2, 1, 1),
+    ("tree", 5, 2, 0, 0), ("rank_far", 1, 1), ("ff_end", 0), ("act_c", 0, 0, 1, 0), ("rank_across", 1, 2),
+    ("tree", 4, 0, 0, 1), ("tree", 4, 1, 1, 1), ("rank_far", 1, 5), ("act_x", 1, 1, 0), ("tree", 3, -1, 1, 0),
+    ("tree", 5, 2, 1, 1), ("tree", 5, 3, 0, 0), ("far_across", 1, 7), ("tree", 3, 3, 1, 1),
+    ("tree", 3, -1, 1, 1), ("tree", 4, -2, 1, 1), ("act_c", 1, 0, 0, 1), ("act_c", 0, 0, 0, 0),
+    ("tree", 4, 0, 1, 1), ("rank_far", 1, 3), ("act_c", 1, 0, 1, 1), ("tree", 3, -2, 1, 0),
+    ("tree", 5, -2, 1, 0), ("rank_far", 1, 4), ("far_across", 1, 0), ("tree", 5, -3, 0, 0),
+    ("tree", 4, 1, 0, 1), ("tree", 3, -2, 1, 1), ("act_c", 1, 1, 1, 0), ("rank_far", 1, 6),
+    ("tree", 4, -1, 0, 1), ("tree", 5, 2, 0, 1), ("tree", 5, -3, 1, 0), ("act_c", 0, 0, 0, 1),
+    ("far_across", 1, 2), ("act_c", 1, 1, 0, 0), ("tree", 5, -3, 0, 1), ("tree", 5, -2, 1, 1),
+    ("tree", 3, 3, 1, 0), ("rank_across", 1, 6), ("rank_across", 1, 3), ("tree", 5, 3, 1, 1),
+    ("rank_across", 1, 4), ("block", 0, 1), ("tree", 4, 2, 0, 1), ("tree", 5, 3, 0, 1), ("tree", 4, -2, 0, 1),
+    ("tree", 3, -3, 1, 1), ("far_across", 1, 1), ("tree", 5, -3, 1, 1), ("block", 0, 0),
+    ("rank_across", 1, 5), ("act_x", 1, 1, 1), ("tree_end", 1), ("attention", 1), ("far_across", 1, 3),
+    ("rank_across", 1, 1), ("act_x", 0, 0, 1), ("block", 0, 2), ("far_across", 1, 5), ("act_c", 0, 0, 1, 1),
+    ("block", 0, 3), ("down_grad", 0), ("act_c", 1, 1, 0, 1), ("far_across", 1, 6), ("act_x", 0, 1, 0),
+    ("act_c", 1, 1, 1, 1), ("act_z", 0, 1), ("far_across", 1, 4), ("gate_grad", 0), ("act_c", 0, 1, 0, 1),
+    ("act_c", 0, 1, 0, 0), ("ff_end", 1), ("act_c", 0, 1, 1, 0), ("block", 1, 1), ("block", 1, 2),
+    ("act_x", 0, 1, 1), ("block", 1, 0), ("act_c", 0, 1, 1, 1), ("block", 1, 3), ("down_grad", 1),
+    ("gate_grad", 1),
+]
+
+
 def forward_kernel(
-    gains_ref,
+    valid_ref,
+    lengths_ref,
+    norm_attn_ref,
+    norm_ff_ref,
     tokens_ref,
+    cot_ref,
     qkv_ref,
     out_ref,
     gate_up_ref,
     down_ref,
-    grads_ref,
     gain_rows,
+    cot_rows,
     qkv_rows,
     context,
     resid_mid,
@@ -493,7 +567,11 @@
     back_stage,
     gate_up_stage,
     down_stage,
+    gains_own,
     gains_all,
+    gate_up_raw,
+    gate_up_parts,
+    grads_own,
     attn_in,
     halves,
     spread,
@@ -518,8 +596,8 @@
     me = 2 * (z * 4 + y * 2 + x) + core
     zh, zl, member, rank, device, far, across = group_place(z, y, x, core)
     own_step = (0, 0, 0)
-    positions, act_height, model = tokens_ref.shape
-    height = gate_up_ref.shape[2]
+    act_height, positions, model = tokens_ref.shape
+    height = gate_up_ref.shape[1]
     down_height = down_ref.shape[1]
     split = 4 * down_height
     sibling = neighbour("s", z, y, x, core)
@@ -597,7 +675,7 @@
     def gains_copy(step):
         other = lax.rem(me + step, 32)
         return push(
-            gains_ref,
+            gains_own,
             gains_all.at[me],
             gains_send.at[step],
             gains_recv.at[me],
@@ -651,7 +729,7 @@
         )
 
     def act_own(which, s):
-        source = act_rows(0, s, own_step) if which == 0 else grads_ref.at[s]
+        source = act_rows(0, s, own_step) if which == 0 else grads_own.at[s]
         for hop in (0, 1, 2):
             send_act(which, s, own_step, source, hop)
 
@@ -661,56 +739,68 @@
         send_act(which, s, step, act_rows(which, s, step), 1)
         send_act(which, s, step, act_rows(which, s, step), 2)
 
-    def act_from_x(which, s, steps=((0, 1, 0), (1, 1, 0))):
-        for step in steps:
-            wait_act(which, s, step)
-            send_act(which, s, step, act_rows(which, s, step), 2)
-
-    def act_from_core(which, s, steps=((0, 0, 1), (1, 0, 1), (0, 1, 1), (1, 1, 1))):
-        for step in steps:
-            wait_act(which, s, step)
+    def act_from_x(which, s, dl):
+        wait_act(which, s, (dl, 1, 0))
+        send_act(which, s, (dl, 1, 0), act_rows(which, s, (dl, 1, 0)), 2)
+
+    def act_from_core(which, s, dl, dx):
+        wait_act(which, s, (dl, dx, 1))
 
     def mine(s):
-        return gate_up_ref.at[rank(own_step), s]
-
-    def ff_to_ranks(s):
-        for slot, step in enumerate(RANK_STEPS):
-            if step != own_step:
-                start(
-                    push(
-                        gate_up_ref.at[rank(step), s],
-                        weight_rows(s, device(own_step)),
-                        rank_send.at[s, slot],
-                        rank_recv.at[s, slot],
-                        member(step),
-                    )
-                )
-
-    def ff_own_far(s):
-        start(push(mine(s), weight_rows(s, device(own_step)), far_send.at[s, 0], far_recv.at[s, 0], far))
-        start(push(down_ref.at[s], down_rows(s, 0, 0), far_send.at[s, 8], far_recv.at[s, 8], far))
-
-    def ff_own_across(s):
-        for slot, source, target in (
-            (0, mine(s), weight_rows(s, device(own_step))),
-            (8, down_ref.at[s], down_rows(s, 0, 0)),
-        ):
-            start(push(source, target, across_send.at[s, 0, slot], across_recv.at[s, 0, slot], across))
-
-    def ff_from_rank(s, slots):
-        for slot in slots:
-            block = weight_rows(s, device(RANK_STEPS[slot]))
-            arrived(block, rank_recv.at[s, slot], sibling)
-            start(push(block, block, far_send.at[s, slot], far_recv.at[s, slot], far))
-            start(push(block, block, across_send.at[s, 0, slot], across_recv.at[s, 0, slot], across))
-
-    def ff_from_far(s, slots):
-        for slot in slots:
-            block = down_rows(s, 1, 0) if slot == 8 else weight_rows(s, device(RANK_STEPS[slot], 1, 0))
-            arrived(block, far_recv.at[s, slot], sibling)
-            start(push(block, block, across_send.at[s, 1, slot], across_recv.at[s, 1, slot], across))
+        return gate_up_parts.at[rank(own_step), s]
+
+    def ff_source(s, slot):
+        return down_ref.at[s] if slot == 8 else mine(s)
+
+    def ff_rows(s, slot, dzh):
+        return down_rows(s, dzh, 0) if slot == 8 else weight_rows(s, device(RANK_STEPS[slot], dzh, 0))
+
+    def to_rank(s, slot):
+        step = RANK_STEPS[slot]
+        start(
+            push(
+                gate_up_parts.at[rank(step), s],
+                weight_rows(s, device(own_step)),
+                rank_send.at[s, slot],
+                rank_recv.at[s, slot],
+                member(step),
+            )
+        )
+
+    def send_far(s, slot, source):
+        start(push(source, ff_rows(s, slot, 0), far_send.at[s, slot], far_recv.at[s, slot], far))
+
+    def send_across(s, slot, source, dzh):
+        start(
+            push(
+                source,
+                ff_rows(s, slot, dzh),
+                across_send.at[s, dzh, slot],
+                across_recv.at[s, dzh, slot],
+                across,
+            )
+        )
+
+    def own_far(s, slot):
+        send_far(s, slot, ff_source(s, slot))
+
+    def own_across(s, slot):
+        send_across(s, slot, ff_source(s, slot), 0)
+
+    def rank_far(s, slot):
+        arrived(ff_rows(s, slot, 0), rank_recv.at[s, slot], sibling)
+        send_far(s, slot, ff_rows(s, slot, 0))
+
+    def rank_across(s, slot):
+        send_across(s, slot, ff_rows(s, slot, 0), 0)
+
+    def far_across(s, slot):
+        arrived(ff_rows(s, slot, 1), far_recv.at[s, slot], sibling)
+        send_across(s, slot, ff_rows(s, slot, 1), 1)
 
     def ff_end(s):
+        for copy in ff_local[s]:
+            copy.wait()
         for dzh in (0, 1):
             for slot, step in enumerate(RANK_STEPS):
                 arrived(weight_rows(s, device(step, dzh, 1)), across_recv.at[s, dzh, slot], sibling)
@@ -722,10 +812,64 @@
             [
                 pltpu.make_async_copy(mine(s), weight_rows(s, device(own_step)), local_sem.at[7 + 3 * s]),
                 pltpu.make_async_copy(down_ref.at[s], down_rows(s, 0, 0), local_sem.at[8 + 3 * s]),
-                pltpu.make_async_copy(grads_ref.at[s], act_rows(1, s, own_step), local_sem.at[9 + 3 * s]),
+                pltpu.make_async_copy(grads_own.at[s], act_rows(1, s, own_step), local_sem.at[9 + 3 * s]),
             ]
         )
-    gains_local = pltpu.make_async_copy(gains_ref, gains_all.at[me], local_sem.at[6])
+    gains_local = pltpu.make_async_copy(gains_own, gains_all.at[me], local_sem.at[6])
+
+    def gains_begin():
+        places = 128 // norm_attn_ref.shape[1]
+        lane = lax.broadcasted_iota(jnp.int32, (positions, 128), 1) // norm_attn_ref.shape[1]
+        gains_own[...] = jnp.zeros_like(gains_own)
+        for index, source in enumerate((norm_attn_ref, norm_ff_ref)):
+            tiled = jnp.concatenate([source[...].astype(F32)] * places, axis=1)
+            gains_own[index * positions : (index + 1) * positions, :] = jnp.where(
+                lane == lax.rem(me, places), tiled, 0.0
+            ).astype(BF16)
+        lax.fori_loop(1, 32, gains_start, 0)
+        gains_local.start()
+
+    raw_copy = pltpu.make_async_copy(gate_up_ref, gate_up_raw, local_sem.at[13])
+
+    def part_units():
+        raw_copy.wait()
+        unit = down_height
+        for number in range(8):
+            low, rest = divmod(number, 4)
+            for s in range(positions):
+                for side in (0, 1):
+                    for group in range(4):
+                        zh_part, y_part = divmod(group, 2)
+                        block = 32 * side + 16 * zh_part + 8 * low + 4 * y_part + rest
+                        gate_up_parts[number, s, :, (4 * side + group) * unit : (4 * side + group + 1) * unit] = (
+                            gate_up_raw[s, :, block * unit : (block + 1) * unit]
+                        )
+        for s in range(positions):
+            ff_local[s][0].start()
+            ff_local[s][1].start()
+
+    def weigh():
+        def one(rows):
+            slot = lax.broadcasted_iota(jnp.int32, (16, 128), 0) + rows.start
+            frame = me * act_height + slot
+            weight = jnp.zeros((16, 128), F32)
+            first = 0
+            for item in range(lengths_ref.shape[0]):
+                length = lengths_ref[item]
+                inside = (frame >= first) & (frame < first + length)
+                share = 8.0 * act_height / jnp.full((16, 128), length, jnp.int32).astype(F32)
+                weight = weight + jnp.where(inside, share, 0.0)
+                first = first + length
+            weight = jnp.where(slot < valid_ref[0], weight, 0.0)[:, :1]
+            values = cot_ref[rows].astype(F32)
+            for p in range(positions):
+                grads = values[:, p, :] * weight
+                cot_rows[p, rows, :] = grads
+                grads_own[p, rows, :] = grads.astype(BF16)
+
+        row_loop(act_height, 16, one)
+        for s in range(positions):
+            ff_local[s][2].start()
 
     def take_gains():
         lax.fori_loop(1, 32, gains_wait, 0)
@@ -737,8 +881,10 @@
             gain_rows[:, 128 * block : 128 * block + 128] = total
 
         def first_norm(rows):
+            values = tokens_ref[rows].astype(F32)
             for p in range(positions):
-                r, _ = normed(tokens_ref[p, rows, :].astype(F32))
+                resid_mid[p, rows, :] = values[:, p, :]
+                r, _ = normed(values[:, p, :])
                 attn_in[p, rows, :] = (r * gain_rows[p : p + 1, :]).astype(BF16)
 
         row_loop(act_height, 16, first_norm)
@@ -771,9 +917,7 @@
         row_loop(act_height, 16, mix)
 
         def attend(columns):
-            resid_mid[p, :, columns] = tokens_ref[p, :, columns].astype(F32) + dot(
-                context[p], out_buf[p, :, columns]
-            )
+            resid_mid[p, :, columns] += dot(context[p], out_buf[p, :, columns])
 
         tile_loop(model, 512, attend)
 
@@ -811,106 +955,80 @@
                 d_gate_up[rows, :], gate_up_buf[s, columns, :]
             ).astype(BF16)
 
-    def ff_blocks(s):
-        def one(number, carry):
-            ff_block(s, number)
-            return carry
-
-        lax.fori_loop(0, 4, one, 0)
-
     stages = []
 
-    def stage_out(s, first):
-        chosen = (
-            [(out_stage, ff_out, 0), (back_stage, ff_back, 1)]
-            if first
-            else [(gate_up_stage, gate_up_grad, 2), (down_stage, down_grad, 3)]
-        )
-        for source, target, slot in chosen:
+    def stage_out(s, *slots):
+        for slot in slots:
+            source, target = (
+                (out_stage, ff_out),
+                (back_stage, ff_back),
+                (gate_up_stage, gate_up_grad),
+                (down_stage, down_grad),
+            )[slot]
             stages.append(pltpu.make_async_copy(source, target.at[s], stage_sem.at[s, slot]))
             stages[-1].start()
 
-    def ff_grads(s):
-        stage_out(s, True)
+    def gate_grad(s):
+        stage_out(s, 0, 1)
 
         def gate_up_tile(columns):
             gate_up_stage[:, columns] = dot_grad(rows_buf[s], d_gate_up[:, columns]).astype(BF16)
 
+        tile_loop(2 * split, 256, gate_up_tile)
+        stage_out(s, 2)
+
+    def down_weights_grad(s):
         def down_tile(columns):
             down_stage[:, columns] = dot_grad(hidden[...], grads_buf[s, :, columns]).astype(BF16)
 
-        tile_loop(2 * split, 256, gate_up_tile)
         tile_loop(model, 256, down_tile)
-        stage_out(s, False)
+        stage_out(s, 3)
 
     def stages_end():
         while stages:
             stages.pop(0).wait()
 
-    tree_steps(0, 0)
-    lax.fori_loop(1, 32, gains_start, 0)
-    ff_to_ranks(0)
-    ff_own_far(0)
-    ff_own_across(0)
-    act_own(1, 0)
-    for copy in tree_own + ff_local[0] + ff_local[1] + [gains_local]:
+    for copy in tree_own:
         copy.start()
+    raw_copy.start()
+    gains_begin()
     make_spread(spread)
-    tree_steps(0, 1)
-    ff_from_rank(0, (1, 2, 3, 4))
-    take_gains()
-    tree_steps(0, 2)
-    ff_from_rank(0, (5, 6, 7))
-    act_from_z(1, 0)
-    tree_steps(1, 0)
-    tree_steps(0, 3)
-    ff_from_far(0, (0, 8, 1, 2))
-    tree_steps(0, 4)
-    tree_steps(0, 5)
-    tree_steps(1, 1)
-    ff_to_ranks(1)
-    tree_end(0)
-    attention(0)
-    act_own(0, 0)
-    ff_from_far(0, (3, 4, 5, 6, 7))
-    act_from_x(1, 0)
-    tree_steps(1, 2)
-    act_from_z(0, 0)
-    ff_own_far(1)
-    ff_own_across(1)
-    act_own(1, 1)
-    tree_steps(1, 3)
-    act_from_x(0, 0)
-    ff_from_rank(1, (1, 2, 3, 4))
-    tree_steps(1, 4)
-    ff_from_rank(1, (5, 6, 7))
-    tree_steps(1, 5)
-    act_from_z(1, 1)
-    tree_end(1)
-    attention(1)
-    act_own(0, 1)
-    ff_from_far(1, (0, 8, 1, 2, 3))
-    act_from_core(1, 0)
-    act_from_core(0, 0)
-    for copy in ff_local[0]:
-        copy.wait()
-    ff_end(0)
-    ff_blocks(0)
-    act_from_z(0, 1)
-    ff_from_far(1, (4, 5, 6, 7))
-    act_from_x(1, 1)
-    act_from_x(0, 1, ((0, 1, 0),))
-    ff_grads(0)
-    act_from_x(0, 1, ((1, 1, 0),))
-    for copy in ff_local[1]:
-        copy.wait()
-    act_from_core(1, 1)
-    ff_end(1)
-    stages_end()
-    for step in ((0, 0, 1), (1, 0, 1), (0, 1, 1), (1, 1, 1)):
-        act_from_core(0, 1, (step,))
-        ff_block(1, 2 * flip(zl, step[0]) + flip(x, step[1]))
-    ff_grads(1)
+    chips = ((0, 0), (1, 0), (0, 1), (1, 1))
+
+    def block(s, order):
+        if s > 0 and order == chosen_first[0]:
+            stages_end()
+        ff_block(s, 2 * flip(zl, chips[order][0]) + flip(x, chips[order][1]))
+
+    def attend_and_send(s):
+        attention(s)
+        act_own(0, s)
+
+    chosen_first = [step[2] for step in FORWARD_STEPS if step[:2] == ("block", 1)]
+    kinds = dict(
+        tree=lambda piece, dz, dy, dx: tree_step(piece, (dz, dy, dx)),
+        tree_end=tree_end,
+        gains=take_gains,
+        parts=part_units,
+        cot=weigh,
+        attention=attend_and_send,
+        grads=lambda s: act_own(1, s),
+        act_z=act_from_z,
+        act_x=act_from_x,
+        act_c=act_from_core,
+        to_rank=to_rank,
+        own_far=own_far,
+        own_across=own_across,
+        rank_far=rank_far,
+        rank_across=rank_across,
+        far_across=far_across,
+        ff_end=ff_end,
+        block=block,
+        gate_grad=gate_grad,
+        down_grad=down_weights_grad,
+    )
+    for kind, *numbers in FORWARD_STEPS:
+        kinds[kind](*numbers)
     for _, _, piece, offset in events:
         tree_step(piece, offset, finish=True)
     for copy in sends:
@@ -920,19 +1038,21 @@
     stages_end()
 
 
-def forward_gather(gains, tokens, w_qkv, w_out, gate_up_parts, w_down, grads):
-    positions, act_height, model = tokens.shape
+def forward_gather(valid, lengths, norm_attn, norm_ff, tokens, cot, w_qkv, w_out, w_gate_up, w_down):
+    act_height, positions, model = tokens.shape
     _, height, qkv_width = w_qkv.shape
-    ranks, _, _, width = gate_up_parts.shape
-    split = 4 * w_down.shape[1]
+    unit = w_down.shape[1]
+    ranks, split, width = 8, 4 * unit, 8 * unit
     group_rows = ranks * act_height
     dma = pltpu.SemaphoreType.DMA
     vmem = pl.BlockSpec(memory_space=pltpu.VMEM)
+    smem = pl.BlockSpec(memory_space=pltpu.SMEM)
     anywhere = pl.BlockSpec(memory_space=pl.ANY)
     return pl.pallas_call(
         forward_kernel,
         out_shape=(
             jax.ShapeDtypeStruct((16, model), F32),
+            jax.ShapeDtypeStruct((positions, act_height, model), F32),
             jax.ShapeDtypeStruct((positions, act_height, 3 * model), BF16),
             jax.ShapeDtypeStruct((positions, act_height, model), BF16),
             jax.ShapeDtypeStruct((positions, act_height, model), F32),
@@ -943,8 +1063,8 @@
             jax.ShapeDtypeStruct((positions, model, width), BF16),
             jax.ShapeDtypeStruct((positions, split, model), BF16),
         ),
-        in_specs=[anywhere, vmem] + [anywhere] * 5,
-        out_specs=(vmem,) * 4 + (anywhere,) * 6,
+        in_specs=[smem] * 2 + [vmem] * 4 + [anywhere] * 4,
+        out_specs=(vmem,) * 5 + (anywhere,) * 6,
         scratch_shapes=[
             pltpu.VMEM((positions, model, qkv_width), BF16),
             pltpu.VMEM((positions, model, model), BF16),
@@ -958,7 +1078,11 @@
             pltpu.VMEM((group_rows, model), BF16),
             pltpu.VMEM((model, width), BF16),
             pltpu.VMEM((split, model), BF16),
+            pltpu.VMEM((16, 128), BF16),
             pltpu.VMEM((32, 16, 128), BF16),
+            pltpu.VMEM(w_gate_up.shape, BF16),
+            pltpu.VMEM((ranks, positions, height, width), BF16),
+            pltpu.VMEM((positions, act_height, model), BF16),
             pltpu.VMEM((positions, act_height, model), BF16),
             pltpu.VMEM((2 * positions, act_height, model), BF16),
             pltpu.VMEM((model, 128), BF16),
@@ -975,7 +1099,7 @@
             dma((2, 2, 9)),
             dma((2, 2, 8, 3)),
             dma((2, 2, 8)),
-            dma((13,)),
+            dma((14,)),
             dma((4,)),
             dma((2, 4)),
         ],
@@ -983,7 +1107,7 @@
             collective_id=4, has_side_effects=True, vmem_limit_bytes=62 * 2**20
         ),
         name="forward_gather",
-    )(gains, tokens, w_qkv, w_out, gate_up_parts, w_down, grads)
+    )(valid, lengths, norm_attn, norm_ff, tokens, cot, w_qkv, w_out, w_gate_up, w_down)
 
 
 def slot_index(order, direction, offset, z, y, x):
@@ -1024,10 +1148,11 @@
     down_ref,
     output,
     grad_tokens,
-    gains_sum,
+    norm_attn_sum,
+    norm_ff_sum,
     qkv_sum,
     attn_out_sum,
-    gate_up_sum,
+    gate_up_total,
     down_sum,
     act_own,
     core_buf,
@@ -1061,6 +1186,8 @@
     gain_acc,
     gains_part,
     gains_buf,
+    gains_sum,
+    gate_up_sum,
     core_send,
     core_recv,
     x_send,
@@ -1087,7 +1214,7 @@
     me = 2 * (z * 4 + y * 2 + x) + core
     zh, zl, member, rank, device, far, across = group_place(z, y, x, core)
     own_step = (0, 0, 0)
-    positions, act_height, model = tokens_ref.shape
+    act_height, positions, model = tokens_ref.shape
     sets = positions
     height = qkv_sum.shape[1]
     down_height = down_sum.shape[1]
@@ -1168,6 +1295,17 @@
             1, s, flip(zl, step[0]), pl.ds(pl.multiple_of(number * height, height), height)
         ]
 
+    def place_units(step, s, source):
+        unit = down_height
+        for side in (0, 1):
+            for group in range(4):
+                zh_part, y_part = divmod(group, 2)
+                number = 8 * flip(zl, step[0]) + 2 * flip(x, step[1]) + flip(core, step[2])
+                left = (32 * side + 16 * zh_part + 4 * y_part + number) * unit
+                gate_up_total[s, :, pl.ds(pl.multiple_of(left, unit), unit)] = source[
+                    :, (4 * side + group) * unit : (4 * side + group + 1) * unit
+                ].astype(F32)
+
     def ff_second():
         for s in range(sets):
             for low in (0, 1):
@@ -1186,7 +1324,7 @@
                             member(step),
                         )
                     )
-            add_into(gate_up_sum.at[rank(own_step), s], [share(own_step, s)])
+            place_units(own_step, s, share(own_step, s))
             arrived(across_down.at[1, s], across_recv.at[1, s, 2], across)
             arrived(far_down.at[s], far_recv.at[s, 2], far)
             add_into(down_sum.at[s], [across_down.at[1, s], far_down.at[s], down_own.at[1, s]])
@@ -1195,7 +1333,9 @@
         for slot, step in enumerate(RANK_STEPS):
             for s in range(sets):
                 if step != own_step:
-                    arrived(gate_up_sum.at[rank(step), s], rank_recv.at[slot, s], member(step))
+                    block = gate_up_sum.at[rank(step), s]
+                    arrived(block, rank_recv.at[slot, s], member(step))
+                    place_units(step, s, block)
 
     acts = [back_ref, out_ref]
 
@@ -1407,8 +1547,9 @@
         return context[p, :, 128 * block : 128 * block + 128].astype(F32)
 
     def attn_norm(rows):
+        values = tokens_ref[rows].astype(F32)
         for p in range(positions):
-            r, _ = normed(tokens_ref[p, rows, :].astype(F32))
+            r, _ = normed(values[:, p, :])
             d_rows[p, rows, :] = r * gain_rows[p : p + 1, :]
 
     row_loop(act_height, 16, attn_norm)
@@ -1581,11 +1722,12 @@
     tree_steps((0, 1, 2, 3), (3,))
 
     def attn_back(rows):
+        values = tokens_ref[rows].astype(F32)
         for p in range(positions):
-            r, inverse = normed(tokens_ref[p, rows, :].astype(F32))
+            r, inverse = normed(values[:, p, :])
             d_attn_in = d_rows[p, rows, :]
             gain_acc[p] += r * d_attn_in
-            grad_tokens[p, rows, :] = d_mid[p, rows, :] + norm_back(
+            grad_tokens[rows, p, :] = d_mid[p, rows, :] + norm_back(
                 r, inverse, d_attn_in * gain_rows[p : p + 1, :]
             )
 
@@ -1600,13 +1742,15 @@
     act_third(1)
 
     def finish_output(rows):
+        rounded = []
         for p in range(positions):
             total = (
                 core_buf[1, 0, 0, p, rows, :].astype(F32)
                 + x_buf[1, 0, p, rows, :].astype(F32)
                 + z_buf[1, p, rows, :].astype(F32)
             )
-            output[p, rows, :] = (resid_mid[p, rows, :] + total).astype(BF16)
+            rounded.append(resid_mid[p, rows, :] + total)
+        output[rows] = jnp.stack(rounded, axis=1).astype(BF16)
 
     row_loop(act_height, 16, finish_output)
     tree_steps((0, 1, 2, 3), (1,))
@@ -1614,6 +1758,18 @@
     ff_last()
     gains_sum[...] = gains_part[lax.div(me, 4)]
     lax.fori_loop(1, 32, gains_wait, 0)
+    own_gain = norm_attn_sum.shape[1]
+    for index, target in enumerate((norm_attn_sum, norm_ff_sum)):
+        picked = jnp.zeros(target.shape, F32)
+        for place in range(128 // own_gain):
+            picked = picked + jnp.where(
+                lax.rem(me, 128 // own_gain) == place,
+                gains_sum[
+                    index * positions : (index + 1) * positions, place * own_gain : (place + 1) * own_gain
+                ],
+                0.0,
+            )
+        target[...] = picked
     for _, _, piece, offset in events:
         if hops(offset) > 0:
             maybe(offset_exists(offset, z), tree_copy(piece, offset).wait_send)
@@ -1635,7 +1791,7 @@
     gate_up_grad,
     down_grad,
 ):
-    sets, act_height, model = tokens.shape
+    act_height, sets, model = tokens.shape
     width = gate_up_grad.shape[2]
     height = model // 32
     down_height = down_grad.shape[1] // 4
@@ -1648,16 +1804,17 @@
     return pl.pallas_call(
         backward_kernel,
         out_shape=(
-            jax.ShapeDtypeStruct(act, BF16),
-            jax.ShapeDtypeStruct(act, F32),
-            jax.ShapeDtypeStruct((8, 128), F32),
+            jax.ShapeDtypeStruct(tokens.shape, BF16),
+            jax.ShapeDtypeStruct(tokens.shape, F32),
+            jax.ShapeDtypeStruct((sets, height), F32),
+            jax.ShapeDtypeStruct((sets, height), F32),
             jax.ShapeDtypeStruct((sets, height, 3 * model), F32),
             jax.ShapeDtypeStruct((sets, height, model), F32),
-            jax.ShapeDtypeStruct((8, sets, height, width), BF16),
+            jax.ShapeDtypeStruct((sets, height, 8 * width), F32),
             jax.ShapeDtypeStruct((sets, down_height, model), F32),
         ),
         in_specs=[vmem] * 6 + [anywhere] * 6,
-        out_specs=(vmem,) * 7,
+        out_specs=(vmem,) * 8,
         scratch_shapes=[
             pltpu.VMEM((2, 2) + act, BF16),
             pltpu.VMEM((2, 2, 2) + act, BF16),
@@ -1691,6 +1848,8 @@
             pltpu.VMEM((2 * sets, 16, model), F32),
             pltpu.VMEM((8, 8, 128), F32),
             pltpu.VMEM((32, 8, 128), F32),
+            pltpu.VMEM((8, 128), F32),
+            pltpu.VMEM((8, sets, height, width), BF16),
             dma((2, 2, 2)),
             dma((2, 2, 2)),
             dma((2, 2)),
@@ -1745,35 +1904,10 @@
     valid_frames,
     item_lengths,
 ):
-    frame_count, positions, model = tokens.shape
-    own_gain = norm_attn.shape[1]
-    device_index = lax.axis_index(("dp", "pair"))
-    local_ids = jnp.arange(frame_count, dtype=jnp.int32)
-    frame_ids = device_index * frame_count + local_ids
-    item_ends = jnp.cumsum(item_lengths)
-    item_starts = item_ends - item_lengths
-    in_item = (frame_ids[:, None] >= item_starts[None, :]) & (
-        frame_ids[:, None] < item_ends[None, :]
-    )
-    item_share = 8 * frame_count / item_lengths.astype(F32)
-    frame_weight = jnp.sum(jnp.where(in_item, item_share[None, :], 0.0), axis=1)
-    frame_weight = jnp.where(local_ids < valid_frames[0], frame_weight, 0.0)
-    grad_out = jnp.swapaxes(cotangent, 0, 1).astype(F32) * frame_weight[None, :, None]
-    grad_low = grad_out.astype(BF16)
-
-    unit_gains = jnp.concatenate([norm_attn, norm_ff], axis=0)
-    lanes = jnp.arange(128, dtype=jnp.int32) // own_gain
-    gains = jnp.where(lanes == lax.rem(device_index, 128 // own_gain), jnp.tile(unit_gains, (1, 128 // own_gain)), 0)
-    gains = jnp.pad(gains, ((0, 16 - 2 * positions), (0, 0)))
-
-    unit = w_down.shape[1]
-    parts = w_gate_up.reshape(positions, -1, 2, 2, 2, 2, 2, 2, unit)
-    parts = parts.transpose(4, 6, 7, 0, 1, 2, 3, 5, 8)
-    parts = parts.reshape(8, positions, w_gate_up.shape[1], 8 * unit)
-    tokens_low = jnp.swapaxes(tokens, 0, 1)
     (
-        gains_rows,
-        qkv,
+        gain_rows,
+        cot_rows,
+        qkv_rows,
         context,
         resid_mid,
         qkv_full,
@@ -1782,12 +1916,32 @@
         back_part,
         gate_up_grad,
         down_grad,
-    ) = forward_gather(gains, tokens_low, w_qkv, w_out, parts, w_down, grad_low)
-    output, grad_tokens, gains_sum, share_qkv, share_out, gate_up_sum, down_sum = backward_scatter(
-        tokens_low,
-        grad_out,
-        gains_rows,
-        qkv,
+    ) = forward_gather(
+        valid_frames,
+        item_lengths,
+        norm_attn,
+        norm_ff,
+        tokens,
+        cotangent,
+        w_qkv,
+        w_out,
+        w_gate_up,
+        w_down,
+    )
+    (
+        output,
+        grad_tokens,
+        share_norm_attn,
+        share_norm_ff,
+        share_qkv,
+        share_out,
+        share_gate_up,
+        share_down,
+    ) = backward_scatter(
+        tokens,
+        cot_rows,
+        gain_rows,
+        qkv_rows,
         context,
         resid_mid,
         qkv_full,
@@ -1797,22 +1951,15 @@
         gate_up_grad,
         down_grad,
     )
-    output = jnp.swapaxes(output, 0, 1)
-    grad_tokens = jnp.swapaxes(grad_tokens, 0, 1)
-    share_gate_up = gate_up_sum.reshape(2, 2, 2, positions, -1, 2, 2, 2, unit)
-    share_gate_up = share_gate_up.transpose(3, 4, 5, 6, 0, 7, 1, 2, 8)
-    share_gate_up = share_gate_up.reshape(w_gate_up.shape).astype(F32)
-    shift = lax.rem(device_index, 128 // own_gain) * own_gain
-    gain_grads = lax.dynamic_slice(gains_sum, (0, shift), (2 * positions, own_gain))
     return (
         output,
         grad_tokens,
-        gain_grads[:positions],
+        share_norm_attn,
         share_qkv,
         share_out,
-        gain_grads[positions:],
+        share_norm_ff,
         share_gate_up,
-        down_sum,
+        share_down,
     )
 
 

time: 379 us -> 351 us (0.926)
  local copies, waits for them, and re-layouts: 26.2 us -> 11.6 us
  Pallas kernels: 346 us -> 337 us
  other arithmetic: 4.27 us -> 0 us
    convert_element_type x3 -> x0, local copies, waits for them, and re-layouts: 10.1 us -> none  [local_fast(): share_gate_up = share_gate_up.reshape(w_gate_up.shape).astype(F32)]
    pallas_call x1, Pallas kernels: 181 us -> 175 us  [forward_gather(): pl.pallas_call(forward_kernel, out_shape=(jax.ShapeDtypeStruct((16, model...]
    reshape x3 -> x0, local copies, waits for them, and re-layouts: 4.22 us -> none  [the longest x2 2.67 us: local_fast(): parts = w_gate_up.reshape(positions, -1, 2, 2, 2, 2, 2, 2, unit)]
    unnamed x14 -> x16, local copies, waits for them, and re-layouts: 9.9 us -> 11.6 us
where the time goes in v5:
time: 351 us; the launch traced here: 350 us
  Pallas kernels  337 us (96%)
  local copies, waits for them, and re-layouts  11.6 us (3%)
    pallas_call x1, Pallas kernels, forward_gather(): pl.pallas_call(forward_kernel, out_shape=(jax.ShapeDtypeStruct((16, model...  175 us
    pallas_call x1, Pallas kernels, backward_scatter(): pl.pallas_call(backward_kernel, out_shape=(jax.ShapeDtypeStruct(tokens.sh...  162 us
    unnamed x16, local copies, waits for them, and re-layouts  11.6 us

profile of v5, /device:TPU:0, one launch (start us, length us, event | category | flops | bytes accessed | tf_op | source)
XLA Modules:
  0.0 350.2 jit_solution(11815903391068338579)
XLA Ops:
  1.3 174.9 %forward_gather.1 = (f32[16,1024]{1,0:T(8,128)}, f32[2,128,1024]{2,1,0:T(8,128)}, bf16[2,128,3072]{2,1,0:T(8,128)(2,1)}, bf16[2,128,1024]{2,1,0:T(8,128)(2,1)}, ...) custom-call(s32[1]{0:T(128)S(6)} %copy.26.valid_ref, ...), custom_call_target="tpu_custom_call" | custom-call | tf_op jit(solution)/shard_map/forward_gather/pallas_call | solution.py:1051
  176.2 162.4 %backward_scatter.1 = (bf16[128,2,1024]{2,1,0:T(2,128)(2,1)}, f32[128,2,1024]{2,1,0:T(2,128)}, f32[2,32]{1,0:T(2,128)}, f32[2,32]{1,0:T(2,128)}, f32[2,32,3072]{...) custom-call(bf16[128,2,1024]{2,1,0:T(2,128)(2,1)} %tokens_ref.3, ...), custom_call_target="tpu_custom_call" | custom-call | tf_op jit(solution)/shard_map/backward_scatter/pallas_call | solution.py:1804
  338.6 0.0 copy-start.2
  338.6 0.0 copy-start.3
  338.6 0.0 copy-start
  338.6 2.3 copy.27
  341.0 0.0 copy-start.1
  341.0 2.4 copy.28
  343.3 1.2 copy.29
  344.6 2.1 copy.30
  346.6 0.0 copy-done.2
  346.6 0.7 copy.31
  347.3 0.0 copy-done.3
  347.3 0.6 copy.32
  347.9 0.0 copy-done
  347.9 1.3 copy.33
  349.2 0.0 copy-done.1
  349.2 1.0 copy.34
Async XLA Ops:
  338.6 8.0 %copy-start.2 = (f32[2,32,1024]{2,1,0:T(8,128)S(1)}, f32[2,32,1024]{2,1,0:T(8,128)}, u32[]{:S(2)}) copy-start(f32[2,32,1024]{2,1,0:T(8,128)} %get-tuple-element.58) | copy-start | bytes 786436
  338.6 8.7 %copy-start.3 = (f32[2,32]{1,0:T(2,128)S(1)}, f32[2,32]{1,0:T(2,128)}, u32[]{:S(2)}) copy-start(f32[2,32]{1,0:T(2,128)} %get-tuple-element.59) | copy-start | bytes 772
  338.6 9.3 %copy-start = (f32[2,32,8192]{2,1,0:T(8,128)S(1)}, f32[2,32,8192]{2,1,0:T(8,128)}, u32[]{:S(2)}) copy-start(f32[2,32,8192]{2,1,0:T(8,128)} %get-tuple-element.60) | copy-start | bytes 6291460
  341.0 8.3 %copy-start.1 = (f32[2,128,1024]{2,1,0:T(8,128)S(1)}, f32[2,128,1024]{2,1,0:T(8,128)}, u32[]{:S(2)}) copy-start(f32[2,128,1024]{2,1,0:T(8,128)} %get-tuple-element.61) | copy-start | bytes 3145732

commit v6 on v5

--- a/solution.py
+++ b/solution.py
@@ -463,73 +463,93 @@
     return [power / total for power in powers]
 
 
+(
+    F_TREE,
+    F_TREE_END,
+    F_GAINS,
+    F_PARTS,
+    F_COT,
+    F_ATTENTION,
+    F_GRADS,
+    F_ACT_Z,
+    F_ACT_X,
+    F_ACT_C,
+    F_TO_RANK,
+    F_OWN_FAR,
+    F_OWN_ACROSS,
+    F_RANK_FAR,
+    F_RANK_ACROSS,
+    F_FAR_ACROSS,
+    F_FF_END,
+    F_BLOCK,
+    F_GATE_GRAD,
+    F_DOWN_GRAD,
+) = range(20)
 FORWARD_STEPS = [
-    ("tree", 3, 0, 0, 0), ("tree", 5, 0, 0, 0), ("tree", 0, 0, 0, 0), ("tree", 2, 0, 0, 0),
-    ("tree", 5, 1, 0, 0), ("parts",), ("to_rank", 0, 7), ("tree", 0, -1, 0, 0), ("tree", 0, 0, 0, 1),
-    ("to_rank", 0, 3), ("tree", 2, 0, 0, 1), ("tree", 1, 0, 0, 0), ("tree", 0, -2, 0, 0), ("cot",),
-    ("rank_far", 0, 3), ("tree", 0, 0, 1, 0), ("tree", 4, 0, 0, 0), ("to_rank", 1, 4), ("tree", 1, -1, 0, 0),
-    ("to_rank", 0, 2), ("to_rank", 1, 2), ("tree", 2, 0, 1, 1), ("tree", 0, 1, 0, 0), ("tree", 2, 0, 1, 0),
-    ("own_across", 0, 0), ("tree", 1, 1, 0, 0), ("tree", 2, -1, 0, 0), ("tree", 0, -1, 0, 1),
-    ("tree", 0, -3, 0, 0), ("to_rank", 0, 1), ("tree", 0, -2, 0, 1), ("tree", 1, 0, 1, 0),
-    ("tree", 2, 1, 0, 1), ("tree", 0, 2, 0, 0), ("grads", 0), ("to_rank", 0, 6), ("rank_far", 0, 1),
-    ("own_across", 1, 8), ("tree", 2, -2, 0, 0), ("own_across", 0, 8), ("tree", 2, -1, 1, 0),
-    ("to_rank", 0, 5), ("rank_far", 0, 2), ("tree", 3, 0, 0, 1), ("own_far", 0, 8), ("tree", 1, -1, 1, 0),
-    ("tree", 2, -1, 1, 1), ("far_across", 0, 2), ("rank_far", 0, 6), ("tree", 3, 0, 1, 1), ("gains",),
-    ("tree", 2, 1, 0, 0), ("tree", 1, 2, 0, 0), ("rank_across", 0, 3), ("tree", 1, -2, 0, 0),
-    ("tree", 0, 3, 0, 0), ("tree", 2, 1, 1, 1), ("tree", 5, 0, 0, 1), ("tree", 2, 2, 0, 0), ("to_rank", 0, 4),
-    ("tree", 1, 2, 1, 0), ("tree", 3, -1, 0, 0), ("tree", 4, 1, 0, 0), ("tree", 0, -1, 1, 1),
-    ("tree", 0, 2, 0, 1), ("rank_far", 0, 7), ("rank_far", 0, 4), ("far_across", 0, 3), ("tree", 2, 2, 1, 1),
-    ("tree", 1, 3, 0, 0), ("tree", 1, 1, 1, 0), ("rank_across", 0, 1), ("to_rank", 1, 6),
-    ("tree", 2, -3, 0, 0), ("tree", 0, -3, 0, 1), ("tree", 0, 0, 1, 1), ("tree", 1, 2, 0, 1),
-    ("tree", 2, 1, 1, 0), ("tree", 2, -1, 0, 1), ("tree", 1, 0, 1, 1), ("tree", 2, -2, 1, 0),
-    ("tree", 2, 3, 1, 1), ("far_across", 0, 6), ("own_far", 0, 0), ("tree", 1, -2, 0, 1),
-    ("tree", 0, 2, 1, 1), ("tree", 4, 2, 0, 0), ("tree", 1, 3, 0, 1), ("tree", 3, 1, 0, 0),
-    ("tree", 2, -2, 1, 1), ("rank_far", 0, 5), ("tree", 0, -2, 1, 1), ("tree", 0, 1, 1, 0),
-    ("tree", 5, 0, 1, 0), ("far_across", 0, 1), ("tree", 1, -2, 1, 0), ("tree", 1, 2, 1, 1),
-    ("tree", 2, 2, 1, 0), ("tree", 1, -3, 0, 0), ("to_rank", 1, 5), ("tree", 0, -1, 1, 0),
-    ("tree", 3, -2, 0, 0), ("tree", 1, 3, 1, 0), ("act_z", 1, 0), ("tree", 0, 1, 0, 1), ("tree", 3, 1, 0, 1),
-    ("tree", 2, 2, 0, 1), ("tree", 0, 3, 1, 0), ("tree", 4, -1, 0, 0), ("tree", 2, -2, 0, 1),
-    ("tree", 2, -3, 1, 1), ("tree", 0, -3, 1, 1), ("far_across", 0, 7), ("tree", 0, -3, 1, 0),
-    ("tree", 0, 2, 1, 0), ("tree", 3, 1, 1, 0), ("tree", 2, -3, 1, 0), ("tree", 1, -1, 0, 1),
-    ("tree", 1, -3, 1, 0), ("rank_across", 0, 7), ("far_across", 0, 0), ("tree", 1, 3, 1, 1),
-    ("tree", 3, 2, 0, 0), ("tree", 2, 3, 0, 0), ("rank_across", 0, 6), ("tree", 5, 1, 1, 0),
-    ("tree", 0, 3, 0, 1), ("tree", 1, -3, 0, 1), ("tree", 3, -2, 0, 1), ("act_c", 1, 0, 0, 0),
-    ("tree", 4, 0, 1, 0), ("tree", 5, 0, 1, 1), ("tree", 4, -2, 0, 0), ("far_across", 0, 4), ("grads", 1),
-    ("tree", 2, -3, 0, 1), ("tree", 5, -1, 1, 0), ("tree", 1, -3, 1, 1), ("act_c", 1, 0, 1, 0),
-    ("far_across", 0, 8), ("tree", 5, 1, 0, 1), ("far_across", 0, 5), ("tree", 1, -1, 1, 1),
-    ("tree", 1, 0, 0, 1), ("rank_across", 0, 5), ("tree", 5, -1, 0, 0), ("tree", 3, -3, 0, 0),
-    ("to_rank", 1, 1), ("act_x", 1, 0, 1), ("tree", 1, 1, 0, 1), ("tree", 5, 2, 1, 0), ("own_far", 1, 8),
-    ("act_x", 1, 0, 0), ("tree", 5, -1, 0, 1), ("tree", 4, -3, 0, 0), ("tree", 0, 1, 1, 1),
-    ("tree", 1, 1, 1, 1), ("tree", 2, 3, 0, 1), ("tree", 3, 1, 1, 1), ("tree", 3, -1, 0, 1),
-    ("tree", 4, -1, 1, 0), ("tree", 3, -3, 0, 1), ("tree", 3, 2, 0, 1), ("own_across", 1, 0),
-    ("tree", 1, -2, 1, 1), ("to_rank", 1, 3), ("tree", 3, 0, 1, 0), ("tree", 0, 3, 1, 1),
-    ("tree", 0, -2, 1, 0), ("tree", 3, 2, 1, 0), ("tree", 2, 3, 1, 0), ("tree", 3, 3, 0, 0), ("tree_end", 0),
-    ("tree", 4, -1, 1, 1), ("to_rank", 1, 7), ("attention", 0), ("tree", 4, 3, 0, 0), ("act_x", 0, 0, 0),
-    ("tree", 4, 3, 1, 0), ("tree", 3, -3, 1, 0), ("tree", 4, 3, 0, 1), ("tree", 4, -2, 1, 0),
-    ("tree", 3, 3, 0, 1), ("tree", 5, -1, 1, 1), ("rank_far", 1, 7), ("rank_across", 0, 2),
-    ("tree", 4, 2, 1, 0), ("tree", 5, 1, 1, 1), ("tree", 5, 3, 1, 0), ("tree", 4, -3, 0, 1),
-    ("rank_across", 0, 4), ("tree", 4, -3, 1, 0), ("own_far", 1, 0), ("rank_far", 1, 2), ("tree", 4, 3, 1, 1),
-    ("rank_across", 1, 7), ("far_across", 1, 8), ("tree", 4, 1, 1, 0), ("act_z", 1, 1), ("tree", 5, -2, 0, 1),
-    ("tree", 4, -3, 1, 1), ("tree", 3, 2, 1, 1), ("tree", 5, -2, 0, 0), ("act_z", 0, 0), ("tree", 4, 2, 1, 1),
-    ("tree", 5, 2, 0, 0), ("rank_far", 1, 1), ("ff_end", 0), ("act_c", 0, 0, 1, 0), ("rank_across", 1, 2),
-    ("tree", 4, 0, 0, 1), ("tree", 4, 1, 1, 1), ("rank_far", 1, 5), ("act_x", 1, 1, 0), ("tree", 3, -1, 1, 0),
-    ("tree", 5, 2, 1, 1), ("tree", 5, 3, 0, 0), ("far_across", 1, 7), ("tree", 3, 3, 1, 1),
-    ("tree", 3, -1, 1, 1), ("tree", 4, -2, 1, 1), ("act_c", 1, 0, 0, 1), ("act_c", 0, 0, 0, 0),
-    ("tree", 4, 0, 1, 1), ("rank_far", 1, 3), ("act_c", 1, 0, 1, 1), ("tree", 3, -2, 1, 0),
-    ("tree", 5, -2, 1, 0), ("rank_far", 1, 4), ("far_across", 1, 0), ("tree", 5, -3, 0, 0),
-    ("tree", 4, 1, 0, 1), ("tree", 3, -2, 1, 1), ("act_c", 1, 1, 1, 0), ("rank_far", 1, 6),
-    ("tree", 4, -1, 0, 1), ("tree", 5, 2, 0, 1), ("tree", 5, -3, 1, 0), ("act_c", 0, 0, 0, 1),
-    ("far_across", 1, 2), ("act_c", 1, 1, 0, 0), ("tree", 5, -3, 0, 1), ("tree", 5, -2, 1, 1),
-    ("tree", 3, 3, 1, 0), ("rank_across", 1, 6), ("rank_across", 1, 3), ("tree", 5, 3, 1, 1),
-    ("rank_across", 1, 4), ("block", 0, 1), ("tree", 4, 2, 0, 1), ("tree", 5, 3, 0, 1), ("tree", 4, -2, 0, 1),
-    ("tree", 3, -3, 1, 1), ("far_across", 1, 1), ("tree", 5, -3, 1, 1), ("block", 0, 0),
-    ("rank_across", 1, 5), ("act_x", 1, 1, 1), ("tree_end", 1), ("attention", 1), ("far_across", 1, 3),
-    ("rank_across", 1, 1), ("act_x", 0, 0, 1), ("block", 0, 2), ("far_across", 1, 5), ("act_c", 0, 0, 1, 1),
-    ("block", 0, 3), ("down_grad", 0), ("act_c", 1, 1, 0, 1), ("far_across", 1, 6), ("act_x", 0, 1, 0),
-    ("act_c", 1, 1, 1, 1), ("act_z", 0, 1), ("far_across", 1, 4), ("gate_grad", 0), ("act_c", 0, 1, 0, 1),
-    ("act_c", 0, 1, 0, 0), ("ff_end", 1), ("act_c", 0, 1, 1, 0), ("block", 1, 1), ("block", 1, 2),
-    ("act_x", 0, 1, 1), ("block", 1, 0), ("act_c", 0, 1, 1, 1), ("block", 1, 3), ("down_grad", 1),
-    ("gate_grad", 1),
+    (F_TREE, 3, 0, 0, 0), (F_TREE, 5, 0, 0, 0), (F_TREE, 0, 0, 0, 0), (F_TREE, 2, 0, 0, 0),
+    (F_TREE, 5, 1, 0, 0), (F_PARTS,), (F_TO_RANK, 0, 7), (F_TREE, 0, -1, 0, 0), (F_TREE, 0, 0, 0, 1),
+    (F_TO_RANK, 0, 3), (F_TREE, 2, 0, 0, 1), (F_TREE, 1, 0, 0, 0), (F_TREE, 0, -2, 0, 0), (F_COT,),
+    (F_RANK_FAR, 0, 3), (F_TREE, 0, 0, 1, 0), (F_TREE, 4, 0, 0, 0), (F_TO_RANK, 1, 4), (F_TREE, 1, -1, 0, 0),
+    (F_TO_RANK, 0, 2), (F_TO_RANK, 1, 2), (F_TREE, 2, 0, 1, 1), (F_TREE, 0, 1, 0, 0), (F_TREE, 2, 0, 1, 0),
+    (F_OWN_ACROSS, 0, 0), (F_TREE, 1, 1, 0, 0), (F_TREE, 2, -1, 0, 0), (F_TREE, 0, -1, 0, 1),
+    (F_TREE, 0, -3, 0, 0), (F_TO_RANK, 0, 1), (F_TREE, 0, -2, 0, 1), (F_TREE, 1, 0, 1, 0), (F_TREE, 2, 1, 0, 1),
+    (F_TREE, 0, 2, 0, 0), (F_GRADS, 0), (F_TO_RANK, 0, 6), (F_RANK_FAR, 0, 1), (F_OWN_ACROSS, 1, 8),
+    (F_TREE, 2, -2, 0, 0), (F_OWN_ACROSS, 0, 8), (F_TREE, 2, -1, 1, 0), (F_TO_RANK, 0, 5), (F_RANK_FAR, 0, 2),
+    (F_TREE, 3, 0, 0, 1), (F_OWN_FAR, 0, 8), (F_TREE, 1, -1, 1, 0), (F_TREE, 2, -1, 1, 1), (F_FAR_ACROSS, 0, 2),
+    (F_RANK_FAR, 0, 6), (F_TREE, 3, 0, 1, 1), (F_GAINS,), (F_TREE, 2, 1, 0, 0), (F_TREE, 1, 2, 0, 0),
+    (F_RANK_ACROSS, 0, 3), (F_TREE, 1, -2, 0, 0), (F_TREE, 0, 3, 0, 0), (F_TREE, 2, 1, 1, 1),
+    (F_TREE, 5, 0, 0, 1), (F_TREE, 2, 2, 0, 0), (F_TO_RANK, 0, 4), (F_TREE, 1, 2, 1, 0), (F_TREE, 3, -1, 0, 0),
+    (F_TREE, 4, 1, 0, 0), (F_TREE, 0, -1, 1, 1), (F_TREE, 0, 2, 0, 1), (F_RANK_FAR, 0, 7), (F_RANK_FAR, 0, 4),
+    (F_FAR_ACROSS, 0, 3), (F_TREE, 2, 2, 1, 1), (F_TREE, 1, 3, 0, 0), (F_TREE, 1, 1, 1, 0),
+    (F_RANK_ACROSS, 0, 1), (F_TO_RANK, 1, 6), (F_TREE, 2, -3, 0, 0), (F_TREE, 0, -3, 0, 1),
+    (F_TREE, 0, 0, 1, 1), (F_TREE, 1, 2, 0, 1), (F_TREE, 2, 1, 1, 0), (F_TREE, 2, -1, 0, 1),
+    (F_TREE, 1, 0, 1, 1), (F_TREE, 2, -2, 1, 0), (F_TREE, 2, 3, 1, 1), (F_FAR_ACROSS, 0, 6), (F_OWN_FAR, 0, 0),
+    (F_TREE, 1, -2, 0, 1), (F_TREE, 0, 2, 1, 1), (F_TREE, 4, 2, 0, 0), (F_TREE, 1, 3, 0, 1),
+    (F_TREE, 3, 1, 0, 0), (F_TREE, 2, -2, 1, 1), (F_RANK_FAR, 0, 5), (F_TREE, 0, -2, 1, 1),
+    (F_TREE, 0, 1, 1, 0), (F_TREE, 5, 0, 1, 0), (F_FAR_ACROSS, 0, 1), (F_TREE, 1, -2, 1, 0),
+    (F_TREE, 1, 2, 1, 1), (F_TREE, 2, 2, 1, 0), (F_TREE, 1, -3, 0, 0), (F_TO_RANK, 1, 5), (F_TREE, 0, -1, 1, 0),
+    (F_TREE, 3, -2, 0, 0), (F_TREE, 1, 3, 1, 0), (F_ACT_Z, 1, 0), (F_TREE, 0, 1, 0, 1), (F_TREE, 3, 1, 0, 1),
+    (F_TREE, 2, 2, 0, 1), (F_TREE, 0, 3, 1, 0), (F_TREE, 4, -1, 0, 0), (F_TREE, 2, -2, 0, 1),
+    (F_TREE, 2, -3, 1, 1), (F_TREE, 0, -3, 1, 1), (F_FAR_ACROSS, 0, 7), (F_TREE, 0, -3, 1, 0),
+    (F_TREE, 0, 2, 1, 0), (F_TREE, 3, 1, 1, 0), (F_TREE, 2, -3, 1, 0), (F_TREE, 1, -1, 0, 1),
+    (F_TREE, 1, -3, 1, 0), (F_RANK_ACROSS, 0, 7), (F_FAR_ACROSS, 0, 0), (F_TREE, 1, 3, 1, 1),
+    (F_TREE, 3, 2, 0, 0), (F_TREE, 2, 3, 0, 0), (F_RANK_ACROSS, 0, 6), (F_TREE, 5, 1, 1, 0),
+    (F_TREE, 0, 3, 0, 1), (F_TREE, 1, -3, 0, 1), (F_TREE, 3, -2, 0, 1), (F_ACT_C, 1, 0, 0, 0),
+    (F_TREE, 4, 0, 1, 0), (F_TREE, 5, 0, 1, 1), (F_TREE, 4, -2, 0, 0), (F_FAR_ACROSS, 0, 4), (F_GRADS, 1),
+    (F_TREE, 2, -3, 0, 1), (F_TREE, 5, -1, 1, 0), (F_TREE, 1, -3, 1, 1), (F_ACT_C, 1, 0, 1, 0),
+    (F_FAR_ACROSS, 0, 8), (F_TREE, 5, 1, 0, 1), (F_FAR_ACROSS, 0, 5), (F_TREE, 1, -1, 1, 1),
+    (F_TREE, 1, 0, 0, 1), (F_RANK_ACROSS, 0, 5), (F_TREE, 5, -1, 0, 0), (F_TREE, 3, -3, 0, 0),
+    (F_TO_RANK, 1, 1), (F_ACT_X, 1, 0, 1), (F_TREE, 1, 1, 0, 1), (F_TREE, 5, 2, 1, 0), (F_OWN_FAR, 1, 8),
+    (F_ACT_X, 1, 0, 0), (F_TREE, 5, -1, 0, 1), (F_TREE, 4, -3, 0, 0), (F_TREE, 0, 1, 1, 1),
+    (F_TREE, 1, 1, 1, 1), (F_TREE, 2, 3, 0, 1), (F_TREE, 3, 1, 1, 1), (F_TREE, 3, -1, 0, 1),
+    (F_TREE, 4, -1, 1, 0), (F_TREE, 3, -3, 0, 1), (F_TREE, 3, 2, 0, 1), (F_OWN_ACROSS, 1, 0),
+    (F_TREE, 1, -2, 1, 1), (F_TO_RANK, 1, 3), (F_TREE, 3, 0, 1, 0), (F_TREE, 0, 3, 1, 1), (F_TREE, 0, -2, 1, 0),
+    (F_TREE, 3, 2, 1, 0), (F_TREE, 2, 3, 1, 0), (F_TREE, 3, 3, 0, 0), (F_TREE_END, 0), (F_TREE, 4, -1, 1, 1),
+    (F_TO_RANK, 1, 7), (F_ATTENTION, 0), (F_TREE, 4, 3, 0, 0), (F_ACT_X, 0, 0, 0), (F_TREE, 4, 3, 1, 0),
+    (F_TREE, 3, -3, 1, 0), (F_TREE, 4, 3, 0, 1), (F_TREE, 4, -2, 1, 0), (F_TREE, 3, 3, 0, 1),
+    (F_TREE, 5, -1, 1, 1), (F_RANK_FAR, 1, 7), (F_RANK_ACROSS, 0, 2), (F_TREE, 4, 2, 1, 0),
+    (F_TREE, 5, 1, 1, 1), (F_TREE, 5, 3, 1, 0), (F_TREE, 4, -3, 0, 1), (F_RANK_ACROSS, 0, 4),
+    (F_TREE, 4, -3, 1, 0), (F_OWN_FAR, 1, 0), (F_RANK_FAR, 1, 2), (F_TREE, 4, 3, 1, 1), (F_RANK_ACROSS, 1, 7),
+    (F_FAR_ACROSS, 1, 8), (F_TREE, 4, 1, 1, 0), (F_ACT_Z, 1, 1), (F_TREE, 5, -2, 0, 1), (F_TREE, 4, -3, 1, 1),
+    (F_TREE, 3, 2, 1, 1), (F_TREE, 5, -2, 0, 0), (F_ACT_Z, 0, 0), (F_TREE, 4, 2, 1, 1), (F_TREE, 5, 2, 0, 0),
+    (F_RANK_FAR, 1, 1), (F_FF_END, 0), (F_ACT_C, 0, 0, 1, 0), (F_RANK_ACROSS, 1, 2), (F_TREE, 4, 0, 0, 1),
+    (F_TREE, 4, 1, 1, 1), (F_RANK_FAR, 1, 5), (F_ACT_X, 1, 1, 0), (F_TREE, 3, -1, 1, 0), (F_TREE, 5, 2, 1, 1),
+    (F_TREE, 5, 3, 0, 0), (F_FAR_ACROSS, 1, 7), (F_TREE, 3, 3, 1, 1), (F_TREE, 3, -1, 1, 1),
+    (F_TREE, 4, -2, 1, 1), (F_ACT_C, 1, 0, 0, 1), (F_ACT_C, 0, 0, 0, 0), (F_TREE, 4, 0, 1, 1),
+    (F_RANK_FAR, 1, 3), (F_ACT_C, 1, 0, 1, 1), (F_TREE, 3, -2, 1, 0), (F_TREE, 5, -2, 1, 0), (F_RANK_FAR, 1, 4),
+    (F_FAR_ACROSS, 1, 0), (F_TREE, 5, -3, 0, 0), (F_TREE, 4, 1, 0, 1), (F_TREE, 3, -2, 1, 1),
+    (F_ACT_C, 1, 1, 1, 0), (F_RANK_FAR, 1, 6), (F_TREE, 4, -1, 0, 1), (F_TREE, 5, 2, 0, 1),
+    (F_TREE, 5, -3, 1, 0), (F_ACT_C, 0, 0, 0, 1), (F_FAR_ACROSS, 1, 2), (F_ACT_C, 1, 1, 0, 0),
+    (F_TREE, 5, -3, 0, 1), (F_TREE, 5, -2, 1, 1), (F_TREE, 3, 3, 1, 0), (F_RANK_ACROSS, 1, 6),
+    (F_RANK_ACROSS, 1, 3), (F_TREE, 5, 3, 1, 1), (F_RANK_ACROSS, 1, 4), (F_BLOCK, 0, 1), (F_TREE, 4, 2, 0, 1),
+    (F_TREE, 5, 3, 0, 1), (F_TREE, 4, -2, 0, 1), (F_TREE, 3, -3, 1, 1), (F_FAR_ACROSS, 1, 1),
+    (F_TREE, 5, -3, 1, 1), (F_BLOCK, 0, 0), (F_RANK_ACROSS, 1, 5), (F_ACT_X, 1, 1, 1), (F_TREE_END, 1),
+    (F_ATTENTION, 1), (F_FAR_ACROSS, 1, 3), (F_RANK_ACROSS, 1, 1), (F_ACT_X, 0, 0, 1), (F_BLOCK, 0, 2),
+    (F_FAR_ACROSS, 1, 5), (F_ACT_C, 0, 0, 1, 1), (F_BLOCK, 0, 3), (F_DOWN_GRAD, 0), (F_ACT_C, 1, 1, 0, 1),
+    (F_FAR_ACROSS, 1, 6), (F_ACT_X, 0, 1, 0), (F_ACT_C, 1, 1, 1, 1), (F_ACT_Z, 0, 1), (F_FAR_ACROSS, 1, 4),
+    (F_GATE_GRAD, 0), (F_ACT_C, 0, 1, 0, 1), (F_ACT_C, 0, 1, 0, 0), (F_FF_END, 1), (F_ACT_C, 0, 1, 1, 0),
+    (F_BLOCK, 1, 1), (F_BLOCK, 1, 2), (F_ACT_X, 0, 1, 1), (F_BLOCK, 1, 0), (F_ACT_C, 0, 1, 1, 1),
+    (F_BLOCK, 1, 3), (F_DOWN_GRAD, 1), (F_GATE_GRAD, 1),
 ]
 
 
@@ -1004,29 +1024,29 @@
         attention(s)
         act_own(0, s)
 
-    chosen_first = [step[2] for step in FORWARD_STEPS if step[:2] == ("block", 1)]
-    kinds = dict(
-        tree=lambda piece, dz, dy, dx: tree_step(piece, (dz, dy, dx)),
-        tree_end=tree_end,
-        gains=take_gains,
-        parts=part_units,
-        cot=weigh,
-        attention=attend_and_send,
-        grads=lambda s: act_own(1, s),
-        act_z=act_from_z,
-        act_x=act_from_x,
-        act_c=act_from_core,
-        to_rank=to_rank,
-        own_far=own_far,
-        own_across=own_across,
-        rank_far=rank_far,
-        rank_across=rank_across,
-        far_across=far_across,
-        ff_end=ff_end,
-        block=block,
-        gate_grad=gate_grad,
-        down_grad=down_weights_grad,
-    )
+    chosen_first = [step[2] for step in FORWARD_STEPS if step[:2] == (F_BLOCK, 1)]
+    kinds = {
+        F_TREE: lambda piece, dz, dy, dx: tree_step(piece, (dz, dy, dx)),
+        F_TREE_END: tree_end,
+        F_GAINS: take_gains,
+        F_PARTS: part_units,
+        F_COT: weigh,
+        F_ATTENTION: attend_and_send,
+        F_GRADS: lambda s: act_own(1, s),
+        F_ACT_Z: act_from_z,
+        F_ACT_X: act_from_x,
+        F_ACT_C: act_from_core,
+        F_TO_RANK: to_rank,
+        F_OWN_FAR: own_far,
+        F_OWN_ACROSS: own_across,
+        F_RANK_FAR: rank_far,
+        F_RANK_ACROSS: rank_across,
+        F_FAR_ACROSS: far_across,
+        F_FF_END: ff_end,
+        F_BLOCK: block,
+        F_GATE_GRAD: gate_grad,
+        F_DOWN_GRAD: down_weights_grad,
+    }
     for kind, *numbers in FORWARD_STEPS:
         kinds[kind](*numbers)
     for _, _, piece, offset in events:
@@ -1131,6 +1151,78 @@
         total += slot_index(order, direction, (0, 0, 0), 0, 0, 0)[1]
     base["u"] = base["d"] = base["z"]
     return base, total
+
+
+(
+    B_TREE,
+    B_RS_ACROSS,
+    B_RS_FIRST,
+    B_RS_SECOND,
+    B_RS_RANK,
+    B_RS_LAST,
+    B_ACT_CORE,
+    B_ACT_LOAD,
+    B_ACT_ADD_X,
+    B_ACT_ADD_Z,
+    B_ACT_SUM,
+    B_NORM_TURN,
+    B_SWAP_TURNED,
+    B_PROBS,
+    B_MID,
+    B_SCORES_BACK,
+    B_SWAP_QKV,
+    B_OUT_W,
+    B_QKV_W,
+    B_ROWS_BACK,
+    B_ATTN_BACK,
+    B_FINISH_OUTPUT,
+) = range(22)
+BACKWARD_STEPS = [
+    (B_RS_ACROSS, 0, 0, 0), (B_ACT_CORE, 0, 0), (B_ACT_ADD_X, 0, 0, 1), (B_NORM_TURN,), (B_RS_FIRST, 0, 0),
+    (B_RS_ACROSS, 0, 0, 1), (B_ACT_CORE, 0, 1), (B_ACT_ADD_Z, 0, 0), (B_ACT_ADD_X, 0, 0, 0),
+    (B_ACT_ADD_X, 0, 1, 1), (B_RS_ACROSS, 1, 1, 0), (B_SWAP_TURNED,), (B_RS_ACROSS, 0, 1, 0),
+    (B_RS_ACROSS, 0, 0, 2), (B_ACT_ADD_X, 0, 1, 0), (B_RS_FIRST, 0, 1), (B_RS_ACROSS, 1, 0, 1),
+    (B_RS_ACROSS, 0, 1, 1), (B_PROBS,), (B_RS_ACROSS, 1, 1, 1), (B_ACT_ADD_Z, 0, 1), (B_RS_FIRST, 0, 2),
+    (B_ACT_CORE, 1, 0), (B_ACT_SUM, 0, 0), (B_ACT_SUM, 0, 1), (B_MID, 1), (B_MID, 0), (B_ACT_LOAD, 1),
+    (B_OUT_W, 0), (B_OUT_W, 1), (B_ACT_CORE, 1, 1), (B_ACT_ADD_X, 1, 0, 1), (B_RS_FIRST, 1, 1),
+    (B_TREE, 2, -3, 0, 0), (B_SCORES_BACK,), (B_TREE, 2, -3, 1, 1), (B_TREE, 3, 3, 0, 0),
+    (B_RS_ACROSS, 1, 0, 2), (B_SWAP_QKV,), (B_ACT_ADD_X, 1, 0, 0), (B_TREE, 3, 3, 0, 1), (B_TREE, 2, 3, 1, 0),
+    (B_TREE, 3, -3, 0, 1), (B_RS_SECOND, 0, 1), (B_TREE, 2, -3, 0, 1), (B_QKV_W, 0), (B_ACT_ADD_X, 1, 1, 1),
+    (B_TREE, 2, 3, 1, 1), (B_RS_FIRST, 1, 2), (B_RS_ACROSS, 0, 1, 2), (B_TREE, 0, -1, 1, 1),
+    (B_RS_ACROSS, 1, 0, 0), (B_QKV_W, 1), (B_TREE, 2, 2, 1, 1), (B_TREE, 1, 2, 1, 1), (B_TREE, 2, 3, 0, 0),
+    (B_TREE, 2, 2, 1, 0), (B_TREE, 0, -3, 1, 1), (B_RS_SECOND, 0, 0), (B_RS_ACROSS, 1, 1, 2),
+    (B_TREE, 1, 1, 1, 1), (B_TREE, 2, 3, 0, 1), (B_TREE, 0, 1, 1, 1), (B_TREE, 1, -3, 1, 1),
+    (B_TREE, 1, -1, 0, 1), (B_TREE, 2, -2, 1, 1), (B_TREE, 0, 3, 1, 0), (B_TREE, 3, -3, 1, 0),
+    (B_TREE, 1, 0, 1, 1), (B_RS_RANK, 0, 1), (B_TREE, 3, 2, 0, 1), (B_TREE, 2, -3, 1, 0), (B_TREE, 2, -1, 1, 1),
+    (B_TREE, 3, 3, 1, 0), (B_TREE, 2, -2, 0, 0), (B_TREE, 3, -2, 0, 1), (B_TREE, 1, -3, 0, 1),
+    (B_TREE, 3, 3, 1, 1), (B_TREE, 0, 3, 1, 1), (B_TREE, 3, -3, 1, 1), (B_RS_SECOND, 1, 1), (B_RS_RANK, 0, 3),
+    (B_RS_FIRST, 1, 0), (B_TREE, 0, -2, 1, 1), (B_TREE, 2, 2, 0, 1), (B_TREE, 0, -3, 0, 1),
+    (B_ACT_ADD_X, 1, 1, 0), (B_RS_RANK, 0, 4), (B_TREE, 3, -2, 1, 1), (B_TREE, 2, 1, 1, 0),
+    (B_TREE, 0, 0, 1, 0), (B_TREE, 0, -3, 1, 0), (B_TREE, 3, -2, 1, 0), (B_ACT_ADD_Z, 1, 1),
+    (B_TREE, 2, 2, 0, 0), (B_TREE, 1, -2, 1, 1), (B_TREE, 3, -1, 0, 1), (B_ROWS_BACK, 0), (B_TREE, 1, 3, 1, 1),
+    (B_TREE, 0, -1, 1, 0), (B_TREE, 3, 2, 1, 0), (B_TREE, 2, -1, 0, 0), (B_TREE, 2, -2, 1, 0),
+    (B_TREE, 2, -2, 0, 1), (B_TREE, 3, 2, 1, 1), (B_TREE, 0, 2, 1, 1), (B_TREE, 1, 3, 0, 1),
+    (B_TREE, 0, 3, 0, 1), (B_RS_RANK, 0, 7), (B_TREE, 1, -3, 1, 0), (B_TREE, 1, 1, 0, 1), (B_TREE, 2, 1, 1, 1),
+    (B_ACT_ADD_Z, 1, 0), (B_TREE, 3, 1, 0, 1), (B_TREE, 1, -2, 1, 0), (B_TREE, 0, -2, 1, 0),
+    (B_TREE, 0, 0, 1, 1), (B_TREE, 1, -1, 1, 1), (B_RS_SECOND, 1, 0), (B_TREE, 2, 1, 0, 0),
+    (B_TREE, 0, -2, 0, 1), (B_TREE, 3, -1, 1, 1), (B_RS_LAST, 0, 4), (B_TREE, 3, 2, 0, 0), (B_RS_RANK, 1, 2),
+    (B_TREE, 3, -3, 0, 0), (B_ACT_SUM, 1, 0), (B_TREE, 1, -2, 0, 1), (B_TREE, 2, 1, 0, 1),
+    (B_TREE, 0, -3, 0, 0), (B_TREE, 1, 3, 1, 0), (B_TREE, 0, 2, 0, 1), (B_RS_RANK, 1, 7), (B_TREE, 0, -1, 0, 1),
+    (B_TREE, 2, -1, 1, 0), (B_TREE, 2, -1, 0, 1), (B_TREE, 1, -3, 0, 0), (B_TREE, 3, 1, 1, 1),
+    (B_RS_RANK, 1, 5), (B_RS_RANK, 0, 6), (B_RS_LAST, 0, 7), (B_TREE, 0, 1, 1, 0), (B_TREE, 0, 2, 1, 0),
+    (B_TREE, 3, 1, 1, 0), (B_TREE, 2, 0, 1, 1), (B_TREE, 0, 3, 0, 0), (B_RS_LAST, 1, 2), (B_TREE, 1, -1, 1, 0),
+    (B_ACT_SUM, 1, 1), (B_FINISH_OUTPUT,), (B_TREE, 1, 3, 0, 0), (B_TREE, 0, -2, 0, 0), (B_TREE, 1, 2, 0, 1),
+    (B_TREE, 1, 0, 1, 0), (B_TREE, 3, 1, 0, 0), (B_RS_RANK, 1, 6), (B_TREE, 3, -1, 1, 0), (B_RS_RANK, 0, 2),
+    (B_RS_RANK, 1, 1), (B_TREE, 0, 2, 0, 0), (B_ROWS_BACK, 1), (B_RS_LAST, 1, 1), (B_TREE, 1, 0, 0, 1),
+    (B_TREE, 0, 1, 0, 1), (B_TREE, 1, 2, 1, 0), (B_TREE, 3, -2, 0, 0), (B_RS_LAST, 0, 6), (B_RS_LAST, 1, 6),
+    (B_TREE, 0, 0, 0, 1), (B_RS_RANK, 0, 5), (B_TREE, 2, 0, 1, 0), (B_TREE, 2, 0, 0, 1), (B_RS_LAST, 1, 5),
+    (B_TREE, 1, 1, 1, 0), (B_TREE, 3, 0, 0, 1), (B_TREE, 1, -2, 0, 0), (B_TREE, 1, 2, 0, 0), (B_ATTN_BACK,),
+    (B_TREE, 3, -1, 0, 0), (B_TREE, 0, -1, 0, 0), (B_TREE, 0, 1, 0, 0), (B_TREE, 1, -1, 0, 0),
+    (B_RS_SECOND, 1, 2), (B_TREE, 1, 1, 0, 0), (B_TREE, 3, 0, 1, 1), (B_RS_SECOND, 0, 2), (B_RS_LAST, 0, 3),
+    (B_RS_LAST, 0, 1), (B_RS_LAST, 0, 2), (B_TREE, 0, 0, 0, 0), (B_TREE, 2, 0, 0, 0), (B_RS_LAST, 0, 5),
+    (B_TREE, 3, 0, 1, 0), (B_RS_LAST, 1, 7), (B_RS_RANK, 1, 4), (B_RS_RANK, 1, 3), (B_TREE, 1, 0, 0, 0),
+    (B_RS_LAST, 1, 4), (B_TREE, 3, 0, 0, 0), (B_RS_LAST, 1, 3),
+]
 
 
 def backward_kernel(
@@ -1237,57 +1329,50 @@
         number = 2 * flip(zh, dzh) + flip(y, dy)
         return pl.ds(pl.multiple_of(number * down_height, down_height), down_height)
 
-    def ff_across(turn):
-        dzh = 1 - turn
-        for s in range(sets):
-            for low in (0, 1):
-                start(
-                    push(
-                        gate_up_ref.at[s, run_rows(dzh, 1, low)],
-                        across_gate.at[turn, s, low],
-                        across_send.at[turn, s, low],
-                        across_recv.at[turn, s, low],
-                        across,
-                    )
-                )
-            start(
-                push(
-                    down_ref.at[s, down_rows(dzh, 1)],
-                    across_down.at[turn, s],
-                    across_send.at[turn, s, 2],
-                    across_recv.at[turn, s, 2],
-                    across,
-                )
+    def ff_from(s, dzh, dy, part):
+        if part == 2:
+            return down_ref.at[s, down_rows(dzh, dy)]
+        return gate_up_ref.at[s, run_rows(dzh, dy, part)]
+
+    def ff_across(s, turn, part):
+        return across_down.at[turn, s] if part == 2 else across_gate.at[turn, s, part]
+
+    def ff_own(s, turn, part):
+        return down_own.at[turn, s] if part == 2 else gate_own.at[turn, s, part]
+
+    def ff_far(s, part):
+        return far_down.at[s] if part == 2 else far_gate.at[s, part]
+
+    def part_copy(s, turn, part):
+        return pltpu.make_async_copy(
+            ff_from(s, 1 - turn, 0, part), ff_own(s, turn, part), part_sem.at[turn, s, part]
+        )
+
+    def rs_across(s, turn, part):
+        start(
+            push(
+                ff_from(s, 1 - turn, 1, part),
+                ff_across(s, turn, part),
+                across_send.at[turn, s, part],
+                across_recv.at[turn, s, part],
+                across,
             )
-
-    part_copies = []
-    for turn in (0, 1):
-        for s in range(sets):
-            for low in (0, 1):
-                part_copies.append(
-                    pltpu.make_async_copy(
-                        gate_up_ref.at[s, run_rows(1 - turn, 0, low)],
-                        gate_own.at[turn, s, low],
-                        part_sem.at[turn, s, low],
-                    )
-                )
-            part_copies.append(
-                pltpu.make_async_copy(
-                    down_ref.at[s, down_rows(1 - turn, 0)], down_own.at[turn, s], part_sem.at[turn, s, 2]
-                )
-            )
-
-    def ff_first():
-        for s in range(sets):
-            for low in (0, 1):
-                block = across_gate.at[0, s, low]
-                arrived(block, across_recv.at[0, s, low], across)
-                add_into(block, [block, gate_own.at[0, s, low]])
-                start(push(block, far_gate.at[s, low], far_send.at[s, low], far_recv.at[s, low], far))
-            block = across_down.at[0, s]
-            arrived(block, across_recv.at[0, s, 2], across)
-            add_into(block, [block, down_own.at[0, s]])
-            start(push(block, far_down.at[s], far_send.at[s, 2], far_recv.at[s, 2], far))
+        )
+
+    def rs_first(s, part):
+        block = ff_across(s, 0, part)
+        part_copy(s, 0, part).wait()
+        arrived(block, across_recv.at[0, s, part], across)
+        add_into(block, [block, ff_own(s, 0, part)])
+        start(push(block, ff_far(s, part), far_send.at[s, part], far_recv.at[s, part], far))
+
+    def rs_second(s, part):
+        block = ff_across(s, 1, part)
+        part_copy(s, 1, part).wait()
+        arrived(block, across_recv.at[1, s, part], across)
+        arrived(ff_far(s, part), far_recv.at[s, part], far)
+        target = down_sum.at[s] if part == 2 else block
+        add_into(target, [block, ff_far(s, part), ff_own(s, 1, part)])
 
     def share(step, s):
         number = 2 * flip(x, step[1]) + flip(core, step[2])
@@ -1297,107 +1382,104 @@
 
     def place_units(step, s, source):
         unit = down_height
+        number = 8 * flip(zl, step[0]) + 2 * flip(x, step[1]) + flip(core, step[2])
         for side in (0, 1):
             for group in range(4):
                 zh_part, y_part = divmod(group, 2)
-                number = 8 * flip(zl, step[0]) + 2 * flip(x, step[1]) + flip(core, step[2])
                 left = (32 * side + 16 * zh_part + 4 * y_part + number) * unit
                 gate_up_total[s, :, pl.ds(pl.multiple_of(left, unit), unit)] = source[
                     :, (4 * side + group) * unit : (4 * side + group + 1) * unit
                 ].astype(F32)
 
-    def ff_second():
-        for s in range(sets):
-            for low in (0, 1):
-                block = across_gate.at[1, s, low]
-                arrived(block, across_recv.at[1, s, low], across)
-                arrived(far_gate.at[s, low], far_recv.at[s, low], far)
-                add_into(block, [block, far_gate.at[s, low], gate_own.at[1, s, low]])
-            for slot, step in enumerate(RANK_STEPS):
-                if step != own_step:
-                    start(
-                        push(
-                            share(step, s),
-                            gate_up_sum.at[rank(own_step), s],
-                            rank_send.at[slot, s],
-                            rank_recv.at[slot, s],
-                            member(step),
-                        )
-                    )
-            place_units(own_step, s, share(own_step, s))
-            arrived(across_down.at[1, s], across_recv.at[1, s, 2], across)
-            arrived(far_down.at[s], far_recv.at[s, 2], far)
-            add_into(down_sum.at[s], [across_down.at[1, s], far_down.at[s], down_own.at[1, s]])
-
-    def ff_last():
-        for slot, step in enumerate(RANK_STEPS):
-            for s in range(sets):
-                if step != own_step:
-                    block = gate_up_sum.at[rank(step), s]
-                    arrived(block, rank_recv.at[slot, s], member(step))
-                    place_units(step, s, block)
+    def rs_rank(s, slot):
+        step = RANK_STEPS[slot]
+        start(
+            push(
+                share(step, s),
+                gate_up_sum.at[rank(own_step), s],
+                rank_send.at[slot, s],
+                rank_recv.at[slot, s],
+                member(step),
+            )
+        )
+
+    def rs_last(s, slot):
+        step = RANK_STEPS[slot]
+        block = gate_up_sum.at[rank(step), s]
+        arrived(block, rank_recv.at[slot, s], member(step))
+        place_units(step, s, block)
 
     acts = [back_ref, out_ref]
 
     def act_rows(step):
         return pl.ds(pl.multiple_of(rank(step) * act_height, act_height), act_height)
 
-    def act_core_sends(which):
+    def act_core(which, s):
         for dl, dx in ((1, 1), (0, 1), (1, 0), (0, 0)):
             start(
                 push(
-                    acts[which].at[:, act_rows((dl, dx, 1))],
-                    core_buf.at[which, dl, dx],
-                    core_send.at[which, dl, dx],
-                    core_recv.at[which, dl, dx],
+                    acts[which].at[s, act_rows((dl, dx, 1))],
+                    core_buf.at[which, s, dl, dx],
+                    core_send.at[which, s, dl, dx],
+                    core_recv.at[which, s, dl, dx],
                     sibling,
                 )
             )
 
+    def act_copy(which, s, dl, dx):
+        return pltpu.make_async_copy(
+            acts[which].at[s, act_rows((dl, dx, 0))],
+            act_own.at[s, dl, dx],
+            own_sem.at[which, s, dl, dx],
+        )
+
     def act_load(which):
-        return [
-            pltpu.make_async_copy(
-                acts[which].at[:, act_rows((dl, dx, 0))], act_own.at[dl, dx], own_sem.at[which, dl, dx]
-            )
-            for dl in (0, 1)
-            for dx in (0, 1)
-        ]
-
-    def core_add(which, dl, dx):
-        block = core_buf.at[which, dl, dx]
-        arrived(block, core_recv.at[which, dl, dx], sibling)
         for s in range(sets):
-            add_into(block.at[s], [block.at[s], act_own.at[dl, dx, s]])
-
-    def act_first(which):
-        for dl in (1, 0):
-            core_add(which, dl, 1)
-            start(
-                push(
-                    core_buf.at[which, dl, 1],
-                    x_buf.at[which, dl],
-                    x_send.at[which, dl],
-                    x_recv.at[which, dl],
-                    member((0, 1, 0)),
-                )
-            )
-        core_add(which, 1, 0)
-        core_add(which, 0, 0)
-
-    def act_second(which):
-        arrived(x_buf.at[which, 1], x_recv.at[which, 1], member((0, 1, 0)))
-        for s in range(sets):
-            block = x_buf.at[which, 1, s]
-            add_into(block, [block, core_buf.at[which, 1, 0, s]])
+            for dl in (0, 1):
+                for dx in (0, 1):
+                    act_copy(which, s, dl, dx).start()
+
+    def act_ready(which, s, dl, dx):
+        act_copy(which, s, dl, dx).wait()
+        arrived(core_buf.at[which, s, dl, dx], core_recv.at[which, s, dl, dx], sibling)
+
+    def act_add_x(which, s, dl):
+        act_ready(which, s, dl, 1)
+        block = core_buf.at[which, s, dl, 1]
+        add_into(block, [block, act_own.at[s, dl, 1]])
         start(
             push(
-                x_buf.at[which, 1], z_buf.at[which], z_send.at[which], z_recv.at[which], member((1, 0, 0))
+                block,
+                x_buf.at[which, s, dl],
+                x_send.at[which, s, dl],
+                x_recv.at[which, s, dl],
+                member((0, 1, 0)),
             )
         )
 
-    def act_third(which):
-        arrived(x_buf.at[which, 0], x_recv.at[which, 0], member((0, 1, 0)))
-        arrived(z_buf.at[which], z_recv.at[which], member((1, 0, 0)))
+    def act_add_z(which, s):
+        act_ready(which, s, 1, 0)
+        block = x_buf.at[which, s, 1]
+        arrived(block, x_recv.at[which, s, 1], member((0, 1, 0)))
+        add_into(block, [block, core_buf.at[which, s, 1, 0], act_own.at[s, 1, 0]])
+        start(
+            push(
+                block, z_buf.at[which, s], z_send.at[which, s], z_recv.at[which, s], member((1, 0, 0))
+            )
+        )
+
+    def act_sum(which, s):
+        act_ready(which, s, 0, 0)
+        arrived(x_buf.at[which, s, 0], x_recv.at[which, s, 0], member((0, 1, 0)))
+        arrived(z_buf.at[which, s], z_recv.at[which, s], member((1, 0, 0)))
+
+    def act_total(which, s, rows):
+        return (
+            act_own[s, 0, 0, rows, :].astype(F32)
+            + core_buf[which, s, 0, 0, rows, :].astype(F32)
+            + x_buf[which, s, 0, rows, :].astype(F32)
+            + z_buf[which, s, rows, :].astype(F32)
+        )
 
     pieces = [
         (qkv_grad, qkv_sum, 0, "zxy", slots_0),
@@ -1471,11 +1553,6 @@
 
         maybe(offset_exists(offset, z), go)
 
-    def tree_steps(which, distances):
-        for hop, _, piece, offset in events:
-            if piece in which and -hop in distances:
-                tree_step(piece, offset)
-
     def gains_copy(step):
         other = lax.rem(me + step, 32)
         return push(
@@ -1497,9 +1574,6 @@
         gains_sum[...] += gains_buf[other]
         return carry
 
-    def swap_copy(index, source, target):
-        return push(source, target, swap_send.at[index], swap_recv.at[index], sibling)
-
     def turn(source, target, slot):
         def one(block, p):
             flat = source(p, block)
@@ -1525,73 +1599,54 @@
         pltpu.make_async_copy(out_full.at[p], out_tiles.at[p], tile_sem.at[2 + p]) for p in range(positions)
     ]
 
-    act_core_sends(0)
-    ff_across(0)
-    ff_across(1)
-    load_back = act_load(0)
-    for copy in load_back + out_loads + part_copies:
-        copy.start()
-    act_core_sends(1)
-    qkv_load(0).start()
-    qkv_load(1).start()
-    make_spread(spread)
-    gain_acc[...] = jnp.zeros_like(gain_acc)
-    for copy in load_back:
-        copy.wait()
-    act_first(0)
-    load_out = act_load(1)
-    for copy in load_out:
-        copy.start()
-
     def context_block(p, block):
         return context[p, :, 128 * block : 128 * block + 128].astype(F32)
 
-    def attn_norm(rows):
-        values = tokens_ref[rows].astype(F32)
+    def attn_block(p, block):
+        return d_rows[p, :, 128 * block : 128 * block + 128]
+
+    def norm_turn():
+        def attn_norm(rows):
+            values = tokens_ref[rows].astype(F32)
+            for p in range(positions):
+                r, _ = normed(values[:, p, :])
+                d_rows[p, rows, :] = r * gain_rows[p : p + 1, :]
+
+        row_loop(act_height, 16, attn_norm)
+        turn(context_block, context_turned, 0)
+        turn(attn_block, attn_turned, 1)
+
+    def landing(kind, p):
+        other = pl.ds(act_height, act_height)
+        return (
+            context_turned.at[p, :, :, other],
+            attn_turned.at[p, :, :, other],
+            d_mid_low.at[p, other],
+            d_qkv.at[p, other],
+        )[kind]
+
+    def swap(kind, p, source):
+        start(
+            push(source, landing(kind, p), swap_send.at[4 * p + kind], swap_recv.at[4 * p + kind], sibling)
+        )
+
+    def swap_wait(kind, p):
+        arrived(landing(kind, p), swap_recv.at[4 * p + kind], sibling)
+
+    def swap_turned():
         for p in range(positions):
-            r, _ = normed(values[:, p, :])
-            d_rows[p, rows, :] = r * gain_rows[p : p + 1, :]
-
-    row_loop(act_height, 16, attn_norm)
-    turn(context_block, context_turned, 0)
-    turn(
-        lambda p, block: d_rows[p, :, 128 * block : 128 * block + 128], attn_turned, 1
-    )
-    swaps = []
-    for p in range(positions):
-        swaps.append(
-            swap_copy(
-                4 * p,
-                turned.at[0, p, :, 1 - core],
-                context_turned.at[p, :, :, pl.ds(act_height, act_height)],
-            )
-        )
-        swaps.append(
-            swap_copy(
-                4 * p + 1,
-                turned.at[1, p, :, 1 - core],
-                attn_turned.at[p, :, :, pl.ds(act_height, act_height)],
-            )
-        )
-        swaps[-1].start()
-        swaps[-2].start()
-    act_second(0)
-    for copy in part_copies:
-        copy.wait()
-    ff_first()
-    for p in range(positions):
-        probs = attention_probs(qkv_rows, halves, spread, model, p)
-        for q in range(p + 1):
-            probs_buf[pairs.index((p, q))] = probs[q]
-    act_third(0)
-
-    def mid_back(rows):
+            swap(0, p, turned.at[0, p, :, 1 - core])
+            swap(1, p, turned.at[1, p, :, 1 - core])
+
+    def find_probs():
         for p in range(positions):
-            d_ff_in = (
-                core_buf[0, 0, 0, p, rows, :].astype(F32)
-                + x_buf[0, 0, p, rows, :].astype(F32)
-                + z_buf[0, p, rows, :].astype(F32)
-            )
+            probs = attention_probs(qkv_rows, halves, spread, model, p)
+            for q in range(p + 1):
+                probs_buf[pairs.index((p, q))] = probs[q]
+
+    def mid(p):
+        def mid_back(rows):
+            d_ff_in = act_total(0, p, rows)
             r, inverse = normed(resid_mid[p, rows, :])
             gain_acc[positions + p] += r * d_ff_in
             total = cot_ref[p, rows, :] + norm_back(
@@ -1600,162 +1655,160 @@
             d_mid[p, rows, :] = total
             d_mid_low[p, rows, :] = total.astype(BF16)
 
-    row_loop(act_height, 16, mid_back)
-    for p in range(positions):
-        swaps.append(
-            swap_copy(
-                4 * p + 2,
-                d_mid_low.at[p, pl.ds(0, act_height)],
-                d_mid_low.at[p, pl.ds(act_height, act_height)],
-            )
-        )
-        swaps[-1].start()
-    for copy in out_loads:
-        copy.wait()
-    for p in range(positions):
-
-        def context_back(columns, p=p):
-            d_context[p, :, columns] = lax.dot_general(
-                d_mid_low[p, :act_height, :],
-                out_tiles[p, columns, :],
-                (((1,), (1,)), ((), ())),
-                preferred_element_type=F32,
+        row_loop(act_height, 16, mid_back)
+        swap(2, p, d_mid_low.at[p, pl.ds(0, act_height)])
+        out_loads[p].wait()
+
+        def context_back(columns):
+            d_context[p, :, columns] = dot_back(
+                d_mid_low[p, :act_height, :], out_tiles[p, columns, :]
             ).astype(BF16)
 
         tile_loop(model, 256, context_back)
 
-    def context_products(rows):
-        for index, (p, q) in enumerate(pairs):
-            product = d_context[p, rows, :].astype(F32) * qkv_rows[q, rows, 2 * model :].astype(F32)
-            halves[2 * index, rows, :], halves[2 * index + 1, rows, :] = split_product(product)
-
-    row_loop(act_height, 16, context_products)
-    d_probs = [sums_over_heads(halves, spread, index) for index in range(len(pairs))]
-    for p in range(positions):
-        own = [index for index, pair in enumerate(pairs) if pair[0] == p]
-        mean = functools.reduce(jnp.add, [probs_buf[index] * d_probs[index] for index in own])
-        for index in own:
-            d_score = (probs_buf[index] * (d_probs[index] - mean)).astype(BF16)
-            halves[2 * index] = to_heads(d_score, spread)
-            halves[2 * index + 1] = to_heads(probs_buf[index].astype(BF16), spread)
-
-    def qkv_back(rows):
-        d_keys = [None] * positions
-        d_values = [None] * positions
+    def scores_back():
+        def context_products(rows):
+            for index, (p, q) in enumerate(pairs):
+                product = d_context[p, rows, :].astype(F32) * qkv_rows[q, rows, 2 * model :].astype(F32)
+                halves[2 * index, rows, :], halves[2 * index + 1, rows, :] = split_product(product)
+
+        row_loop(act_height, 16, context_products)
+        d_probs = [sums_over_heads(halves, spread, index) for index in range(len(pairs))]
+        for p in range(positions):
+            own = [index for index, pair in enumerate(pairs) if pair[0] == p]
+            mean = functools.reduce(jnp.add, [probs_buf[index] * d_probs[index] for index in own])
+            for index in own:
+                d_score = (probs_buf[index] * (d_probs[index] - mean)).astype(BF16)
+                halves[2 * index] = to_heads(d_score, spread)
+                halves[2 * index + 1] = to_heads(probs_buf[index].astype(BF16), spread)
 
         def plus(total, term):
             return term if total is None else total + term
 
+        def qkv_back(rows):
+            d_keys = [None] * positions
+            d_values = [None] * positions
+            for p in range(positions):
+                d_query = None
+                d_own = d_context[p, rows, :].astype(F32)
+                query = qkv_rows[p, rows, :model].astype(F32)
+                for index, (own, q) in enumerate(pairs):
+                    if own == p:
+                        d_score = halves[2 * index, rows, :].astype(F32)
+                        key = qkv_rows[q, rows, model : 2 * model].astype(F32)
+                        d_query = plus(d_query, d_score * key)
+                        d_keys[q] = plus(d_keys[q], d_score * query)
+                        d_values[q] = plus(
+                            d_values[q], halves[2 * index + 1, rows, :].astype(F32) * d_own
+                        )
+                d_qkv[p, rows, :model] = (d_query * scale).astype(BF16)
+            for p in range(positions):
+                d_qkv[p, rows, model : 2 * model] = (d_keys[p] * scale).astype(BF16)
+                d_qkv[p, rows, 2 * model :] = d_values[p].astype(BF16)
+
+        row_loop(act_height, 16, qkv_back)
+
+    def swap_qkv():
         for p in range(positions):
-            d_query = None
-            d_own = d_context[p, rows, :].astype(F32)
-            query = qkv_rows[p, rows, :model].astype(F32)
-            for index, (own, q) in enumerate(pairs):
-                if own == p:
-                    d_score = halves[2 * index, rows, :].astype(F32)
-                    key = qkv_rows[q, rows, model : 2 * model].astype(F32)
-                    d_query = plus(d_query, d_score * key)
-                    d_keys[q] = plus(d_keys[q], d_score * query)
-                    d_values[q] = plus(d_values[q], halves[2 * index + 1, rows, :].astype(F32) * d_own)
-            d_qkv[p, rows, :model] = (d_query * scale).astype(BF16)
-        for p in range(positions):
-            d_qkv[p, rows, model : 2 * model] = (d_keys[p] * scale).astype(BF16)
-            d_qkv[p, rows, 2 * model :] = d_values[p].astype(BF16)
-
-    row_loop(act_height, 16, qkv_back)
-    for p in range(positions):
-        swaps.append(
-            swap_copy(
-                4 * p + 3,
-                d_qkv.at[p, pl.ds(0, act_height)],
-                d_qkv.at[p, pl.ds(act_height, act_height)],
+            swap(3, p, d_qkv.at[p, pl.ds(0, act_height)])
+
+    def out_weights(p):
+        swap_wait(0, p)
+        swap_wait(2, p)
+
+        def tile(columns):
+            out_grad[p, :, columns] = dot(
+                context_turned[p].reshape(half, 2 * act_height), d_mid_low[p, :, columns]
+            ).astype(BF16)
+
+        tile_loop(model, 256, tile)
+
+    def qkv_weights(p):
+        swap_wait(1, p)
+        swap_wait(3, p)
+
+        def tile(columns):
+            qkv_grad[p, :, columns] = dot(
+                attn_turned[p].reshape(half, 2 * act_height), d_qkv[p, :, columns]
+            ).astype(BF16)
+
+        tile_loop(3 * model, 256, tile)
+
+    def rows_back(p):
+        for tile in range(tile_count):
+            number = p * tile_count + tile
+            qkv_load(number).wait()
+            d_rows[p, :, tile * qkv_tile : (tile + 1) * qkv_tile] = dot_back(
+                d_qkv[p, :act_height, :], qkv_tiles[number % 2]
             )
-        )
-        swaps[-1].start()
-
-    def swap_wait(index, target):
-        arrived(target, swap_recv.at[index], sibling)
-
-    for p in range(positions):
-        swap_wait(4 * p, context_turned.at[p, :, :, pl.ds(act_height, act_height)])
-        swap_wait(4 * p + 2, d_mid_low.at[p, pl.ds(act_height, act_height)])
-
-        def out_weights(columns, p=p):
-            out_grad[p, :, columns] = jnp.dot(
-                context_turned[p].reshape(half, 2 * act_height),
-                d_mid_low[p, :, columns],
-                preferred_element_type=F32,
-            ).astype(BF16)
-
-        tile_loop(model, 256, out_weights)
-    tree_steps((2, 3), (5,))
-    for copy in load_out:
-        copy.wait()
-    act_first(1)
-    for p in range(positions):
-        swap_wait(4 * p + 1, attn_turned.at[p, :, :, pl.ds(act_height, act_height)])
-        swap_wait(4 * p + 3, d_qkv.at[p, pl.ds(act_height, act_height)])
-
-        def qkv_weights(columns, p=p):
-            qkv_grad[p, :, columns] = jnp.dot(
-                attn_turned[p].reshape(half, 2 * act_height),
-                d_qkv[p, :, columns],
-                preferred_element_type=F32,
-            ).astype(BF16)
-
-        tile_loop(3 * model, 256, qkv_weights)
-        tree_steps((p,), (5,))
-    tree_steps((0, 1, 2, 3), (4,))
-    act_second(1)
-    ff_second()
-    for number in range(positions * tile_count):
-        p, tile = divmod(number, tile_count)
-        qkv_load(number).wait()
-        d_rows[p, :, tile * qkv_tile : (tile + 1) * qkv_tile] = lax.dot_general(
-            d_qkv[p, :act_height, :],
-            qkv_tiles[number % 2],
-            (((1,), (1,)), ((), ())),
-            preferred_element_type=F32,
-        )
-        if number + 2 < positions * tile_count:
-            qkv_load(number + 2).start()
-    tree_steps((0, 1, 2, 3), (3,))
-
-    def attn_back(rows):
-        values = tokens_ref[rows].astype(F32)
-        for p in range(positions):
-            r, inverse = normed(values[:, p, :])
-            d_attn_in = d_rows[p, rows, :]
-            gain_acc[p] += r * d_attn_in
-            grad_tokens[rows, p, :] = d_mid[p, rows, :] + norm_back(
-                r, inverse, d_attn_in * gain_rows[p : p + 1, :]
-            )
-
-    row_loop(act_height, 16, attn_back)
-    gains_part[...] = jnp.zeros_like(gains_part)
-    for index in range(2 * positions):
-        sums = jnp.sum(gain_acc[index], axis=0, keepdims=True)
-        for block in range(8):
-            gains_part[block, index : index + 1, :] = sums[:, 128 * block : 128 * block + 128]
-    lax.fori_loop(1, 32, gains_start, 0)
-    tree_steps((0, 1, 2, 3), (2,))
-    act_third(1)
-
-    def finish_output(rows):
-        rounded = []
-        for p in range(positions):
-            total = (
-                core_buf[1, 0, 0, p, rows, :].astype(F32)
-                + x_buf[1, 0, p, rows, :].astype(F32)
-                + z_buf[1, p, rows, :].astype(F32)
-            )
-            rounded.append(resid_mid[p, rows, :] + total)
-        output[rows] = jnp.stack(rounded, axis=1).astype(BF16)
-
-    row_loop(act_height, 16, finish_output)
-    tree_steps((0, 1, 2, 3), (1,))
-    tree_steps((0, 1, 2, 3), (0,))
-    ff_last()
+            if number + 2 < positions * tile_count:
+                qkv_load(number + 2).start()
+
+    def attn_back():
+        def norm_one_back(rows):
+            values = tokens_ref[rows].astype(F32)
+            for p in range(positions):
+                r, inverse = normed(values[:, p, :])
+                d_attn_in = d_rows[p, rows, :]
+                gain_acc[p] += r * d_attn_in
+                grad_tokens[rows, p, :] = d_mid[p, rows, :] + norm_back(
+                    r, inverse, d_attn_in * gain_rows[p : p + 1, :]
+                )
+
+        row_loop(act_height, 16, norm_one_back)
+        gains_part[...] = jnp.zeros_like(gains_part)
+        for index in range(2 * positions):
+            sums = jnp.sum(gain_acc[index], axis=0, keepdims=True)
+            for block in range(8):
+                gains_part[block, index : index + 1, :] = sums[:, 128 * block : 128 * block + 128]
+        lax.fori_loop(1, 32, gains_start, 0)
+
+    def finish_output():
+        def finish(rows):
+            rounded = [resid_mid[p, rows, :] + act_total(1, p, rows) for p in range(positions)]
+            output[rows] = jnp.stack(rounded, axis=1).astype(BF16)
+
+        row_loop(act_height, 16, finish)
+
+    for s in range(sets):
+        for turn_number in (0, 1):
+            for part in (0, 1, 2):
+                part_copy(s, turn_number, part).start()
+    for copy in out_loads:
+        copy.start()
+    act_load(0)
+    qkv_load(0).start()
+    qkv_load(1).start()
+    make_spread(spread)
+    gain_acc[...] = jnp.zeros_like(gain_acc)
+    kinds = {
+        B_TREE: lambda piece, dz, dy, dx: tree_step(piece, (dz, dy, dx)),
+        B_RS_ACROSS: rs_across,
+        B_RS_FIRST: rs_first,
+        B_RS_SECOND: rs_second,
+        B_RS_RANK: rs_rank,
+        B_RS_LAST: rs_last,
+        B_ACT_CORE: act_core,
+        B_ACT_LOAD: act_load,
+        B_ACT_ADD_X: act_add_x,
+        B_ACT_ADD_Z: act_add_z,
+        B_ACT_SUM: act_sum,
+        B_NORM_TURN: norm_turn,
+        B_SWAP_TURNED: swap_turned,
+        B_PROBS: find_probs,
+        B_MID: mid,
+        B_SCORES_BACK: scores_back,
+        B_SWAP_QKV: swap_qkv,
+        B_OUT_W: out_weights,
+        B_QKV_W: qkv_weights,
+        B_ROWS_BACK: rows_back,
+        B_ATTN_BACK: attn_back,
+        B_FINISH_OUTPUT: finish_output,
+    }
+    for kind, *numbers in BACKWARD_STEPS:
+        kinds[kind](*numbers)
+    for s in range(sets):
+        place_units(own_step, s, share(own_step, s))
     gains_sum[...] = gains_part[lax.div(me, 4)]
     lax.fori_loop(1, 32, gains_wait, 0)
     own_gain = norm_attn_sum.shape[1]
@@ -1773,7 +1826,7 @@
     for _, _, piece, offset in events:
         if hops(offset) > 0:
             maybe(offset_exists(offset, z), tree_copy(piece, offset).wait_send)
-    for copy in sends + swaps:
+    for copy in sends:
         copy.wait_send()
 
 
@@ -1816,10 +1869,10 @@
         in_specs=[vmem] * 6 + [anywhere] * 6,
         out_specs=(vmem,) * 8,
         scratch_shapes=[
-            pltpu.VMEM((2, 2) + act, BF16),
-            pltpu.VMEM((2, 2, 2) + act, BF16),
-            pltpu.VMEM((2, 2) + act, BF16),
-            pltpu.VMEM((2,) + act, BF16),
+            pltpu.VMEM((sets, 2, 2, act_height, model), BF16),
+            pltpu.VMEM((2, sets, 2, 2, act_height, model), BF16),
+            pltpu.VMEM((2, sets, 2, act_height, model), BF16),
+            pltpu.VMEM((2, sets, act_height, model), BF16),
             pltpu.VMEM((2, sets, 2, 4 * height, width), BF16),
             pltpu.VMEM((2, sets, down_height, model), BF16),
             pltpu.VMEM((2, sets, 2, 4 * height, width), BF16),
@@ -1850,12 +1903,12 @@
             pltpu.VMEM((32, 8, 128), F32),
             pltpu.VMEM((8, 128), F32),
             pltpu.VMEM((8, sets, height, width), BF16),
-            dma((2, 2, 2)),
-            dma((2, 2, 2)),
-            dma((2, 2)),
-            dma((2, 2)),
-            dma((2,)),
-            dma((2,)),
+            dma((2, sets, 2, 2)),
+            dma((2, sets, 2, 2)),
+            dma((2, sets, 2)),
+            dma((2, sets, 2)),
+            dma((2, sets)),
+            dma((2, sets)),
             dma((2, sets, 3)),
             dma((2, sets, 3)),
             dma((sets, 3)),
@@ -1868,7 +1921,7 @@
             dma((4, max(places))),
             dma((32,)),
             dma((32,)),
-            dma((2, 2, 2)),
+            dma((2, sets, 2, 2)),
             dma((2, sets, 3)),
             dma((2 + sets,)),
         ],
@@ -1890,6 +1943,30 @@
         gate_up_grad,
         down_grad,
     )
+
+
+def settle_kernel(*refs):
+    count = len(refs) // 2
+    sems = refs[-1]
+    copies = [
+        pltpu.make_async_copy(refs[index], refs[count + index], sems.at[index]) for index in range(count)
+    ]
+    for copy in copies:
+        copy.start()
+    for copy in copies:
+        copy.wait()
+
+
+def settle(arrays):
+    anywhere = pl.BlockSpec(memory_space=pl.ANY)
+    return pl.pallas_call(
+        settle_kernel,
+        out_shape=tuple(jax.ShapeDtypeStruct(array.shape, array.dtype) for array in arrays),
+        in_specs=[anywhere] * len(arrays),
+        out_specs=(anywhere,) * len(arrays),
+        scratch_shapes=[pltpu.SemaphoreType.DMA((len(arrays),))],
+        name="settle",
+    )(*arrays)
 
 
 def local_fast(
@@ -1937,7 +2014,7 @@
         share_out,
         share_gate_up,
         share_down,
-    ) = backward_scatter(
+    ) = settle(backward_scatter(
         tokens,
         cot_rows,
         gain_rows,
@@ -1950,7 +2027,7 @@
         back_part,
         gate_up_grad,
         down_grad,
-    )
+    ))
     return (
         output,
         grad_tokens,

time: 351 us -> 509 us (1.45)
  Pallas kernels: 337 us -> 507 us
  local copies, waits for them, and re-layouts: 11.6 us -> 0 us
    pallas_call x0 -> x1, Pallas kernels: none -> 176 us  [settle(): pl.pallas_call(settle_kernel, out_shape=tuple((jax.ShapeDtypeStruct(array...]
    unnamed x16 -> x0, local copies, waits for them, and re-layouts: 11.6 us -> none
    pallas_call x1, Pallas kernels: 162 us -> 157 us  [backward_scatter(): pl.pallas_call(backward_kernel, out_shape=(jax.ShapeDtypeStruct(tokens.sh...]
where the time goes in v6:
time: 509 us
  Pallas kernels  507 us (100%)
    pallas_call x1, Pallas kernels, settle(): pl.pallas_call(settle_kernel, out_shape=tuple((jax.ShapeDtypeStruct(array...  176 us
    pallas_call x1, Pallas kernels, forward_gather(): pl.pallas_call(forward_kernel, out_shape=(jax.ShapeDtypeStruct((16, model...  175 us
    pallas_call x1, Pallas kernels, backward_scatter(): pl.pallas_call(backward_kernel, out_shape=(jax.ShapeDtypeStruct(tokens.sh...  157 us

profile of v6, /device:TPU:0, one launch (start us, length us, event | category | flops | bytes accessed | tf_op | source)
XLA Modules:
  0.0 508.9 jit_solution(9686169747805772364)
XLA Ops:
  1.3 174.8 %forward_gather.1 = (f32[16,1024]{1,0:T(8,128)}, f32[2,128,1024]{2,1,0:T(8,128)}, bf16[2,128,3072]{2,1,0:T(8,128)(2,1)}, bf16[2,128,1024]{2,1,0:T(8,128)(2,1)}, ...) custom-call(s32[1]{0:T(128)S(6)} %copy.18.valid_ref, ...), custom_call_target="tpu_custom_call" | custom-call | tf_op jit(solution)/shard_map/forward_gather/pallas_call | solution.py:1071
  176.1 156.7 %backward_scatter.1 = (bf16[128,2,1024]{2,1,0:T(2,128)(2,1)}, f32[128,2,1024]{2,1,0:T(2,128)}, f32[2,32]{1,0:T(2,128)}, f32[2,32]{1,0:T(2,128)}, f32[2,32,3072]{...) custom-call(bf16[128,2,1024]{2,1,0:T(2,128)(2,1)} %tokens_ref.3, ...), custom_call_target="tpu_custom_call" | custom-call | tf_op jit(solution)/shard_map/backward_scatter/pallas_call | solution.py:1857
  332.8 175.9 %settle.1 = (bf16[128,2,1024]{2,1,0:T(2,128)(2,1)}, f32[128,2,1024]{2,1,0:T(2,128)}, f32[2,32]{1,0:T(2,128)}, f32[2,32]{1,0:T(2,128)}, f32[2,32,3072]{2,1,0:T(8,...) custom-call(bf16[128,2,1024]{2,1,0:T(2,128)(2,1)} %get-tuple-element.46.refs_0_, ...), custom_call_target="tpu_custom_call" | custom-call | tf_op jit(solution)/shard_map/settle/pallas_call | solution.py:1962

commit v7 on v6

--- a/solution.py
+++ b/solution.py
@@ -1962,7 +1962,7 @@
     return pl.pallas_call(
         settle_kernel,
         out_shape=tuple(jax.ShapeDtypeStruct(array.shape, array.dtype) for array in arrays),
-        in_specs=[anywhere] * len(arrays),
+        in_specs=[pl.BlockSpec(memory_space=pltpu.VMEM)] * len(arrays),
         out_specs=(anywhere,) * len(arrays),
         scratch_shapes=[pltpu.SemaphoreType.DMA((len(arrays),))],
         name="settle",

time: 509 us -> 339 us (0.67)
  Pallas kernels: 507 us -> 337 us
    pallas_call x1, Pallas kernels: 176 us -> 5.26 us  [settle(): pl.pallas_call(settle_kernel, out_shape=tuple((jax.ShapeDtypeStruct(array...]
where the time goes in v7:
time: 339 us; the launch traced here: 338 us
  Pallas kernels  337 us (99%)
    pallas_call x1, Pallas kernels, forward_gather(): pl.pallas_call(forward_kernel, out_shape=(jax.ShapeDtypeStruct((16, model...  175 us
    pallas_call x1, Pallas kernels, backward_scatter(): pl.pallas_call(backward_kernel, out_shape=(jax.ShapeDtypeStruct(tokens.sh...  157 us

profile of v7, /device:TPU:0, one launch (start us, length us, event | category | flops | bytes accessed | tf_op | source)
XLA Modules:
  0.0 338.3 jit_solution(17712847311220698060)
XLA Ops:
  1.3 174.8 %forward_gather.1 = (f32[16,1024]{1,0:T(8,128)}, f32[2,128,1024]{2,1,0:T(8,128)}, bf16[2,128,3072]{2,1,0:T(8,128)(2,1)}, bf16[2,128,1024]{2,1,0:T(8,128)(2,1)}, ...) custom-call(s32[1]{0:T(128)S(6)} %copy.18.valid_ref, ...), custom_call_target="tpu_custom_call" | custom-call | tf_op jit(solution)/shard_map/forward_gather/pallas_call | solution.py:1071
  176.1 156.7 %backward_scatter.1 = (bf16[128,2,1024]{2,1,0:T(2,128)(2,1)}, f32[128,2,1024]{2,1,0:T(2,128)}, f32[2,32]{1,0:T(2,128)}, f32[2,32]{1,0:T(2,128)}, f32[2,32,3072]{...) custom-call(bf16[128,2,1024]{2,1,0:T(2,128)(2,1)} %tokens_ref.3, ...), custom_call_target="tpu_custom_call" | custom-call | tf_op jit(solution)/shard_map/backward_scatter/pallas_call | solution.py:1857
  332.8 5.3 %settle.1 = (bf16[128,2,1024]{2,1,0:T(2,128)(2,1)}, f32[128,2,1024]{2,1,0:T(2,128)}, f32[2,32]{1,0:T(2,128)}, f32[2,32]{1,0:T(2,128)}, f32[2,32,3072]{2,1,0:T(8,...) custom-call(bf16[128,2,1024]{2,1,0:T(2,128)(2,1)} %get-tuple-element.46.refs_0_, ...), custom_call_target="tpu_custom_call" | custom-call | tf_op jit(solution)/shard_map/settle/pallas_call | solution.py:1962

commit v8 on v7

--- a/solution.py
+++ b/solution.py
@@ -331,6 +331,20 @@
 
 def direction_exists(direction, z):
     return {"u": z < 3, "d": z > 0}.get(direction)
+
+
+def return_count(order, direction, level):
+    return sum(
+        hops(offset) > 0 and came_from(order, offset) == direction
+        for offset in OFFSETS
+        if 0 <= level + offset[0] <= 3
+    )
+
+
+def tree_count(order, direction, level):
+    return sum(
+        direction in onward(order, offset) for offset in OFFSETS if 0 <= level + offset[0] <= 3
+    )
 
 
 DIRECTIONS = ("x", "y", "u", "d", "s")
@@ -637,51 +651,53 @@
         source, _, index, columns, _ = pieces[piece]
         chip = chip_of(offset, z, y, x)
         block = piece_rows(piece, 2 * chip + core)
-        recv = sibling_sem if direction == "s" else plane_sem
         return push(
             source.at[index, :, columns] if hops(offset) == 0 else block,
             block,
-            send_sem.at[piece, chip, DIRECTIONS.index(direction)],
-            recv.at[piece, chip],
+            send_sem.at[piece, DIRECTIONS.index(direction)],
+            sibling_sem.at[piece] if direction == "s" else plane_sem.at[piece, chip],
             neighbour(direction, z, y, x, core),
         )
 
-    def tree_step(piece, offset, finish=False):
+    def tree_step(piece, offset):
         order = pieces[piece][4]
 
         def go():
             chip = chip_of(offset, z, y, x)
-            if hops(offset) > 0 and not finish:
+            if hops(offset) > 0:
                 arrived(piece_rows(piece, 2 * chip + core), plane_sem.at[piece, chip], sibling)
             for direction in onward(order, offset) + ["s"]:
                 copy = tree_send(piece, offset, direction)
-                maybe(direction_exists(direction, z), copy.wait_send if finish else copy.start)
+                maybe(direction_exists(direction, z), copy.start)
 
         maybe(offset_exists(offset, z), go)
 
-    events = sorted(
-        (
-            (hops(offset), place, piece, offset)
-            for piece in range(len(pieces))
-            for place, offset in enumerate(OFFSETS)
-        ),
-        key=lambda event: event[:3],
-    )
-
-    def tree_steps(s, distance):
-        for hop, _, piece, offset in events:
-            if hop == distance and pieces[piece][2] == s:
-                tree_step(piece, offset)
+    def tree_bytes(piece, count):
+        _, full, index, columns, _ = pieces[piece]
+        return full.at[index, pl.ds(0, count * height), columns]
+
+    def tree_sent(piece):
+        order = pieces[piece][4]
+
+        def sent(direction, count):
+            block = tree_bytes(piece, count)
+            push(block, block, send_sem.at[piece, DIRECTIONS.index(direction)], gains_recv, sibling).wait_send()
+
+        sent("s", 16)
+        for direction in "xy":
+            sent(direction, tree_count(order, direction, 3))
+        for direction in "ud":
+            for level in range(4):
+                if level != (3 if direction == "u" else 0):
+                    pl.when(z == level)(
+                        functools.partial(sent, direction, tree_count(order, direction, level))
+                    )
 
     def tree_end(s):
         mine = [piece for piece in range(len(pieces)) if pieces[piece][2] == s]
 
-        def sibling_wait(chip, carry):
-            for piece in mine:
-                arrived(piece_rows(piece, 2 * chip + 1 - core), sibling_sem.at[piece, chip], sibling)
-            return carry
-
-        lax.fori_loop(0, 16, sibling_wait, 0)
+        for piece in mine:
+            arrived(tree_bytes(piece, 16), sibling_sem.at[piece], sibling)
         for piece in mine:
             tree_own[piece].wait()
 
@@ -697,8 +713,8 @@
         return push(
             gains_own,
             gains_all.at[me],
-            gains_send.at[step],
-            gains_recv.at[me],
+            gains_send,
+            gains_recv,
             (lax.div(other, 2), lax.rem(other, 2)),
         )
 
@@ -706,17 +722,8 @@
         gains_copy(step).start()
         return carry
 
-    def gains_wait(step, carry):
-        other = lax.rem(me + step, 32)
-        gains_copy(step).wait_send()
-        arrived(gains_all.at[other], gains_recv.at[other], sibling)
-        return carry
-
-    sends = []
-
     def start(copy):
         copy.start()
-        sends.append(copy)
 
     def weight_rows(s, number):
         return gate_up_buf.at[s, pl.ds(pl.multiple_of(number * height, height), height), :]
@@ -735,7 +742,7 @@
             push(
                 source,
                 act_rows(which, s, step),
-                act_send.at[which, s, 4 * step[0] + 2 * step[1] + step[2], hop],
+                act_send.at[which, s, hop],
                 act_recv.at[which, s, 4 * landed[0] + 2 * landed[1] + landed[2]],
                 member(tuple(1 if axis == hop else 0 for axis in range(3))),
             )
@@ -781,22 +788,22 @@
             push(
                 gate_up_parts.at[rank(step), s],
                 weight_rows(s, device(own_step)),
-                rank_send.at[s, slot],
+                rank_send.at[s],
                 rank_recv.at[s, slot],
                 member(step),
             )
         )
 
     def send_far(s, slot, source):
-        start(push(source, ff_rows(s, slot, 0), far_send.at[s, slot], far_recv.at[s, slot], far))
+        start(push(source, ff_rows(s, slot, 0), far_send.at[s], far_recv.at[s, slot], far))
 
     def send_across(s, slot, source, dzh):
         start(
             push(
                 source,
                 ff_rows(s, slot, dzh),
-                across_send.at[s, dzh, slot],
-                across_recv.at[s, dzh, slot],
+                across_send.at[s],
+                across_recv.at[s],
                 across,
             )
         )
@@ -821,10 +828,21 @@
     def ff_end(s):
         for copy in ff_local[s]:
             copy.wait()
-        for dzh in (0, 1):
-            for slot, step in enumerate(RANK_STEPS):
-                arrived(weight_rows(s, device(step, dzh, 1)), across_recv.at[s, dzh, slot], sibling)
-            arrived(down_rows(s, dzh, 1), across_recv.at[s, dzh, 8], sibling)
+        arrived(ff_bytes(s, 2 * share), across_recv.at[s], sibling)
+
+    share = 8 * height + down_height * model // gate_up_buf.shape[2]
+
+    def ff_bytes(s, rows):
+        return gate_up_buf.at[s, pl.ds(0, rows), :]
+
+    def ff_sent(s):
+        for sem, rows in ((rank_send, 7 * height), (far_send, share), (across_send, 2 * share)):
+            block = ff_bytes(s, rows)
+            push(block, block, sem.at[s], gains_recv, sibling).wait_send()
+        for which, full in enumerate((rows_buf, grads_buf)):
+            for hop, count in enumerate((1, 2, 4)):
+                block = full.at[s, pl.ds(0, count * act_height), :]
+                push(block, block, act_send.at[which, s, hop], gains_recv, sibling).wait_send()
 
     ff_local = []
     for s in range(positions):
@@ -892,7 +910,9 @@
             ff_local[s][2].start()
 
     def take_gains():
-        lax.fori_loop(1, 32, gains_wait, 0)
+        others = gains_all.at[pl.ds(0, 31)]
+        arrived(others, gains_recv, sibling)
+        push(others, others, gains_send, gains_recv, sibling).wait_send()
         gains_local.wait()
         for block in range(8):
             total = gains_all[4 * block].astype(F32)
@@ -1049,10 +1069,10 @@
     }
     for kind, *numbers in FORWARD_STEPS:
         kinds[kind](*numbers)
-    for _, _, piece, offset in events:
-        tree_step(piece, offset, finish=True)
-    for copy in sends:
-        copy.wait_send()
+    for piece in range(len(pieces)):
+        tree_sent(piece)
+    for s in range(positions):
+        ff_sent(s)
     for copy in keep:
         copy.wait()
     stages_end()
@@ -1107,17 +1127,17 @@
             pltpu.VMEM((2 * positions, act_height, model), BF16),
             pltpu.VMEM((model, 128), BF16),
             dma((6, 16)),
-            dma((6, 16)),
-            dma((6, 16, 5)),
-            dma((32,)),
-            dma((32,)),
+            dma((6,)),
+            dma((6, 5)),
+            dma,
+            dma,
+            dma((2,)),
             dma((2, 8)),
-            dma((2, 8)),
+            dma((2,)),
             dma((2, 9)),
-            dma((2, 9)),
-            dma((2, 2, 9)),
-            dma((2, 2, 9)),
-            dma((2, 2, 8, 3)),
+            dma((2,)),
+            dma((2,)),
+            dma((2, 2, 3)),
             dma((2, 2, 8)),
             dma((14,)),
             dma((4,)),
@@ -1178,50 +1198,49 @@
     B_FINISH_OUTPUT,
 ) = range(22)
 BACKWARD_STEPS = [
-    (B_RS_ACROSS, 0, 0, 0), (B_ACT_CORE, 0, 0), (B_ACT_ADD_X, 0, 0, 1), (B_NORM_TURN,), (B_RS_FIRST, 0, 0),
-    (B_RS_ACROSS, 0, 0, 1), (B_ACT_CORE, 0, 1), (B_ACT_ADD_Z, 0, 0), (B_ACT_ADD_X, 0, 0, 0),
-    (B_ACT_ADD_X, 0, 1, 1), (B_RS_ACROSS, 1, 1, 0), (B_SWAP_TURNED,), (B_RS_ACROSS, 0, 1, 0),
-    (B_RS_ACROSS, 0, 0, 2), (B_ACT_ADD_X, 0, 1, 0), (B_RS_FIRST, 0, 1), (B_RS_ACROSS, 1, 0, 1),
-    (B_RS_ACROSS, 0, 1, 1), (B_PROBS,), (B_RS_ACROSS, 1, 1, 1), (B_ACT_ADD_Z, 0, 1), (B_RS_FIRST, 0, 2),
-    (B_ACT_CORE, 1, 0), (B_ACT_SUM, 0, 0), (B_ACT_SUM, 0, 1), (B_MID, 1), (B_MID, 0), (B_ACT_LOAD, 1),
-    (B_OUT_W, 0), (B_OUT_W, 1), (B_ACT_CORE, 1, 1), (B_ACT_ADD_X, 1, 0, 1), (B_RS_FIRST, 1, 1),
-    (B_TREE, 2, -3, 0, 0), (B_SCORES_BACK,), (B_TREE, 2, -3, 1, 1), (B_TREE, 3, 3, 0, 0),
-    (B_RS_ACROSS, 1, 0, 2), (B_SWAP_QKV,), (B_ACT_ADD_X, 1, 0, 0), (B_TREE, 3, 3, 0, 1), (B_TREE, 2, 3, 1, 0),
-    (B_TREE, 3, -3, 0, 1), (B_RS_SECOND, 0, 1), (B_TREE, 2, -3, 0, 1), (B_QKV_W, 0), (B_ACT_ADD_X, 1, 1, 1),
-    (B_TREE, 2, 3, 1, 1), (B_RS_FIRST, 1, 2), (B_RS_ACROSS, 0, 1, 2), (B_TREE, 0, -1, 1, 1),
-    (B_RS_ACROSS, 1, 0, 0), (B_QKV_W, 1), (B_TREE, 2, 2, 1, 1), (B_TREE, 1, 2, 1, 1), (B_TREE, 2, 3, 0, 0),
-    (B_TREE, 2, 2, 1, 0), (B_TREE, 0, -3, 1, 1), (B_RS_SECOND, 0, 0), (B_RS_ACROSS, 1, 1, 2),
-    (B_TREE, 1, 1, 1, 1), (B_TREE, 2, 3, 0, 1), (B_TREE, 0, 1, 1, 1), (B_TREE, 1, -3, 1, 1),
-    (B_TREE, 1, -1, 0, 1), (B_TREE, 2, -2, 1, 1), (B_TREE, 0, 3, 1, 0), (B_TREE, 3, -3, 1, 0),
-    (B_TREE, 1, 0, 1, 1), (B_RS_RANK, 0, 1), (B_TREE, 3, 2, 0, 1), (B_TREE, 2, -3, 1, 0), (B_TREE, 2, -1, 1, 1),
-    (B_TREE, 3, 3, 1, 0), (B_TREE, 2, -2, 0, 0), (B_TREE, 3, -2, 0, 1), (B_TREE, 1, -3, 0, 1),
-    (B_TREE, 3, 3, 1, 1), (B_TREE, 0, 3, 1, 1), (B_TREE, 3, -3, 1, 1), (B_RS_SECOND, 1, 1), (B_RS_RANK, 0, 3),
-    (B_RS_FIRST, 1, 0), (B_TREE, 0, -2, 1, 1), (B_TREE, 2, 2, 0, 1), (B_TREE, 0, -3, 0, 1),
-    (B_ACT_ADD_X, 1, 1, 0), (B_RS_RANK, 0, 4), (B_TREE, 3, -2, 1, 1), (B_TREE, 2, 1, 1, 0),
-    (B_TREE, 0, 0, 1, 0), (B_TREE, 0, -3, 1, 0), (B_TREE, 3, -2, 1, 0), (B_ACT_ADD_Z, 1, 1),
-    (B_TREE, 2, 2, 0, 0), (B_TREE, 1, -2, 1, 1), (B_TREE, 3, -1, 0, 1), (B_ROWS_BACK, 0), (B_TREE, 1, 3, 1, 1),
-    (B_TREE, 0, -1, 1, 0), (B_TREE, 3, 2, 1, 0), (B_TREE, 2, -1, 0, 0), (B_TREE, 2, -2, 1, 0),
-    (B_TREE, 2, -2, 0, 1), (B_TREE, 3, 2, 1, 1), (B_TREE, 0, 2, 1, 1), (B_TREE, 1, 3, 0, 1),
-    (B_TREE, 0, 3, 0, 1), (B_RS_RANK, 0, 7), (B_TREE, 1, -3, 1, 0), (B_TREE, 1, 1, 0, 1), (B_TREE, 2, 1, 1, 1),
-    (B_ACT_ADD_Z, 1, 0), (B_TREE, 3, 1, 0, 1), (B_TREE, 1, -2, 1, 0), (B_TREE, 0, -2, 1, 0),
-    (B_TREE, 0, 0, 1, 1), (B_TREE, 1, -1, 1, 1), (B_RS_SECOND, 1, 0), (B_TREE, 2, 1, 0, 0),
-    (B_TREE, 0, -2, 0, 1), (B_TREE, 3, -1, 1, 1), (B_RS_LAST, 0, 4), (B_TREE, 3, 2, 0, 0), (B_RS_RANK, 1, 2),
-    (B_TREE, 3, -3, 0, 0), (B_ACT_SUM, 1, 0), (B_TREE, 1, -2, 0, 1), (B_TREE, 2, 1, 0, 1),
-    (B_TREE, 0, -3, 0, 0), (B_TREE, 1, 3, 1, 0), (B_TREE, 0, 2, 0, 1), (B_RS_RANK, 1, 7), (B_TREE, 0, -1, 0, 1),
-    (B_TREE, 2, -1, 1, 0), (B_TREE, 2, -1, 0, 1), (B_TREE, 1, -3, 0, 0), (B_TREE, 3, 1, 1, 1),
-    (B_RS_RANK, 1, 5), (B_RS_RANK, 0, 6), (B_RS_LAST, 0, 7), (B_TREE, 0, 1, 1, 0), (B_TREE, 0, 2, 1, 0),
-    (B_TREE, 3, 1, 1, 0), (B_TREE, 2, 0, 1, 1), (B_TREE, 0, 3, 0, 0), (B_RS_LAST, 1, 2), (B_TREE, 1, -1, 1, 0),
-    (B_ACT_SUM, 1, 1), (B_FINISH_OUTPUT,), (B_TREE, 1, 3, 0, 0), (B_TREE, 0, -2, 0, 0), (B_TREE, 1, 2, 0, 1),
-    (B_TREE, 1, 0, 1, 0), (B_TREE, 3, 1, 0, 0), (B_RS_RANK, 1, 6), (B_TREE, 3, -1, 1, 0), (B_RS_RANK, 0, 2),
-    (B_RS_RANK, 1, 1), (B_TREE, 0, 2, 0, 0), (B_ROWS_BACK, 1), (B_RS_LAST, 1, 1), (B_TREE, 1, 0, 0, 1),
-    (B_TREE, 0, 1, 0, 1), (B_TREE, 1, 2, 1, 0), (B_TREE, 3, -2, 0, 0), (B_RS_LAST, 0, 6), (B_RS_LAST, 1, 6),
-    (B_TREE, 0, 0, 0, 1), (B_RS_RANK, 0, 5), (B_TREE, 2, 0, 1, 0), (B_TREE, 2, 0, 0, 1), (B_RS_LAST, 1, 5),
-    (B_TREE, 1, 1, 1, 0), (B_TREE, 3, 0, 0, 1), (B_TREE, 1, -2, 0, 0), (B_TREE, 1, 2, 0, 0), (B_ATTN_BACK,),
-    (B_TREE, 3, -1, 0, 0), (B_TREE, 0, -1, 0, 0), (B_TREE, 0, 1, 0, 0), (B_TREE, 1, -1, 0, 0),
-    (B_RS_SECOND, 1, 2), (B_TREE, 1, 1, 0, 0), (B_TREE, 3, 0, 1, 1), (B_RS_SECOND, 0, 2), (B_RS_LAST, 0, 3),
-    (B_RS_LAST, 0, 1), (B_RS_LAST, 0, 2), (B_TREE, 0, 0, 0, 0), (B_TREE, 2, 0, 0, 0), (B_RS_LAST, 0, 5),
-    (B_TREE, 3, 0, 1, 0), (B_RS_LAST, 1, 7), (B_RS_RANK, 1, 4), (B_RS_RANK, 1, 3), (B_TREE, 1, 0, 0, 0),
-    (B_RS_LAST, 1, 4), (B_TREE, 3, 0, 0, 0), (B_RS_LAST, 1, 3),
+    (B_RS_ACROSS, 0, 0, 0), (B_ACT_CORE, 0, 0), (B_RS_ACROSS, 0, 1, 0), (B_ACT_CORE, 1, 0),
+    (B_RS_ACROSS, 0, 0, 1), (B_ACT_ADD_X, 0, 0, 1), (B_ACT_CORE, 0, 1), (B_RS_FIRST, 0, 0), (B_ACT_ADD_Z, 0, 0),
+    (B_ACT_ADD_X, 0, 1, 1), (B_ACT_ADD_X, 0, 0, 0), (B_PROBS,), (B_ACT_ADD_X, 0, 1, 0), (B_NORM_TURN,),
+    (B_RS_FIRST, 0, 1), (B_RS_ACROSS, 1, 1, 1), (B_ACT_ADD_Z, 0, 1), (B_RS_ACROSS, 0, 0, 2), (B_ACT_SUM, 0, 0),
+    (B_RS_ACROSS, 0, 1, 1), (B_MID, 0), (B_RS_FIRST, 0, 2), (B_ACT_SUM, 0, 1), (B_MID, 1), (B_ACT_CORE, 1, 1),
+    (B_RS_ACROSS, 1, 0, 1), (B_RS_ACROSS, 1, 0, 0), (B_SWAP_TURNED,), (B_ACT_LOAD, 1), (B_SCORES_BACK,),
+    (B_SWAP_QKV,), (B_ACT_ADD_X, 1, 1, 1), (B_RS_ACROSS, 0, 1, 2), (B_RS_SECOND, 0, 1), (B_OUT_W, 0),
+    (B_RS_FIRST, 1, 1), (B_ACT_ADD_X, 1, 1, 0), (B_OUT_W, 1), (B_RS_ACROSS, 1, 0, 2), (B_TREE, 3, 2, 0, 0),
+    (B_TREE, 3, -3, 0, 0), (B_QKV_W, 1), (B_TREE, 1, -2, 1, 1), (B_ACT_ADD_X, 1, 0, 0), (B_TREE, 3, -3, 0, 1),
+    (B_QKV_W, 0), (B_TREE, 1, -3, 0, 1), (B_TREE, 1, 0, 1, 1), (B_TREE, 3, -3, 1, 0), (B_TREE, 0, 1, 1, 0),
+    (B_TREE, 0, -2, 1, 1), (B_TREE, 0, 1, 1, 1), (B_TREE, 3, 3, 0, 0), (B_TREE, 1, -1, 0, 1),
+    (B_TREE, 0, 3, 1, 1), (B_TREE, 2, -3, 1, 1), (B_TREE, 3, 3, 1, 1), (B_TREE, 1, 2, 1, 1),
+    (B_TREE, 3, 3, 0, 1), (B_TREE, 2, -2, 0, 0), (B_TREE, 2, 2, 0, 0), (B_ACT_ADD_X, 1, 0, 1),
+    (B_TREE, 1, 3, 1, 1), (B_TREE, 2, -2, 1, 1), (B_TREE, 2, 3, 1, 0), (B_RS_SECOND, 0, 0),
+    (B_TREE, 1, 1, 1, 1), (B_TREE, 1, 2, 0, 1), (B_RS_RANK, 0, 4), (B_RS_FIRST, 1, 0), (B_RS_FIRST, 1, 2),
+    (B_TREE, 2, 3, 0, 0), (B_TREE, 2, 2, 1, 0), (B_TREE, 2, -3, 0, 0), (B_RS_ACROSS, 1, 1, 0),
+    (B_TREE, 0, -3, 1, 1), (B_TREE, 0, 1, 0, 1), (B_TREE, 0, -2, 1, 0), (B_TREE, 0, -1, 1, 1),
+    (B_TREE, 1, 3, 0, 1), (B_TREE, 0, 3, 1, 0), (B_TREE, 1, -3, 1, 1), (B_TREE, 3, 3, 1, 0),
+    (B_TREE, 1, -1, 1, 1), (B_TREE, 3, 2, 1, 1), (B_ACT_ADD_Z, 1, 1), (B_TREE, 0, 2, 1, 1),
+    (B_TREE, 2, -2, 1, 0), (B_TREE, 3, -2, 0, 1), (B_TREE, 2, -3, 1, 0), (B_TREE, 2, 3, 0, 1),
+    (B_TREE, 0, -3, 0, 1), (B_TREE, 2, 2, 1, 1), (B_TREE, 3, -2, 0, 0), (B_TREE, 3, 2, 0, 1), (B_ROWS_BACK, 0),
+    (B_TREE, 2, 3, 1, 1), (B_TREE, 0, -2, 0, 1), (B_TREE, 3, 2, 1, 0), (B_TREE, 2, -2, 0, 1),
+    (B_TREE, 1, -2, 0, 1), (B_TREE, 2, 1, 0, 0), (B_TREE, 1, 1, 0, 1), (B_TREE, 0, 0, 1, 1),
+    (B_TREE, 1, 3, 1, 0), (B_TREE, 2, 1, 1, 0), (B_RS_SECOND, 1, 1), (B_RS_RANK, 0, 1), (B_TREE, 0, 3, 0, 1),
+    (B_ACT_ADD_Z, 1, 0), (B_TREE, 0, -1, 0, 1), (B_TREE, 0, 2, 0, 1), (B_TREE, 0, -3, 1, 0), (B_RS_RANK, 0, 2),
+    (B_RS_ACROSS, 1, 1, 2), (B_TREE, 1, 3, 0, 0), (B_TREE, 2, -3, 0, 1), (B_TREE, 2, -1, 0, 0),
+    (B_RS_SECOND, 1, 0), (B_RS_RANK, 1, 7), (B_TREE, 1, 2, 1, 0), (B_TREE, 1, -3, 1, 0), (B_RS_RANK, 1, 6),
+    (B_TREE, 1, -2, 1, 0), (B_TREE, 3, -1, 0, 0), (B_RS_RANK, 1, 2), (B_TREE, 3, -2, 1, 0), (B_RS_RANK, 0, 6),
+    (B_ACT_SUM, 1, 1), (B_RS_RANK, 1, 1), (B_TREE, 2, -1, 1, 0), (B_RS_RANK, 1, 4), (B_RS_RANK, 0, 3),
+    (B_TREE, 3, 1, 0, 1), (B_TREE, 3, 1, 1, 1), (B_ROWS_BACK, 1), (B_RS_RANK, 0, 5), (B_TREE, 3, -2, 1, 1),
+    (B_TREE, 3, 1, 1, 0), (B_TREE, 3, -1, 1, 0), (B_TREE, 0, 0, 1, 0), (B_TREE, 0, 2, 1, 0),
+    (B_TREE, 0, 3, 0, 0), (B_TREE, 3, -3, 1, 1), (B_RS_LAST, 1, 1), (B_TREE, 3, -1, 0, 1),
+    (B_TREE, 1, -3, 0, 0), (B_TREE, 0, -1, 1, 0), (B_ACT_SUM, 1, 0), (B_TREE, 2, 0, 1, 0),
+    (B_TREE, 0, -3, 0, 0), (B_TREE, 1, 0, 1, 0), (B_RS_LAST, 0, 1), (B_TREE, 1, 2, 0, 0), (B_RS_RANK, 1, 5),
+    (B_RS_RANK, 0, 7), (B_TREE, 1, 1, 1, 0), (B_TREE, 1, -1, 1, 0), (B_FINISH_OUTPUT,), (B_TREE, 0, 0, 0, 1),
+    (B_TREE, 1, -2, 0, 0), (B_TREE, 0, -2, 0, 0), (B_TREE, 2, 2, 0, 1), (B_TREE, 3, 1, 0, 0), (B_RS_LAST, 0, 4),
+    (B_TREE, 0, 2, 0, 0), (B_RS_LAST, 1, 7), (B_RS_SECOND, 1, 2), (B_RS_LAST, 0, 6), (B_TREE, 3, 0, 0, 1),
+    (B_RS_LAST, 0, 7), (B_TREE, 2, -1, 1, 1), (B_RS_LAST, 1, 4), (B_TREE, 2, 1, 1, 1), (B_TREE, 2, 1, 0, 1),
+    (B_TREE, 3, -1, 1, 1), (B_TREE, 1, 0, 0, 1), (B_RS_LAST, 0, 5), (B_TREE, 2, -1, 0, 1), (B_ATTN_BACK,),
+    (B_RS_LAST, 1, 2), (B_TREE, 0, -1, 0, 0), (B_TREE, 0, 1, 0, 0), (B_RS_SECOND, 0, 2), (B_TREE, 2, 0, 1, 1),
+    (B_TREE, 1, -1, 0, 0), (B_TREE, 1, 1, 0, 0), (B_RS_LAST, 1, 6), (B_TREE, 3, 0, 1, 1), (B_RS_LAST, 0, 2),
+    (B_TREE, 2, 0, 0, 1), (B_RS_LAST, 0, 3), (B_RS_LAST, 1, 5), (B_RS_RANK, 1, 3), (B_TREE, 3, 0, 1, 0),
+    (B_TREE, 3, 0, 0, 0), (B_TREE, 0, 0, 0, 0), (B_TREE, 2, 0, 0, 0), (B_TREE, 1, 0, 0, 0), (B_RS_LAST, 1, 3),
 ]
 
 
@@ -1393,15 +1412,13 @@
 
     def rs_rank(s, slot):
         step = RANK_STEPS[slot]
-        start(
-            push(
+        push(
                 share(step, s),
                 gate_up_sum.at[rank(own_step), s],
-                rank_send.at[slot, s],
+                rank_send.at[s],
                 rank_recv.at[slot, s],
                 member(step),
-            )
-        )
+            ).start()
 
     def rs_last(s, slot):
         step = RANK_STEPS[slot]
@@ -1517,7 +1534,7 @@
         return push(
             tree_block(piece, offset),
             slots.at[place],
-            tree_send.at[piece, chip_of(offset, z, y, x)],
+            tree_send.at[piece, DIRECTIONS.index(toward)],
             tree_recv.at[piece, place],
             neighbour(toward, z, y, x, core),
         )
@@ -1558,8 +1575,8 @@
         return push(
             gains_part.at[lax.div(other, 4)],
             gains_buf.at[me],
-            gains_send.at[step],
-            gains_recv.at[me],
+            gains_send,
+            gains_recv,
             (lax.div(other, 2), lax.rem(other, 2)),
         )
 
@@ -1567,11 +1584,8 @@
         gains_copy(step).start()
         return carry
 
-    def gains_wait(step, carry):
-        other = lax.rem(me + step, 32)
-        gains_copy(step).wait_send()
-        arrived(gains_buf.at[other], gains_recv.at[other], sibling)
-        gains_sum[...] += gains_buf[other]
+    def gains_add(step, carry):
+        gains_sum[...] += gains_buf[lax.rem(me + step, 32)]
         return carry
 
     def turn(source, target, slot):
@@ -1810,7 +1824,10 @@
     for s in range(sets):
         place_units(own_step, s, share(own_step, s))
     gains_sum[...] = gains_part[lax.div(me, 4)]
-    lax.fori_loop(1, 32, gains_wait, 0)
+    others = gains_buf.at[pl.ds(0, 31)]
+    arrived(others, gains_recv, sibling)
+    push(others, others, gains_send, gains_recv, sibling).wait_send()
+    lax.fori_loop(1, 32, gains_add, 0)
     own_gain = norm_attn_sum.shape[1]
     for index, target in enumerate((norm_attn_sum, norm_ff_sum)):
         picked = jnp.zeros(target.shape, F32)
@@ -1823,9 +1840,26 @@
                 0.0,
             )
         target[...] = picked
-    for _, _, piece, offset in events:
-        if hops(offset) > 0:
-            maybe(offset_exists(offset, z), tree_copy(piece, offset).wait_send)
+    def tree_sent(piece, direction, count):
+        source, _, index, _, _ = pieces[piece]
+        block = source.at[index, pl.ds(0, count * height), :]
+        push(block, block, tree_send.at[piece, DIRECTIONS.index(direction)], gains_recv, sibling).wait_send()
+
+    for piece in range(len(pieces)):
+        order = pieces[piece][3]
+        for direction in "xy":
+            tree_sent(piece, direction, return_count(order, direction, 3))
+        for direction in "ud":
+            for level in range(4):
+                if level != (3 if direction == "u" else 0):
+                    pl.when(z == level)(
+                        functools.partial(
+                            tree_sent, piece, direction, return_count(order, direction, level)
+                        )
+                    )
+    for s in range(sets):
+        block = gate_up_sum.at[pl.ds(0, 7), s]
+        push(block, block, rank_send.at[s], gains_recv, sibling).wait_send()
     for copy in sends:
         copy.wait_send()
 
@@ -1913,14 +1947,14 @@
             dma((2, sets, 3)),
             dma((sets, 3)),
             dma((sets, 3)),
-            dma((8, sets)),
+            dma((sets,)),
             dma((8, sets)),
             dma((4 * sets,)),
             dma((4 * sets,)),
-            dma((4, 16)),
+            dma((4, 4)),
             dma((4, max(places))),
-            dma((32,)),
-            dma((32,)),
+            dma,
+            dma,
             dma((2, sets, 2, 2)),
             dma((2, sets, 3)),
             dma((2 + sets,)),

time: 339 us -> 331 us (0.976)
  Pallas kernels: 337 us -> 329 us
    pallas_call x1, Pallas kernels: 175 us -> 169 us  [forward_gather(): pl.pallas_call(forward_kernel, out_shape=(jax.ShapeDtypeStruct((16, model...]
where the time goes in v8:
time: 331 us
  Pallas kernels  329 us (99%)
    pallas_call x1, Pallas kernels, forward_gather(): pl.pallas_call(forward_kernel, out_shape=(jax.ShapeDtypeStruct((16, model...  169 us
    pallas_call x1, Pallas kernels, backward_scatter(): pl.pallas_call(backward_kernel, out_shape=(jax.ShapeDtypeStruct(tokens.sh...  155 us

profile of v8, /device:TPU:0, one launch (start us, length us, event | category | flops | bytes accessed | tf_op | source)
XLA Modules:
  0.0 330.7 jit_solution(1939953736726443075)
XLA Ops:
  1.3 169.0 %forward_gather.1 = (f32[16,1024]{1,0:T(8,128)}, f32[2,128,1024]{2,1,0:T(8,128)}, bf16[2,128,3072]{2,1,0:T(8,128)(2,1)}, bf16[2,128,1024]{2,1,0:T(8,128)(2,1)}, ...) custom-call(s32[1]{0:T(128)S(6)} %copy.18.valid_ref, ...), custom_call_target="tpu_custom_call" | custom-call | tf_op jit(solution)/shard_map/forward_gather/pallas_call | solution.py:1091
  170.3 155.0 %backward_scatter.1 = (bf16[128,2,1024]{2,1,0:T(2,128)(2,1)}, f32[128,2,1024]{2,1,0:T(2,128)}, f32[2,32]{1,0:T(2,128)}, f32[2,32]{1,0:T(2,128)}, f32[2,32,3072]{...) custom-call(bf16[128,2,1024]{2,1,0:T(2,128)(2,1)} %tokens_ref.3, ...), custom_call_target="tpu_custom_call" | custom-call | tf_op jit(solution)/shard_map/backward_scatter/pallas_call | solution.py:1891
  325.3 5.3 %settle.1 = (bf16[128,2,1024]{2,1,0:T(2,128)(2,1)}, f32[128,2,1024]{2,1,0:T(2,128)}, f32[2,32]{1,0:T(2,128)}, f32[2,32]{1,0:T(2,128)}, f32[2,32,3072]{2,1,0:T(8,...) custom-call(bf16[128,2,1024]{2,1,0:T(2,128)(2,1)} %get-tuple-element.46.refs_0_, ...), custom_call_target="tpu_custom_call" | custom-call | tf_op jit(solution)/shard_map/settle/pallas_call | solution.py:1996

commit v9 on v8

--- a/solution.py
+++ b/solution.py
@@ -285,7 +285,7 @@
 OFFSETS = [
     (dz, dy, dx) for dz in (0, -1, 1, -2, 2, -3, 3) for dy in (0, 1) for dx in (0, 1)
 ]
-ORDERS = ("zxy", "zyx", "xyz", "yxz")
+ORDERS = ("zxy", "zyx", "zyx", "yxz")
 
 
 def hops(offset):
@@ -500,69 +500,68 @@
     F_DOWN_GRAD,
 ) = range(20)
 FORWARD_STEPS = [
-    (F_TREE, 3, 0, 0, 0), (F_TREE, 5, 0, 0, 0), (F_TREE, 0, 0, 0, 0), (F_TREE, 2, 0, 0, 0),
-    (F_TREE, 5, 1, 0, 0), (F_PARTS,), (F_TO_RANK, 0, 7), (F_TREE, 0, -1, 0, 0), (F_TREE, 0, 0, 0, 1),
-    (F_TO_RANK, 0, 3), (F_TREE, 2, 0, 0, 1), (F_TREE, 1, 0, 0, 0), (F_TREE, 0, -2, 0, 0), (F_COT,),
-    (F_RANK_FAR, 0, 3), (F_TREE, 0, 0, 1, 0), (F_TREE, 4, 0, 0, 0), (F_TO_RANK, 1, 4), (F_TREE, 1, -1, 0, 0),
-    (F_TO_RANK, 0, 2), (F_TO_RANK, 1, 2), (F_TREE, 2, 0, 1, 1), (F_TREE, 0, 1, 0, 0), (F_TREE, 2, 0, 1, 0),
-    (F_OWN_ACROSS, 0, 0), (F_TREE, 1, 1, 0, 0), (F_TREE, 2, -1, 0, 0), (F_TREE, 0, -1, 0, 1),
-    (F_TREE, 0, -3, 0, 0), (F_TO_RANK, 0, 1), (F_TREE, 0, -2, 0, 1), (F_TREE, 1, 0, 1, 0), (F_TREE, 2, 1, 0, 1),
-    (F_TREE, 0, 2, 0, 0), (F_GRADS, 0), (F_TO_RANK, 0, 6), (F_RANK_FAR, 0, 1), (F_OWN_ACROSS, 1, 8),
-    (F_TREE, 2, -2, 0, 0), (F_OWN_ACROSS, 0, 8), (F_TREE, 2, -1, 1, 0), (F_TO_RANK, 0, 5), (F_RANK_FAR, 0, 2),
-    (F_TREE, 3, 0, 0, 1), (F_OWN_FAR, 0, 8), (F_TREE, 1, -1, 1, 0), (F_TREE, 2, -1, 1, 1), (F_FAR_ACROSS, 0, 2),
-    (F_RANK_FAR, 0, 6), (F_TREE, 3, 0, 1, 1), (F_GAINS,), (F_TREE, 2, 1, 0, 0), (F_TREE, 1, 2, 0, 0),
-    (F_RANK_ACROSS, 0, 3), (F_TREE, 1, -2, 0, 0), (F_TREE, 0, 3, 0, 0), (F_TREE, 2, 1, 1, 1),
-    (F_TREE, 5, 0, 0, 1), (F_TREE, 2, 2, 0, 0), (F_TO_RANK, 0, 4), (F_TREE, 1, 2, 1, 0), (F_TREE, 3, -1, 0, 0),
-    (F_TREE, 4, 1, 0, 0), (F_TREE, 0, -1, 1, 1), (F_TREE, 0, 2, 0, 1), (F_RANK_FAR, 0, 7), (F_RANK_FAR, 0, 4),
-    (F_FAR_ACROSS, 0, 3), (F_TREE, 2, 2, 1, 1), (F_TREE, 1, 3, 0, 0), (F_TREE, 1, 1, 1, 0),
-    (F_RANK_ACROSS, 0, 1), (F_TO_RANK, 1, 6), (F_TREE, 2, -3, 0, 0), (F_TREE, 0, -3, 0, 1),
-    (F_TREE, 0, 0, 1, 1), (F_TREE, 1, 2, 0, 1), (F_TREE, 2, 1, 1, 0), (F_TREE, 2, -1, 0, 1),
-    (F_TREE, 1, 0, 1, 1), (F_TREE, 2, -2, 1, 0), (F_TREE, 2, 3, 1, 1), (F_FAR_ACROSS, 0, 6), (F_OWN_FAR, 0, 0),
-    (F_TREE, 1, -2, 0, 1), (F_TREE, 0, 2, 1, 1), (F_TREE, 4, 2, 0, 0), (F_TREE, 1, 3, 0, 1),
-    (F_TREE, 3, 1, 0, 0), (F_TREE, 2, -2, 1, 1), (F_RANK_FAR, 0, 5), (F_TREE, 0, -2, 1, 1),
-    (F_TREE, 0, 1, 1, 0), (F_TREE, 5, 0, 1, 0), (F_FAR_ACROSS, 0, 1), (F_TREE, 1, -2, 1, 0),
-    (F_TREE, 1, 2, 1, 1), (F_TREE, 2, 2, 1, 0), (F_TREE, 1, -3, 0, 0), (F_TO_RANK, 1, 5), (F_TREE, 0, -1, 1, 0),
-    (F_TREE, 3, -2, 0, 0), (F_TREE, 1, 3, 1, 0), (F_ACT_Z, 1, 0), (F_TREE, 0, 1, 0, 1), (F_TREE, 3, 1, 0, 1),
-    (F_TREE, 2, 2, 0, 1), (F_TREE, 0, 3, 1, 0), (F_TREE, 4, -1, 0, 0), (F_TREE, 2, -2, 0, 1),
-    (F_TREE, 2, -3, 1, 1), (F_TREE, 0, -3, 1, 1), (F_FAR_ACROSS, 0, 7), (F_TREE, 0, -3, 1, 0),
-    (F_TREE, 0, 2, 1, 0), (F_TREE, 3, 1, 1, 0), (F_TREE, 2, -3, 1, 0), (F_TREE, 1, -1, 0, 1),
-    (F_TREE, 1, -3, 1, 0), (F_RANK_ACROSS, 0, 7), (F_FAR_ACROSS, 0, 0), (F_TREE, 1, 3, 1, 1),
-    (F_TREE, 3, 2, 0, 0), (F_TREE, 2, 3, 0, 0), (F_RANK_ACROSS, 0, 6), (F_TREE, 5, 1, 1, 0),
-    (F_TREE, 0, 3, 0, 1), (F_TREE, 1, -3, 0, 1), (F_TREE, 3, -2, 0, 1), (F_ACT_C, 1, 0, 0, 0),
-    (F_TREE, 4, 0, 1, 0), (F_TREE, 5, 0, 1, 1), (F_TREE, 4, -2, 0, 0), (F_FAR_ACROSS, 0, 4), (F_GRADS, 1),
-    (F_TREE, 2, -3, 0, 1), (F_TREE, 5, -1, 1, 0), (F_TREE, 1, -3, 1, 1), (F_ACT_C, 1, 0, 1, 0),
-    (F_FAR_ACROSS, 0, 8), (F_TREE, 5, 1, 0, 1), (F_FAR_ACROSS, 0, 5), (F_TREE, 1, -1, 1, 1),
-    (F_TREE, 1, 0, 0, 1), (F_RANK_ACROSS, 0, 5), (F_TREE, 5, -1, 0, 0), (F_TREE, 3, -3, 0, 0),
-    (F_TO_RANK, 1, 1), (F_ACT_X, 1, 0, 1), (F_TREE, 1, 1, 0, 1), (F_TREE, 5, 2, 1, 0), (F_OWN_FAR, 1, 8),
-    (F_ACT_X, 1, 0, 0), (F_TREE, 5, -1, 0, 1), (F_TREE, 4, -3, 0, 0), (F_TREE, 0, 1, 1, 1),
-    (F_TREE, 1, 1, 1, 1), (F_TREE, 2, 3, 0, 1), (F_TREE, 3, 1, 1, 1), (F_TREE, 3, -1, 0, 1),
-    (F_TREE, 4, -1, 1, 0), (F_TREE, 3, -3, 0, 1), (F_TREE, 3, 2, 0, 1), (F_OWN_ACROSS, 1, 0),
-    (F_TREE, 1, -2, 1, 1), (F_TO_RANK, 1, 3), (F_TREE, 3, 0, 1, 0), (F_TREE, 0, 3, 1, 1), (F_TREE, 0, -2, 1, 0),
-    (F_TREE, 3, 2, 1, 0), (F_TREE, 2, 3, 1, 0), (F_TREE, 3, 3, 0, 0), (F_TREE_END, 0), (F_TREE, 4, -1, 1, 1),
-    (F_TO_RANK, 1, 7), (F_ATTENTION, 0), (F_TREE, 4, 3, 0, 0), (F_ACT_X, 0, 0, 0), (F_TREE, 4, 3, 1, 0),
-    (F_TREE, 3, -3, 1, 0), (F_TREE, 4, 3, 0, 1), (F_TREE, 4, -2, 1, 0), (F_TREE, 3, 3, 0, 1),
-    (F_TREE, 5, -1, 1, 1), (F_RANK_FAR, 1, 7), (F_RANK_ACROSS, 0, 2), (F_TREE, 4, 2, 1, 0),
-    (F_TREE, 5, 1, 1, 1), (F_TREE, 5, 3, 1, 0), (F_TREE, 4, -3, 0, 1), (F_RANK_ACROSS, 0, 4),
-    (F_TREE, 4, -3, 1, 0), (F_OWN_FAR, 1, 0), (F_RANK_FAR, 1, 2), (F_TREE, 4, 3, 1, 1), (F_RANK_ACROSS, 1, 7),
-    (F_FAR_ACROSS, 1, 8), (F_TREE, 4, 1, 1, 0), (F_ACT_Z, 1, 1), (F_TREE, 5, -2, 0, 1), (F_TREE, 4, -3, 1, 1),
-    (F_TREE, 3, 2, 1, 1), (F_TREE, 5, -2, 0, 0), (F_ACT_Z, 0, 0), (F_TREE, 4, 2, 1, 1), (F_TREE, 5, 2, 0, 0),
-    (F_RANK_FAR, 1, 1), (F_FF_END, 0), (F_ACT_C, 0, 0, 1, 0), (F_RANK_ACROSS, 1, 2), (F_TREE, 4, 0, 0, 1),
-    (F_TREE, 4, 1, 1, 1), (F_RANK_FAR, 1, 5), (F_ACT_X, 1, 1, 0), (F_TREE, 3, -1, 1, 0), (F_TREE, 5, 2, 1, 1),
-    (F_TREE, 5, 3, 0, 0), (F_FAR_ACROSS, 1, 7), (F_TREE, 3, 3, 1, 1), (F_TREE, 3, -1, 1, 1),
-    (F_TREE, 4, -2, 1, 1), (F_ACT_C, 1, 0, 0, 1), (F_ACT_C, 0, 0, 0, 0), (F_TREE, 4, 0, 1, 1),
-    (F_RANK_FAR, 1, 3), (F_ACT_C, 1, 0, 1, 1), (F_TREE, 3, -2, 1, 0), (F_TREE, 5, -2, 1, 0), (F_RANK_FAR, 1, 4),
-    (F_FAR_ACROSS, 1, 0), (F_TREE, 5, -3, 0, 0), (F_TREE, 4, 1, 0, 1), (F_TREE, 3, -2, 1, 1),
-    (F_ACT_C, 1, 1, 1, 0), (F_RANK_FAR, 1, 6), (F_TREE, 4, -1, 0, 1), (F_TREE, 5, 2, 0, 1),
-    (F_TREE, 5, -3, 1, 0), (F_ACT_C, 0, 0, 0, 1), (F_FAR_ACROSS, 1, 2), (F_ACT_C, 1, 1, 0, 0),
-    (F_TREE, 5, -3, 0, 1), (F_TREE, 5, -2, 1, 1), (F_TREE, 3, 3, 1, 0), (F_RANK_ACROSS, 1, 6),
-    (F_RANK_ACROSS, 1, 3), (F_TREE, 5, 3, 1, 1), (F_RANK_ACROSS, 1, 4), (F_BLOCK, 0, 1), (F_TREE, 4, 2, 0, 1),
-    (F_TREE, 5, 3, 0, 1), (F_TREE, 4, -2, 0, 1), (F_TREE, 3, -3, 1, 1), (F_FAR_ACROSS, 1, 1),
-    (F_TREE, 5, -3, 1, 1), (F_BLOCK, 0, 0), (F_RANK_ACROSS, 1, 5), (F_ACT_X, 1, 1, 1), (F_TREE_END, 1),
-    (F_ATTENTION, 1), (F_FAR_ACROSS, 1, 3), (F_RANK_ACROSS, 1, 1), (F_ACT_X, 0, 0, 1), (F_BLOCK, 0, 2),
-    (F_FAR_ACROSS, 1, 5), (F_ACT_C, 0, 0, 1, 1), (F_BLOCK, 0, 3), (F_DOWN_GRAD, 0), (F_ACT_C, 1, 1, 0, 1),
-    (F_FAR_ACROSS, 1, 6), (F_ACT_X, 0, 1, 0), (F_ACT_C, 1, 1, 1, 1), (F_ACT_Z, 0, 1), (F_FAR_ACROSS, 1, 4),
-    (F_GATE_GRAD, 0), (F_ACT_C, 0, 1, 0, 1), (F_ACT_C, 0, 1, 0, 0), (F_FF_END, 1), (F_ACT_C, 0, 1, 1, 0),
-    (F_BLOCK, 1, 1), (F_BLOCK, 1, 2), (F_ACT_X, 0, 1, 1), (F_BLOCK, 1, 0), (F_ACT_C, 0, 1, 1, 1),
+    (F_TREE, 0, 0, 0, 0), (F_TREE, 2, 0, 0, 0), (F_COT,), (F_PARTS,), (F_TREE, 1, 0, 0, 0), (F_TO_RANK, 0, 3),
+    (F_OWN_ACROSS, 0, 8), (F_TREE, 4, 0, 0, 0), (F_TREE, 3, 0, 0, 0), (F_TREE, 2, 0, 1, 0),
+    (F_TREE, 0, -1, 0, 0), (F_TO_RANK, 0, 7), (F_TO_RANK, 1, 5), (F_TO_RANK, 0, 1), (F_TREE, 0, 0, 0, 1),
+    (F_GAINS,), (F_TO_RANK, 0, 6), (F_RANK_FAR, 0, 3), (F_TO_RANK, 0, 2), (F_TREE, 1, 1, 0, 0),
+    (F_TO_RANK, 0, 4), (F_TREE, 2, 1, 0, 0), (F_TREE, 2, -1, 0, 0), (F_TREE, 5, 0, 0, 0), (F_TREE, 2, 2, 0, 0),
+    (F_TREE, 3, 0, 0, 1), (F_TREE, 1, -1, 0, 0), (F_TO_RANK, 1, 2), (F_TREE, 0, -2, 0, 0), (F_OWN_ACROSS, 1, 8),
+    (F_TREE, 1, 0, 1, 0), (F_RANK_FAR, 0, 1), (F_TREE, 0, 1, 0, 0), (F_RANK_FAR, 0, 6), (F_TREE, 2, 1, 0, 1),
+    (F_TREE, 2, -2, 0, 0), (F_RANK_FAR, 0, 7), (F_TREE, 0, 2, 0, 0), (F_TREE, 1, -2, 0, 0),
+    (F_TREE, 0, -2, 0, 1), (F_OWN_FAR, 0, 8), (F_OWN_FAR, 0, 0), (F_TREE, 1, 2, 0, 0), (F_TREE, 0, -1, 0, 1),
+    (F_GRADS, 0), (F_TO_RANK, 1, 4), (F_TREE, 3, -1, 0, 0), (F_TREE, 4, 1, 0, 0), (F_RANK_FAR, 0, 2),
+    (F_TREE, 1, -2, 1, 0), (F_RANK_ACROSS, 0, 3), (F_TREE, 1, -3, 0, 0), (F_TREE, 2, 3, 0, 0),
+    (F_TREE, 3, 1, 0, 0), (F_TREE, 2, 2, 1, 0), (F_TREE, 2, -2, 1, 0), (F_TREE, 2, -3, 0, 0),
+    (F_TREE, 0, 0, 1, 1), (F_TREE, 5, 0, 1, 0), (F_TREE, 0, -1, 1, 1), (F_TREE, 0, 3, 0, 0),
+    (F_TREE, 2, 0, 0, 1), (F_TREE, 0, -3, 0, 0), (F_TREE, 3, 0, 1, 1), (F_TREE, 2, 1, 1, 0),
+    (F_TREE, 0, 2, 0, 1), (F_TREE, 1, 3, 0, 0), (F_TREE, 1, 2, 1, 0), (F_TREE, 0, 1, 1, 0), (F_ACT_X, 1, 0, 0),
+    (F_TO_RANK, 0, 5), (F_TREE, 2, -1, 1, 0), (F_TREE, 2, -2, 0, 1), (F_RANK_ACROSS, 0, 1),
+    (F_TREE, 0, 1, 0, 1), (F_RANK_FAR, 0, 4), (F_TREE, 5, 0, 0, 1), (F_TREE, 3, -2, 0, 0), (F_FAR_ACROSS, 0, 6),
+    (F_TREE, 1, 2, 0, 1), (F_TREE, 4, -1, 0, 0), (F_FAR_ACROSS, 0, 7), (F_TREE, 1, 1, 1, 0),
+    (F_TREE, 1, 3, 1, 0), (F_TREE, 4, 0, 1, 0), (F_TO_RANK, 1, 6), (F_TREE, 0, 1, 1, 1), (F_TREE, 2, -3, 0, 1),
+    (F_FAR_ACROSS, 0, 3), (F_ACT_C, 1, 0, 0, 1), (F_RANK_FAR, 0, 5), (F_TO_RANK, 1, 1), (F_TREE, 1, -1, 0, 1),
+    (F_TREE, 0, 3, 0, 1), (F_TREE, 2, -1, 0, 1), (F_RANK_ACROSS, 0, 5), (F_TREE, 3, 2, 0, 0),
+    (F_TREE, 3, -1, 1, 0), (F_TREE, 3, 1, 0, 1), (F_RANK_ACROSS, 0, 6), (F_TREE, 0, -2, 1, 1),
+    (F_TREE, 1, -3, 1, 0), (F_TREE, 5, 1, 0, 0), (F_TREE, 1, -1, 1, 0), (F_TREE, 1, -2, 1, 1),
+    (F_TREE, 5, 0, 1, 1), (F_ACT_Z, 1, 0), (F_TREE, 2, 3, 1, 0), (F_TREE, 0, 3, 1, 0), (F_TREE, 3, 3, 0, 0),
+    (F_FAR_ACROSS, 0, 4), (F_TREE, 4, -2, 0, 0), (F_TREE, 3, 0, 1, 0), (F_TREE, 0, -3, 0, 1),
+    (F_TREE, 0, 2, 1, 0), (F_TREE, 5, -1, 0, 0), (F_TREE, 1, 3, 1, 1), (F_TREE, 4, 2, 0, 0),
+    (F_TREE, 1, -3, 1, 1), (F_ACT_C, 1, 0, 1, 0), (F_TREE, 1, 0, 0, 1), (F_TREE, 0, -1, 1, 0),
+    (F_FAR_ACROSS, 0, 2), (F_OWN_FAR, 1, 8), (F_TREE, 2, -2, 1, 1), (F_TREE, 0, 0, 1, 0), (F_TREE, 0, 3, 1, 1),
+    (F_RANK_ACROSS, 0, 7), (F_TREE, 1, 0, 1, 1), (F_TREE, 4, 1, 0, 1), (F_RANK_FAR, 1, 4),
+    (F_TREE, 2, -1, 1, 1), (F_FAR_ACROSS, 0, 8), (F_GRADS, 1), (F_TREE, 3, -2, 0, 1), (F_TREE, 3, 1, 1, 1),
+    (F_TREE, 5, 1, 0, 1), (F_TREE, 3, 3, 1, 0), (F_TREE, 2, 1, 1, 1), (F_TREE, 2, -3, 1, 0),
+    (F_TREE, 1, 1, 0, 1), (F_TREE, 4, 2, 1, 0), (F_TO_RANK, 1, 3), (F_TREE, 4, 3, 0, 0), (F_TREE, 5, 1, 1, 0),
+    (F_TREE, 4, -3, 0, 0), (F_TREE, 5, -1, 0, 1), (F_TREE, 3, -2, 1, 0), (F_FAR_ACROSS, 0, 0),
+    (F_TREE, 3, -3, 0, 0), (F_TREE, 4, -1, 1, 0), (F_FAR_ACROSS, 0, 1), (F_TREE, 1, 2, 1, 1),
+    (F_TREE, 0, -2, 1, 0), (F_TREE, 2, 3, 1, 1), (F_FAR_ACROSS, 0, 5), (F_TREE, 1, 1, 1, 1),
+    (F_TREE, 2, 2, 1, 1), (F_TREE, 4, -2, 1, 0), (F_TREE, 2, -3, 1, 1), (F_TREE, 2, 2, 0, 1),
+    (F_TREE, 2, 3, 0, 1), (F_TREE, 2, 0, 1, 1), (F_TREE, 0, 2, 1, 1), (F_TREE, 4, -3, 1, 0),
+    (F_TREE, 4, -3, 0, 1), (F_TREE, 0, -3, 1, 1), (F_FAR_ACROSS, 1, 8), (F_RANK_FAR, 1, 2),
+    (F_TREE, 1, -1, 1, 1), (F_TREE, 0, -3, 1, 0), (F_TREE, 3, -1, 0, 1), (F_TREE, 1, -2, 0, 1),
+    (F_TREE, 4, 0, 1, 1), (F_TO_RANK, 1, 7), (F_OWN_ACROSS, 1, 0), (F_TREE, 1, 3, 0, 1), (F_ACT_X, 1, 0, 1),
+    (F_TREE, 3, 2, 0, 1), (F_TREE, 1, -3, 0, 1), (F_TREE_END, 0), (F_TREE, 4, -1, 0, 1), (F_TREE, 5, -1, 1, 0),
+    (F_TREE, 4, 3, 1, 0), (F_ATTENTION, 0), (F_TREE, 5, 1, 1, 1), (F_TREE, 3, 2, 1, 0), (F_TREE, 5, -2, 1, 0),
+    (F_TREE, 5, 2, 1, 0), (F_TREE, 5, -1, 1, 1), (F_TREE, 3, 3, 0, 1), (F_RANK_ACROSS, 0, 4),
+    (F_TREE, 3, -3, 0, 1), (F_TREE, 4, -1, 1, 1), (F_TREE, 4, 2, 0, 1), (F_TREE, 5, -2, 0, 1),
+    (F_TREE, 5, -2, 0, 0), (F_TREE, 4, 2, 1, 1), (F_TREE, 4, 1, 1, 0), (F_TREE, 4, -3, 1, 1), (F_ACT_Z, 0, 0),
+    (F_FAR_ACROSS, 1, 2), (F_RANK_ACROSS, 0, 2), (F_TREE, 5, 2, 0, 1), (F_RANK_FAR, 1, 7), (F_TREE, 5, 2, 0, 0),
+    (F_OWN_FAR, 1, 0), (F_OWN_ACROSS, 0, 0), (F_TREE, 5, -2, 1, 1), (F_RANK_ACROSS, 1, 4), (F_RANK_FAR, 1, 3),
+    (F_ACT_X, 0, 0, 0), (F_TREE, 5, 3, 0, 1), (F_RANK_ACROSS, 1, 2), (F_ACT_Z, 1, 1), (F_TREE, 4, 0, 0, 1),
+    (F_TREE, 3, 3, 1, 1), (F_TREE, 5, 2, 1, 1), (F_RANK_FAR, 1, 5), (F_TREE, 4, 3, 1, 1), (F_ACT_C, 1, 0, 1, 1),
+    (F_RANK_ACROSS, 1, 5), (F_FAR_ACROSS, 1, 4), (F_TREE, 5, -3, 0, 1), (F_TREE, 5, 3, 1, 0),
+    (F_TREE, 5, 3, 0, 0), (F_TREE, 3, -3, 1, 1), (F_RANK_FAR, 1, 6), (F_TREE, 4, -2, 1, 1), (F_RANK_FAR, 1, 1),
+    (F_ACT_C, 1, 0, 0, 0), (F_TREE, 3, -1, 1, 1), (F_TREE, 3, -2, 1, 1), (F_TREE, 3, 2, 1, 1), (F_FF_END, 0),
+    (F_ACT_C, 1, 1, 0, 0), (F_TREE, 4, 1, 1, 1), (F_TREE, 4, -2, 0, 1), (F_ACT_C, 0, 0, 1, 0),
+    (F_ACT_C, 0, 0, 0, 1), (F_BLOCK, 0, 2), (F_FAR_ACROSS, 1, 7), (F_TREE, 4, 3, 0, 1), (F_RANK_ACROSS, 1, 1),
+    (F_RANK_ACROSS, 1, 7), (F_TREE, 5, -3, 1, 0), (F_TREE, 3, -3, 1, 0), (F_TREE, 3, 1, 1, 0),
+    (F_TREE, 5, -3, 0, 0), (F_TREE, 5, 3, 1, 1), (F_BLOCK, 0, 1), (F_ACT_C, 0, 0, 0, 0), (F_RANK_ACROSS, 1, 3),
+    (F_TREE, 5, -3, 1, 1), (F_ACT_X, 1, 1, 0), (F_ACT_X, 0, 0, 1), (F_TREE_END, 1), (F_RANK_ACROSS, 1, 6),
+    (F_ATTENTION, 1), (F_FAR_ACROSS, 1, 3), (F_ACT_C, 1, 1, 0, 1), (F_ACT_X, 1, 1, 1), (F_FAR_ACROSS, 1, 0),
+    (F_BLOCK, 0, 0), (F_ACT_C, 0, 0, 1, 1), (F_BLOCK, 0, 3), (F_ACT_C, 1, 1, 1, 1), (F_FAR_ACROSS, 1, 1),
+    (F_FAR_ACROSS, 1, 5), (F_DOWN_GRAD, 0), (F_ACT_Z, 0, 1), (F_ACT_C, 0, 1, 0, 0), (F_ACT_X, 0, 1, 0),
+    (F_FAR_ACROSS, 1, 6), (F_GATE_GRAD, 0), (F_ACT_C, 1, 1, 1, 0), (F_ACT_C, 0, 1, 0, 1), (F_ACT_C, 0, 1, 1, 0),
+    (F_FF_END, 1), (F_BLOCK, 1, 1), (F_BLOCK, 1, 2), (F_ACT_X, 0, 1, 1), (F_BLOCK, 1, 0), (F_ACT_C, 0, 1, 1, 1),
     (F_BLOCK, 1, 3), (F_DOWN_GRAD, 1), (F_GATE_GRAD, 1),
 ]
 
@@ -636,12 +635,13 @@
     split = 4 * down_height
     sibling = neighbour("s", z, y, x, core)
     greet_all(z, y, x, core)
-    part = qkv_ref.shape[2] // 2
+    part = qkv_ref.shape[2] * 12 // 24
+    rest = qkv_ref.shape[2] - part
     pieces = []
     for s in range(positions):
         pieces.append((qkv_ref, qkv_buf, s, pl.ds(0, part), "zxy"))
-        pieces.append((qkv_ref, qkv_buf, s, pl.ds(part, part), "zyx"))
-        pieces.append((out_ref, out_buf, s, pl.ds(0, model), ("xyz", "yxz")[s % 2]))
+        pieces.append((qkv_ref, qkv_buf, s, pl.ds(part, rest), "zyx"))
+        pieces.append((out_ref, out_buf, s, pl.ds(0, model), ("zyx", "yxz")[s % 2]))
 
     def piece_rows(piece, number):
         _, full, index, columns, _ = pieces[piece]
@@ -1198,49 +1198,49 @@
     B_FINISH_OUTPUT,
 ) = range(22)
 BACKWARD_STEPS = [
-    (B_RS_ACROSS, 0, 0, 0), (B_ACT_CORE, 0, 0), (B_RS_ACROSS, 0, 1, 0), (B_ACT_CORE, 1, 0),
-    (B_RS_ACROSS, 0, 0, 1), (B_ACT_ADD_X, 0, 0, 1), (B_ACT_CORE, 0, 1), (B_RS_FIRST, 0, 0), (B_ACT_ADD_Z, 0, 0),
-    (B_ACT_ADD_X, 0, 1, 1), (B_ACT_ADD_X, 0, 0, 0), (B_PROBS,), (B_ACT_ADD_X, 0, 1, 0), (B_NORM_TURN,),
-    (B_RS_FIRST, 0, 1), (B_RS_ACROSS, 1, 1, 1), (B_ACT_ADD_Z, 0, 1), (B_RS_ACROSS, 0, 0, 2), (B_ACT_SUM, 0, 0),
-    (B_RS_ACROSS, 0, 1, 1), (B_MID, 0), (B_RS_FIRST, 0, 2), (B_ACT_SUM, 0, 1), (B_MID, 1), (B_ACT_CORE, 1, 1),
-    (B_RS_ACROSS, 1, 0, 1), (B_RS_ACROSS, 1, 0, 0), (B_SWAP_TURNED,), (B_ACT_LOAD, 1), (B_SCORES_BACK,),
-    (B_SWAP_QKV,), (B_ACT_ADD_X, 1, 1, 1), (B_RS_ACROSS, 0, 1, 2), (B_RS_SECOND, 0, 1), (B_OUT_W, 0),
-    (B_RS_FIRST, 1, 1), (B_ACT_ADD_X, 1, 1, 0), (B_OUT_W, 1), (B_RS_ACROSS, 1, 0, 2), (B_TREE, 3, 2, 0, 0),
-    (B_TREE, 3, -3, 0, 0), (B_QKV_W, 1), (B_TREE, 1, -2, 1, 1), (B_ACT_ADD_X, 1, 0, 0), (B_TREE, 3, -3, 0, 1),
-    (B_QKV_W, 0), (B_TREE, 1, -3, 0, 1), (B_TREE, 1, 0, 1, 1), (B_TREE, 3, -3, 1, 0), (B_TREE, 0, 1, 1, 0),
-    (B_TREE, 0, -2, 1, 1), (B_TREE, 0, 1, 1, 1), (B_TREE, 3, 3, 0, 0), (B_TREE, 1, -1, 0, 1),
-    (B_TREE, 0, 3, 1, 1), (B_TREE, 2, -3, 1, 1), (B_TREE, 3, 3, 1, 1), (B_TREE, 1, 2, 1, 1),
-    (B_TREE, 3, 3, 0, 1), (B_TREE, 2, -2, 0, 0), (B_TREE, 2, 2, 0, 0), (B_ACT_ADD_X, 1, 0, 1),
-    (B_TREE, 1, 3, 1, 1), (B_TREE, 2, -2, 1, 1), (B_TREE, 2, 3, 1, 0), (B_RS_SECOND, 0, 0),
-    (B_TREE, 1, 1, 1, 1), (B_TREE, 1, 2, 0, 1), (B_RS_RANK, 0, 4), (B_RS_FIRST, 1, 0), (B_RS_FIRST, 1, 2),
-    (B_TREE, 2, 3, 0, 0), (B_TREE, 2, 2, 1, 0), (B_TREE, 2, -3, 0, 0), (B_RS_ACROSS, 1, 1, 0),
-    (B_TREE, 0, -3, 1, 1), (B_TREE, 0, 1, 0, 1), (B_TREE, 0, -2, 1, 0), (B_TREE, 0, -1, 1, 1),
-    (B_TREE, 1, 3, 0, 1), (B_TREE, 0, 3, 1, 0), (B_TREE, 1, -3, 1, 1), (B_TREE, 3, 3, 1, 0),
-    (B_TREE, 1, -1, 1, 1), (B_TREE, 3, 2, 1, 1), (B_ACT_ADD_Z, 1, 1), (B_TREE, 0, 2, 1, 1),
-    (B_TREE, 2, -2, 1, 0), (B_TREE, 3, -2, 0, 1), (B_TREE, 2, -3, 1, 0), (B_TREE, 2, 3, 0, 1),
-    (B_TREE, 0, -3, 0, 1), (B_TREE, 2, 2, 1, 1), (B_TREE, 3, -2, 0, 0), (B_TREE, 3, 2, 0, 1), (B_ROWS_BACK, 0),
-    (B_TREE, 2, 3, 1, 1), (B_TREE, 0, -2, 0, 1), (B_TREE, 3, 2, 1, 0), (B_TREE, 2, -2, 0, 1),
-    (B_TREE, 1, -2, 0, 1), (B_TREE, 2, 1, 0, 0), (B_TREE, 1, 1, 0, 1), (B_TREE, 0, 0, 1, 1),
-    (B_TREE, 1, 3, 1, 0), (B_TREE, 2, 1, 1, 0), (B_RS_SECOND, 1, 1), (B_RS_RANK, 0, 1), (B_TREE, 0, 3, 0, 1),
-    (B_ACT_ADD_Z, 1, 0), (B_TREE, 0, -1, 0, 1), (B_TREE, 0, 2, 0, 1), (B_TREE, 0, -3, 1, 0), (B_RS_RANK, 0, 2),
-    (B_RS_ACROSS, 1, 1, 2), (B_TREE, 1, 3, 0, 0), (B_TREE, 2, -3, 0, 1), (B_TREE, 2, -1, 0, 0),
-    (B_RS_SECOND, 1, 0), (B_RS_RANK, 1, 7), (B_TREE, 1, 2, 1, 0), (B_TREE, 1, -3, 1, 0), (B_RS_RANK, 1, 6),
-    (B_TREE, 1, -2, 1, 0), (B_TREE, 3, -1, 0, 0), (B_RS_RANK, 1, 2), (B_TREE, 3, -2, 1, 0), (B_RS_RANK, 0, 6),
-    (B_ACT_SUM, 1, 1), (B_RS_RANK, 1, 1), (B_TREE, 2, -1, 1, 0), (B_RS_RANK, 1, 4), (B_RS_RANK, 0, 3),
-    (B_TREE, 3, 1, 0, 1), (B_TREE, 3, 1, 1, 1), (B_ROWS_BACK, 1), (B_RS_RANK, 0, 5), (B_TREE, 3, -2, 1, 1),
-    (B_TREE, 3, 1, 1, 0), (B_TREE, 3, -1, 1, 0), (B_TREE, 0, 0, 1, 0), (B_TREE, 0, 2, 1, 0),
-    (B_TREE, 0, 3, 0, 0), (B_TREE, 3, -3, 1, 1), (B_RS_LAST, 1, 1), (B_TREE, 3, -1, 0, 1),
-    (B_TREE, 1, -3, 0, 0), (B_TREE, 0, -1, 1, 0), (B_ACT_SUM, 1, 0), (B_TREE, 2, 0, 1, 0),
-    (B_TREE, 0, -3, 0, 0), (B_TREE, 1, 0, 1, 0), (B_RS_LAST, 0, 1), (B_TREE, 1, 2, 0, 0), (B_RS_RANK, 1, 5),
-    (B_RS_RANK, 0, 7), (B_TREE, 1, 1, 1, 0), (B_TREE, 1, -1, 1, 0), (B_FINISH_OUTPUT,), (B_TREE, 0, 0, 0, 1),
-    (B_TREE, 1, -2, 0, 0), (B_TREE, 0, -2, 0, 0), (B_TREE, 2, 2, 0, 1), (B_TREE, 3, 1, 0, 0), (B_RS_LAST, 0, 4),
-    (B_TREE, 0, 2, 0, 0), (B_RS_LAST, 1, 7), (B_RS_SECOND, 1, 2), (B_RS_LAST, 0, 6), (B_TREE, 3, 0, 0, 1),
-    (B_RS_LAST, 0, 7), (B_TREE, 2, -1, 1, 1), (B_RS_LAST, 1, 4), (B_TREE, 2, 1, 1, 1), (B_TREE, 2, 1, 0, 1),
-    (B_TREE, 3, -1, 1, 1), (B_TREE, 1, 0, 0, 1), (B_RS_LAST, 0, 5), (B_TREE, 2, -1, 0, 1), (B_ATTN_BACK,),
-    (B_RS_LAST, 1, 2), (B_TREE, 0, -1, 0, 0), (B_TREE, 0, 1, 0, 0), (B_RS_SECOND, 0, 2), (B_TREE, 2, 0, 1, 1),
-    (B_TREE, 1, -1, 0, 0), (B_TREE, 1, 1, 0, 0), (B_RS_LAST, 1, 6), (B_TREE, 3, 0, 1, 1), (B_RS_LAST, 0, 2),
-    (B_TREE, 2, 0, 0, 1), (B_RS_LAST, 0, 3), (B_RS_LAST, 1, 5), (B_RS_RANK, 1, 3), (B_TREE, 3, 0, 1, 0),
-    (B_TREE, 3, 0, 0, 0), (B_TREE, 0, 0, 0, 0), (B_TREE, 2, 0, 0, 0), (B_TREE, 1, 0, 0, 0), (B_RS_LAST, 1, 3),
+    (B_ACT_CORE, 0, 0), (B_RS_ACROSS, 0, 0, 0), (B_RS_ACROSS, 0, 0, 1), (B_NORM_TURN,), (B_ACT_CORE, 0, 1),
+    (B_ACT_ADD_X, 0, 0, 1), (B_RS_ACROSS, 0, 1, 0), (B_ACT_ADD_X, 0, 0, 0), (B_ACT_ADD_X, 0, 1, 1),
+    (B_RS_ACROSS, 0, 0, 2), (B_RS_ACROSS, 1, 0, 1), (B_ACT_CORE, 1, 1), (B_SWAP_TURNED,), (B_RS_FIRST, 0, 0),
+    (B_ACT_ADD_X, 0, 1, 0), (B_ACT_ADD_Z, 0, 0), (B_RS_FIRST, 0, 1), (B_ACT_ADD_Z, 0, 1),
+    (B_RS_ACROSS, 1, 1, 1), (B_PROBS,), (B_ACT_SUM, 0, 0), (B_MID, 0), (B_OUT_W, 0), (B_RS_ACROSS, 1, 0, 0),
+    (B_TREE, 2, -3, 1, 1), (B_RS_FIRST, 0, 2), (B_ACT_CORE, 1, 0), (B_TREE, 2, 1, 1, 1), (B_TREE, 2, 0, 0, 1),
+    (B_RS_SECOND, 0, 0), (B_TREE, 2, 0, 1, 1), (B_RS_ACROSS, 0, 1, 1), (B_ACT_SUM, 0, 1), (B_TREE, 2, -1, 1, 1),
+    (B_MID, 1), (B_ACT_LOAD, 1), (B_ACT_ADD_X, 1, 1, 0), (B_RS_ACROSS, 1, 1, 0), (B_SCORES_BACK,),
+    (B_ACT_ADD_X, 1, 0, 0), (B_TREE, 2, 2, 1, 1), (B_OUT_W, 1), (B_SWAP_QKV,), (B_RS_FIRST, 1, 1),
+    (B_ACT_ADD_X, 1, 1, 1), (B_RS_SECOND, 0, 1), (B_QKV_W, 0), (B_TREE, 2, 0, 1, 0), (B_TREE, 2, -1, 1, 0),
+    (B_RS_RANK, 0, 4), (B_TREE, 3, -3, 1, 1), (B_QKV_W, 1), (B_TREE, 0, 1, 1, 1), (B_RS_ACROSS, 1, 0, 2),
+    (B_TREE, 1, 2, 1, 1), (B_TREE, 0, -2, 1, 1), (B_TREE, 3, 3, 1, 0), (B_TREE, 0, -3, 1, 1),
+    (B_TREE, 3, 3, 0, 1), (B_TREE, 3, -2, 0, 1), (B_TREE, 3, -3, 0, 1), (B_TREE, 1, -1, 1, 1),
+    (B_TREE, 2, 3, 0, 1), (B_TREE, 3, 2, 1, 0), (B_TREE, 2, 3, 1, 1), (B_RS_RANK, 0, 7), (B_TREE, 3, -3, 1, 0),
+    (B_RS_RANK, 0, 5), (B_ACT_ADD_X, 1, 0, 1), (B_RS_RANK, 0, 3), (B_TREE, 3, 3, 0, 0), (B_TREE, 1, 3, 0, 1),
+    (B_TREE, 3, -2, 1, 0), (B_TREE, 0, 3, 1, 1), (B_TREE, 3, -3, 0, 0), (B_TREE, 3, 2, 0, 1),
+    (B_TREE, 0, -3, 1, 0), (B_TREE, 1, 3, 1, 1), (B_TREE, 3, -2, 1, 1), (B_TREE, 0, 3, 1, 0),
+    (B_TREE, 2, -3, 1, 0), (B_TREE, 3, 3, 1, 1), (B_TREE, 2, 1, 0, 1), (B_TREE, 2, 3, 1, 0),
+    (B_TREE, 0, 2, 1, 1), (B_TREE, 2, -2, 1, 1), (B_TREE, 2, -2, 0, 1), (B_TREE, 2, 2, 0, 1),
+    (B_TREE, 0, 0, 1, 1), (B_TREE, 2, -3, 0, 1), (B_TREE, 0, 1, 1, 0), (B_RS_FIRST, 1, 0), (B_TREE, 0, 3, 0, 1),
+    (B_TREE, 3, 2, 1, 1), (B_TREE, 1, -3, 1, 1), (B_RS_SECOND, 1, 1), (B_TREE, 1, -3, 0, 1),
+    (B_TREE, 1, 2, 1, 0), (B_TREE, 1, 2, 0, 1), (B_TREE, 2, 3, 0, 0), (B_RS_RANK, 0, 1), (B_TREE, 3, 1, 1, 1),
+    (B_TREE, 1, -2, 0, 1), (B_RS_LAST, 0, 1), (B_ACT_ADD_Z, 1, 1), (B_RS_ACROSS, 1, 1, 2),
+    (B_TREE, 0, -3, 0, 1), (B_RS_SECOND, 1, 0), (B_TREE, 3, -1, 0, 1), (B_RS_RANK, 1, 3), (B_TREE, 1, 3, 1, 0),
+    (B_TREE, 2, 2, 1, 0), (B_RS_RANK, 0, 2), (B_TREE, 3, -1, 1, 0), (B_TREE, 0, 2, 1, 0), (B_TREE, 0, 2, 0, 1),
+    (B_ACT_ADD_Z, 1, 0), (B_TREE, 1, 1, 1, 1), (B_TREE, 3, -1, 1, 1), (B_TREE, 1, -3, 1, 0),
+    (B_TREE, 1, -3, 0, 0), (B_TREE, 3, 1, 1, 0), (B_TREE, 1, 0, 1, 1), (B_TREE, 1, -2, 1, 1),
+    (B_RS_FIRST, 1, 2), (B_TREE, 0, -2, 0, 1), (B_TREE, 1, -1, 0, 1), (B_TREE, 0, -1, 1, 1), (B_RS_RANK, 1, 6),
+    (B_RS_RANK, 1, 4), (B_ROWS_BACK, 0), (B_TREE, 0, 1, 0, 1), (B_TREE, 1, -1, 1, 0), (B_ROWS_BACK, 1),
+    (B_TREE, 0, 3, 0, 0), (B_RS_LAST, 0, 3), (B_TREE, 1, 3, 0, 0), (B_TREE, 1, 1, 1, 0), (B_TREE, 2, 1, 1, 0),
+    (B_ACT_SUM, 1, 1), (B_TREE, 1, 1, 0, 1), (B_TREE, 1, -2, 1, 0), (B_ACT_SUM, 1, 0), (B_RS_LAST, 0, 5),
+    (B_RS_RANK, 1, 2), (B_RS_LAST, 0, 7), (B_TREE, 0, -3, 0, 0), (B_TREE, 0, 2, 0, 0), (B_TREE, 3, 1, 0, 1),
+    (B_TREE, 1, 2, 0, 0), (B_TREE, 3, 0, 1, 1), (B_TREE, 2, -2, 1, 0), (B_TREE, 3, 2, 0, 0),
+    (B_TREE, 2, -3, 0, 0), (B_FINISH_OUTPUT,), (B_RS_LAST, 1, 3), (B_TREE, 0, -2, 1, 0), (B_TREE, 1, -2, 0, 0),
+    (B_TREE, 0, -1, 1, 0), (B_RS_LAST, 1, 6), (B_TREE, 0, -2, 0, 0), (B_TREE, 0, 0, 1, 0), (B_RS_RANK, 1, 1),
+    (B_RS_ACROSS, 0, 1, 2), (B_TREE, 2, -1, 0, 1), (B_TREE, 0, 1, 0, 0), (B_TREE, 1, 0, 1, 0),
+    (B_TREE, 0, -1, 0, 1), (B_RS_RANK, 0, 6), (B_TREE, 1, 0, 0, 1), (B_RS_LAST, 0, 4), (B_TREE, 3, -2, 0, 0),
+    (B_TREE, 3, 0, 0, 1), (B_TREE, 2, -2, 0, 0), (B_RS_RANK, 1, 5), (B_TREE, 2, 2, 0, 0), (B_TREE, 1, -1, 0, 0),
+    (B_TREE, 1, 1, 0, 0), (B_TREE, 0, 0, 0, 1), (B_RS_LAST, 0, 2), (B_TREE, 3, -1, 0, 0), (B_RS_LAST, 1, 1),
+    (B_TREE, 0, -1, 0, 0), (B_TREE, 3, 0, 1, 0), (B_ATTN_BACK,), (B_TREE, 2, -1, 0, 0), (B_RS_RANK, 1, 7),
+    (B_RS_LAST, 0, 6), (B_RS_SECOND, 1, 2), (B_RS_LAST, 1, 2), (B_TREE, 3, 1, 0, 0), (B_RS_SECOND, 0, 2),
+    (B_TREE, 2, 1, 0, 0), (B_RS_LAST, 1, 5), (B_TREE, 3, 0, 0, 0), (B_RS_LAST, 1, 4), (B_TREE, 1, 0, 0, 0),
+    (B_TREE, 0, 0, 0, 0), (B_TREE, 2, 0, 0, 0), (B_RS_LAST, 1, 7),
 ]
 
 
@@ -1501,7 +1501,7 @@
     pieces = [
         (qkv_grad, qkv_sum, 0, "zxy", slots_0),
         (qkv_grad, qkv_sum, 1, "zyx", slots_1),
-        (out_grad, attn_out_sum, 0, "xyz", slots_2),
+        (out_grad, attn_out_sum, 0, "zyx", slots_2),
         (out_grad, attn_out_sum, 1, "yxz", slots_3),
     ]
     events = sorted(
@@ -1980,15 +1980,22 @@
 
 
 def settle_kernel(*refs):
-    count = len(refs) // 2
+    count = (len(refs) - 1) // 3
     sems = refs[-1]
-    copies = [
-        pltpu.make_async_copy(refs[index], refs[count + index], sems.at[index]) for index in range(count)
+    stages = [
+        (
+            pltpu.make_async_copy(refs[index], refs[2 * count + index], sems.at[0, index]),
+            pltpu.make_async_copy(refs[2 * count + index], refs[count + index], sems.at[1, index]),
+        )
+        for index in range(count)
     ]
-    for copy in copies:
-        copy.start()
-    for copy in copies:
-        copy.wait()
+    for read, _ in stages:
+        read.start()
+    for read, write in stages:
+        read.wait()
+        write.start()
+    for _, write in stages:
+        write.wait()
 
 
 def settle(arrays):
@@ -1996,9 +2003,10 @@
     return pl.pallas_call(
         settle_kernel,
         out_shape=tuple(jax.ShapeDtypeStruct(array.shape, array.dtype) for array in arrays),
-        in_specs=[pl.BlockSpec(memory_space=pltpu.VMEM)] * len(arrays),
+        in_specs=[anywhere] * len(arrays),
         out_specs=(anywhere,) * len(arrays),
-        scratch_shapes=[pltpu.SemaphoreType.DMA((len(arrays),))],
+        scratch_shapes=[pltpu.VMEM(array.shape, array.dtype) for array in arrays]
+        + [pltpu.SemaphoreType.DMA((2, len(arrays)))],
         name="settle",
     )(*arrays)
 

time: 331 us -> 312 us (0.943)
  Pallas kernels: 329 us -> 310 us
    pallas_call x1, Pallas kernels: 169 us -> 157 us  [forward_gather(): pl.pallas_call(forward_kernel, out_shape=(jax.ShapeDtypeStruct((16, model...]
    pallas_call x1, Pallas kernels: 155 us -> 148 us  [backward_scatter(): pl.pallas_call(backward_kernel, out_shape=(jax.ShapeDtypeStruct(tokens.sh...]
where the time goes in v9:
time: 312 us
  Pallas kernels  310 us (99%)
    pallas_call x1, Pallas kernels, forward_gather(): pl.pallas_call(forward_kernel, out_shape=(jax.ShapeDtypeStruct((16, model...  157 us
    pallas_call x1, Pallas kernels, backward_scatter(): pl.pallas_call(backward_kernel, out_shape=(jax.ShapeDtypeStruct(tokens.sh...  148 us

profile of v9, /device:TPU:0, one launch (start us, length us, event | category | flops | bytes accessed | tf_op | source)
XLA Modules:
  0.0 311.8 jit_solution(10420387122619380543)
XLA Ops:
  1.3 157.2 %forward_gather.1 = (f32[16,1024]{1,0:T(8,128)}, f32[2,128,1024]{2,1,0:T(8,128)}, bf16[2,128,3072]{2,1,0:T(8,128)(2,1)}, bf16[2,128,1024]{2,1,0:T(8,128)(2,1)}, ...) custom-call(s32[1]{0:T(128)S(6)} %copy.18.valid_ref, ...), custom_call_target="tpu_custom_call" | custom-call | tf_op jit(solution)/shard_map/forward_gather/pallas_call | solution.py:1091
  158.4 148.2 %backward_scatter.1 = (bf16[128,2,1024]{2,1,0:T(2,128)(2,1)}, f32[128,2,1024]{2,1,0:T(2,128)}, f32[2,32]{1,0:T(2,128)}, f32[2,32]{1,0:T(2,128)}, f32[2,32,3072]{...) custom-call(bf16[128,2,1024]{2,1,0:T(2,128)(2,1)} %tokens_ref.3, ...), custom_call_target="tpu_custom_call" | custom-call | tf_op jit(solution)/shard_map/backward_scatter/pallas_call | solution.py:1891
  306.6 4.9 %settle.1 = (bf16[128,2,1024]{2,1,0:T(2,128)(2,1)}, f32[128,2,1024]{2,1,0:T(2,128)}, f32[2,32]{1,0:T(2,128)}, f32[2,32]{1,0:T(2,128)}, f32[2,32,3072]{2,1,0:T(8,...) custom-call(bf16[128,2,1024]{2,1,0:T(2,128)(2,1)} %get-tuple-element.46.refs_0_, ...), custom_call_target="tpu_custom_call" | custom-call | tf_op jit(solution)/shard_map/settle/pallas_call | solution.py:2003

commit v10 on v9

--- a/solution.py
+++ b/solution.py
@@ -500,69 +500,69 @@
     F_DOWN_GRAD,
 ) = range(20)
 FORWARD_STEPS = [
-    (F_TREE, 0, 0, 0, 0), (F_TREE, 2, 0, 0, 0), (F_COT,), (F_PARTS,), (F_TREE, 1, 0, 0, 0), (F_TO_RANK, 0, 3),
-    (F_OWN_ACROSS, 0, 8), (F_TREE, 4, 0, 0, 0), (F_TREE, 3, 0, 0, 0), (F_TREE, 2, 0, 1, 0),
-    (F_TREE, 0, -1, 0, 0), (F_TO_RANK, 0, 7), (F_TO_RANK, 1, 5), (F_TO_RANK, 0, 1), (F_TREE, 0, 0, 0, 1),
-    (F_GAINS,), (F_TO_RANK, 0, 6), (F_RANK_FAR, 0, 3), (F_TO_RANK, 0, 2), (F_TREE, 1, 1, 0, 0),
-    (F_TO_RANK, 0, 4), (F_TREE, 2, 1, 0, 0), (F_TREE, 2, -1, 0, 0), (F_TREE, 5, 0, 0, 0), (F_TREE, 2, 2, 0, 0),
-    (F_TREE, 3, 0, 0, 1), (F_TREE, 1, -1, 0, 0), (F_TO_RANK, 1, 2), (F_TREE, 0, -2, 0, 0), (F_OWN_ACROSS, 1, 8),
-    (F_TREE, 1, 0, 1, 0), (F_RANK_FAR, 0, 1), (F_TREE, 0, 1, 0, 0), (F_RANK_FAR, 0, 6), (F_TREE, 2, 1, 0, 1),
-    (F_TREE, 2, -2, 0, 0), (F_RANK_FAR, 0, 7), (F_TREE, 0, 2, 0, 0), (F_TREE, 1, -2, 0, 0),
-    (F_TREE, 0, -2, 0, 1), (F_OWN_FAR, 0, 8), (F_OWN_FAR, 0, 0), (F_TREE, 1, 2, 0, 0), (F_TREE, 0, -1, 0, 1),
-    (F_GRADS, 0), (F_TO_RANK, 1, 4), (F_TREE, 3, -1, 0, 0), (F_TREE, 4, 1, 0, 0), (F_RANK_FAR, 0, 2),
-    (F_TREE, 1, -2, 1, 0), (F_RANK_ACROSS, 0, 3), (F_TREE, 1, -3, 0, 0), (F_TREE, 2, 3, 0, 0),
-    (F_TREE, 3, 1, 0, 0), (F_TREE, 2, 2, 1, 0), (F_TREE, 2, -2, 1, 0), (F_TREE, 2, -3, 0, 0),
-    (F_TREE, 0, 0, 1, 1), (F_TREE, 5, 0, 1, 0), (F_TREE, 0, -1, 1, 1), (F_TREE, 0, 3, 0, 0),
-    (F_TREE, 2, 0, 0, 1), (F_TREE, 0, -3, 0, 0), (F_TREE, 3, 0, 1, 1), (F_TREE, 2, 1, 1, 0),
-    (F_TREE, 0, 2, 0, 1), (F_TREE, 1, 3, 0, 0), (F_TREE, 1, 2, 1, 0), (F_TREE, 0, 1, 1, 0), (F_ACT_X, 1, 0, 0),
-    (F_TO_RANK, 0, 5), (F_TREE, 2, -1, 1, 0), (F_TREE, 2, -2, 0, 1), (F_RANK_ACROSS, 0, 1),
-    (F_TREE, 0, 1, 0, 1), (F_RANK_FAR, 0, 4), (F_TREE, 5, 0, 0, 1), (F_TREE, 3, -2, 0, 0), (F_FAR_ACROSS, 0, 6),
-    (F_TREE, 1, 2, 0, 1), (F_TREE, 4, -1, 0, 0), (F_FAR_ACROSS, 0, 7), (F_TREE, 1, 1, 1, 0),
-    (F_TREE, 1, 3, 1, 0), (F_TREE, 4, 0, 1, 0), (F_TO_RANK, 1, 6), (F_TREE, 0, 1, 1, 1), (F_TREE, 2, -3, 0, 1),
-    (F_FAR_ACROSS, 0, 3), (F_ACT_C, 1, 0, 0, 1), (F_RANK_FAR, 0, 5), (F_TO_RANK, 1, 1), (F_TREE, 1, -1, 0, 1),
-    (F_TREE, 0, 3, 0, 1), (F_TREE, 2, -1, 0, 1), (F_RANK_ACROSS, 0, 5), (F_TREE, 3, 2, 0, 0),
-    (F_TREE, 3, -1, 1, 0), (F_TREE, 3, 1, 0, 1), (F_RANK_ACROSS, 0, 6), (F_TREE, 0, -2, 1, 1),
-    (F_TREE, 1, -3, 1, 0), (F_TREE, 5, 1, 0, 0), (F_TREE, 1, -1, 1, 0), (F_TREE, 1, -2, 1, 1),
-    (F_TREE, 5, 0, 1, 1), (F_ACT_Z, 1, 0), (F_TREE, 2, 3, 1, 0), (F_TREE, 0, 3, 1, 0), (F_TREE, 3, 3, 0, 0),
-    (F_FAR_ACROSS, 0, 4), (F_TREE, 4, -2, 0, 0), (F_TREE, 3, 0, 1, 0), (F_TREE, 0, -3, 0, 1),
-    (F_TREE, 0, 2, 1, 0), (F_TREE, 5, -1, 0, 0), (F_TREE, 1, 3, 1, 1), (F_TREE, 4, 2, 0, 0),
-    (F_TREE, 1, -3, 1, 1), (F_ACT_C, 1, 0, 1, 0), (F_TREE, 1, 0, 0, 1), (F_TREE, 0, -1, 1, 0),
-    (F_FAR_ACROSS, 0, 2), (F_OWN_FAR, 1, 8), (F_TREE, 2, -2, 1, 1), (F_TREE, 0, 0, 1, 0), (F_TREE, 0, 3, 1, 1),
-    (F_RANK_ACROSS, 0, 7), (F_TREE, 1, 0, 1, 1), (F_TREE, 4, 1, 0, 1), (F_RANK_FAR, 1, 4),
-    (F_TREE, 2, -1, 1, 1), (F_FAR_ACROSS, 0, 8), (F_GRADS, 1), (F_TREE, 3, -2, 0, 1), (F_TREE, 3, 1, 1, 1),
-    (F_TREE, 5, 1, 0, 1), (F_TREE, 3, 3, 1, 0), (F_TREE, 2, 1, 1, 1), (F_TREE, 2, -3, 1, 0),
-    (F_TREE, 1, 1, 0, 1), (F_TREE, 4, 2, 1, 0), (F_TO_RANK, 1, 3), (F_TREE, 4, 3, 0, 0), (F_TREE, 5, 1, 1, 0),
-    (F_TREE, 4, -3, 0, 0), (F_TREE, 5, -1, 0, 1), (F_TREE, 3, -2, 1, 0), (F_FAR_ACROSS, 0, 0),
-    (F_TREE, 3, -3, 0, 0), (F_TREE, 4, -1, 1, 0), (F_FAR_ACROSS, 0, 1), (F_TREE, 1, 2, 1, 1),
-    (F_TREE, 0, -2, 1, 0), (F_TREE, 2, 3, 1, 1), (F_FAR_ACROSS, 0, 5), (F_TREE, 1, 1, 1, 1),
-    (F_TREE, 2, 2, 1, 1), (F_TREE, 4, -2, 1, 0), (F_TREE, 2, -3, 1, 1), (F_TREE, 2, 2, 0, 1),
-    (F_TREE, 2, 3, 0, 1), (F_TREE, 2, 0, 1, 1), (F_TREE, 0, 2, 1, 1), (F_TREE, 4, -3, 1, 0),
-    (F_TREE, 4, -3, 0, 1), (F_TREE, 0, -3, 1, 1), (F_FAR_ACROSS, 1, 8), (F_RANK_FAR, 1, 2),
-    (F_TREE, 1, -1, 1, 1), (F_TREE, 0, -3, 1, 0), (F_TREE, 3, -1, 0, 1), (F_TREE, 1, -2, 0, 1),
-    (F_TREE, 4, 0, 1, 1), (F_TO_RANK, 1, 7), (F_OWN_ACROSS, 1, 0), (F_TREE, 1, 3, 0, 1), (F_ACT_X, 1, 0, 1),
-    (F_TREE, 3, 2, 0, 1), (F_TREE, 1, -3, 0, 1), (F_TREE_END, 0), (F_TREE, 4, -1, 0, 1), (F_TREE, 5, -1, 1, 0),
-    (F_TREE, 4, 3, 1, 0), (F_ATTENTION, 0), (F_TREE, 5, 1, 1, 1), (F_TREE, 3, 2, 1, 0), (F_TREE, 5, -2, 1, 0),
-    (F_TREE, 5, 2, 1, 0), (F_TREE, 5, -1, 1, 1), (F_TREE, 3, 3, 0, 1), (F_RANK_ACROSS, 0, 4),
-    (F_TREE, 3, -3, 0, 1), (F_TREE, 4, -1, 1, 1), (F_TREE, 4, 2, 0, 1), (F_TREE, 5, -2, 0, 1),
-    (F_TREE, 5, -2, 0, 0), (F_TREE, 4, 2, 1, 1), (F_TREE, 4, 1, 1, 0), (F_TREE, 4, -3, 1, 1), (F_ACT_Z, 0, 0),
-    (F_FAR_ACROSS, 1, 2), (F_RANK_ACROSS, 0, 2), (F_TREE, 5, 2, 0, 1), (F_RANK_FAR, 1, 7), (F_TREE, 5, 2, 0, 0),
-    (F_OWN_FAR, 1, 0), (F_OWN_ACROSS, 0, 0), (F_TREE, 5, -2, 1, 1), (F_RANK_ACROSS, 1, 4), (F_RANK_FAR, 1, 3),
-    (F_ACT_X, 0, 0, 0), (F_TREE, 5, 3, 0, 1), (F_RANK_ACROSS, 1, 2), (F_ACT_Z, 1, 1), (F_TREE, 4, 0, 0, 1),
-    (F_TREE, 3, 3, 1, 1), (F_TREE, 5, 2, 1, 1), (F_RANK_FAR, 1, 5), (F_TREE, 4, 3, 1, 1), (F_ACT_C, 1, 0, 1, 1),
-    (F_RANK_ACROSS, 1, 5), (F_FAR_ACROSS, 1, 4), (F_TREE, 5, -3, 0, 1), (F_TREE, 5, 3, 1, 0),
-    (F_TREE, 5, 3, 0, 0), (F_TREE, 3, -3, 1, 1), (F_RANK_FAR, 1, 6), (F_TREE, 4, -2, 1, 1), (F_RANK_FAR, 1, 1),
-    (F_ACT_C, 1, 0, 0, 0), (F_TREE, 3, -1, 1, 1), (F_TREE, 3, -2, 1, 1), (F_TREE, 3, 2, 1, 1), (F_FF_END, 0),
-    (F_ACT_C, 1, 1, 0, 0), (F_TREE, 4, 1, 1, 1), (F_TREE, 4, -2, 0, 1), (F_ACT_C, 0, 0, 1, 0),
-    (F_ACT_C, 0, 0, 0, 1), (F_BLOCK, 0, 2), (F_FAR_ACROSS, 1, 7), (F_TREE, 4, 3, 0, 1), (F_RANK_ACROSS, 1, 1),
-    (F_RANK_ACROSS, 1, 7), (F_TREE, 5, -3, 1, 0), (F_TREE, 3, -3, 1, 0), (F_TREE, 3, 1, 1, 0),
-    (F_TREE, 5, -3, 0, 0), (F_TREE, 5, 3, 1, 1), (F_BLOCK, 0, 1), (F_ACT_C, 0, 0, 0, 0), (F_RANK_ACROSS, 1, 3),
-    (F_TREE, 5, -3, 1, 1), (F_ACT_X, 1, 1, 0), (F_ACT_X, 0, 0, 1), (F_TREE_END, 1), (F_RANK_ACROSS, 1, 6),
-    (F_ATTENTION, 1), (F_FAR_ACROSS, 1, 3), (F_ACT_C, 1, 1, 0, 1), (F_ACT_X, 1, 1, 1), (F_FAR_ACROSS, 1, 0),
-    (F_BLOCK, 0, 0), (F_ACT_C, 0, 0, 1, 1), (F_BLOCK, 0, 3), (F_ACT_C, 1, 1, 1, 1), (F_FAR_ACROSS, 1, 1),
-    (F_FAR_ACROSS, 1, 5), (F_DOWN_GRAD, 0), (F_ACT_Z, 0, 1), (F_ACT_C, 0, 1, 0, 0), (F_ACT_X, 0, 1, 0),
-    (F_FAR_ACROSS, 1, 6), (F_GATE_GRAD, 0), (F_ACT_C, 1, 1, 1, 0), (F_ACT_C, 0, 1, 0, 1), (F_ACT_C, 0, 1, 1, 0),
-    (F_FF_END, 1), (F_BLOCK, 1, 1), (F_BLOCK, 1, 2), (F_ACT_X, 0, 1, 1), (F_BLOCK, 1, 0), (F_ACT_C, 0, 1, 1, 1),
-    (F_BLOCK, 1, 3), (F_DOWN_GRAD, 1), (F_GATE_GRAD, 1),
+    (F_TREE, 5, 0, 0, 0), (F_TREE, 4, 0, 0, 0), (F_TREE, 0, 0, 0, 0), (F_PARTS,), (F_TREE, 2, 0, 0, 0),
+    (F_TREE, 1, 0, 0, 0), (F_TREE, 0, 1, 0, 0), (F_TREE, 5, 0, 0, 1), (F_TO_RANK, 0, 2), (F_TREE, 0, -1, 0, 0),
+    (F_TO_RANK, 0, 7), (F_TREE, 0, 0, 0, 1), (F_TO_RANK, 0, 1), (F_TO_RANK, 0, 6), (F_TREE, 2, -1, 0, 0),
+    (F_TREE, 2, 1, 0, 0), (F_TREE, 0, -1, 0, 1), (F_TO_RANK, 0, 3), (F_OWN_ACROSS, 0, 8), (F_TREE, 0, -2, 0, 0),
+    (F_TREE, 4, -1, 0, 0), (F_TREE, 1, 1, 0, 0), (F_TREE, 2, 2, 0, 0), (F_TREE, 3, 0, 0, 0),
+    (F_TREE, 1, 0, 1, 0), (F_TREE, 4, 0, 1, 0), (F_RANK_FAR, 0, 3), (F_RANK_FAR, 0, 1), (F_TREE, 1, -1, 0, 0),
+    (F_TO_RANK, 1, 5), (F_OWN_ACROSS, 1, 8), (F_TREE, 1, 2, 0, 0), (F_TREE, 2, -2, 0, 0), (F_COT,),
+    (F_TREE, 3, 1, 0, 0), (F_OWN_FAR, 0, 0), (F_TREE, 0, 2, 0, 0), (F_TREE, 0, -1, 1, 1), (F_TREE, 3, -1, 0, 0),
+    (F_RANK_FAR, 0, 7), (F_GRADS, 0), (F_TREE, 1, -2, 0, 0), (F_TREE, 2, 2, 1, 0), (F_RANK_FAR, 0, 6),
+    (F_TREE, 0, -2, 0, 1), (F_TO_RANK, 0, 4), (F_TO_RANK, 0, 5), (F_TREE, 1, 1, 1, 0), (F_TREE, 0, -3, 0, 0),
+    (F_TREE, 2, 3, 0, 0), (F_OWN_FAR, 0, 8), (F_TREE, 5, 0, 1, 0), (F_TREE, 1, -2, 1, 0), (F_TREE, 2, -3, 0, 0),
+    (F_TREE, 0, -2, 1, 0), (F_RANK_ACROSS, 0, 3), (F_TREE, 0, -3, 0, 1), (F_TREE, 2, -2, 1, 0),
+    (F_TREE, 0, 2, 0, 1), (F_TREE, 0, 1, 1, 0), (F_TREE, 5, 1, 0, 1), (F_GAINS,), (F_RANK_ACROSS, 0, 6),
+    (F_RANK_FAR, 0, 2), (F_TREE, 2, 0, 1, 0), (F_TREE, 0, 1, 0, 1), (F_TREE, 3, -2, 0, 0),
+    (F_TREE, 1, -3, 0, 0), (F_TREE, 2, 1, 1, 0), (F_TREE, 1, 0, 1, 1), (F_TREE, 1, 3, 0, 0),
+    (F_TREE, 3, 0, 0, 1), (F_TREE, 2, 1, 0, 1), (F_TREE, 3, 1, 1, 0), (F_TREE, 0, 3, 0, 0),
+    (F_TREE, 3, 2, 0, 0), (F_RANK_FAR, 0, 4), (F_RANK_FAR, 0, 5), (F_FAR_ACROSS, 0, 0), (F_TREE, 2, 3, 0, 1),
+    (F_FAR_ACROSS, 0, 8), (F_TO_RANK, 1, 4), (F_TREE, 5, 1, 0, 0), (F_TREE, 0, 2, 1, 1), (F_TREE, 1, 3, 1, 0),
+    (F_TREE, 2, -3, 0, 1), (F_TREE, 1, 2, 1, 0), (F_TREE, 4, -2, 0, 0), (F_TREE, 5, 2, 0, 1),
+    (F_FAR_ACROSS, 0, 2), (F_TREE, 1, -1, 1, 0), (F_RANK_ACROSS, 0, 4), (F_TREE, 1, -3, 1, 0),
+    (F_TREE, 4, 1, 0, 0), (F_TREE, 1, 3, 1, 1), (F_TREE, 2, 0, 0, 1), (F_TO_RANK, 1, 6), (F_TREE, 0, 1, 1, 1),
+    (F_TREE, 3, -1, 1, 0), (F_TO_RANK, 1, 2), (F_TREE, 2, 3, 1, 0), (F_TREE, 0, -2, 1, 1),
+    (F_TREE, 2, -1, 1, 0), (F_TREE, 3, 0, 1, 1), (F_TREE, 4, -1, 1, 0), (F_TREE, 1, 2, 0, 1),
+    (F_TREE, 1, -3, 0, 1), (F_OWN_FAR, 1, 8), (F_TREE, 5, 0, 1, 1), (F_ACT_C, 1, 0, 0, 0), (F_TREE, 0, 3, 0, 1),
+    (F_TREE, 4, -3, 0, 0), (F_ACT_Z, 1, 0), (F_TREE, 5, 1, 1, 0), (F_TREE, 1, 2, 1, 1), (F_TREE, 5, 3, 0, 1),
+    (F_TREE, 3, 3, 0, 0), (F_TREE, 0, -1, 1, 0), (F_TREE, 2, -3, 1, 0), (F_TREE, 2, -2, 1, 1),
+    (F_TREE, 4, 0, 0, 1), (F_TREE, 1, 0, 0, 1), (F_TREE, 3, -1, 0, 1), (F_TO_RANK, 1, 1), (F_TREE, 4, 2, 0, 0),
+    (F_TREE, 5, -1, 0, 1), (F_GRADS, 1), (F_TREE, 0, -3, 1, 1), (F_TREE, 0, 2, 1, 0), (F_RANK_ACROSS, 0, 1),
+    (F_TREE, 4, 0, 1, 1), (F_TREE, 1, -1, 0, 1), (F_TREE, 5, 2, 0, 0), (F_TREE, 3, 2, 0, 1),
+    (F_FAR_ACROSS, 0, 6), (F_TREE, 2, -2, 0, 1), (F_ACT_C, 1, 1, 0, 0), (F_TREE, 4, -3, 1, 0),
+    (F_TREE, 1, 3, 0, 1), (F_TREE, 0, 0, 1, 0), (F_TREE, 3, -2, 1, 0), (F_RANK_ACROSS, 0, 5),
+    (F_TREE, 0, 3, 1, 1), (F_TREE, 5, -1, 1, 0), (F_RANK_FAR, 1, 2), (F_FAR_ACROSS, 0, 1), (F_TREE, 3, 3, 1, 0),
+    (F_FAR_ACROSS, 0, 3), (F_TREE, 2, 1, 1, 1), (F_TREE, 1, -2, 1, 1), (F_FAR_ACROSS, 0, 7),
+    (F_ACT_C, 1, 0, 1, 0), (F_RANK_ACROSS, 1, 2), (F_TREE, 5, -1, 0, 0), (F_TREE, 1, 1, 1, 1),
+    (F_TREE, 0, 0, 1, 1), (F_FAR_ACROSS, 0, 5), (F_TREE, 4, -3, 0, 1), (F_TO_RANK, 1, 3), (F_TREE, 2, 3, 1, 1),
+    (F_TREE, 1, -1, 1, 1), (F_TREE, 3, -3, 0, 0), (F_TREE, 4, 1, 1, 0), (F_TREE, 1, 1, 0, 1),
+    (F_TREE, 0, -3, 1, 0), (F_TREE, 4, -2, 1, 0), (F_TREE, 1, -3, 1, 1), (F_TREE, 0, 3, 1, 0),
+    (F_TREE, 2, 0, 1, 1), (F_TREE, 2, -1, 0, 1), (F_TREE, 1, -2, 0, 1), (F_TREE, 2, 2, 0, 1),
+    (F_TREE, 2, -3, 1, 1), (F_TREE, 4, 2, 1, 0), (F_TREE, 4, 3, 0, 0), (F_FAR_ACROSS, 1, 8),
+    (F_TREE, 2, -1, 1, 1), (F_TO_RANK, 1, 7), (F_TREE, 2, 2, 1, 1), (F_TREE, 4, 3, 1, 0), (F_RANK_FAR, 1, 4),
+    (F_RANK_ACROSS, 0, 7), (F_TREE, 5, -1, 1, 1), (F_RANK_ACROSS, 0, 2), (F_OWN_ACROSS, 1, 0),
+    (F_TREE, 4, -1, 0, 1), (F_TREE, 3, -1, 1, 1), (F_FAR_ACROSS, 0, 4), (F_TREE_END, 0), (F_TREE, 3, 1, 0, 1),
+    (F_TREE, 3, 0, 1, 0), (F_TREE, 3, -2, 0, 1), (F_ACT_X, 1, 0, 0), (F_ATTENTION, 0), (F_TREE, 5, 1, 1, 1),
+    (F_TREE, 4, -2, 1, 1), (F_TREE, 3, -3, 0, 1), (F_ACT_X, 1, 0, 1), (F_RANK_FAR, 1, 3), (F_TREE, 3, 3, 0, 1),
+    (F_TREE, 5, -2, 0, 0), (F_TREE, 4, 2, 1, 1), (F_TREE, 5, -2, 1, 1), (F_ACT_C, 1, 0, 0, 1),
+    (F_TREE, 5, -3, 0, 0), (F_TREE, 4, -3, 1, 1), (F_ACT_Z, 0, 0), (F_TREE, 4, 2, 0, 1), (F_TREE, 3, -3, 1, 0),
+    (F_TREE, 4, 1, 1, 1), (F_OWN_ACROSS, 0, 0), (F_ACT_X, 1, 1, 0), (F_TREE, 5, -2, 1, 0),
+    (F_ACT_C, 1, 0, 1, 1), (F_TREE, 5, 2, 1, 0), (F_TREE, 5, -2, 0, 1), (F_FAR_ACROSS, 1, 3), (F_ACT_Z, 1, 1),
+    (F_TREE, 5, 2, 1, 1), (F_FAR_ACROSS, 1, 2), (F_TREE, 5, -3, 1, 1), (F_RANK_FAR, 1, 1), (F_RANK_FAR, 1, 7),
+    (F_TREE, 3, 2, 1, 1), (F_RANK_ACROSS, 1, 3), (F_TREE, 5, 3, 1, 0), (F_TREE, 4, 1, 0, 1), (F_ACT_X, 0, 0, 0),
+    (F_TREE, 4, -1, 1, 1), (F_TREE, 4, -2, 0, 1), (F_RANK_FAR, 1, 6), (F_RANK_FAR, 1, 5), (F_TREE, 5, -3, 0, 1),
+    (F_ACT_C, 0, 0, 0, 0), (F_TREE, 3, 2, 1, 0), (F_TREE, 4, 3, 0, 1), (F_ACT_C, 1, 1, 1, 0),
+    (F_TREE, 3, -3, 1, 1), (F_TREE, 5, -3, 1, 0), (F_TREE, 3, 3, 1, 1), (F_ACT_C, 0, 0, 0, 1),
+    (F_TREE, 3, 1, 1, 1), (F_RANK_ACROSS, 1, 6), (F_TREE, 4, 3, 1, 1), (F_TREE, 5, 3, 1, 1),
+    (F_TREE, 3, -2, 1, 1), (F_FAR_ACROSS, 1, 4), (F_OWN_FAR, 1, 0), (F_FF_END, 0), (F_TREE, 5, 3, 0, 0),
+    (F_RANK_ACROSS, 1, 1), (F_BLOCK, 0, 2), (F_TREE_END, 1), (F_RANK_ACROSS, 1, 7), (F_ACT_X, 0, 0, 1),
+    (F_RANK_ACROSS, 1, 4), (F_ACT_C, 0, 0, 1, 0), (F_RANK_ACROSS, 1, 5), (F_ATTENTION, 1), (F_FAR_ACROSS, 1, 1),
+    (F_BLOCK, 0, 1), (F_ACT_X, 1, 1, 1), (F_FAR_ACROSS, 1, 7), (F_FAR_ACROSS, 1, 6), (F_ACT_C, 0, 0, 1, 1),
+    (F_BLOCK, 0, 3), (F_BLOCK, 0, 0), (F_FAR_ACROSS, 1, 5), (F_ACT_C, 1, 1, 0, 1), (F_FAR_ACROSS, 1, 0),
+    (F_DOWN_GRAD, 0), (F_ACT_Z, 0, 1), (F_ACT_C, 1, 1, 1, 1), (F_ACT_X, 0, 1, 0), (F_GATE_GRAD, 0),
+    (F_FF_END, 1), (F_ACT_C, 0, 1, 0, 1), (F_BLOCK, 1, 2), (F_ACT_C, 0, 1, 1, 0), (F_ACT_C, 0, 1, 0, 0),
+    (F_BLOCK, 1, 1), (F_ACT_X, 0, 1, 1), (F_BLOCK, 1, 0), (F_ACT_C, 0, 1, 1, 1), (F_BLOCK, 1, 3),
+    (F_DOWN_GRAD, 1), (F_GATE_GRAD, 1),
 ]
 
 
@@ -1198,49 +1198,49 @@
     B_FINISH_OUTPUT,
 ) = range(22)
 BACKWARD_STEPS = [
-    (B_ACT_CORE, 0, 0), (B_RS_ACROSS, 0, 0, 0), (B_RS_ACROSS, 0, 0, 1), (B_NORM_TURN,), (B_ACT_CORE, 0, 1),
-    (B_ACT_ADD_X, 0, 0, 1), (B_RS_ACROSS, 0, 1, 0), (B_ACT_ADD_X, 0, 0, 0), (B_ACT_ADD_X, 0, 1, 1),
-    (B_RS_ACROSS, 0, 0, 2), (B_RS_ACROSS, 1, 0, 1), (B_ACT_CORE, 1, 1), (B_SWAP_TURNED,), (B_RS_FIRST, 0, 0),
-    (B_ACT_ADD_X, 0, 1, 0), (B_ACT_ADD_Z, 0, 0), (B_RS_FIRST, 0, 1), (B_ACT_ADD_Z, 0, 1),
-    (B_RS_ACROSS, 1, 1, 1), (B_PROBS,), (B_ACT_SUM, 0, 0), (B_MID, 0), (B_OUT_W, 0), (B_RS_ACROSS, 1, 0, 0),
-    (B_TREE, 2, -3, 1, 1), (B_RS_FIRST, 0, 2), (B_ACT_CORE, 1, 0), (B_TREE, 2, 1, 1, 1), (B_TREE, 2, 0, 0, 1),
-    (B_RS_SECOND, 0, 0), (B_TREE, 2, 0, 1, 1), (B_RS_ACROSS, 0, 1, 1), (B_ACT_SUM, 0, 1), (B_TREE, 2, -1, 1, 1),
-    (B_MID, 1), (B_ACT_LOAD, 1), (B_ACT_ADD_X, 1, 1, 0), (B_RS_ACROSS, 1, 1, 0), (B_SCORES_BACK,),
-    (B_ACT_ADD_X, 1, 0, 0), (B_TREE, 2, 2, 1, 1), (B_OUT_W, 1), (B_SWAP_QKV,), (B_RS_FIRST, 1, 1),
-    (B_ACT_ADD_X, 1, 1, 1), (B_RS_SECOND, 0, 1), (B_QKV_W, 0), (B_TREE, 2, 0, 1, 0), (B_TREE, 2, -1, 1, 0),
-    (B_RS_RANK, 0, 4), (B_TREE, 3, -3, 1, 1), (B_QKV_W, 1), (B_TREE, 0, 1, 1, 1), (B_RS_ACROSS, 1, 0, 2),
-    (B_TREE, 1, 2, 1, 1), (B_TREE, 0, -2, 1, 1), (B_TREE, 3, 3, 1, 0), (B_TREE, 0, -3, 1, 1),
-    (B_TREE, 3, 3, 0, 1), (B_TREE, 3, -2, 0, 1), (B_TREE, 3, -3, 0, 1), (B_TREE, 1, -1, 1, 1),
-    (B_TREE, 2, 3, 0, 1), (B_TREE, 3, 2, 1, 0), (B_TREE, 2, 3, 1, 1), (B_RS_RANK, 0, 7), (B_TREE, 3, -3, 1, 0),
-    (B_RS_RANK, 0, 5), (B_ACT_ADD_X, 1, 0, 1), (B_RS_RANK, 0, 3), (B_TREE, 3, 3, 0, 0), (B_TREE, 1, 3, 0, 1),
-    (B_TREE, 3, -2, 1, 0), (B_TREE, 0, 3, 1, 1), (B_TREE, 3, -3, 0, 0), (B_TREE, 3, 2, 0, 1),
-    (B_TREE, 0, -3, 1, 0), (B_TREE, 1, 3, 1, 1), (B_TREE, 3, -2, 1, 1), (B_TREE, 0, 3, 1, 0),
-    (B_TREE, 2, -3, 1, 0), (B_TREE, 3, 3, 1, 1), (B_TREE, 2, 1, 0, 1), (B_TREE, 2, 3, 1, 0),
-    (B_TREE, 0, 2, 1, 1), (B_TREE, 2, -2, 1, 1), (B_TREE, 2, -2, 0, 1), (B_TREE, 2, 2, 0, 1),
-    (B_TREE, 0, 0, 1, 1), (B_TREE, 2, -3, 0, 1), (B_TREE, 0, 1, 1, 0), (B_RS_FIRST, 1, 0), (B_TREE, 0, 3, 0, 1),
-    (B_TREE, 3, 2, 1, 1), (B_TREE, 1, -3, 1, 1), (B_RS_SECOND, 1, 1), (B_TREE, 1, -3, 0, 1),
-    (B_TREE, 1, 2, 1, 0), (B_TREE, 1, 2, 0, 1), (B_TREE, 2, 3, 0, 0), (B_RS_RANK, 0, 1), (B_TREE, 3, 1, 1, 1),
-    (B_TREE, 1, -2, 0, 1), (B_RS_LAST, 0, 1), (B_ACT_ADD_Z, 1, 1), (B_RS_ACROSS, 1, 1, 2),
-    (B_TREE, 0, -3, 0, 1), (B_RS_SECOND, 1, 0), (B_TREE, 3, -1, 0, 1), (B_RS_RANK, 1, 3), (B_TREE, 1, 3, 1, 0),
-    (B_TREE, 2, 2, 1, 0), (B_RS_RANK, 0, 2), (B_TREE, 3, -1, 1, 0), (B_TREE, 0, 2, 1, 0), (B_TREE, 0, 2, 0, 1),
-    (B_ACT_ADD_Z, 1, 0), (B_TREE, 1, 1, 1, 1), (B_TREE, 3, -1, 1, 1), (B_TREE, 1, -3, 1, 0),
-    (B_TREE, 1, -3, 0, 0), (B_TREE, 3, 1, 1, 0), (B_TREE, 1, 0, 1, 1), (B_TREE, 1, -2, 1, 1),
-    (B_RS_FIRST, 1, 2), (B_TREE, 0, -2, 0, 1), (B_TREE, 1, -1, 0, 1), (B_TREE, 0, -1, 1, 1), (B_RS_RANK, 1, 6),
-    (B_RS_RANK, 1, 4), (B_ROWS_BACK, 0), (B_TREE, 0, 1, 0, 1), (B_TREE, 1, -1, 1, 0), (B_ROWS_BACK, 1),
-    (B_TREE, 0, 3, 0, 0), (B_RS_LAST, 0, 3), (B_TREE, 1, 3, 0, 0), (B_TREE, 1, 1, 1, 0), (B_TREE, 2, 1, 1, 0),
-    (B_ACT_SUM, 1, 1), (B_TREE, 1, 1, 0, 1), (B_TREE, 1, -2, 1, 0), (B_ACT_SUM, 1, 0), (B_RS_LAST, 0, 5),
-    (B_RS_RANK, 1, 2), (B_RS_LAST, 0, 7), (B_TREE, 0, -3, 0, 0), (B_TREE, 0, 2, 0, 0), (B_TREE, 3, 1, 0, 1),
-    (B_TREE, 1, 2, 0, 0), (B_TREE, 3, 0, 1, 1), (B_TREE, 2, -2, 1, 0), (B_TREE, 3, 2, 0, 0),
-    (B_TREE, 2, -3, 0, 0), (B_FINISH_OUTPUT,), (B_RS_LAST, 1, 3), (B_TREE, 0, -2, 1, 0), (B_TREE, 1, -2, 0, 0),
-    (B_TREE, 0, -1, 1, 0), (B_RS_LAST, 1, 6), (B_TREE, 0, -2, 0, 0), (B_TREE, 0, 0, 1, 0), (B_RS_RANK, 1, 1),
-    (B_RS_ACROSS, 0, 1, 2), (B_TREE, 2, -1, 0, 1), (B_TREE, 0, 1, 0, 0), (B_TREE, 1, 0, 1, 0),
-    (B_TREE, 0, -1, 0, 1), (B_RS_RANK, 0, 6), (B_TREE, 1, 0, 0, 1), (B_RS_LAST, 0, 4), (B_TREE, 3, -2, 0, 0),
-    (B_TREE, 3, 0, 0, 1), (B_TREE, 2, -2, 0, 0), (B_RS_RANK, 1, 5), (B_TREE, 2, 2, 0, 0), (B_TREE, 1, -1, 0, 0),
-    (B_TREE, 1, 1, 0, 0), (B_TREE, 0, 0, 0, 1), (B_RS_LAST, 0, 2), (B_TREE, 3, -1, 0, 0), (B_RS_LAST, 1, 1),
-    (B_TREE, 0, -1, 0, 0), (B_TREE, 3, 0, 1, 0), (B_ATTN_BACK,), (B_TREE, 2, -1, 0, 0), (B_RS_RANK, 1, 7),
-    (B_RS_LAST, 0, 6), (B_RS_SECOND, 1, 2), (B_RS_LAST, 1, 2), (B_TREE, 3, 1, 0, 0), (B_RS_SECOND, 0, 2),
-    (B_TREE, 2, 1, 0, 0), (B_RS_LAST, 1, 5), (B_TREE, 3, 0, 0, 0), (B_RS_LAST, 1, 4), (B_TREE, 1, 0, 0, 0),
-    (B_TREE, 0, 0, 0, 0), (B_TREE, 2, 0, 0, 0), (B_RS_LAST, 1, 7),
+    (B_ACT_CORE, 0, 0), (B_RS_ACROSS, 0, 0, 0), (B_ACT_ADD_X, 0, 0, 1), (B_RS_ACROSS, 0, 0, 1),
+    (B_RS_ACROSS, 0, 1, 0), (B_ACT_CORE, 0, 1), (B_ACT_CORE, 1, 1), (B_NORM_TURN,), (B_ACT_ADD_X, 0, 0, 0),
+    (B_ACT_ADD_X, 0, 1, 1), (B_RS_ACROSS, 0, 1, 1), (B_RS_FIRST, 0, 0), (B_ACT_ADD_Z, 0, 0), (B_RS_FIRST, 0, 1),
+    (B_ACT_ADD_Z, 0, 1), (B_RS_ACROSS, 0, 0, 2), (B_PROBS,), (B_SWAP_TURNED,), (B_ACT_ADD_X, 0, 1, 0),
+    (B_ACT_CORE, 1, 0), (B_ACT_SUM, 0, 0), (B_RS_ACROSS, 1, 0, 2), (B_MID, 0), (B_RS_ACROSS, 1, 0, 1),
+    (B_OUT_W, 0), (B_TREE, 2, -1, 1, 1), (B_TREE, 2, -3, 1, 1), (B_TREE, 2, 2, 1, 1), (B_RS_FIRST, 0, 2),
+    (B_TREE, 2, 3, 1, 1), (B_TREE, 2, 0, 0, 1), (B_TREE, 2, 1, 0, 1), (B_ACT_SUM, 0, 1), (B_TREE, 2, 3, 0, 1),
+    (B_TREE, 2, 0, 1, 1), (B_TREE, 2, 1, 1, 1), (B_MID, 1), (B_ACT_LOAD, 1), (B_RS_ACROSS, 1, 0, 0),
+    (B_ACT_ADD_X, 1, 1, 0), (B_ACT_ADD_X, 1, 0, 0), (B_SCORES_BACK,), (B_SWAP_QKV,), (B_OUT_W, 1),
+    (B_RS_FIRST, 1, 1), (B_ACT_ADD_X, 1, 1, 1), (B_RS_ACROSS, 1, 1, 0), (B_QKV_W, 0), (B_TREE, 3, 2, 0, 1),
+    (B_TREE, 0, -1, 1, 1), (B_RS_SECOND, 0, 1), (B_RS_SECOND, 0, 0), (B_ACT_ADD_X, 1, 0, 1), (B_QKV_W, 1),
+    (B_RS_RANK, 0, 3), (B_TREE, 3, 3, 0, 1), (B_TREE, 2, -3, 1, 0), (B_RS_ACROSS, 1, 1, 1),
+    (B_TREE, 2, 3, 1, 0), (B_ROWS_BACK, 0), (B_TREE, 1, -3, 1, 1), (B_TREE, 0, 2, 1, 1), (B_TREE, 1, 2, 1, 1),
+    (B_TREE, 0, 3, 1, 1), (B_TREE, 2, -2, 1, 1), (B_RS_RANK, 0, 7), (B_TREE, 1, -2, 1, 1),
+    (B_TREE, 3, -2, 1, 1), (B_TREE, 3, 3, 1, 0), (B_TREE, 0, -2, 1, 1), (B_TREE, 0, 0, 1, 1),
+    (B_TREE, 3, 2, 1, 0), (B_RS_FIRST, 1, 0), (B_TREE, 1, -1, 0, 1), (B_TREE, 3, 3, 1, 1),
+    (B_TREE, 3, -3, 1, 1), (B_TREE, 0, -3, 1, 1), (B_TREE, 3, -2, 1, 0), (B_TREE, 1, -3, 0, 1),
+    (B_TREE, 3, 2, 1, 1), (B_TREE, 3, -3, 1, 0), (B_TREE, 3, -1, 1, 0), (B_TREE, 0, 2, 1, 0),
+    (B_TREE, 3, -3, 0, 1), (B_RS_SECOND, 1, 1), (B_TREE, 3, -2, 0, 1), (B_TREE, 3, -3, 0, 0),
+    (B_TREE, 0, 3, 0, 1), (B_TREE, 1, -1, 1, 1), (B_TREE, 1, 3, 1, 1), (B_TREE, 0, -1, 1, 0),
+    (B_TREE, 0, 3, 1, 0), (B_TREE, 2, 3, 0, 0), (B_TREE, 1, 0, 1, 1), (B_TREE, 1, 1, 0, 1),
+    (B_TREE, 2, 2, 1, 0), (B_ACT_ADD_Z, 1, 0), (B_ACT_ADD_Z, 1, 1), (B_TREE, 3, -1, 1, 1), (B_RS_LAST, 0, 7),
+    (B_TREE, 2, -2, 1, 0), (B_TREE, 2, -2, 0, 1), (B_TREE, 0, 3, 0, 0), (B_TREE, 2, -1, 1, 0),
+    (B_RS_SECOND, 1, 0), (B_TREE, 2, -3, 0, 1), (B_TREE, 1, 3, 0, 1), (B_RS_RANK, 1, 3), (B_TREE, 1, 3, 1, 0),
+    (B_TREE, 3, 1, 1, 0), (B_RS_RANK, 1, 1), (B_TREE, 1, -3, 1, 0), (B_TREE, 1, 1, 1, 1), (B_RS_RANK, 1, 5),
+    (B_TREE, 3, 1, 0, 1), (B_TREE, 0, -3, 0, 1), (B_TREE, 3, -2, 0, 0), (B_RS_FIRST, 1, 2),
+    (B_TREE, 0, 1, 1, 1), (B_TREE, 1, -2, 0, 1), (B_TREE, 3, 1, 1, 1), (B_TREE, 0, -3, 1, 0), (B_RS_RANK, 1, 2),
+    (B_TREE, 0, 2, 0, 1), (B_ROWS_BACK, 1), (B_RS_RANK, 0, 5), (B_TREE, 3, 3, 0, 0), (B_RS_ACROSS, 0, 1, 2),
+    (B_TREE, 1, 3, 0, 0), (B_TREE, 0, 1, 1, 0), (B_RS_RANK, 0, 1), (B_RS_RANK, 0, 4), (B_RS_RANK, 1, 4),
+    (B_TREE, 0, -2, 0, 1), (B_TREE, 2, 2, 0, 1), (B_TREE, 1, -2, 1, 0), (B_TREE, 3, -1, 0, 1),
+    (B_TREE, 0, -2, 1, 0), (B_TREE, 2, -3, 0, 0), (B_TREE, 1, 2, 1, 0), (B_TREE, 3, 0, 1, 1), (B_ACT_SUM, 1, 0),
+    (B_TREE, 1, 2, 0, 1), (B_RS_ACROSS, 1, 1, 2), (B_RS_RANK, 0, 6), (B_TREE, 0, -3, 0, 0),
+    (B_TREE, 1, -3, 0, 0), (B_TREE, 0, 2, 0, 0), (B_RS_RANK, 0, 2), (B_RS_RANK, 1, 6), (B_ACT_SUM, 1, 1),
+    (B_TREE, 1, -1, 1, 0), (B_TREE, 2, 1, 1, 0), (B_FINISH_OUTPUT,), (B_TREE, 2, 2, 0, 0), (B_RS_LAST, 0, 4),
+    (B_RS_LAST, 0, 5), (B_TREE, 0, 1, 0, 1), (B_RS_LAST, 0, 3), (B_TREE, 0, -1, 0, 1), (B_TREE, 1, -2, 0, 0),
+    (B_RS_LAST, 1, 1), (B_TREE, 0, -2, 0, 0), (B_TREE, 3, 2, 0, 0), (B_RS_SECOND, 0, 2), (B_RS_LAST, 1, 2),
+    (B_TREE, 1, 1, 1, 0), (B_RS_LAST, 1, 3), (B_TREE, 2, -1, 0, 1), (B_TREE, 0, 0, 0, 1), (B_TREE, 1, 0, 0, 1),
+    (B_TREE, 2, 0, 1, 0), (B_TREE, 2, -2, 0, 0), (B_RS_LAST, 1, 4), (B_RS_SECOND, 1, 2), (B_TREE, 1, 2, 0, 0),
+    (B_RS_LAST, 0, 2), (B_TREE, 3, 1, 0, 0), (B_TREE, 3, -1, 0, 0), (B_TREE, 3, 0, 1, 0), (B_TREE, 1, -1, 0, 0),
+    (B_TREE, 1, 1, 0, 0), (B_RS_RANK, 1, 7), (B_TREE, 1, 0, 1, 0), (B_RS_LAST, 0, 1), (B_TREE, 0, 1, 0, 0),
+    (B_TREE, 3, 0, 0, 1), (B_TREE, 0, 0, 1, 0), (B_TREE, 0, -1, 0, 0), (B_RS_LAST, 1, 5), (B_TREE, 2, 1, 0, 0),
+    (B_RS_LAST, 0, 6), (B_ATTN_BACK,), (B_RS_LAST, 1, 6), (B_TREE, 2, -1, 0, 0), (B_TREE, 1, 0, 0, 0),
+    (B_RS_LAST, 1, 7), (B_TREE, 0, 0, 0, 0), (B_TREE, 2, 0, 0, 0), (B_TREE, 3, 0, 0, 0),
 ]
 
 

time: 312 us -> 310 us (level)
  no operation moved by 1% of the time
where the time goes in v10:
time: 310 us; the launch traced here: 309 us
  Pallas kernels  308 us (99%)
    pallas_call x1, Pallas kernels, forward_gather(): pl.pallas_call(forward_kernel, out_shape=(jax.ShapeDtypeStruct((16, model...  156 us
    pallas_call x1, Pallas kernels, backward_scatter(): pl.pallas_call(backward_kernel, out_shape=(jax.ShapeDtypeStruct(tokens.sh...  147 us

profile of v10, /device:TPU:0, one launch (start us, length us, event | category | flops | bytes accessed | tf_op | source)
XLA Modules:
  0.0 309.2 jit_solution(1240983292030809840)
XLA Ops:
  1.3 156.2 %forward_gather.1 = (f32[16,1024]{1,0:T(8,128)}, f32[2,128,1024]{2,1,0:T(8,128)}, bf16[2,128,3072]{2,1,0:T(8,128)(2,1)}, bf16[2,128,1024]{2,1,0:T(8,128)(2,1)}, ...) custom-call(s32[1]{0:T(128)S(6)} %copy.18.valid_ref, ...), custom_call_target="tpu_custom_call" | custom-call | tf_op jit(solution)/shard_map/forward_gather/pallas_call | solution.py:1091
  157.5 146.6 %backward_scatter.1 = (bf16[128,2,1024]{2,1,0:T(2,128)(2,1)}, f32[128,2,1024]{2,1,0:T(2,128)}, f32[2,32]{1,0:T(2,128)}, f32[2,32]{1,0:T(2,128)}, f32[2,32,3072]{...) custom-call(bf16[128,2,1024]{2,1,0:T(2,128)(2,1)} %tokens_ref.3, ...), custom_call_target="tpu_custom_call" | custom-call | tf_op jit(solution)/shard_map/backward_scatter/pallas_call | solution.py:1891
  304.1 4.9 %settle.1 = (bf16[128,2,1024]{2,1,0:T(2,128)(2,1)}, f32[128,2,1024]{2,1,0:T(2,128)}, f32[2,32]{1,0:T(2,128)}, f32[2,32]{1,0:T(2,128)}, f32[2,32,3072]{2,1,0:T(8,...) custom-call(bf16[128,2,1024]{2,1,0:T(2,128)(2,1)} %get-tuple-element.46.refs_0_, ...), custom_call_target="tpu_custom_call" | custom-call | tf_op jit(solution)/shard_map/settle/pallas_call | solution.py:2003

commit v11 on v10

--- a/solution.py
+++ b/solution.py
@@ -1014,14 +1014,14 @@
         def gate_up_tile(columns):
             gate_up_stage[:, columns] = dot_grad(rows_buf[s], d_gate_up[:, columns]).astype(BF16)
 
-        tile_loop(2 * split, 256, gate_up_tile)
+        tile_loop(2 * split, 1024, gate_up_tile)
         stage_out(s, 2)
 
     def down_weights_grad(s):
         def down_tile(columns):
             down_stage[:, columns] = dot_grad(hidden[...], grads_buf[s, :, columns]).astype(BF16)
 
-        tile_loop(model, 256, down_tile)
+        tile_loop(model, 1024, down_tile)
         stage_out(s, 3)
 
     def stages_end():
@@ -1746,7 +1746,7 @@
                 attn_turned[p].reshape(half, 2 * act_height), d_qkv[p, :, columns]
             ).astype(BF16)
 
-        tile_loop(3 * model, 256, tile)
+        tile_loop(3 * model, 512, tile)
 
     def rows_back(p):
         for tile in range(tile_count):

time: 310 us -> 305 us (0.984)
  Pallas kernels: 308 us -> 303 us
where the time goes in v11:
time: 305 us
  Pallas kernels  303 us (99%)
    pallas_call x1, Pallas kernels, forward_gather(): pl.pallas_call(forward_kernel, out_shape=(jax.ShapeDtypeStruct((16, model...  154 us
    pallas_call x1, Pallas kernels, backward_scatter(): pl.pallas_call(backward_kernel, out_shape=(jax.ShapeDtypeStruct(tokens.sh...  145 us

profile of v11, /device:TPU:0, one launch (start us, length us, event | category | flops | bytes accessed | tf_op | source)
XLA Modules:
  0.0 305.0 jit_solution(2186767966046081602)
XLA Ops:
  1.3 153.6 %forward_gather.1 = (f32[16,1024]{1,0:T(8,128)}, f32[2,128,1024]{2,1,0:T(8,128)}, bf16[2,128,3072]{2,1,0:T(8,128)(2,1)}, bf16[2,128,1024]{2,1,0:T(8,128)(2,1)}, ...) custom-call(s32[1]{0:T(128)S(6)} %copy.18.valid_ref, ...), custom_call_target="tpu_custom_call" | custom-call | tf_op jit(solution)/shard_map/forward_gather/pallas_call | solution.py:1091
  154.9 144.9 %backward_scatter.1 = (bf16[128,2,1024]{2,1,0:T(2,128)(2,1)}, f32[128,2,1024]{2,1,0:T(2,128)}, f32[2,32]{1,0:T(2,128)}, f32[2,32]{1,0:T(2,128)}, f32[2,32,3072]{...) custom-call(bf16[128,2,1024]{2,1,0:T(2,128)(2,1)} %tokens_ref.3, ...), custom_call_target="tpu_custom_call" | custom-call | tf_op jit(solution)/shard_map/backward_scatter/pallas_call | solution.py:1891
  299.9 4.9 %settle.1 = (bf16[128,2,1024]{2,1,0:T(2,128)(2,1)}, f32[128,2,1024]{2,1,0:T(2,128)}, f32[2,32]{1,0:T(2,128)}, f32[2,32]{1,0:T(2,128)}, f32[2,32,3072]{2,1,0:T(8,...) custom-call(bf16[128,2,1024]{2,1,0:T(2,128)(2,1)} %get-tuple-element.46.refs_0_, ...), custom_call_target="tpu_custom_call" | custom-call | tf_op jit(solution)/shard_map/settle/pallas_call | solution.py:2003
